TPU v7x, 32 devices: a whole 2x2x4 slice. The times are simulated.
32 devices in a mesh: row: 16 (over z, y, core), col: 2 (over x).
Axes of the slice: x: 2, y: 2, z: 4, core: 2. Of those that a mesh axis runs over, the one named last changes fastest.
Arguments:
- frames: bfloat16 [64, 3, 12288], P('col', None, 'row'), may hold values from -6 to 6
- rotations: float32 [3, 3, 64], replicated, may hold values from -1 to 1, as said below
- inverse_cov: float32 [12288, 12288], P('row', 'col'), may hold values from -1 to 11, as said below
Outputs:
- covariance: float32 [12288, 12288], P('row', 'col')
- fitted_rotations: float32 [3, 3, 64], P(None, None, 'col')
Inputs may be any that keep to these rules, and one draw needn't show every extreme that they name: `rotations`: each frame's 3 x 3 matrix is a rotation. `inverse_cov`: symmetric.
All inputs are finite; a program needn't handle non-finite values.
Results may differ from a plain program's by a relative error of at most 0.00031.
Values may be sent and summed in bfloat16 or wider, within the bound.
No kernel may reach another device: no remote copies, remote signals or barrier semaphores. Data moves between devices by JAX's collectives and lax.ppermute only.
A program may use at most 128 MiB of HBM per device.

v0:
```python
import jax
import jax.numpy as jnp
from jax import lax
from jax.sharding import PartitionSpec as P

POLAR = 12


def orthogonalize(fitted):
    scaling = jnp.sqrt(1.0 + jnp.sum(fitted * fitted, axis=(0, 1)))
    current = jnp.transpose(fitted, (1, 0, 2)) / scaling
    for sweep in range(POLAR):
        square = jnp.einsum("ijf,kjf->ikf", current, current, precision=lax.Precision.HIGHEST)
        cubed_term = jnp.einsum("ikf,klf->ilf", square, current, precision=lax.Precision.HIGHEST)
        current = 1.5 * current - 0.5 * cubed_term
    return current


def deviations_of(transforms, coords_half, centre_block):
    moved = jnp.einsum(
        "klf,fla->fka", transforms, coords_half.astype(jnp.float32), precision=lax.Precision.HIGHEST
    )
    values = (moved - centre_block[None]).astype(jnp.bfloat16)
    return values.reshape(values.shape[0] * 3, values.shape[2])


def tile_block(rows_operand, column_panel):
    return lax.dot_general(
        rows_operand, column_panel, (((0,), (0,)), ((), ())), preferred_element_type=jnp.float32
    )


def per_device(frames, rotations, inverse_cov):
    col_width = inverse_cov.shape[1]
    col_count = lax.axis_size("col")
    col_index = lax.axis_index("col")
    frame_total = frames.shape[0] * col_count
    offset = col_index * frames.shape[0]
    local_rot = lax.dynamic_slice_in_dim(rotations, offset, frames.shape[0], 2)
    coords = frames.astype(jnp.float32)
    partial_value = jnp.einsum("klf,fla->ka", local_rot, coords, precision=lax.Precision.HIGHEST)
    centre_rows = lax.psum(partial_value, "col") / frame_total
    centre_all = lax.all_gather(centre_rows, "row", axis=1, tiled=True)
    centre_cols = lax.dynamic_slice_in_dim(centre_all, col_index * col_width, col_width, 1)
    local_weight = lax.dot_general(
        centre_cols, inverse_cov, (((1,), (1,)), ((), ())), precision=lax.Precision.HIGHEST
    )
    weighted = lax.psum(local_weight, "col")
    fit_part = jnp.einsum("fka,la->klf", coords, weighted, precision=lax.Precision.HIGHEST)
    fitted = lax.psum(fit_part, "row")
    transforms = orthogonalize(fitted)
    local_dev = deviations_of(transforms, frames, centre_rows)
    rows_operand = lax.all_gather(local_dev, "col", axis=0, tiled=True)
    dev_atoms = lax.all_gather(local_dev, "row", axis=1, tiled=True)
    column_panel = lax.all_to_all(dev_atoms, "col", split_axis=1, concat_axis=0, tiled=True)
    covariance = tile_block(rows_operand, column_panel) / (3 * frame_total)
    return (covariance, transforms)


def solution(mesh):
    placed = (P("col", None, "row"), P(), P("row", "col"))
    return jax.shard_map(
        per_device,
        mesh=mesh,
        in_specs=placed,
        out_specs=(P("row", "col"), P(None, None, "col")),
        check_vma=False,
    )
```

profile of v0, /device:TPU:0, one launch (start us, length us, event | category | flops | bytes accessed | tf_op | source)
XLA Modules:
  0.0 203.4 jit_solution(15822696244282940801)
XLA Ops:
  7.2 0.8 constant_dynamic-slice_fusion
  8.1 0.2 convolution_bitcast_fusion.12
  8.3 9.6 %psum.21 = f32[3,768]{1,0:T(4,128)S(1)} all-reduce(f32[3,768]{1,0:T(4,128)S(1)} %convolution_bitcast_fusion.12), channel_id=1, replica_groups=mesh['row'=16,'col'=2] {'col'}, use_global_device_ids=true, to_apply=%region_0.0 | all-reduce | flops 2304 | bytes 18432 | tf_op jit(solution)/shard_map/psum | solution.py:42
  17.9 22.1 %all_gather.9 = f32[3,12288]{1,0:T(4,128)S(1)} all-gather(f32[3,768]{1,0:T(4,128)S(1)} %broadcast_multiply_fusion), channel_id=1, replica_groups=mesh['row'=16,'col'=2] {'row'}, dimensions={1}, use_global_device_ids=true | all-gather | bytes 156672 | tf_op jit(solution)/shard_map/all_gather | solution.py:43
  40.0 18.1 %fusion.2 = f32[3,768]{1,0:T(4,128)S(1)} fusion(f32[768,6144]{1,0:T(8,128)} %param.5, f32[3,12288]{1,0:T(4,128)S(1)} %all_gather.9, s32[]{:T(128)S(6)} %select_n.7), kind=kOutput, calls=%fused_computation.19 | convolution fusion | flops 169869312 | bytes 18981892 | tf_op jit(solution)/shard_map/dot_general | solution.py:45
  58.2 7.1 %psum.22 = f32[3,768]{1,0:T(4,128)S(1)} all-reduce(f32[3,768]{1,0:T(4,128)S(1)} %fusion.2), channel_id=1, replica_groups=mesh['row'=16,'col'=2] {'col'}, use_global_device_ids=true, to_apply=%region_1.0 | all-reduce | flops 2304 | bytes 18432 | tf_op jit(solution)/shard_map/psum | solution.py:48
  65.3 0.3 convolution_bitcast_fusion.13
  65.6 30.2 %psum.23 = f32[3,3,32]{2,1,0:T(4,128)S(1)} all-reduce(f32[3,3,32]{2,1,0:T(4,128)S(1)} %convolution_bitcast_fusion.13), channel_id=1, replica_groups=mesh['row'=16,'col'=2] {'row'}, use_global_device_ids=true, to_apply=%region_2.0 | all-reduce | flops 288 | bytes 2304 | tf_op jit(solution)/shard_map/psum | solution.py:50
  96.0 0.4 convolution_bitcast_fusion.11
  96.4 0.3 fusion.7
  96.9 0.1 copy.38
  97.0 0.4 convolution_bitcast_fusion.10
  97.4 0.3 fusion.8
  97.9 0.1 copy.40
  98.0 0.4 convolution_bitcast_fusion.9
  98.4 0.3 fusion.9
  98.9 0.1 copy.42
  99.0 0.4 convolution_bitcast_fusion.8
  99.4 0.3 fusion.10
  99.9 0.1 copy.44
  100.0 0.4 convolution_bitcast_fusion.7
  100.4 0.3 fusion.11
  100.9 0.1 copy.46
  101.0 0.4 convolution_bitcast_fusion.6
  101.5 0.3 fusion.12
  101.9 0.1 copy.48
  102.0 0.4 convolution_bitcast_fusion.5
  102.5 0.3 fusion.13
  102.9 0.1 copy.50
  103.0 0.4 convolution_bitcast_fusion.4
  103.5 0.3 fusion.14
  104.1 0.4 convolution_bitcast_fusion.3
  104.5 0.3 fusion.15
  104.9 0.1 copy.54
  105.1 0.4 convolution_bitcast_fusion.2
  105.5 0.3 fusion.16
  106.1 0.4 convolution_bitcast_fusion.1
  106.5 0.3 fusion.17
  107.1 0.4 convolution_bitcast_fusion
  107.5 0.3 fusion.18
  108.1 0.5 fusion
  108.6 0.8 reshape.15
  109.4 40.3 %all-gather.2.cloned.1.call-done = bf16[96,12288]{1,0:T(8,128)(2,1)} async-done(((bf16[96,768]{1,0:T(8,128)(2,1)}), bf16[96,12288]{1,0:T(8,128)(2,1)}) %all-gather.2.cloned.1.call-update) | async-done | bytes 2359312 | tf_op jit(solution)/shard_map/all_gather | solution.py:54
  149.7 3.3 %copy.83 = bf16[12,2,8,6144]{3,2,0,1:T(8,128)(2,1)} copy(bf16[12,2,8,6144]{3,2,1,0:T(8,128)(2,1)} %bitcast.119) | data formatting | bytes 4718592 | tf_op jit(solution)/shard_map/all_to_all | solution.py:55
  153.0 3.8 %all-to-all-start = ((bf16[96,2,6144]{2,0,1:T(8,128)(2,1)}), bf16[96,2,6144]{2,0,1:T(8,128)(2,1)S(1)}, u32[]{:S(2)}, u32[]{:S(2)}) async-start(bf16[96,2,6144]{2,0,1:T(8,128)(2,1)} %bitcast.117), calls=%async_computation | async-start | bytes 4718592 | tf_op jit(solution)/shard_map/all_to_all | solution.py:55
  156.8 0.6 copy.63
  157.4 30.9 %all_gather.10 = bf16[192,768]{1,0:T(8,128)(2,1)S(1)} all-gather(bf16[96,768]{1,0:T(8,128)(2,1)} %reshape.15), channel_id=1, replica_groups=mesh['row'=16,'col'=2] {'col'}, dimensions={0}, use_global_device_ids=true | all-gather | bytes 442368 | tf_op jit(solution)/shard_map/all_gather | solution.py:53
  188.3 8.3 %convolution_multiply_fusion = f32[768,6144]{1,0:T(8,128)} fusion(bf16[192,768]{1,0:T(8,128)(2,1)S(1)} %all_gather.10, bf16[192,6144]{1,0:T(8,128)(2,1)S(1)} %bitcast.118), kind=kOutput, calls=%fused_computation | convolution fusion | flops 1816657920 | bytes 21528576 | tf_op jit(solution)/shard_map/dot_general | solution.py:28
  (38 shorter events, 1.9 us)
Async XLA Ops:
  7.2 0.9 copy-start
  7.2 142.5 %all-gather.2.cloned.1.call-start = ((), (), s32[]{:S(2)}) async-start(), calls=%async_computation.1 | async-start | bytes 2506752 | tf_op jit(solution)/shard_map/all_gather | solution.py:54
  153.0 35.3 %all-to-all-start = ((bf16[96,2,6144]{2,0,1:T(8,128)(2,1)}), bf16[96,2,6144]{2,0,1:T(8,128)(2,1)S(1)}, u32[]{:S(2)}, u32[]{:S(2)}) async-start(bf16[96,2,6144]{2,0,1:T(8,128)(2,1)} %bitcast.117), calls=%async_computation | async-start | bytes 4718592 | tf_op jit(solution)/shard_map/all_to_all | solution.py:55
Sparse Core Ops, SparseCore 0:
  109.5 40.1 all-gather.1
where the time goes:
time: 204 us; the launch traced here: 203 us
  blocking collectives  99.9 us (49%)
  waiting for transfers between devices  40.3 us (20%)
  matrix products  36.7 us (18%)
  between operations  14.3 us (7%)
  local copies, waits for them, and re-layouts  8.16 us (4%)
  starting transfers between devices  3.85 us (2%)
    all_gather x1, waiting for transfers between devices, per_device(): dev_atoms = lax.all_gather(local_dev, 'row', axis=1, tiled=True)  40.3 us
    all_gather x1, blocking collectives, per_device(): rows_operand = lax.all_gather(local_dev, 'col', axis=0, tiled=True)  30.9 us
    psum x1, blocking collectives, per_device(): fitted = lax.psum(fit_part, 'row')  30.2 us
    all_gather x1, blocking collectives, per_device(): centre_all = lax.all_gather(centre_rows, 'row', axis=1, tiled=True)  22.1 us
    dot_general x1, matrix products, per_device(): lax.dot_general(centre_cols, inverse_cov, (((1,), (1,)), ((), ())), preci...  18.1 us
    psum x1, blocking collectives, per_device(): centre_rows = lax.psum(partial_value, 'col') / frame_total  9.59 us
    dot_general x1, matrix products, tile_block(): lax.dot_general(rows_operand, column_panel, (((0,), (0,)), ((), ())), pre...  8.27 us
    psum x1, blocking collectives, per_device(): weighted = lax.psum(local_weight, 'col')  7.14 us
  transfers between devices with their start and end apart: 2, of which 1 were waited for; matrix products, arithmetic and copies ran while one was open for 0% of the time, Pallas kernels for 0%

commit v1 on v0

v1 whole, which is shorter than its diff:
```python
import functools

import jax
import jax.numpy as jnp
from jax import lax
from jax.experimental import pallas as pl
from jax.experimental.pallas import tpu as pltpu
from jax.sharding import PartitionSpec as P

POLAR = 12
F32 = jnp.float32
BF16 = jnp.bfloat16
VMEM = pltpu.VMEM
MIB = 1 << 20


def whole_vmem():
    return pl.BlockSpec(memory_space=VMEM)


def smem():
    return pl.BlockSpec(memory_space=pltpu.SMEM)


def three_pieces(value):
    high = value.astype(BF16)
    rest = value - high.astype(F32)
    mid = rest.astype(BF16)
    low = (rest - mid.astype(F32)).astype(BF16)
    return high, mid, low


def rotated_sum(rot, coords):
    depth = coords.shape[0] * coords.shape[1]
    flat = jnp.concatenate([rot[:, part, :] for part in range(3)], axis=1)
    padded = jnp.concatenate([flat, jnp.zeros((5, depth), F32)], axis=0)
    stacked = jnp.concatenate(three_pieces(padded), axis=0)
    product = jnp.dot(stacked, coords.reshape(depth, coords.shape[2]), preferred_element_type=F32)
    return (product[16:19] + product[8:11]) + product[0:3]


def partial_centre_kernel(frame_total, where, rot_ref, coords_ref, out_ref):
    local = coords_ref.shape[1]
    col_count = frame_total // local
    block = lax.broadcasted_iota(jnp.int32, rot_ref.shape, 2) // local
    rot = jnp.where(block == where[1], rot_ref[...], 0.0)
    coords = coords_ref[...]
    out_ref[...] = rotated_sum(rot, jnp.concatenate([coords] * col_count, axis=1)) * (1.0 / frame_total)


def assemble_kernel(col_count, group_size, where, *refs):
    out_ref = refs[-1]
    local = refs[0].shape[1]
    group = where[0] // group_size
    for step in range(col_count):
        block = lax.rem(group + step, col_count)
        out_ref[:, pl.ds(pl.multiple_of(block * local, local), local), :] = refs[step][...]


def product_kernel(col_count, where, rot_ref, *refs):
    coords_refs = refs[:col_count]
    inv_ref, product_ref, rows_ref, centre_ref = refs[col_count:]
    local = coords_refs[0].shape[1]

    @pl.when(pl.program_id(0) == 0)
    def _():
        for step in range(col_count):
            block = lax.rem(where[1] + step, col_count)
            rows_ref[:, pl.ds(pl.multiple_of(block * local, local), local), :] = coords_refs[step][...]
        centre_ref[...] = rotated_sum(rot_ref[...], rows_ref[...]) * (1.0 / (local * col_count))

    value = inv_ref[...]
    high = value.astype(BF16)
    low = (value - high.astype(F32)).astype(BF16)
    rows = rows_ref[...].reshape(3 * local * col_count, rows_ref.shape[2])
    product_ref[...] = jnp.dot(rows, low, preferred_element_type=F32) + jnp.dot(rows, high, preferred_element_type=F32)


def fit_kernel(members, where, product_ref, *refs):
    centre_refs, out_ref = refs[:members], refs[members]
    member = lax.rem(where[0], members)
    frame_total = product_ref.shape[0] // 3
    width = centre_refs[0].shape[1]
    lanes = 128
    entries = []
    for part in range(3):
        sums = [jnp.zeros((frame_total, lanes), F32)] * 3
        for mask in range(members):
            block = member ^ mask
            for chunk in range(width // lanes):
                start = pl.multiple_of(block * width + chunk * lanes, lanes)
                value = product_ref[pl.ds(part * frame_total, frame_total), pl.ds(start, lanes)]
                for comp in range(3):
                    factor = centre_refs[mask][comp : comp + 1, chunk * lanes : (chunk + 1) * lanes]
                    sums[comp] = sums[comp] + value * factor
        entries += [jnp.sum(total.T, axis=0, keepdims=True) for total in sums]
    first = jnp.concatenate(entries[:8], axis=0)
    last = jnp.concatenate([entries[8], jnp.zeros((7, frame_total), F32)], axis=0)
    message = jnp.concatenate([first, last], axis=1)
    out_ref[...] = jnp.broadcast_to(message[None], out_ref.shape)


def orthogonalized(message, frame_total):
    fitted = [message[entry : entry + 1, :frame_total] for entry in range(8)]
    fitted.append(message[0:1, frame_total:])
    norm = functools.reduce(lambda a, b: a + b, [value * value for value in fitted])
    scaling = jnp.sqrt(1.0 + norm)
    current = [[fitted[3 * col + row] / scaling for col in range(3)] for row in range(3)]
    for _ in range(POLAR):
        square = [[None] * 3 for _ in range(3)]
        for a in range(3):
            for b in range(a, 3):
                x, y = current[a], current[b]
                square[a][b] = square[b][a] = x[0] * y[0] + x[1] * y[1] + x[2] * y[2]
        cubed = [
            [sum(square[a][k] * current[k][b] for k in range(1, 3)) + square[a][0] * current[0][b] for b in range(3)]
            for a in range(3)
        ]
        current = [[1.5 * current[a][b] - 0.5 * cubed[a][b] for b in range(3)] for a in range(3)]
    return current


def covariance_kernel(members, where, fits_ref, rows_ref, rows_centre_ref, *refs):
    panel_refs, centre_refs = refs[:members], refs[members : 2 * members]
    out_ref, rot_out_ref, wide_ref, rows_dev_ref, dev_ref = refs[2 * members :]
    frame_total = rows_ref.shape[1]
    local = rot_out_ref.shape[2]
    lanes = 128

    def deviations(coords_ref, centre_ref):
        for chunk in range(coords_ref.shape[2] // lanes):
            span = slice(chunk * lanes, (chunk + 1) * lanes)
            coords = [coords_ref[part, :, span].astype(F32) for part in range(3)]
            for comp in range(3):
                moved = wide_ref[3 * comp] * coords[0]
                moved = moved + wide_ref[3 * comp + 1] * coords[1]
                moved = moved + wide_ref[3 * comp + 2] * coords[2]
                value = moved - centre_ref[comp : comp + 1, span]
                dev_ref[comp * frame_total : (comp + 1) * frame_total, span] = value.astype(BF16)

    @pl.when(pl.program_id(0) == 0)
    def _():
        message = jnp.sum(fits_ref[...], axis=0)
        current = orthogonalized(message, frame_total)
        for a in range(3):
            flat = jnp.concatenate(current[a], axis=0)
            kept = flat[:, :local]
            for block in range(1, frame_total // local):
                kept = jnp.where(where[1] == block, flat[:, block * local : (block + 1) * local], kept)
            rot_out_ref[a] = kept
        for a in range(3):
            for b in range(3):
                column = jnp.broadcast_to(current[a][b], (lanes, frame_total)).T
                wide_ref[3 * a + b] = column
        deviations(rows_ref, rows_centre_ref)
        rows_dev_ref[...] = dev_ref[...].T

    for mask in range(members):

        @pl.when(pl.program_id(0) == mask)
        def _(mask=mask):
            deviations(panel_refs[mask], centre_refs[mask])

    product = jnp.dot(rows_dev_ref[...], dev_ref[...], preferred_element_type=F32)
    out_ref[...] = product * (1.0 / (3 * frame_total))


def per_device(frames, rotations, inverse_cov):
    row_count, col_count = lax.axis_size("row"), lax.axis_size("col")
    members = row_count // col_count
    row, col = lax.axis_index("row"), lax.axis_index("col")
    where = jnp.stack([row, col]).astype(jnp.int32)
    local, _, width = frames.shape
    frame_total = local * col_count
    device_total = row_count * col_count
    coords = jnp.transpose(frames, (1, 0, 2))
    axes = ("row", "col")

    def move(value, source_of):
        pairs = []
        for group in range(col_count):
            for member in range(members):
                for place in range(col_count):
                    from_group, from_member, from_col = source_of(group, member, place)
                    source = (from_group * members + from_member) * col_count + from_col
                    pairs.append((source, (group * members + member) * col_count + place))
        return lax.ppermute(value, axes, pairs)

    def from_panel_row(value, step):
        return move(value, lambda g, m, c: (c, m, (g + step) % col_count))

    def from_member(value, mask):
        return move(value, lambda g, m, c: (g, m ^ mask, c))

    partial = pl.pallas_call(
        functools.partial(partial_centre_kernel, frame_total),
        out_shape=jax.ShapeDtypeStruct((3, width), F32),
        in_specs=[smem(), whole_vmem(), whole_vmem()],
        out_specs=whole_vmem(),
        name="partial_centre",
    )(where, rotations, coords)
    parts = [from_panel_row(partial, step) for step in range(col_count)]
    panel_parts = [from_panel_row(coords, step) for step in range(col_count)]
    others = [move(coords, lambda g, m, c, s=step: (g, m, (c + s) % col_count)) for step in range(1, col_count)]

    own_centre = functools.reduce(lambda a, b: a + b, parts)
    centres = [own_centre] + [from_member(own_centre, mask) for mask in range(1, members)]

    own_block = pl.pallas_call(
        functools.partial(assemble_kernel, col_count, members),
        out_shape=jax.ShapeDtypeStruct((3, frame_total, width), BF16),
        in_specs=[smem()] + [whole_vmem()] * col_count,
        out_specs=whole_vmem(),
        name="assemble",
    )(where, *panel_parts)
    panel = [own_block] + [None] * (members - 1)
    for mask in range(2, members, 2):
        panel[mask] = from_member(own_block, mask)
    for mask in range(1, members, 2):
        panel[mask] = from_member(panel[mask - 1], 1)

    col_width = inverse_cov.shape[1]
    step_width = 512 if col_width % 512 == 0 else 128
    const2 = lambda i: (0, 0)
    const3 = lambda i: (0, 0, 0)
    product, rows_all, rows_centre = pl.pallas_call(
        functools.partial(product_kernel, col_count),
        grid=(col_width // step_width,),
        out_shape=(
            jax.ShapeDtypeStruct((3 * frame_total, col_width), F32),
            jax.ShapeDtypeStruct((3, frame_total, width), BF16),
            jax.ShapeDtypeStruct((3, width), F32),
        ),
        in_specs=[smem(), whole_vmem()]
        + [whole_vmem()] * col_count
        + [pl.BlockSpec((width, step_width), lambda i: (0, i))],
        out_specs=(
            pl.BlockSpec((3 * frame_total, step_width), lambda i: (0, i)),
            pl.BlockSpec((3, frame_total, width), const3),
            pl.BlockSpec((3, width), const2),
        ),
        compiler_params=pltpu.CompilerParams(vmem_limit_bytes=32 * MIB),
        cost_estimate=pl.CostEstimate(
            flops=12 * frame_total * width * col_width, bytes_accessed=4 * width * col_width, transcendentals=0
        ),
        name="frames_times_inverse",
    )(where, rotations, coords, *others, inverse_cov)

    message = pl.pallas_call(
        functools.partial(fit_kernel, members),
        out_shape=jax.ShapeDtypeStruct((device_total, 8, 2 * frame_total), F32),
        in_specs=[smem(), whole_vmem()] + [whole_vmem()] * members,
        out_specs=whole_vmem(),
        compiler_params=pltpu.CompilerParams(vmem_limit_bytes=32 * MIB),
        name="fit_part",
    )(where, product, *centres)
    fits = lax.all_to_all(message, axes, split_axis=0, concat_axis=0, tiled=True)

    covariance, transforms = pl.pallas_call(
        functools.partial(covariance_kernel, members),
        grid_spec=pltpu.PrefetchScalarGridSpec(
            num_scalar_prefetch=1,
            grid=(members,),
            in_specs=[whole_vmem()] * (3 + 2 * members),
            out_specs=(
                pl.BlockSpec((width, width), lambda i, where: (0, lax.rem(where[0], members) ^ i)),
                pl.BlockSpec((3, 3, local), lambda i, where: (0, 0, 0)),
            ),
            scratch_shapes=[
                pltpu.VMEM((9, frame_total, 128), F32),
                pltpu.VMEM((width, 3 * frame_total), BF16),
                pltpu.VMEM((3 * frame_total, width), BF16),
            ],
        ),
        out_shape=(
            jax.ShapeDtypeStruct((width, col_width), F32),
            jax.ShapeDtypeStruct((3, 3, local), F32),
        ),
        compiler_params=pltpu.CompilerParams(vmem_limit_bytes=40 * MIB),
        cost_estimate=pl.CostEstimate(
            flops=6 * frame_total * width * col_width, bytes_accessed=4 * width * col_width, transcendentals=0
        ),
        name="covariance",
    )(where, fits, rows_all, rows_centre, *panel, *centres)
    return (covariance, transforms)


def solution(mesh):
    placed = (P("col", None, "row"), P(), P("row", "col"))
    return jax.shard_map(
        per_device,
        mesh=mesh,
        in_specs=placed,
        out_specs=(P("row", "col"), P(None, None, "col")),
        check_vma=False,
    )
```

time: 204 us -> 103 us (0.50)
  blocking collectives: 99.9 us -> 18.4 us
  matrix products: 36.7 us -> 0 us
  Pallas kernels: 0 us -> 31 us
  starting transfers between devices: 3.85 us -> 21.9 us
  between operations: 14.3 us -> 0.71 us
  waiting for transfers between devices: 40.3 us -> 26.8 us
  local copies, waits for them, and re-layouts: 8.16 us -> 3.55 us
    all_gather x2 -> x0, blocking collectives: 53 us -> none  [the longest x1 30.9 us: per_device(): rows_operand = lax.all_gather(local_dev, 'col', axis=0, tiled=True)]
    psum x3 -> x0, blocking collectives: 46.9 us -> none  [the longest x1 30.2 us: per_device(): fitted = lax.psum(fit_part, 'row')]
    all_gather x1 -> x0, waiting for transfers between devices: 40.3 us -> none  [per_device(): dev_atoms = lax.all_gather(local_dev, 'row', axis=1, tiled=True)]
    dot_general x29 -> x0, matrix products: 36.7 us -> none  [the longest x1 18.1 us: per_device(): lax.dot_general(centre_cols, inverse_cov, (((1,), (1,)), ((), ())), preci...]
    pallas_call x0 -> x5, Pallas kernels: none -> 31 us  [the longest x1 13 us: per_device(): pl.pallas_call(functools.partial(product_kernel, col_count), grid=(col_wi...]
    ppermute x0 -> x19, waiting for transfers between devices: none -> 26.8 us  [move(): return lax.ppermute(value, axes, pairs)]
    ppermute x0 -> x19, starting transfers between devices: none -> 21.9 us  [move(): return lax.ppermute(value, axes, pairs)]
    all_to_all x0 -> x1, blocking collectives: none -> 18.4 us  [per_device(): lax.all_to_all(message, axes, split_axis=0, concat_axis=0, tiled=True)]
  transfers between devices with their start and end apart: 2 -> 19, of which waited for: 1 -> 8; matrix products, arithmetic and copies ran while one was open for 0% -> 1% of each run, Pallas kernels for 0% -> 17%
where the time goes in v1:
time: 103 us
  Pallas kernels  31 us (30%)
  waiting for transfers between devices  26.8 us (26%)
  starting transfers between devices  21.9 us (21%)
  blocking collectives  18.4 us (18%)
  local copies, waits for them, and re-layouts  3.55 us (3%)
    ppermute x19, waiting for transfers between devices, move(): return lax.ppermute(value, axes, pairs)  26.8 us
    ppermute x19, starting transfers between devices, move(): return lax.ppermute(value, axes, pairs)  21.9 us
    all_to_all x1, blocking collectives, per_device(): lax.all_to_all(message, axes, split_axis=0, concat_axis=0, tiled=True)  18.4 us
    pallas_call x1, Pallas kernels, per_device(): pl.pallas_call(functools.partial(product_kernel, col_count), grid=(col_wi...  13 us
    pallas_call x1, Pallas kernels, per_device(): pl.pallas_call(functools.partial(covariance_kernel, members), grid_spec=p...  11.9 us
    unnamed x12, local copies, waits for them, and re-layouts  3.55 us
    pallas_call x1, Pallas kernels, per_device(): pl.pallas_call(functools.partial(fit_kernel, members), out_shape=jax.Shap...  2.61 us
  transfers between devices with their start and end apart: 19, of which 8 were waited for; matrix products, arithmetic and copies ran while one was open for 1% of the time, Pallas kernels for 17%

profile of v1, /device:TPU:0, one launch (start us, length us, event | category | flops | bytes accessed | tf_op | source)
XLA Modules:
  0.0 103.0 jit_solution(16207327347458353735)
XLA Ops:
  0.6 4.1 %collective-permute-start.11 = (bf16[3,32,768]{2,1,0:T(8,128)(2,1)}, bf16[3,32,768]{2,1,0:T(8,128)(2,1)S(1)}, u32[]{:S(2)}, u32[]{:S(2)}) collective-permute-start(bf16[3,32,768]{2,1,0:T(8,128)(2,1)} %bitcast.3), channel_id=1, source_target_pairs={{1,0},{17,1},{3,2},{19,3},{5,4},{21,5},{7,6},{23,7},{9,8},{25,9},{... | collective-permute-start | bytes 442376 | tf_op jit(solution)/shard_map/ppermute | solution.py:187
  4.7 1.6 %collective-permute-start.10 = (bf16[3,32,768]{2,1,0:T(8,128)(2,1)}, bf16[3,32,768]{2,1,0:T(8,128)(2,1)S(1)}, u32[]{:S(2)}, u32[]{:S(2)}) collective-permute-start(bf16[3,32,768]{2,1,0:T(8,128)(2,1)} %bitcast.4), channel_id=1, source_target_pairs={{0,0},{16,1},{2,2},{18,3},{4,4},{20,5},{6,6},{22,7},{8,8},{24,9},{... | collective-permute-start | bytes 442376 | tf_op jit(solution)/shard_map/ppermute | solution.py:187
  6.3 0.6 pad_add_fusion.where
  6.9 1.3 %collective-permute-done.11.refs_1_ = bf16[3,32,768]{2,1,0:T(8,128)(2,1)S(1)} collective-permute-done((bf16[3,32,768]{2,1,0:T(8,128)(2,1)}, bf16[3,32,768]{2,1,0:T(8,128)(2,1)S(1)}, u32[]{:S(2)}, u32[]{:S(2)}) %collective-permute-start.11) | collective-permute-done | bytes 147488 | tf_op jit(solution)/shard_map/ppermute | solution.py:187
  8.2 0.0 collective-permute-done.10.refs_0_
  8.2 0.6 copy-done.4
  8.8 0.7 copy-done.5
  9.5 1.7 %assemble.1.refs_0_ = bf16[3,64,768]{2,1,0:T(8,128)(2,1)} custom-call(s32[2]{0:T(128)} %pad_add_fusion.where, bf16[3,32,768]{2,1,0:T(8,128)(2,1)} %copy-done.5, bf16[3,32,768]{2,1,0:T(8,128)(2,1)} %copy-done.4), custom_call_target="tpu_custom_call" | custom-call | tf_op jit(solution)/shard_map/assemble/pallas_call | solution.py:209
  11.2 5.5 %collective-permute-start.17 = (bf16[3,64,768]{2,1,0:T(8,128)(2,1)}, bf16[3,64,768]{2,1,0:T(8,128)(2,1)S(1)}, u32[]{:S(2)}, u32[]{:S(2)}) collective-permute-start(bf16[3,64,768]{2,1,0:T(8,128)(2,1)} %assemble.1.refs_0_), channel_id=1, source_target_pairs={{12,0},{13,1},{14,2},{15,3},{8,4},{9,5},{10,6},{11,7},{4,8},{5,9},... | collective-permute-start | bytes 884744 | tf_op jit(solution)/shard_map/ppermute | solution.py:187
  16.8 0.0 collective-permute-start.15
  16.8 0.6 collective-permute-start.13
  17.3 5.1 %collective-permute-start = (bf16[3,32,768]{2,1,0:T(8,128)(2,1)}, bf16[3,32,768]{2,1,0:T(8,128)(2,1)S(1)}, u32[]{:S(2)}, u32[]{:S(2)}) collective-permute-start(bf16[3,32,768]{2,1,0:T(8,128)(2,1)} %bitcast.5), channel_id=1, source_target_pairs={{1,0},{0,1},{3,2},{2,3},{5,4},{4,5},{7,6},{6,7},{9,8},{8,9},{11,10... | collective-permute-start | bytes 442376 | tf_op jit(solution)/shard_map/ppermute | solution.py:187
  22.4 1.8 %partial_centre.1 = f32[3,768]{1,0:T(4,128)} custom-call(s32[2]{0:T(128)} %pad_add_fusion.where, f32[3,3,64]{2,1,0:T(4,128)} %rot_ref.3, bf16[3,32,768]{2,1,0:T(8,128)(2,1)} %bitcast.6), custom_call_target="tpu_custom_call" | custom-call | tf_op jit(solution)/shard_map/partial_centre/pallas_call | solution.py:195
  24.2 1.7 %collective-permute-start.2 = (f32[3,768]{1,0:T(4,128)}, f32[3,768]{1,0:T(4,128)S(1)}, u32[]{:S(2)}, u32[]{:S(2)}) collective-permute-start(f32[3,768]{1,0:T(4,128)} %partial_centre.1), channel_id=1, source_target_pairs={{1,0},{17,1},{3,2},{19,3},{5,4},{21,5},{7,6},{23,7},{9,8},{25,9},{... | collective-permute-start | bytes 27656 | tf_op jit(solution)/shard_map/ppermute | solution.py:187
  25.8 4.2 %collective-permute-done.2 = f32[3,768]{1,0:T(4,128)S(1)} collective-permute-done((f32[3,768]{1,0:T(4,128)}, f32[3,768]{1,0:T(4,128)S(1)}, u32[]{:S(2)}, u32[]{:S(2)}) %collective-permute-start.2) | collective-permute-done | bytes 9248 | tf_op jit(solution)/shard_map/ppermute | solution.py:187
  30.1 1.4 %collective-permute-start.1 = (f32[3,768]{1,0:T(4,128)}, f32[3,768]{1,0:T(4,128)S(1)}, u32[]{:S(2)}, u32[]{:S(2)}) collective-permute-start(f32[3,768]{1,0:T(4,128)} %partial_centre.1), channel_id=1, source_target_pairs={{0,0},{16,1},{2,2},{18,3},{4,4},{20,5},{6,6},{22,7},{8,8},{24,9},{... | collective-permute-start | bytes 27656 | tf_op jit(solution)/shard_map/ppermute | solution.py:187
  31.4 0.0 collective-permute-done.1
  31.4 0.1 collective-permute-start.9
  31.5 4.0 %collective-permute-done.9.refs_7_.refs_15_ = f32[3,768]{1,0:T(4,128)S(1)} collective-permute-done((f32[3,768]{1,0:T(4,128)S(1)}, f32[3,768]{1,0:T(4,128)S(1)}, u32[]{:S(2)}, u32[]{:S(2)}) %collective-permute-start.9) | collective-permute-done | bytes 9248 | tf_op jit(solution)/shard_map/ppermute | solution.py:187
  35.5 0.3 collective-permute-start.8
  35.8 4.3 %collective-permute-done.8.refs_6_.refs_14_ = f32[3,768]{1,0:T(4,128)S(1)} collective-permute-done((f32[3,768]{1,0:T(4,128)S(1)}, f32[3,768]{1,0:T(4,128)S(1)}, u32[]{:S(2)}, u32[]{:S(2)}) %collective-permute-start.8) | collective-permute-done | bytes 9248 | tf_op jit(solution)/shard_map/ppermute | solution.py:187
  40.1 0.0 collective-permute-start.7
  40.1 3.1 %collective-permute-done.7.refs_5_.refs_13_ = f32[3,768]{1,0:T(4,128)S(1)} collective-permute-done((f32[3,768]{1,0:T(4,128)S(1)}, f32[3,768]{1,0:T(4,128)S(1)}, u32[]{:S(2)}, u32[]{:S(2)}) %collective-permute-start.7) | collective-permute-done | bytes 9248 | tf_op jit(solution)/shard_map/ppermute | solution.py:187
  43.2 0.0 collective-permute-start.6
  43.2 3.7 %collective-permute-done.6.refs_4_.refs_12_ = f32[3,768]{1,0:T(4,128)S(1)} collective-permute-done((f32[3,768]{1,0:T(4,128)S(1)}, f32[3,768]{1,0:T(4,128)S(1)}, u32[]{:S(2)}, u32[]{:S(2)}) %collective-permute-start.6) | collective-permute-done | bytes 9248 | tf_op jit(solution)/shard_map/ppermute | solution.py:187
  46.9 0.0 collective-permute-start.5
  46.9 3.1 %collective-permute-done.5.refs_3_.refs_11_ = f32[3,768]{1,0:T(4,128)S(1)} collective-permute-done((f32[3,768]{1,0:T(4,128)S(1)}, f32[3,768]{1,0:T(4,128)S(1)}, u32[]{:S(2)}, u32[]{:S(2)}) %collective-permute-start.5) | collective-permute-done | bytes 9248 | tf_op jit(solution)/shard_map/ppermute | solution.py:187
  50.0 0.6 collective-permute-start.4
  50.6 3.1 %collective-permute-done.4.refs_2_.refs_10_ = f32[3,768]{1,0:T(4,128)S(1)} collective-permute-done((f32[3,768]{1,0:T(4,128)S(1)}, f32[3,768]{1,0:T(4,128)S(1)}, u32[]{:S(2)}, u32[]{:S(2)}) %collective-permute-start.4) | collective-permute-done | bytes 9248 | tf_op jit(solution)/shard_map/ppermute | solution.py:187
  53.7 0.0 collective-permute-start.3
  53.7 0.0 collective-permute-done.refs_1_
  53.7 0.5 collective-permute-start.12
  54.2 0.0 collective-permute-done.17.refs_6_
  54.2 0.1 collective-permute-start.18
  54.3 0.0 collective-permute-done.15.refs_4_
  54.3 0.4 collective-permute-start.16
  54.8 0.1 collective-permute-start.14
  54.8 0.9 copy-done
  55.8 0.7 copy-done.2
  56.4 0.6 copy-done.3
  57.1 13.0 %frames_times_inverse.1 = (f32[192,6144]{1,0:T(8,128)S(1)}, bf16[3,64,768]{2,1,0:T(8,128)(2,1)S(1)}, f32[3,768]{1,0:T(4,128)S(1)}) custom-call(s32[2]{0:T(128)S(1)} %copy-done.3, f32[3,3,64]{2,1,0:T(4,128)S(1)} %copy-done.2, bf16[3,32,768]{2,1,0:T(8,128)(2,1)S(1)} %bitcast.7, bf16[3,32,768]{2,1,0:T(8,128)(2,1)S(1)} %collective-permute-done.refs_1_, ...), custom_call_target="tpu_custom_call" | custom-call | flops 3623878656 | bytes 18874368 | tf_op jit(solution)/shard_map/frames_times_inverse/pallas_call | solution.py:226
  70.1 0.0 collective-permute-done.3.refs_1_.refs_9_
  70.1 2.6 %fit_part.1 = f32[32,8,128]{2,1,0:T(8,128)S(1)} custom-call(s32[2]{0:T(128)S(1)} %copy-done.3, f32[192,6144]{1,0:T(8,128)S(1)} %get-tuple-element.5.product_ref, f32[3,768]{1,0:T(4,128)S(1)} %add.3.refs_0_.refs_8_, f32[3,768]{1,0:T(4,128)S(1)} %collective-permute-done.3.refs_1_.refs_9_, f32[3,768]{1,0:T(4,128)S(1)} %collective-permute-done.4.refs_2_.refs_10_, ...), custom_call_target="tpu_custom_call" | custom-call | tf_op jit(solution)/shard_map/fit_part/pallas_call | solution.py:249
  72.7 18.4 %all_to_all.5.fits_ref = f32[32,8,128]{2,1,0:T(8,128)S(1)} all-to-all(f32[32,8,128]{2,1,0:T(8,128)S(1)} %fit_part.1), channel_id=1, replica_groups=mesh['row'=16,'col'=2] {'row','col'}, dimensions={0} | all-to-all | bytes 262144 | tf_op jit(solution)/shard_map/all_to_all | solution.py:257
  91.1 0.0 collective-permute-done.12.refs_1_
  91.1 0.0 collective-permute-done.18.refs_7_
  91.1 0.0 collective-permute-done.16.refs_5_
  91.1 11.9 %covariance.1 = (f32[768,6144]{1,0:T(8,128)}, f32[3,3,32]{2,1,0:T(4,128)}) custom-call(s32[2]{0:T(128)S(1)} %copy-done.3, f32[32,8,128]{2,1,0:T(8,128)S(1)} %all_to_all.5.fits_ref, bf16[3,64,768]{2,1,0:T(8,128)(2,1)S(1)} %get-tuple-element.6.rows_ref, f32[3,768]{1,0:T(4,128)S(1)} %get-tuple-element.7.rows_centre_ref, bf16[3,64,768]{2,1,0:T(8,128)(2,1)S(1)} %copy-done.1, ...), custom_call_target="tpu_custom_call" | custom-call | flops 1811939328 | bytes 18874368 | tf_op jit(solution)/shard_map/covariance/pallas_call | solution.py:259
  (10 shorter events, 0.0 us)
Async XLA Ops:
  0.6 7.6 %collective-permute-start.11 = (bf16[3,32,768]{2,1,0:T(8,128)(2,1)}, bf16[3,32,768]{2,1,0:T(8,128)(2,1)S(1)}, u32[]{:S(2)}, u32[]{:S(2)}) collective-permute-start(bf16[3,32,768]{2,1,0:T(8,128)(2,1)} %bitcast.3), channel_id=1, source_target_pairs={{1,0},{17,1},{3,2},{19,3},{5,4},{21,5},{7,6},{23,7},{9,8},{25,9},{... | collective-permute-start | bytes 442376 | tf_op jit(solution)/shard_map/ppermute | solution.py:187
  4.7 3.5 %collective-permute-start.10 = (bf16[3,32,768]{2,1,0:T(8,128)(2,1)}, bf16[3,32,768]{2,1,0:T(8,128)(2,1)S(1)}, u32[]{:S(2)}, u32[]{:S(2)}) collective-permute-start(bf16[3,32,768]{2,1,0:T(8,128)(2,1)} %bitcast.4), channel_id=1, source_target_pairs={{0,0},{16,1},{2,2},{18,3},{4,4},{20,5},{6,6},{22,7},{8,8},{24,9},{... | collective-permute-start | bytes 442376 | tf_op jit(solution)/shard_map/ppermute | solution.py:187
  8.2 0.7 copy-start.4
  8.8 0.7 copy-start.5
  11.2 43.0 %collective-permute-start.17 = (bf16[3,64,768]{2,1,0:T(8,128)(2,1)}, bf16[3,64,768]{2,1,0:T(8,128)(2,1)S(1)}, u32[]{:S(2)}, u32[]{:S(2)}) collective-permute-start(bf16[3,64,768]{2,1,0:T(8,128)(2,1)} %assemble.1.refs_0_), channel_id=1, source_target_pairs={{12,0},{13,1},{14,2},{15,3},{8,4},{9,5},{10,6},{11,7},{4,8},{5,9},... | collective-permute-start | bytes 884744 | tf_op jit(solution)/shard_map/ppermute | solution.py:187
  16.8 37.6 %collective-permute-start.15 = (bf16[3,64,768]{2,1,0:T(8,128)(2,1)}, bf16[3,64,768]{2,1,0:T(8,128)(2,1)S(1)}, u32[]{:S(2)}, u32[]{:S(2)}) collective-permute-start(bf16[3,64,768]{2,1,0:T(8,128)(2,1)} %assemble.1.refs_0_), channel_id=1, source_target_pairs={{8,0},{9,1},{10,2},{11,3},{12,4},{13,5},{14,6},{15,7},{0,8},{1,9},... | collective-permute-start | bytes 884744 | tf_op jit(solution)/shard_map/ppermute | solution.py:187
  16.8 38.0 %collective-permute-start.13 = (bf16[3,64,768]{2,1,0:T(8,128)(2,1)}, bf16[3,64,768]{2,1,0:T(8,128)(2,1)S(1)}, u32[]{:S(2)}, u32[]{:S(2)}) collective-permute-start(bf16[3,64,768]{2,1,0:T(8,128)(2,1)} %assemble.1.refs_0_), channel_id=1, source_target_pairs={{4,0},{5,1},{6,2},{7,3},{0,4},{1,5},{2,6},{3,7},{12,8},{13,9},{14,... | collective-permute-start | bytes 884744 | tf_op jit(solution)/shard_map/ppermute | solution.py:187
  17.3 36.4 %collective-permute-start = (bf16[3,32,768]{2,1,0:T(8,128)(2,1)}, bf16[3,32,768]{2,1,0:T(8,128)(2,1)S(1)}, u32[]{:S(2)}, u32[]{:S(2)}) collective-permute-start(bf16[3,32,768]{2,1,0:T(8,128)(2,1)} %bitcast.5), channel_id=1, source_target_pairs={{1,0},{0,1},{3,2},{2,3},{5,4},{4,5},{7,6},{6,7},{9,8},{8,9},{11,10... | collective-permute-start | bytes 442376 | tf_op jit(solution)/shard_map/ppermute | solution.py:187
  24.2 5.9 %collective-permute-start.2 = (f32[3,768]{1,0:T(4,128)}, f32[3,768]{1,0:T(4,128)S(1)}, u32[]{:S(2)}, u32[]{:S(2)}) collective-permute-start(f32[3,768]{1,0:T(4,128)} %partial_centre.1), channel_id=1, source_target_pairs={{1,0},{17,1},{3,2},{19,3},{5,4},{21,5},{7,6},{23,7},{9,8},{25,9},{... | collective-permute-start | bytes 27656 | tf_op jit(solution)/shard_map/ppermute | solution.py:187
  30.1 1.4 %collective-permute-start.1 = (f32[3,768]{1,0:T(4,128)}, f32[3,768]{1,0:T(4,128)S(1)}, u32[]{:S(2)}, u32[]{:S(2)}) collective-permute-start(f32[3,768]{1,0:T(4,128)} %partial_centre.1), channel_id=1, source_target_pairs={{0,0},{16,1},{2,2},{18,3},{4,4},{20,5},{6,6},{22,7},{8,8},{24,9},{... | collective-permute-start | bytes 27656 | tf_op jit(solution)/shard_map/ppermute | solution.py:187
  31.4 4.1 %collective-permute-start.9 = (f32[3,768]{1,0:T(4,128)S(1)}, f32[3,768]{1,0:T(4,128)S(1)}, u32[]{:S(2)}, u32[]{:S(2)}) collective-permute-start(f32[3,768]{1,0:T(4,128)S(1)} %add.3.refs_0_.refs_8_), channel_id=1, source_target_pairs={{14,0},{15,1},{12,2},{13,3},{10,4},{11,5},{8,6},{9,7},{6,8},{7,9},... | collective-permute-start | bytes 27656 | tf_op jit(solution)/shard_map/ppermute | solution.py:187
  35.5 4.6 %collective-permute-start.8 = (f32[3,768]{1,0:T(4,128)S(1)}, f32[3,768]{1,0:T(4,128)S(1)}, u32[]{:S(2)}, u32[]{:S(2)}) collective-permute-start(f32[3,768]{1,0:T(4,128)S(1)} %add.3.refs_0_.refs_8_), channel_id=1, source_target_pairs={{12,0},{13,1},{14,2},{15,3},{8,4},{9,5},{10,6},{11,7},{4,8},{5,9},... | collective-permute-start | bytes 27656 | tf_op jit(solution)/shard_map/ppermute | solution.py:187
  40.1 3.1 %collective-permute-start.7 = (f32[3,768]{1,0:T(4,128)S(1)}, f32[3,768]{1,0:T(4,128)S(1)}, u32[]{:S(2)}, u32[]{:S(2)}) collective-permute-start(f32[3,768]{1,0:T(4,128)S(1)} %add.3.refs_0_.refs_8_), channel_id=1, source_target_pairs={{10,0},{11,1},{8,2},{9,3},{14,4},{15,5},{12,6},{13,7},{2,8},{3,9},... | collective-permute-start | bytes 27656 | tf_op jit(solution)/shard_map/ppermute | solution.py:187
  43.2 3.7 %collective-permute-start.6 = (f32[3,768]{1,0:T(4,128)S(1)}, f32[3,768]{1,0:T(4,128)S(1)}, u32[]{:S(2)}, u32[]{:S(2)}) collective-permute-start(f32[3,768]{1,0:T(4,128)S(1)} %add.3.refs_0_.refs_8_), channel_id=1, source_target_pairs={{8,0},{9,1},{10,2},{11,3},{12,4},{13,5},{14,6},{15,7},{0,8},{1,9},... | collective-permute-start | bytes 27656 | tf_op jit(solution)/shard_map/ppermute | solution.py:187
  46.9 3.1 %collective-permute-start.5 = (f32[3,768]{1,0:T(4,128)S(1)}, f32[3,768]{1,0:T(4,128)S(1)}, u32[]{:S(2)}, u32[]{:S(2)}) collective-permute-start(f32[3,768]{1,0:T(4,128)S(1)} %add.3.refs_0_.refs_8_), channel_id=1, source_target_pairs={{6,0},{7,1},{4,2},{5,3},{2,4},{3,5},{0,6},{1,7},{14,8},{15,9},{12,... | collective-permute-start | bytes 27656 | tf_op jit(solution)/shard_map/ppermute | solution.py:187
  50.0 3.7 %collective-permute-start.4 = (f32[3,768]{1,0:T(4,128)S(1)}, f32[3,768]{1,0:T(4,128)S(1)}, u32[]{:S(2)}, u32[]{:S(2)}) collective-permute-start(f32[3,768]{1,0:T(4,128)S(1)} %add.3.refs_0_.refs_8_), channel_id=1, source_target_pairs={{4,0},{5,1},{6,2},{7,3},{0,4},{1,5},{2,6},{3,7},{12,8},{13,9},{14,... | collective-permute-start | bytes 27656 | tf_op jit(solution)/shard_map/ppermute | solution.py:187
  53.7 16.3 %collective-permute-start.3 = (f32[3,768]{1,0:T(4,128)S(1)}, f32[3,768]{1,0:T(4,128)S(1)}, u32[]{:S(2)}, u32[]{:S(2)}) collective-permute-start(f32[3,768]{1,0:T(4,128)S(1)} %add.3.refs_0_.refs_8_), channel_id=1, source_target_pairs={{2,0},{3,1},{0,2},{1,3},{6,4},{7,5},{4,6},{5,7},{10,8},{11,9},{8,1... | collective-permute-start | bytes 27656 | tf_op jit(solution)/shard_map/ppermute | solution.py:187
  53.7 37.3 %collective-permute-start.12 = (bf16[3,64,768]{2,1,0:T(8,128)(2,1)}, bf16[3,64,768]{2,1,0:T(8,128)(2,1)S(1)}, u32[]{:S(2)}, u32[]{:S(2)}) collective-permute-start(bf16[3,64,768]{2,1,0:T(8,128)(2,1)} %assemble.1.refs_0_), channel_id=1, source_target_pairs={{2,0},{3,1},{0,2},{1,3},{6,4},{7,5},{4,6},{5,7},{10,8},{11,9},{8,1... | collective-permute-start | bytes 884744 | tf_op jit(solution)/shard_map/ppermute | solution.py:187
  54.2 36.8 %collective-permute-start.18 = (bf16[3,64,768]{2,1,0:T(8,128)(2,1)S(1)}, bf16[3,64,768]{2,1,0:T(8,128)(2,1)S(1)}, u32[]{:S(2)}, u32[]{:S(2)}) collective-permute-start(bf16[3,64,768]{2,1,0:T(8,128)(2,1)S(1)} %collective-permute-done.17.refs_6_), channel_id=1, source_target_pairs={{2,0},{3,1},{0,2},{1,3},{6,4},{7,5},{4,6},{5,7},{10,8},{11,9},{8,1... | collective-permute-start | bytes 884744 | tf_op jit(solution)/shard_map/ppermute | solution.py:187
  54.3 36.8 %collective-permute-start.16 = (bf16[3,64,768]{2,1,0:T(8,128)(2,1)S(1)}, bf16[3,64,768]{2,1,0:T(8,128)(2,1)S(1)}, u32[]{:S(2)}, u32[]{:S(2)}) collective-permute-start(bf16[3,64,768]{2,1,0:T(8,128)(2,1)S(1)} %collective-permute-done.15.refs_4_), channel_id=1, source_target_pairs={{2,0},{3,1},{0,2},{1,3},{6,4},{7,5},{4,6},{5,7},{10,8},{11,9},{8,1... | collective-permute-start | bytes 884744 | tf_op jit(solution)/shard_map/ppermute | solution.py:187
  54.8 36.3 %collective-permute-start.14 = (bf16[3,64,768]{2,1,0:T(8,128)(2,1)S(1)}, bf16[3,64,768]{2,1,0:T(8,128)(2,1)S(1)}, u32[]{:S(2)}, u32[]{:S(2)}) collective-permute-start(bf16[3,64,768]{2,1,0:T(8,128)(2,1)S(1)} %collective-permute-done.13.refs_2_), channel_id=1, source_target_pairs={{2,0},{3,1},{0,2},{1,3},{6,4},{7,5},{4,6},{5,7},{10,8},{11,9},{8,1... | collective-permute-start | bytes 884744 | tf_op jit(solution)/shard_map/ppermute | solution.py:187
  54.8 0.9 copy-start
  55.7 0.7 copy-start.2
  56.4 0.6 copy-start.3
  57.1 34.0 %copy-start.1 = (bf16[3,64,768]{2,1,0:T(8,128)(2,1)S(1)}, bf16[3,64,768]{2,1,0:T(8,128)(2,1)}, u32[]{:S(2)}) copy-start(bf16[3,64,768]{2,1,0:T(8,128)(2,1)} %assemble.1.refs_0_) | copy-start | bytes 884740

commit v2 on v0

v2 whole, which is shorter than its diff:
```python
import functools

import jax
import jax.numpy as jnp
from jax import lax
from jax.experimental import pallas as pl
from jax.experimental.pallas import tpu as pltpu
from jax.sharding import PartitionSpec as P

POLAR = 12
LANES = 128
F32 = jnp.float32
BF16 = jnp.bfloat16
MIB = 1 << 20


def vmem():
    return pl.BlockSpec(memory_space=pltpu.VMEM)


def smem():
    return pl.BlockSpec(memory_space=pltpu.SMEM)


def three_pieces(value):
    high = value.astype(BF16)
    rest = value - high.astype(F32)
    mid = rest.astype(BF16)
    low = (rest - mid.astype(F32)).astype(BF16)
    return high, mid, low


def rotated_sum(rot, coords):
    depth = coords.shape[0] * coords.shape[1]
    flat = jnp.concatenate([rot[:, part, :] for part in range(3)], axis=1)
    padded = jnp.concatenate([flat, jnp.zeros((5, depth), F32)], axis=0)
    stacked = jnp.concatenate(three_pieces(padded), axis=0)
    product = jnp.dot(stacked, coords.reshape(depth, coords.shape[2]), preferred_element_type=F32)
    return (product[16:19] + product[8:11]) + product[0:3]


def partial_centre_kernel(frame_total, col, rot_ref, coords_ref, out_ref):
    local = coords_ref.shape[1]
    block = lax.broadcasted_iota(jnp.int32, rot_ref.shape, 2) // local
    rot = jnp.where(block == col[0], rot_ref[...], 0.0)
    coords = jnp.concatenate([coords_ref[...]] * (frame_total // local), axis=1)
    out_ref[...] = rotated_sum(rot, coords) * (1.0 / frame_total)


def put_block(out_ref, block, value):
    local = value.shape[1]
    out_ref[:, pl.ds(pl.multiple_of(block * local, local), local), :] = value


def assemble_kernel(members, row, *refs):
    blocks, out_ref = refs[:-1], refs[-1]
    for step, ref in enumerate(blocks):
        put_block(out_ref, lax.rem(row[0] // members + step, len(blocks)), ref[...])


def rows_kernel(members, row, col, rot_ref, own_ref, panel_ref, *refs):
    others, (rows_ref, centre_ref) = refs[:-2], refs[-2:]
    at_home = row[0] // members == col[0]

    @pl.when(at_home)
    def _():
        rows_ref[...] = panel_ref[...]

    @pl.when(jnp.logical_not(at_home))
    def _():
        for step, ref in enumerate((own_ref, *others)):
            put_block(rows_ref, lax.rem(col[0] + step, len(others) + 1), ref[...])

    centre_ref[...] = rotated_sum(rot_ref[...], rows_ref[...]) * (1.0 / rows_ref.shape[1])


def add_weighted(inv_ref, centre, sums_ref):
    height, width = inv_ref.shape
    group = 64 if height % 64 == 0 else 8

    def body(step, carry):
        rows = pl.ds(pl.multiple_of(step * group, group), group)
        sums = [sums_ref[comp, rows, :] for comp in range(3)]
        for chunk in range(width // LANES):
            span = slice(chunk * LANES, (chunk + 1) * LANES)
            value = inv_ref[rows, span]
            for comp in range(3):
                sums[comp] = sums[comp] + value * centre[comp : comp + 1, span]
        for comp in range(3):
            sums_ref[comp, rows, :] = sums[comp]
        return carry

    lax.fori_loop(0, height // group, body, 0)


def weighted_kernel(halves, row, inv_ref, centre_ref, *refs):
    sums_ref = refs[-1]
    step = pl.program_id(0)

    @pl.when(step == 0)
    def _():
        sums_ref[...] = jnp.zeros_like(sums_ref)

    width = inv_ref.shape[1]
    for half in range(halves):

        @pl.when(lax.rem(step, halves) == half)
        def _(half=half):
            add_weighted(inv_ref, centre_ref[step // halves, :, half * width : (half + 1) * width], sums_ref)


def weighted_fit_kernel(halves, row, inv_ref, centre_ref, before_ref, rows_ref, out_ref, sums_ref):
    step = pl.program_id(0)

    @pl.when(step == 0)
    def _():
        sums_ref[...] = before_ref[...]

    width = inv_ref.shape[1]
    for half in range(halves):

        @pl.when(lax.rem(step, halves) == half)
        def _(half=half):
            add_weighted(inv_ref, centre_ref[step // halves, :, half * width : (half + 1) * width], sums_ref)

    @pl.when(step == pl.num_programs(0) - 1)
    def _():
        frame_total = rows_ref.shape[1]
        rows = rows_ref[...].reshape(3 * frame_total, rows_ref.shape[2])
        sums = jnp.concatenate([sums_ref[comp] for comp in range(3)], axis=1)
        high, mid, low = (jnp.dot(rows, piece, preferred_element_type=F32) for piece in three_pieces(sums))
        spread = (low + mid) + high
        entries = []
        for part in range(3):
            for comp in range(3):
                tile = spread[part * frame_total : (part + 1) * frame_total, comp * LANES : (comp + 1) * LANES]
                entries.append(jnp.sum(tile.T, axis=0, keepdims=True))
        first = jnp.concatenate(entries[:8], axis=0)
        last = jnp.concatenate([entries[8], jnp.zeros((7, frame_total), F32)], axis=0)
        message = jnp.concatenate([first, last], axis=1)
        out_ref[...] = jnp.broadcast_to(message[None], out_ref.shape)


def orthogonalized(message, frame_total):
    fitted = [message[entry : entry + 1, :frame_total] for entry in range(8)]
    fitted.append(message[0:1, frame_total:])
    norm = functools.reduce(lambda a, b: a + b, [value * value for value in fitted])
    scaling = jnp.sqrt(1.0 + norm)
    current = [[fitted[3 * col + row] / scaling for col in range(3)] for row in range(3)]
    for _ in range(POLAR):
        square = [[None] * 3 for _ in range(3)]
        for a in range(3):
            for b in range(a, 3):
                x, y = current[a], current[b]
                square[a][b] = square[b][a] = x[0] * y[0] + x[1] * y[1] + x[2] * y[2]
        cubed = [
            [square[a][0] * current[0][b] + square[a][1] * current[1][b] + square[a][2] * current[2][b] for b in range(3)]
            for a in range(3)
        ]
        current = [[1.5 * current[a][b] - 0.5 * cubed[a][b] for b in range(3)] for a in range(3)]
    return current


def put_deviations(wide_ref, coords_ref, centre, chunk, dev_ref):
    frame_total = coords_ref.shape[1]
    span = slice(chunk * LANES, (chunk + 1) * LANES)
    coords = [coords_ref[part, :, span].astype(F32) for part in range(3)]
    for comp in range(3):
        moved = wide_ref[3 * comp] * coords[0]
        moved = moved + wide_ref[3 * comp + 1] * coords[1]
        moved = moved + wide_ref[3 * comp + 2] * coords[2]
        value = moved - centre[comp : comp + 1, span]
        dev_ref[comp * frame_total : (comp + 1) * frame_total, span] = value.astype(BF16)


def put_tile(wide_ref, coords_ref, centre, rows_dev_ref, dev_ref, out_ref):
    width = coords_ref.shape[2]
    scale = 1.0 / (3 * coords_ref.shape[1])
    stride = 2 * LANES if width % (2 * LANES) == 0 else LANES
    for start in range(0, width, stride):
        for chunk in range(start // LANES, (start + stride) // LANES):
            put_deviations(wide_ref, coords_ref, centre, chunk, dev_ref)
        product = jnp.dot(rows_dev_ref[...], dev_ref[:, start : start + stride], preferred_element_type=F32)
        out_ref[:, start : start + stride] = product * scale


def first_tiles_kernel(count, row, col, fits_ref, rows_ref, rows_centre_ref, centre_ref, *refs):
    panel_refs = refs[:count]
    out_ref, rot_out_ref, wide_ref, rows_dev_ref, dev_ref = refs[count:]
    frame_total = rows_ref.shape[1]
    local = rot_out_ref.shape[2]

    @pl.when(pl.program_id(0) == 0)
    def _():
        current = orthogonalized(jnp.sum(fits_ref[...], axis=0), frame_total)
        for a in range(3):
            flat = jnp.concatenate(current[a], axis=0)
            kept = flat[:, :local]
            for block in range(1, frame_total // local):
                kept = jnp.where(col[0] == block, flat[:, block * local : (block + 1) * local], kept)
            rot_out_ref[a] = kept
            for b in range(3):
                wide_ref[3 * a + b] = jnp.broadcast_to(current[a][b], (LANES, frame_total)).T
        centre = rows_centre_ref[...]
        for chunk in range(rows_ref.shape[2] // LANES):
            put_deviations(wide_ref, rows_ref, centre, chunk, dev_ref)
        rows_dev_ref[...] = dev_ref[...].T

    for step in range(count):

        @pl.when(pl.program_id(0) == step)
        def _(step=step):
            put_tile(wide_ref, panel_refs[step], centre_ref[step], rows_dev_ref, dev_ref, out_ref)


def last_tiles_kernel(count, row, before_ref, wide_ref, rows_dev_ref, centre_ref, *refs):
    panel_refs = refs[:count]
    out_ref, dev_ref = refs[count:]
    for step in range(count):

        @pl.when(pl.program_id(0) == step)
        def _(step=step):
            put_tile(wide_ref, panel_refs[step], centre_ref[step], rows_dev_ref, dev_ref, out_ref)


def per_device(frames, rotations, inverse_cov):
    row_count, col_count = lax.axis_size("row"), lax.axis_size("col")
    members = row_count // col_count
    row = lax.axis_index("row").astype(jnp.int32).reshape(1)
    col = lax.axis_index("col").astype(jnp.int32).reshape(1)
    local, _, width = frames.shape
    frame_total = local * col_count
    device_total = row_count * col_count
    col_width = inverse_cov.shape[1]
    pairs_of_members = members // 2
    coords = jnp.transpose(frames, (1, 0, 2))

    def move(value, source_of, receives=lambda group, col: True):
        pairs = []
        for group in range(col_count):
            for member in range(members):
                for place in range(col_count):
                    if receives(group, place):
                        from_group, from_member, from_col = source_of(group, member, place)
                        source = (from_group * members + from_member) * col_count + from_col
                        pairs.append((source, (group * members + member) * col_count + place))
        return lax.ppermute(value, ("row", "col"), pairs)

    def from_panel_row(value, step):
        return move(value, lambda g, m, c: (c, m, (g + step) % col_count))

    def from_member(value, mask):
        return move(value, lambda g, m, c: (g, m ^ mask, c))

    panel_parts = [from_panel_row(coords, step) for step in range(col_count)]
    partial = pl.pallas_call(
        functools.partial(partial_centre_kernel, frame_total),
        out_shape=jax.ShapeDtypeStruct((3, width), F32),
        in_specs=[smem(), vmem(), vmem()],
        out_specs=vmem(),
        name="partial_centre",
    )(col, rotations, coords)
    parts = [from_panel_row(partial, step) for step in range(col_count)]
    own_centre = functools.reduce(lambda a, b: a + b, parts)
    centres = [own_centre] + [from_member(own_centre, 2 * step) for step in range(1, pairs_of_members)]
    centres, panel_parts, late_coords = lax.optimization_barrier((centres, panel_parts, coords))
    even_centres = jnp.stack(centres)
    odd_centres = from_member(even_centres, 1)

    others = [
        move(late_coords, lambda g, m, c, s=step: (g, m, (c + s) % col_count), lambda g, c: g != c)
        for step in range(1, col_count)
    ]
    own_block = pl.pallas_call(
        functools.partial(assemble_kernel, members),
        out_shape=jax.ShapeDtypeStruct((3, frame_total, width), BF16),
        in_specs=[smem()] + [vmem()] * col_count,
        out_specs=vmem(),
        name="assemble",
    )(row, *panel_parts)
    even_panel = [own_block] + [from_member(own_block, 2 * step) for step in range(1, pairs_of_members)]

    rows_all, rows_centre = pl.pallas_call(
        functools.partial(rows_kernel, members),
        out_shape=(
            jax.ShapeDtypeStruct((3, frame_total, width), BF16),
            jax.ShapeDtypeStruct((3, width), F32),
        ),
        in_specs=[smem(), smem()] + [vmem()] * (2 + col_count),
        out_specs=(vmem(), vmem()),
        name="rows",
    )(row, col, rotations, coords, own_block, *others)

    halves = 2 if width % (2 * LANES) == 0 else 1
    piece = width // halves
    steps = pairs_of_members * halves

    def inv_spec(odd):
        def index(i, row):
            return (0, (lax.rem(row[0], members) ^ (2 * (i // halves) + odd)) * halves + lax.rem(i, halves))

        return pl.BlockSpec((width, piece), index)

    weighted_cost = pl.CostEstimate(
        flops=3 * width * col_width, bytes_accessed=2 * width * col_width, transcendentals=0
    )
    even_sums = pl.pallas_call(
        functools.partial(weighted_kernel, halves),
        grid_spec=pltpu.PrefetchScalarGridSpec(
            num_scalar_prefetch=1, grid=(steps,), in_specs=[inv_spec(0), vmem()], out_specs=vmem()
        ),
        out_shape=jax.ShapeDtypeStruct((3, width, LANES), F32),
        compiler_params=pltpu.CompilerParams(vmem_limit_bytes=24 * MIB),
        cost_estimate=weighted_cost,
        name="weighted_even",
    )(row, inverse_cov, even_centres)
    message = pl.pallas_call(
        functools.partial(weighted_fit_kernel, halves),
        grid_spec=pltpu.PrefetchScalarGridSpec(
            num_scalar_prefetch=1,
            grid=(steps,),
            in_specs=[inv_spec(1)] + [vmem()] * 3,
            out_specs=vmem(),
            scratch_shapes=[pltpu.VMEM((3, width, LANES), F32)],
        ),
        out_shape=jax.ShapeDtypeStruct((device_total, 8, 2 * frame_total), F32),
        compiler_params=pltpu.CompilerParams(vmem_limit_bytes=24 * MIB),
        cost_estimate=weighted_cost,
        name="weighted_odd_and_fit",
    )(row, inverse_cov, odd_centres, even_sums, rows_all)
    fits = lax.all_to_all(message, ("row", "col"), split_axis=0, concat_axis=0, tiled=True)
    fits, even_panel = lax.optimization_barrier((fits, even_panel))
    odd_panel = [from_member(block, 1) for block in even_panel]

    def tile_spec(odd):
        return pl.BlockSpec((width, width), lambda i, row, *_: (0, lax.rem(row[0], members) ^ (2 * i + odd)))

    tiles_cost = pl.CostEstimate(
        flops=3 * frame_total * width * col_width, bytes_accessed=2 * width * col_width, transcendentals=0
    )
    dev_scratch = pltpu.VMEM((3 * frame_total, width), BF16)
    half_done, transforms, wide, rows_dev = pl.pallas_call(
        functools.partial(first_tiles_kernel, pairs_of_members),
        grid_spec=pltpu.PrefetchScalarGridSpec(
            num_scalar_prefetch=2,
            grid=(pairs_of_members,),
            in_specs=[vmem()] * (4 + pairs_of_members),
            out_specs=(tile_spec(0), vmem(), vmem(), vmem()),
            scratch_shapes=[dev_scratch],
        ),
        out_shape=(
            jax.ShapeDtypeStruct((width, col_width), F32),
            jax.ShapeDtypeStruct((3, 3, local), F32),
            jax.ShapeDtypeStruct((9, frame_total, LANES), F32),
            jax.ShapeDtypeStruct((width, 3 * frame_total), BF16),
        ),
        compiler_params=pltpu.CompilerParams(vmem_limit_bytes=32 * MIB),
        cost_estimate=tiles_cost,
        name="steps_and_even_tiles",
    )(row, col, fits, rows_all, rows_centre, even_centres, *even_panel)
    covariance = pl.pallas_call(
        functools.partial(last_tiles_kernel, pairs_of_members),
        grid_spec=pltpu.PrefetchScalarGridSpec(
            num_scalar_prefetch=1,
            grid=(pairs_of_members,),
            in_specs=[pl.BlockSpec(memory_space=pl.ANY)] + [vmem()] * (3 + pairs_of_members),
            out_specs=tile_spec(1),
            scratch_shapes=[dev_scratch],
        ),
        out_shape=jax.ShapeDtypeStruct((width, col_width), F32),
        input_output_aliases={1: 0},
        compiler_params=pltpu.CompilerParams(vmem_limit_bytes=32 * MIB),
        cost_estimate=tiles_cost,
        name="odd_tiles",
    )(row, half_done, wide, rows_dev, odd_centres, *odd_panel)
    return (covariance, transforms)


def solution(mesh):
    placed = (P("col", None, "row"), P(), P("row", "col"))
    return jax.shard_map(
        per_device,
        mesh=mesh,
        in_specs=placed,
        out_specs=(P("row", "col"), P(None, None, "col")),
        check_vma=False,
    )
```

time: 204 us -> 83.7 us (0.41)
  blocking collectives: 99.9 us -> 0 us
  matrix products: 36.7 us -> 0 us
  waiting for transfers between devices: 40.3 us -> 13.8 us
  Pallas kernels: 0 us -> 26.1 us
  starting transfers between devices: 3.85 us -> 27.6 us
  between operations: 14.3 us -> 0.76 us
  local copies, waits for them, and re-layouts: 8.16 us -> 15 us
    all_gather x2 -> x0, blocking collectives: 53 us -> none  [the longest x1 30.9 us: per_device(): rows_operand = lax.all_gather(local_dev, 'col', axis=0, tiled=True)]
    psum x3 -> x0, blocking collectives: 46.9 us -> none  [the longest x1 30.2 us: per_device(): fitted = lax.psum(fit_part, 'row')]
    all_gather x1 -> x0, waiting for transfers between devices: 40.3 us -> none  [per_device(): dev_atoms = lax.all_gather(local_dev, 'row', axis=1, tiled=True)]
    dot_general x29 -> x0, matrix products: 36.7 us -> none  [the longest x1 18.1 us: per_device(): lax.dot_general(centre_cols, inverse_cov, (((1,), (1,)), ((), ())), preci...]
    pallas_call x0 -> x7, Pallas kernels: none -> 26.1 us  [the longest x1 7.02 us: per_device(): pl.pallas_call(functools.partial(first_tiles_kernel, pairs_of_members), g...]
    ppermute x0 -> x16, starting transfers between devices: none -> 24.6 us  [move(): return lax.ppermute(value, ('row', 'col'), pairs)]
    unnamed x3 -> x18, local copies, waits for them, and re-layouts: 0.66 us -> 15 us
    all_to_all x1, waiting for transfers between devices: 0.01 us -> 8.59 us  [per_device(): lax.all_to_all(message, ('row', 'col'), split_axis=0, concat_axis=0, tile...]
  transfers between devices with their start and end apart: 2 -> 17, of which waited for: 1 -> 5; matrix products, arithmetic and copies ran while one was open for 0% -> 0% of each run, Pallas kernels for 0% -> 24%
where the time goes in v2:
time: 83.7 us; the launch traced here: 83.2 us
  starting transfers between devices  27.6 us (33%)
  Pallas kernels  26.1 us (31%)
  local copies, waits for them, and re-layouts  15 us (18%)
  waiting for transfers between devices  13.8 us (16%)
    ppermute x16, starting transfers between devices, move(): return lax.ppermute(value, ('row', 'col'), pairs)  24.6 us
    unnamed x18, local copies, waits for them, and re-layouts  15 us
    all_to_all x1, waiting for transfers between devices, per_device(): lax.all_to_all(message, ('row', 'col'), split_axis=0, concat_axis=0, tile...  8.59 us
    pallas_call x1, Pallas kernels, per_device(): pl.pallas_call(functools.partial(first_tiles_kernel, pairs_of_members), g...  7.02 us
    ppermute x16, waiting for transfers between devices, move(): return lax.ppermute(value, ('row', 'col'), pairs)  5.2 us
    pallas_call x1, Pallas kernels, per_device(): pl.pallas_call(functools.partial(weighted_fit_kernel, halves), grid_spec=...  5.11 us
    pallas_call x1, Pallas kernels, per_device(): pl.pallas_call(functools.partial(last_tiles_kernel, pairs_of_members), gr...  4.74 us
    pallas_call x1, Pallas kernels, per_device(): pl.pallas_call(functools.partial(weighted_kernel, halves), grid_spec=pltp...  3.75 us
  transfers between devices with their start and end apart: 17, of which 5 were waited for; matrix products, arithmetic and copies ran while one was open for 0% of the time, Pallas kernels for 24%

profile of v2, /device:TPU:0, one launch (start us, length us, event | category | flops | bytes accessed | tf_op | source)
XLA Modules:
  0.0 83.2 jit_solution(221582781787889100)
XLA Ops:
  0.6 4.1 %collective-permute-start.6 = (bf16[3,32,768]{2,1,0:T(8,128)(2,1)}, bf16[3,32,768]{2,1,0:T(8,128)(2,1)S(1)}, u32[]{:S(2)}, u32[]{:S(2)}) collective-permute-start(bf16[3,32,768]{2,1,0:T(8,128)(2,1)} %bitcast.7), channel_id=1, source_target_pairs={{1,0},{17,1},{3,2},{19,3},{5,4},{21,5},{7,6},{23,7},{9,8},{25,9},{... | collective-permute-start | bytes 442376 | tf_op jit(solution)/shard_map/ppermute | solution.py:247
  4.7 1.6 %collective-permute-start.5 = (bf16[3,32,768]{2,1,0:T(8,128)(2,1)}, bf16[3,32,768]{2,1,0:T(8,128)(2,1)S(1)}, u32[]{:S(2)}, u32[]{:S(2)}) collective-permute-start(bf16[3,32,768]{2,1,0:T(8,128)(2,1)} %bitcast.8), channel_id=1, source_target_pairs={{0,0},{16,1},{2,2},{18,3},{4,4},{20,5},{6,6},{22,7},{8,8},{24,9},{... | collective-permute-start | bytes 442376 | tf_op jit(solution)/shard_map/ppermute | solution.py:247
  6.3 1.8 %partial_centre.1 = f32[3,768]{1,0:T(4,128)} custom-call(s32[1]{0:T(128)} %bitcast.1.col, f32[3,3,64]{2,1,0:T(4,128)} %rot_ref.3, bf16[3,32,768]{2,1,0:T(8,128)(2,1)} %bitcast.9), custom_call_target="tpu_custom_call" | custom-call | tf_op jit(solution)/shard_map/partial_centre/pallas_call | solution.py:256
  8.0 1.9 %collective-permute-start.1 = (f32[3,768]{1,0:T(4,128)}, f32[3,768]{1,0:T(4,128)S(1)}, u32[]{:S(2)}, u32[]{:S(2)}) collective-permute-start(f32[3,768]{1,0:T(4,128)} %partial_centre.1), channel_id=1, source_target_pairs={{1,0},{17,1},{3,2},{19,3},{5,4},{21,5},{7,6},{23,7},{9,8},{25,9},{... | collective-permute-start | bytes 27656 | tf_op jit(solution)/shard_map/ppermute | solution.py:247
  9.9 1.4 %collective-permute-start = (f32[3,768]{1,0:T(4,128)}, f32[3,768]{1,0:T(4,128)S(1)}, u32[]{:S(2)}, u32[]{:S(2)}) collective-permute-start(f32[3,768]{1,0:T(4,128)} %partial_centre.1), channel_id=1, source_target_pairs={{0,0},{16,1},{2,2},{18,3},{4,4},{20,5},{6,6},{22,7},{8,8},{24,9},{... | collective-permute-start | bytes 27656 | tf_op jit(solution)/shard_map/ppermute | solution.py:247
  11.3 2.0 %collective-permute-done.1 = f32[3,768]{1,0:T(4,128)S(1)} collective-permute-done((f32[3,768]{1,0:T(4,128)}, f32[3,768]{1,0:T(4,128)S(1)}, u32[]{:S(2)}, u32[]{:S(2)}) %collective-permute-start.1) | collective-permute-done | bytes 9248 | tf_op jit(solution)/shard_map/ppermute | solution.py:247
  13.3 0.0 collective-permute-done
  13.3 2.6 %collective-permute-start.4 = (f32[3,768]{1,0:T(4,128)S(1)}, f32[3,768]{1,0:T(4,128)S(1)}, u32[]{:S(2)}, u32[]{:S(2)}) collective-permute-start(f32[3,768]{1,0:T(4,128)S(1)} %add.3), channel_id=1, source_target_pairs={{12,0},{13,1},{14,2},{15,3},{8,4},{9,5},{10,6},{11,7},{4,8},{5,9},... | collective-permute-start | bytes 27656 | tf_op jit(solution)/shard_map/ppermute | solution.py:247
  15.9 0.4 collective-permute-start.3
  16.3 0.5 collective-permute-start.2
  16.8 1.1 %collective-permute-done.4 = f32[3,768]{1,0:T(4,128)S(1)} collective-permute-done((f32[3,768]{1,0:T(4,128)S(1)}, f32[3,768]{1,0:T(4,128)S(1)}, u32[]{:S(2)}, u32[]{:S(2)}) %collective-permute-start.4) | collective-permute-done | bytes 9248 | tf_op jit(solution)/shard_map/ppermute | solution.py:247
  17.9 1.6 %collective-permute-done.3 = f32[3,768]{1,0:T(4,128)S(1)} collective-permute-done((f32[3,768]{1,0:T(4,128)S(1)}, f32[3,768]{1,0:T(4,128)S(1)}, u32[]{:S(2)}, u32[]{:S(2)}) %collective-permute-start.3) | collective-permute-done | bytes 9248 | tf_op jit(solution)/shard_map/ppermute | solution.py:247
  19.6 0.4 collective-permute-done.2
  20.0 0.0 collective-permute-done.6.refs_1_
  20.0 0.0 collective-permute-done.5.refs_0_
  20.0 0.6 copy-done.6
  20.7 0.1 copy-done.7
  20.7 1.7 %assemble.1.panel_ref.refs_0_ = bf16[3,64,768]{2,1,0:T(8,128)(2,1)} custom-call(s32[1]{0:T(128)} %bitcast.row, bf16[3,32,768]{2,1,0:T(8,128)(2,1)} %copy-done.7, bf16[3,32,768]{2,1,0:T(8,128)(2,1)} %copy-done.6), custom_call_target="tpu_custom_call" | custom-call | tf_op jit(solution)/shard_map/assemble/pallas_call | solution.py:274
  22.5 1.5 %collective-permute-start.11 = (bf16[3,64,768]{2,1,0:T(8,128)(2,1)}, bf16[3,64,768]{2,1,0:T(8,128)(2,1)S(1)}, u32[]{:S(2)}, u32[]{:S(2)}) collective-permute-start(bf16[3,64,768]{2,1,0:T(8,128)(2,1)} %assemble.1.panel_ref.refs_0_), channel_id=1, source_target_pairs={{12,0},{13,1},{14,2},{15,3},{8,4},{9,5},{10,6},{11,7},{4,8},{5,9},... | collective-permute-start | bytes 884744 | tf_op jit(solution)/shard_map/ppermute | solution.py:247
  24.0 0.4 collective-permute-start.10
  24.4 1.5 %collective-permute-start.9 = (bf16[3,64,768]{2,1,0:T(8,128)(2,1)}, bf16[3,64,768]{2,1,0:T(8,128)(2,1)S(1)}, u32[]{:S(2)}, u32[]{:S(2)}) collective-permute-start(bf16[3,64,768]{2,1,0:T(8,128)(2,1)} %assemble.1.panel_ref.refs_0_), channel_id=1, source_target_pairs={{4,0},{5,1},{6,2},{7,3},{0,4},{1,5},{2,6},{3,7},{12,8},{13,9},{14,... | collective-permute-start | bytes 884744 | tf_op jit(solution)/shard_map/ppermute | solution.py:247
  25.9 7.5 %collective-permute-start.8 = (bf16[3,32,768]{2,1,0:T(8,128)(2,1)}, bf16[3,32,768]{2,1,0:T(8,128)(2,1)S(1)}, u32[]{:S(2)}, u32[]{:S(2)}) collective-permute-start(bf16[3,32,768]{2,1,0:T(8,128)(2,1)} %bitcast.10), channel_id=1, source_target_pairs={{0,1},{2,3},{4,5},{6,7},{8,9},{10,11},{12,13},{14,15},{17,16},{19,... | collective-permute-start | bytes 442376 | tf_op jit(solution)/shard_map/ppermute | solution.py:247
  33.5 0.1 collective-permute-start.7
  33.6 0.0 copy-start
  33.6 6.4 %copy-done = f32[768,6144]{1,0:T(8,128)S(1)} copy-done((f32[768,6144]{1,0:T(8,128)S(1)}, f32[768,6144]{1,0:T(8,128)}, u32[]{:S(2)}) %copy-start) | copy-done | bytes 18874392
  40.0 3.8 %weighted_even.1.before_ref = f32[3,768,128]{2,1,0:T(8,128)S(1)} custom-call(s32[1]{0:T(128)} %bitcast.row, f32[768,6144]{1,0:T(8,128)S(1)} %copy-done, f32[4,3,768]{2,1,0:T(4,128)S(1)} %pad_maximum_fusion.centre_ref), custom_call_target="tpu_custom_call" | custom-call | flops 14155776 | bytes 9437184 | tf_op jit(solution)/shard_map/weighted_even/pallas_call | solution.py:307
  43.7 0.0 collective-permute-done.8.refs_0_
  43.7 0.6 copy-done.8
  44.4 1.9 %rows.1 = (bf16[3,64,768]{2,1,0:T(8,128)(2,1)}, f32[3,768]{1,0:T(4,128)}) custom-call(s32[1]{0:T(128)} %bitcast.row, s32[1]{0:T(128)} %bitcast.1.col, f32[3,3,64]{2,1,0:T(4,128)} %rot_ref.3, bf16[3,32,768]{2,1,0:T(8,128)(2,1)} %bitcast.11, bf16[3,64,768]{2,1,0:T(8,128)(2,1)} %assemble.1.panel_ref.refs_0_, bf16[3,32,768]{2,1,0:T(8,128)(2,1)} %copy-done.8), custom_call_target="tpu_custom_call" | custom-call | tf_op jit(solution)/shard_map/rows/pallas_call | solution.py:283
  46.3 0.0 collective-permute-done.7.centre_ref
  46.3 6.4 %copy-done.1 = f32[768,6144]{1,0:T(8,128)S(1)} copy-done((f32[768,6144]{1,0:T(8,128)S(1)}, f32[768,6144]{1,0:T(8,128)}, u32[]{:S(2)}) %copy-start.1) | copy-done | bytes 18874392
  52.7 1.0 %copy-done.3 = bf16[3,64,768]{2,1,0:T(8,128)(2,1)S(1)} copy-done((bf16[3,64,768]{2,1,0:T(8,128)(2,1)S(1)}, bf16[3,64,768]{2,1,0:T(8,128)(2,1)}, u32[]{:S(2)}) %copy-start.3) | copy-done | bytes 294936
  53.7 5.1 %weighted_odd_and_fit.1 = f32[32,8,128]{2,1,0:T(8,128)} custom-call(s32[1]{0:T(128)} %bitcast.row, f32[768,6144]{1,0:T(8,128)S(1)} %copy-done.1, f32[4,3,768]{2,1,0:T(4,128)S(1)} %collective-permute-done.7.centre_ref, f32[3,768,128]{2,1,0:T(8,128)S(1)} %weighted_even.1.before_ref, bf16[3,64,768]{2,1,0:T(8,128)(2,1)S(1)} %copy-done.3), custom_call_target="tpu_custom_call" | custom-call | flops 14155776 | bytes 9437184 | tf_op jit(solution)/shard_map/weighted_odd_and_fit/pallas_call | solution.py:317
  58.8 3.0 %all-to-all-start = ((f32[32,8,128]{2,1,0:T(8,128)}), f32[32,8,128]{2,1,0:T(8,128)S(1)}, u32[]{:S(2)}, u32[]{:S(2)}) async-start(f32[32,8,128]{2,1,0:T(8,128)} %weighted_odd_and_fit.1), calls=%async_computation | async-start | bytes 262144 | tf_op jit(solution)/shard_map/all_to_all | solution.py:331
  61.8 0.0 collective-permute-done.11.refs_3_
  61.8 0.0 collective-permute-done.10.refs_2_
  61.8 0.0 collective-permute-done.9.refs_1_
  61.8 8.6 %all-to-all-done.fits_ref = f32[32,8,128]{2,1,0:T(8,128)S(1)} async-done(((f32[32,8,128]{2,1,0:T(8,128)}), f32[32,8,128]{2,1,0:T(8,128)S(1)}, u32[]{:S(2)}, u32[]{:S(2)}) %all-to-all-start) | async-done | bytes 131104 | tf_op jit(solution)/shard_map/all_to_all | solution.py:331
  70.4 0.0 collective-permute-start.12
  70.4 0.5 collective-permute-start.13
  70.9 0.0 collective-permute-start.14
  70.9 0.5 collective-permute-start.15
  71.4 7.0 %steps_and_even_tiles.1 = (f32[768,6144]{1,0:T(8,128)}, f32[3,3,32]{2,1,0:T(4,128)}, f32[9,64,128]{2,1,0:T(8,128)S(1)}, bf16[768,192]{1,0:T(8,128)(2,1)S(1)}) custom-call(s32[1]{0:T(128)} %bitcast.row, s32[1]{0:T(128)} %bitcast.1.col, f32[32,8,128]{2,1,0:T(8,128)S(1)} %all-to-all-done.fits_ref, bf16[3,64,768]{2,1,0:T(8,128)(2,1)S(1)} %copy-done.4, ...), custom_call_target="tpu_custom_call" | custom-call | flops 905969664 | bytes 9437184 | tf_op jit(solution)/shard_map/steps_and_even_tiles/pallas_call | solution.py:342
  78.5 0.0 collective-permute-done.12.refs_0_
  78.5 0.0 collective-permute-done.13.refs_1_
  78.5 0.0 collective-permute-done.14.refs_2_
  78.5 0.0 collective-permute-done.15.refs_3_
  78.5 4.7 %odd_tiles.1 = f32[768,6144]{1,0:T(8,128)} custom-call(s32[1]{0:T(128)} %bitcast.row, f32[768,6144]{1,0:T(8,128)} %get-tuple-element.34.before_ref, f32[9,64,128]{2,1,0:T(8,128)S(1)} %get-tuple-element.35.wide_ref, bf16[768,192]{1,0:T(8,128)(2,1)S(1)} %get-tuple-element.36.rows_dev_ref, ...), custom_call_target="tpu_custom_call", output_to_operand_aliasing={{}: (1, {})} | custom-call | flops 905969664 | bytes 9437184 | tf_op jit(solution)/shard_map/odd_tiles/pallas_call | solution.py:361
  (13 shorter events, 0.0 us)
Async XLA Ops:
  0.6 19.4 %collective-permute-start.6 = (bf16[3,32,768]{2,1,0:T(8,128)(2,1)}, bf16[3,32,768]{2,1,0:T(8,128)(2,1)S(1)}, u32[]{:S(2)}, u32[]{:S(2)}) collective-permute-start(bf16[3,32,768]{2,1,0:T(8,128)(2,1)} %bitcast.7), channel_id=1, source_target_pairs={{1,0},{17,1},{3,2},{19,3},{5,4},{21,5},{7,6},{23,7},{9,8},{25,9},{... | collective-permute-start | bytes 442376 | tf_op jit(solution)/shard_map/ppermute | solution.py:247
  4.7 15.3 %collective-permute-start.5 = (bf16[3,32,768]{2,1,0:T(8,128)(2,1)}, bf16[3,32,768]{2,1,0:T(8,128)(2,1)S(1)}, u32[]{:S(2)}, u32[]{:S(2)}) collective-permute-start(bf16[3,32,768]{2,1,0:T(8,128)(2,1)} %bitcast.8), channel_id=1, source_target_pairs={{0,0},{16,1},{2,2},{18,3},{4,4},{20,5},{6,6},{22,7},{8,8},{24,9},{... | collective-permute-start | bytes 442376 | tf_op jit(solution)/shard_map/ppermute | solution.py:247
  8.0 5.2 %collective-permute-start.1 = (f32[3,768]{1,0:T(4,128)}, f32[3,768]{1,0:T(4,128)S(1)}, u32[]{:S(2)}, u32[]{:S(2)}) collective-permute-start(f32[3,768]{1,0:T(4,128)} %partial_centre.1), channel_id=1, source_target_pairs={{1,0},{17,1},{3,2},{19,3},{5,4},{21,5},{7,6},{23,7},{9,8},{25,9},{... | collective-permute-start | bytes 27656 | tf_op jit(solution)/shard_map/ppermute | solution.py:247
  9.9 3.3 %collective-permute-start = (f32[3,768]{1,0:T(4,128)}, f32[3,768]{1,0:T(4,128)S(1)}, u32[]{:S(2)}, u32[]{:S(2)}) collective-permute-start(f32[3,768]{1,0:T(4,128)} %partial_centre.1), channel_id=1, source_target_pairs={{0,0},{16,1},{2,2},{18,3},{4,4},{20,5},{6,6},{22,7},{8,8},{24,9},{... | collective-permute-start | bytes 27656 | tf_op jit(solution)/shard_map/ppermute | solution.py:247
  13.3 4.7 %collective-permute-start.4 = (f32[3,768]{1,0:T(4,128)S(1)}, f32[3,768]{1,0:T(4,128)S(1)}, u32[]{:S(2)}, u32[]{:S(2)}) collective-permute-start(f32[3,768]{1,0:T(4,128)S(1)} %add.3), channel_id=1, source_target_pairs={{12,0},{13,1},{14,2},{15,3},{8,4},{9,5},{10,6},{11,7},{4,8},{5,9},... | collective-permute-start | bytes 27656 | tf_op jit(solution)/shard_map/ppermute | solution.py:247
  15.9 3.7 %collective-permute-start.3 = (f32[3,768]{1,0:T(4,128)S(1)}, f32[3,768]{1,0:T(4,128)S(1)}, u32[]{:S(2)}, u32[]{:S(2)}) collective-permute-start(f32[3,768]{1,0:T(4,128)S(1)} %add.3), channel_id=1, source_target_pairs={{8,0},{9,1},{10,2},{11,3},{12,4},{13,5},{14,6},{15,7},{0,8},{1,9},... | collective-permute-start | bytes 27656 | tf_op jit(solution)/shard_map/ppermute | solution.py:247
  16.3 3.7 %collective-permute-start.2 = (f32[3,768]{1,0:T(4,128)S(1)}, f32[3,768]{1,0:T(4,128)S(1)}, u32[]{:S(2)}, u32[]{:S(2)}) collective-permute-start(f32[3,768]{1,0:T(4,128)S(1)} %add.3), channel_id=1, source_target_pairs={{4,0},{5,1},{6,2},{7,3},{0,4},{1,5},{2,6},{3,7},{12,8},{13,9},{14,... | collective-permute-start | bytes 27656 | tf_op jit(solution)/shard_map/ppermute | solution.py:247
  20.0 0.7 copy-start.6
  20.0 0.7 copy-start.7
  22.5 39.3 %collective-permute-start.11 = (bf16[3,64,768]{2,1,0:T(8,128)(2,1)}, bf16[3,64,768]{2,1,0:T(8,128)(2,1)S(1)}, u32[]{:S(2)}, u32[]{:S(2)}) collective-permute-start(bf16[3,64,768]{2,1,0:T(8,128)(2,1)} %assemble.1.panel_ref.refs_0_), channel_id=1, source_target_pairs={{12,0},{13,1},{14,2},{15,3},{8,4},{9,5},{10,6},{11,7},{4,8},{5,9},... | collective-permute-start | bytes 884744 | tf_op jit(solution)/shard_map/ppermute | solution.py:247
  24.0 37.8 %collective-permute-start.10 = (bf16[3,64,768]{2,1,0:T(8,128)(2,1)}, bf16[3,64,768]{2,1,0:T(8,128)(2,1)S(1)}, u32[]{:S(2)}, u32[]{:S(2)}) collective-permute-start(bf16[3,64,768]{2,1,0:T(8,128)(2,1)} %assemble.1.panel_ref.refs_0_), channel_id=1, source_target_pairs={{8,0},{9,1},{10,2},{11,3},{12,4},{13,5},{14,6},{15,7},{0,8},{1,9},... | collective-permute-start | bytes 884744 | tf_op jit(solution)/shard_map/ppermute | solution.py:247
  24.4 37.4 %collective-permute-start.9 = (bf16[3,64,768]{2,1,0:T(8,128)(2,1)}, bf16[3,64,768]{2,1,0:T(8,128)(2,1)S(1)}, u32[]{:S(2)}, u32[]{:S(2)}) collective-permute-start(bf16[3,64,768]{2,1,0:T(8,128)(2,1)} %assemble.1.panel_ref.refs_0_), channel_id=1, source_target_pairs={{4,0},{5,1},{6,2},{7,3},{0,4},{1,5},{2,6},{3,7},{12,8},{13,9},{14,... | collective-permute-start | bytes 884744 | tf_op jit(solution)/shard_map/ppermute | solution.py:247
  25.9 17.8 %collective-permute-start.8 = (bf16[3,32,768]{2,1,0:T(8,128)(2,1)}, bf16[3,32,768]{2,1,0:T(8,128)(2,1)S(1)}, u32[]{:S(2)}, u32[]{:S(2)}) collective-permute-start(bf16[3,32,768]{2,1,0:T(8,128)(2,1)} %bitcast.10), channel_id=1, source_target_pairs={{0,1},{2,3},{4,5},{6,7},{8,9},{10,11},{12,13},{14,15},{17,16},{19,... | collective-permute-start | bytes 442376 | tf_op jit(solution)/shard_map/ppermute | solution.py:247
  33.5 12.8 %collective-permute-start.7 = (f32[4,3,768]{2,1,0:T(4,128)S(1)}, f32[4,3,768]{2,1,0:T(4,128)S(1)}, u32[]{:S(2)}, u32[]{:S(2)}) collective-permute-start(f32[4,3,768]{2,1,0:T(4,128)S(1)} %pad_maximum_fusion.centre_ref), channel_id=1, source_target_pairs={{2,0},{3,1},{0,2},{1,3},{6,4},{7,5},{4,6},{5,7},{10,8},{11,9},{8,1... | collective-permute-start | bytes 110600 | tf_op jit(solution)/shard_map/ppermute | solution.py:247
  33.6 6.4 %copy-start = (f32[768,6144]{1,0:T(8,128)S(1)}, f32[768,6144]{1,0:T(8,128)}, u32[]{:S(2)}) copy-start(f32[768,6144]{1,0:T(8,128)} %inv_ref.3) | copy-start | bytes 56623108
  40.0 30.5 %copy-start.2 = (bf16[3,64,768]{2,1,0:T(8,128)(2,1)S(1)}, bf16[3,64,768]{2,1,0:T(8,128)(2,1)}, u32[]{:S(2)}) copy-start(bf16[3,64,768]{2,1,0:T(8,128)(2,1)} %assemble.1.panel_ref.refs_0_) | copy-start | bytes 884740
  43.7 0.7 copy-start.8
  46.3 6.4 %copy-start.1 = (f32[768,6144]{1,0:T(8,128)S(1)}, f32[768,6144]{1,0:T(8,128)}, u32[]{:S(2)}) copy-start(f32[768,6144]{1,0:T(8,128)} %inv_ref.3) | copy-start | bytes 56623108
  52.7 1.0 %copy-start.3 = (bf16[3,64,768]{2,1,0:T(8,128)(2,1)S(1)}, bf16[3,64,768]{2,1,0:T(8,128)(2,1)}, u32[]{:S(2)}) copy-start(bf16[3,64,768]{2,1,0:T(8,128)(2,1)} %get-tuple-element.27.rows_ref) | copy-start | bytes 884740
  53.7 17.8 %copy-start.4 = (bf16[3,64,768]{2,1,0:T(8,128)(2,1)S(1)}, bf16[3,64,768]{2,1,0:T(8,128)(2,1)}, u32[]{:S(2)}) copy-start(bf16[3,64,768]{2,1,0:T(8,128)(2,1)} %get-tuple-element.27.rows_ref) | copy-start | bytes 884740
  53.7 17.8 %copy-start.5 = (f32[3,768]{1,0:T(4,128)S(1)}, f32[3,768]{1,0:T(4,128)}, u32[]{:S(2)}) copy-start(f32[3,768]{1,0:T(4,128)} %get-tuple-element.29.rows_centre_ref) | copy-start | bytes 27652
  58.8 11.6 %all-to-all-start = ((f32[32,8,128]{2,1,0:T(8,128)}), f32[32,8,128]{2,1,0:T(8,128)S(1)}, u32[]{:S(2)}, u32[]{:S(2)}) async-start(f32[32,8,128]{2,1,0:T(8,128)} %weighted_odd_and_fit.1), calls=%async_computation | async-start | bytes 262144 | tf_op jit(solution)/shard_map/all_to_all | solution.py:331
  70.4 8.1 %collective-permute-start.12 = (bf16[3,64,768]{2,1,0:T(8,128)(2,1)S(1)}, bf16[3,64,768]{2,1,0:T(8,128)(2,1)S(1)}, u32[]{:S(2)}, u32[]{:S(2)}) collective-permute-start(bf16[3,64,768]{2,1,0:T(8,128)(2,1)S(1)} %copy-done.2), channel_id=1, source_target_pairs={{2,0},{3,1},{0,2},{1,3},{6,4},{7,5},{4,6},{5,7},{10,8},{11,9},{8,1... | collective-permute-start | bytes 884744 | tf_op jit(solution)/shard_map/ppermute | solution.py:247
  70.4 8.1 %collective-permute-start.13 = (bf16[3,64,768]{2,1,0:T(8,128)(2,1)S(1)}, bf16[3,64,768]{2,1,0:T(8,128)(2,1)S(1)}, u32[]{:S(2)}, u32[]{:S(2)}) collective-permute-start(bf16[3,64,768]{2,1,0:T(8,128)(2,1)S(1)} %collective-permute-done.9.refs_1_), channel_id=1, source_target_pairs={{2,0},{3,1},{0,2},{1,3},{6,4},{7,5},{4,6},{5,7},{10,8},{11,9},{8,1... | collective-permute-start | bytes 884744 | tf_op jit(solution)/shard_map/ppermute | solution.py:247
  70.9 7.5 %collective-permute-start.14 = (bf16[3,64,768]{2,1,0:T(8,128)(2,1)S(1)}, bf16[3,64,768]{2,1,0:T(8,128)(2,1)S(1)}, u32[]{:S(2)}, u32[]{:S(2)}) collective-permute-start(bf16[3,64,768]{2,1,0:T(8,128)(2,1)S(1)} %collective-permute-done.10.refs_2_), channel_id=1, source_target_pairs={{2,0},{3,1},{0,2},{1,3},{6,4},{7,5},{4,6},{5,7},{10,8},{11,9},{8,1... | collective-permute-start | bytes 884744 | tf_op jit(solution)/shard_map/ppermute | solution.py:247
  70.9 7.5 %collective-permute-start.15 = (bf16[3,64,768]{2,1,0:T(8,128)(2,1)S(1)}, bf16[3,64,768]{2,1,0:T(8,128)(2,1)S(1)}, u32[]{:S(2)}, u32[]{:S(2)}) collective-permute-start(bf16[3,64,768]{2,1,0:T(8,128)(2,1)S(1)} %collective-permute-done.11.refs_3_), channel_id=1, source_target_pairs={{2,0},{3,1},{0,2},{1,3},{6,4},{7,5},{4,6},{5,7},{10,8},{11,9},{8,1... | collective-permute-start | bytes 884744 | tf_op jit(solution)/shard_map/ppermute | solution.py:247

commit v3 on v2

--- a/solution.py
+++ b/solution.py
@@ -56,22 +56,6 @@
     blocks, out_ref = refs[:-1], refs[-1]
     for step, ref in enumerate(blocks):
         put_block(out_ref, lax.rem(row[0] // members + step, len(blocks)), ref[...])
-
-
-def rows_kernel(members, row, col, rot_ref, own_ref, panel_ref, *refs):
-    others, (rows_ref, centre_ref) = refs[:-2], refs[-2:]
-    at_home = row[0] // members == col[0]
-
-    @pl.when(at_home)
-    def _():
-        rows_ref[...] = panel_ref[...]
-
-    @pl.when(jnp.logical_not(at_home))
-    def _():
-        for step, ref in enumerate((own_ref, *others)):
-            put_block(rows_ref, lax.rem(col[0] + step, len(others) + 1), ref[...])
-
-    centre_ref[...] = rotated_sum(rot_ref[...], rows_ref[...]) * (1.0 / rows_ref.shape[1])
 
 
 def add_weighted(inv_ref, centre, sums_ref):
@@ -93,28 +77,25 @@
     lax.fori_loop(0, height // group, body, 0)
 
 
-def weighted_kernel(halves, row, inv_ref, centre_ref, *refs):
-    sums_ref = refs[-1]
+def weighted_fit_kernel(members, halves, row, col, inv_ref, centre_ref, rot_ref, own_ref, panel_ref, *refs):
+    others, (out_ref, rows_ref, rows_centre_ref, sums_ref) = refs[:-4], refs[-4:]
     step = pl.program_id(0)
+    at_home = row[0] // members == col[0]
 
     @pl.when(step == 0)
     def _():
         sums_ref[...] = jnp.zeros_like(sums_ref)
 
-    width = inv_ref.shape[1]
-    for half in range(halves):
-
-        @pl.when(lax.rem(step, halves) == half)
-        def _(half=half):
-            add_weighted(inv_ref, centre_ref[step // halves, :, half * width : (half + 1) * width], sums_ref)
-
-
-def weighted_fit_kernel(halves, row, inv_ref, centre_ref, before_ref, rows_ref, out_ref, sums_ref):
-    step = pl.program_id(0)
-
-    @pl.when(step == 0)
-    def _():
-        sums_ref[...] = before_ref[...]
+        @pl.when(at_home)
+        def _():
+            rows_ref[...] = panel_ref[...]
+
+        @pl.when(jnp.logical_not(at_home))
+        def _():
+            for shift, ref in enumerate((own_ref, *others)):
+                put_block(rows_ref, lax.rem(col[0] + shift, len(others) + 1), ref[...])
+
+        rows_centre_ref[...] = rotated_sum(rot_ref[...], rows_ref[...]) * (1.0 / rows_ref.shape[1])
 
     width = inv_ref.shape[1]
     for half in range(halves):
@@ -184,9 +165,9 @@
         out_ref[:, start : start + stride] = product * scale
 
 
-def first_tiles_kernel(count, row, col, fits_ref, rows_ref, rows_centre_ref, centre_ref, *refs):
-    panel_refs = refs[:count]
-    out_ref, rot_out_ref, wide_ref, rows_dev_ref, dev_ref = refs[count:]
+def covariance_kernel(members, row, col, fits_ref, rows_ref, rows_centre_ref, centre_ref, *refs):
+    panel_refs = refs[:members]
+    out_ref, rot_out_ref, wide_ref, rows_dev_ref, dev_ref = refs[members:]
     frame_total = rows_ref.shape[1]
     local = rot_out_ref.shape[2]
 
@@ -199,28 +180,21 @@
             for block in range(1, frame_total // local):
                 kept = jnp.where(col[0] == block, flat[:, block * local : (block + 1) * local], kept)
             rot_out_ref[a] = kept
-            for b in range(3):
-                wide_ref[3 * a + b] = jnp.broadcast_to(current[a][b], (LANES, frame_total)).T
+        entries = [current[a][b] for a in range(3) for b in range(3)]
+        columns = jnp.concatenate(entries + [jnp.zeros((7, frame_total), F32)], axis=0).T
+        for entry in range(9):
+            wide_ref[entry] = jnp.broadcast_to(columns[:, entry : entry + 1], (frame_total, LANES))
         centre = rows_centre_ref[...]
         for chunk in range(rows_ref.shape[2] // LANES):
             put_deviations(wide_ref, rows_ref, centre, chunk, dev_ref)
         rows_dev_ref[...] = dev_ref[...].T
 
-    for step in range(count):
+    member = lax.rem(row[0], members)
+    for step in range(members):
 
         @pl.when(pl.program_id(0) == step)
         def _(step=step):
-            put_tile(wide_ref, panel_refs[step], centre_ref[step], rows_dev_ref, dev_ref, out_ref)
-
-
-def last_tiles_kernel(count, row, before_ref, wide_ref, rows_dev_ref, centre_ref, *refs):
-    panel_refs = refs[:count]
-    out_ref, dev_ref = refs[count:]
-    for step in range(count):
-
-        @pl.when(pl.program_id(0) == step)
-        def _(step=step):
-            put_tile(wide_ref, panel_refs[step], centre_ref[step], rows_dev_ref, dev_ref, out_ref)
+            put_tile(wide_ref, panel_refs[step], centre_ref[member ^ step], rows_dev_ref, dev_ref, out_ref)
 
 
 def per_device(frames, rotations, inverse_cov):
@@ -232,7 +206,6 @@
     frame_total = local * col_count
     device_total = row_count * col_count
     col_width = inverse_cov.shape[1]
-    pairs_of_members = members // 2
     coords = jnp.transpose(frames, (1, 0, 2))
 
     def move(value, source_of, receives=lambda group, col: True):
@@ -252,7 +225,6 @@
     def from_member(value, mask):
         return move(value, lambda g, m, c: (g, m ^ mask, c))
 
-    panel_parts = [from_panel_row(coords, step) for step in range(col_count)]
     partial = pl.pallas_call(
         functools.partial(partial_centre_kernel, frame_total),
         out_shape=jax.ShapeDtypeStruct((3, width), F32),
@@ -261,16 +233,19 @@
         name="partial_centre",
     )(col, rotations, coords)
     parts = [from_panel_row(partial, step) for step in range(col_count)]
-    own_centre = functools.reduce(lambda a, b: a + b, parts)
-    centres = [own_centre] + [from_member(own_centre, 2 * step) for step in range(1, pairs_of_members)]
-    centres, panel_parts, late_coords = lax.optimization_barrier((centres, panel_parts, coords))
-    even_centres = jnp.stack(centres)
-    odd_centres = from_member(even_centres, 1)
-
+    _, late_coords = lax.optimization_barrier((partial, coords))
+    panel_parts = [from_panel_row(late_coords, step) for step in range(col_count)]
     others = [
         move(late_coords, lambda g, m, c, s=step: (g, m, (c + s) % col_count), lambda g, c: g != c)
         for step in range(1, col_count)
     ]
+
+    own_centre = functools.reduce(lambda a, b: a + b, parts)
+    repeated = jnp.broadcast_to(own_centre[None], (members, 3, width))
+    _, panel_parts = lax.optimization_barrier((repeated, panel_parts))
+    groups = [[group * members + member for member in range(members)] for group in range(col_count)]
+    centres = lax.all_to_all(repeated, "row", split_axis=0, concat_axis=0, axis_index_groups=groups, tiled=True)
+
     own_block = pl.pallas_call(
         functools.partial(assemble_kernel, members),
         out_shape=jax.ShapeDtypeStruct((3, frame_total, width), BF16),
@@ -278,101 +253,71 @@
         out_specs=vmem(),
         name="assemble",
     )(row, *panel_parts)
-    even_panel = [own_block] + [from_member(own_block, 2 * step) for step in range(1, pairs_of_members)]
-
-    rows_all, rows_centre = pl.pallas_call(
-        functools.partial(rows_kernel, members),
+    even_panel = [own_block] + [from_member(own_block, 2 * step) for step in range(1, members // 2)]
+
+    halves = 2 if width % (2 * LANES) == 0 else 1
+    piece = width // halves
+    message, rows_all, rows_centre = pl.pallas_call(
+        functools.partial(weighted_fit_kernel, members, halves),
+        grid_spec=pltpu.PrefetchScalarGridSpec(
+            num_scalar_prefetch=2,
+            grid=(members * halves,),
+            in_specs=[pl.BlockSpec((width, piece), lambda i, *_: (0, i))] + [vmem()] * (3 + col_count),
+            out_specs=(vmem(), vmem(), vmem()),
+            scratch_shapes=[pltpu.VMEM((3, width, LANES), F32)],
+        ),
         out_shape=(
+            jax.ShapeDtypeStruct((device_total, 8, 2 * frame_total), F32),
             jax.ShapeDtypeStruct((3, frame_total, width), BF16),
             jax.ShapeDtypeStruct((3, width), F32),
         ),
-        in_specs=[smem(), smem()] + [vmem()] * (2 + col_count),
-        out_specs=(vmem(), vmem()),
-        name="rows",
-    )(row, col, rotations, coords, own_block, *others)
-
-    halves = 2 if width % (2 * LANES) == 0 else 1
-    piece = width // halves
-    steps = pairs_of_members * halves
-
-    def inv_spec(odd):
-        def index(i, row):
-            return (0, (lax.rem(row[0], members) ^ (2 * (i // halves) + odd)) * halves + lax.rem(i, halves))
-
-        return pl.BlockSpec((width, piece), index)
-
-    weighted_cost = pl.CostEstimate(
-        flops=3 * width * col_width, bytes_accessed=2 * width * col_width, transcendentals=0
+        compiler_params=pltpu.CompilerParams(vmem_limit_bytes=40 * MIB),
+        cost_estimate=pl.CostEstimate(
+            flops=6 * width * col_width, bytes_accessed=4 * width * col_width, transcendentals=0
+        ),
+        name="weighted_fit",
+    )(
+        row,
+        col,
+        pltpu.with_memory_space_constraint(inverse_cov, pltpu.HBM),
+        centres,
+        rotations,
+        coords,
+        own_block,
+        *others,
     )
-    even_sums = pl.pallas_call(
-        functools.partial(weighted_kernel, halves),
-        grid_spec=pltpu.PrefetchScalarGridSpec(
-            num_scalar_prefetch=1, grid=(steps,), in_specs=[inv_spec(0), vmem()], out_specs=vmem()
-        ),
-        out_shape=jax.ShapeDtypeStruct((3, width, LANES), F32),
-        compiler_params=pltpu.CompilerParams(vmem_limit_bytes=24 * MIB),
-        cost_estimate=weighted_cost,
-        name="weighted_even",
-    )(row, inverse_cov, even_centres)
-    message = pl.pallas_call(
-        functools.partial(weighted_fit_kernel, halves),
-        grid_spec=pltpu.PrefetchScalarGridSpec(
-            num_scalar_prefetch=1,
-            grid=(steps,),
-            in_specs=[inv_spec(1)] + [vmem()] * 3,
-            out_specs=vmem(),
-            scratch_shapes=[pltpu.VMEM((3, width, LANES), F32)],
-        ),
-        out_shape=jax.ShapeDtypeStruct((device_total, 8, 2 * frame_total), F32),
-        compiler_params=pltpu.CompilerParams(vmem_limit_bytes=24 * MIB),
-        cost_estimate=weighted_cost,
-        name="weighted_odd_and_fit",
-    )(row, inverse_cov, odd_centres, even_sums, rows_all)
+    _, even_panel = lax.optimization_barrier((message, even_panel))
     fits = lax.all_to_all(message, ("row", "col"), split_axis=0, concat_axis=0, tiled=True)
-    fits, even_panel = lax.optimization_barrier((fits, even_panel))
-    odd_panel = [from_member(block, 1) for block in even_panel]
-
-    def tile_spec(odd):
-        return pl.BlockSpec((width, width), lambda i, row, *_: (0, lax.rem(row[0], members) ^ (2 * i + odd)))
-
-    tiles_cost = pl.CostEstimate(
-        flops=3 * frame_total * width * col_width, bytes_accessed=2 * width * col_width, transcendentals=0
-    )
-    dev_scratch = pltpu.VMEM((3 * frame_total, width), BF16)
-    half_done, transforms, wide, rows_dev = pl.pallas_call(
-        functools.partial(first_tiles_kernel, pairs_of_members),
+    panel = [None] * members
+    panel[0::2] = even_panel
+    panel[1::2] = [from_member(block, 1) for block in even_panel]
+
+    covariance, transforms = pl.pallas_call(
+        functools.partial(covariance_kernel, members),
         grid_spec=pltpu.PrefetchScalarGridSpec(
             num_scalar_prefetch=2,
-            grid=(pairs_of_members,),
-            in_specs=[vmem()] * (4 + pairs_of_members),
-            out_specs=(tile_spec(0), vmem(), vmem(), vmem()),
-            scratch_shapes=[dev_scratch],
+            grid=(members,),
+            in_specs=[vmem()] * (4 + members),
+            out_specs=(
+                pl.BlockSpec((width, width), lambda i, row, col: (0, lax.rem(row[0], members) ^ i)),
+                vmem(),
+            ),
+            scratch_shapes=[
+                pltpu.VMEM((9, frame_total, LANES), F32),
+                pltpu.VMEM((width, 3 * frame_total), BF16),
+                pltpu.VMEM((3 * frame_total, width), BF16),
+            ],
         ),
         out_shape=(
             jax.ShapeDtypeStruct((width, col_width), F32),
             jax.ShapeDtypeStruct((3, 3, local), F32),
-            jax.ShapeDtypeStruct((9, frame_total, LANES), F32),
-            jax.ShapeDtypeStruct((width, 3 * frame_total), BF16),
         ),
         compiler_params=pltpu.CompilerParams(vmem_limit_bytes=32 * MIB),
-        cost_estimate=tiles_cost,
-        name="steps_and_even_tiles",
-    )(row, col, fits, rows_all, rows_centre, even_centres, *even_panel)
-    covariance = pl.pallas_call(
-        functools.partial(last_tiles_kernel, pairs_of_members),
-        grid_spec=pltpu.PrefetchScalarGridSpec(
-            num_scalar_prefetch=1,
-            grid=(pairs_of_members,),
-            in_specs=[pl.BlockSpec(memory_space=pl.ANY)] + [vmem()] * (3 + pairs_of_members),
-            out_specs=tile_spec(1),
-            scratch_shapes=[dev_scratch],
-        ),
-        out_shape=jax.ShapeDtypeStruct((width, col_width), F32),
-        input_output_aliases={1: 0},
-        compiler_params=pltpu.CompilerParams(vmem_limit_bytes=32 * MIB),
-        cost_estimate=tiles_cost,
-        name="odd_tiles",
-    )(row, half_done, wide, rows_dev, odd_centres, *odd_panel)
+        cost_estimate=pl.CostEstimate(
+            flops=6 * frame_total * width * col_width, bytes_accessed=4 * width * col_width, transcendentals=0
+        ),
+        name="covariance",
+    )(row, col, fits, rows_all, rows_centre, centres, *panel)
     return (covariance, transforms)
 
 

time: 83.7 us -> 81.8 us (0.977)
  blocking collectives: 0 us -> 24.5 us
  waiting for transfers between devices: 13.8 us -> 2.01 us
  local copies, waits for them, and re-layouts: 15 us -> 3.26 us
  starting transfers between devices: 27.6 us -> 21 us
  Pallas kernels: 26.1 us -> 29.6 us
    all_to_all x0 -> x2, blocking collectives: none -> 24.5 us  [the longest x1 16 us: per_device(): lax.all_to_all(message, ('row', 'col'), split_axis=0, concat_axis=0, tile...]
    unnamed x18 -> x10, local copies, waits for them, and re-layouts: 15 us -> 3.24 us
    all_to_all x1 -> x0, waiting for transfers between devices: 8.59 us -> none  [per_device(): lax.all_to_all(message, ('row', 'col'), split_axis=0, concat_axis=0, tile...]
    ppermute x16 -> x12, starting transfers between devices: 24.6 us -> 21 us  [move(): return lax.ppermute(value, ('row', 'col'), pairs)]
    pallas_call x5 -> x2, Pallas kernels: 22.6 us -> 26.1 us  [the longest x1 14.8 us: per_device(): pl.pallas_call(functools.partial(weighted_fit_kernel, members, halves), g...]
    ppermute x16 -> x12, waiting for transfers between devices: 5.2 us -> 2.01 us  [move(): return lax.ppermute(value, ('row', 'col'), pairs)]
    all_to_all x1 -> x0, starting transfers between devices: 3.01 us -> none  [per_device(): lax.all_to_all(message, ('row', 'col'), split_axis=0, concat_axis=0, tile...]
  transfers between devices with their start and end apart: 17 -> 12, of which waited for: 5 -> 1; matrix products, arithmetic and copies ran while one was open for 0% -> 0% of each run, Pallas kernels for 24% -> 18%
where the time goes in v3:
time: 81.8 us; the launch traced here: 81.1 us
  Pallas kernels  29.6 us (36%)
  blocking collectives  24.5 us (30%)
  starting transfers between devices  21 us (26%)
  local copies, waits for them, and re-layouts  3.26 us (4%)
  waiting for transfers between devices  2.01 us (2%)
    ppermute x12, starting transfers between devices, move(): return lax.ppermute(value, ('row', 'col'), pairs)  21 us
    all_to_all x1, blocking collectives, per_device(): lax.all_to_all(message, ('row', 'col'), split_axis=0, concat_axis=0, tile...  16 us
    pallas_call x1, Pallas kernels, per_device(): pl.pallas_call(functools.partial(weighted_fit_kernel, members, halves), g...  14.8 us
    pallas_call x1, Pallas kernels, per_device(): pl.pallas_call(functools.partial(covariance_kernel, members), grid_spec=p...  11.2 us
    all_to_all x1, blocking collectives, per_device(): lax.all_to_all(repeated, 'row', split_axis=0, concat_axis=0, axis_index_g...  8.54 us
    unnamed x10, local copies, waits for them, and re-layouts  3.24 us
    ppermute x12, waiting for transfers between devices, move(): return lax.ppermute(value, ('row', 'col'), pairs)  2.01 us
    pallas_call x1, Pallas kernels, per_device(): pl.pallas_call(functools.partial(partial_centre_kernel, frame_total), out...  1.77 us
  transfers between devices with their start and end apart: 12, of which 1 were waited for; matrix products, arithmetic and copies ran while one was open for 0% of the time, Pallas kernels for 18%

profile of v3, /device:TPU:0, one launch (start us, length us, event | category | flops | bytes accessed | tf_op | source)
XLA Modules:
  0.0 81.1 jit_solution(11036144875364687933)
XLA Ops:
  0.6 1.8 %partial_centre.1 = f32[3,768]{1,0:T(4,128)} custom-call(s32[1]{0:T(128)} %bitcast.1.col, f32[3,3,64]{2,1,0:T(4,128)} %rot_ref.3, bf16[3,32,768]{2,1,0:T(8,128)(2,1)} %bitcast.3), custom_call_target="tpu_custom_call" | custom-call | tf_op jit(solution)/shard_map/partial_centre/pallas_call | solution.py:228
  2.4 4.0 %collective-permute-start.3 = (bf16[3,32,768]{2,1,0:T(8,128)(2,1)}, bf16[3,32,768]{2,1,0:T(8,128)(2,1)S(1)}, u32[]{:S(2)}, u32[]{:S(2)}) collective-permute-start(bf16[3,32,768]{2,1,0:T(8,128)(2,1)} %bitcast.4), channel_id=1, source_target_pairs={{1,0},{17,1},{3,2},{19,3},{5,4},{21,5},{7,6},{23,7},{9,8},{25,9},{... | collective-permute-start | bytes 442376 | tf_op jit(solution)/shard_map/ppermute | solution.py:220
  6.4 1.6 %collective-permute-start.2 = (bf16[3,32,768]{2,1,0:T(8,128)(2,1)}, bf16[3,32,768]{2,1,0:T(8,128)(2,1)S(1)}, u32[]{:S(2)}, u32[]{:S(2)}) collective-permute-start(bf16[3,32,768]{2,1,0:T(8,128)(2,1)} %bitcast.5), channel_id=1, source_target_pairs={{0,0},{16,1},{2,2},{18,3},{4,4},{20,5},{6,6},{22,7},{8,8},{24,9},{... | collective-permute-start | bytes 442376 | tf_op jit(solution)/shard_map/ppermute | solution.py:220
  8.0 1.9 %collective-permute-start.1 = (f32[3,768]{1,0:T(4,128)}, f32[3,768]{1,0:T(4,128)S(1)}, u32[]{:S(2)}, u32[]{:S(2)}) collective-permute-start(f32[3,768]{1,0:T(4,128)} %partial_centre.1), channel_id=1, source_target_pairs={{1,0},{17,1},{3,2},{19,3},{5,4},{21,5},{7,6},{23,7},{9,8},{25,9},{... | collective-permute-start | bytes 27656 | tf_op jit(solution)/shard_map/ppermute | solution.py:220
  9.9 1.4 %collective-permute-start = (f32[3,768]{1,0:T(4,128)}, f32[3,768]{1,0:T(4,128)S(1)}, u32[]{:S(2)}, u32[]{:S(2)}) collective-permute-start(f32[3,768]{1,0:T(4,128)} %partial_centre.1), channel_id=1, source_target_pairs={{0,0},{16,1},{2,2},{18,3},{4,4},{20,5},{6,6},{22,7},{8,8},{24,9},{... | collective-permute-start | bytes 27656 | tf_op jit(solution)/shard_map/ppermute | solution.py:220
  11.3 2.0 %collective-permute-done.1 = f32[3,768]{1,0:T(4,128)S(1)} collective-permute-done((f32[3,768]{1,0:T(4,128)}, f32[3,768]{1,0:T(4,128)S(1)}, u32[]{:S(2)}, u32[]{:S(2)}) %collective-permute-start.1) | collective-permute-done | bytes 9248 | tf_op jit(solution)/shard_map/ppermute | solution.py:220
  13.2 0.0 collective-permute-done
  13.2 0.0 collective-permute-done.3.refs_1_
  13.3 0.0 copy-start.3
  13.3 0.0 collective-permute-done.2.refs_0_
  13.3 0.0 copy-start.4
  13.3 0.6 copy-done.3
  13.9 0.1 copy-done.4
  14.0 1.7 %assemble.1.panel_ref.refs_0_ = bf16[3,64,768]{2,1,0:T(8,128)(2,1)} custom-call(s32[1]{0:T(128)} %bitcast.row, bf16[3,32,768]{2,1,0:T(8,128)(2,1)} %copy-done.4, bf16[3,32,768]{2,1,0:T(8,128)(2,1)} %copy-done.3), custom_call_target="tpu_custom_call" | custom-call | tf_op jit(solution)/shard_map/assemble/pallas_call | solution.py:249
  15.7 2.6 %collective-permute-start.7 = (bf16[3,64,768]{2,1,0:T(8,128)(2,1)}, bf16[3,64,768]{2,1,0:T(8,128)(2,1)S(1)}, u32[]{:S(2)}, u32[]{:S(2)}) collective-permute-start(bf16[3,64,768]{2,1,0:T(8,128)(2,1)} %assemble.1.panel_ref.refs_0_), channel_id=1, source_target_pairs={{12,0},{13,1},{14,2},{15,3},{8,4},{9,5},{10,6},{11,7},{4,8},{5,9},... | collective-permute-start | bytes 884744 | tf_op jit(solution)/shard_map/ppermute | solution.py:220
  18.3 0.4 collective-permute-start.6
  18.7 0.5 collective-permute-start.5
  19.2 7.6 %collective-permute-start.4 = (bf16[3,32,768]{2,1,0:T(8,128)(2,1)}, bf16[3,32,768]{2,1,0:T(8,128)(2,1)S(1)}, u32[]{:S(2)}, u32[]{:S(2)}) collective-permute-start(bf16[3,32,768]{2,1,0:T(8,128)(2,1)} %bitcast.6), channel_id=1, source_target_pairs={{0,1},{2,3},{4,5},{6,7},{8,9},{10,11},{12,13},{14,15},{17,16},{19,... | collective-permute-start | bytes 442376 | tf_op jit(solution)/shard_map/ppermute | solution.py:220
  26.8 8.5 %all_to_all.10.centre_ref = f32[8,3,768]{2,1,0:T(4,128)S(1)} all-to-all(f32[8,3,768]{2,1,0:T(4,128)S(1)} %broadcast_in_dim.2), channel_id=1, replica_groups={{0,2,4,6,8,10,12,14},{16,18,20,22,24,26,28,30},{1,3,5,7,9,11,13,15},{17..., dimensions={0} | all-to-all | bytes 147456 | tf_op jit(solution)/shard_map/all_to_all | solution.py:247
  35.4 0.0 collective-permute-done.4.refs_0_
  35.4 0.0 copy-start
  35.4 1.0 %copy-done = bf16[3,64,768]{2,1,0:T(8,128)(2,1)S(1)} copy-done((bf16[3,64,768]{2,1,0:T(8,128)(2,1)S(1)}, bf16[3,64,768]{2,1,0:T(8,128)(2,1)}, u32[]{:S(2)}) %copy-start) | copy-done | bytes 294936
  36.3 0.0 copy-start.1
  36.3 0.9 %copy-done.1 = bf16[32,3,768]{2,0,1:T(8,128)(2,1)S(1)} copy-done((bf16[32,3,768]{2,0,1:T(8,128)(2,1)S(1)}, bf16[32,3,768]{2,0,1:T(8,128)(2,1)}, u32[]{:S(2)}) %copy-start.1) | copy-done | bytes 147480
  37.2 0.0 copy-start.2
  37.2 0.7 copy-done.2
  37.9 14.8 %weighted_fit.1 = (f32[32,8,128]{2,1,0:T(8,128)S(1)}, bf16[3,64,768]{2,1,0:T(8,128)(2,1)S(1)}, f32[3,768]{1,0:T(4,128)S(1)}) custom-call(s32[1]{0:T(128)} %bitcast.row, s32[1]{0:T(128)} %bitcast.1.col, f32[768,6144]{1,0:T(8,128)} %inv_ref.1, f32[8,3,768]{2,1,0:T(4,128)S(1)} %all_to_all.10.centre_ref, f32[3,3,64]{2,1,0:T(4,128)S(1)} %copy-done.2, ...), custom_call_target="tpu_custom_call" | custom-call | flops 28311552 | bytes 18874368 | tf_op jit(solution)/shard_map/weighted_fit/pallas_call | solution.py:260
  52.8 0.0 collective-permute-done.7.refs_6_
  52.8 0.0 collective-permute-done.6.refs_4_
  52.8 0.0 collective-permute-done.5.refs_2_
  52.8 0.1 collective-permute-start.8
  52.9 0.5 collective-permute-start.9
  53.4 0.1 collective-permute-start.10
  53.5 0.4 collective-permute-start.11
  53.9 16.0 %all_to_all.11.fits_ref = f32[32,8,128]{2,1,0:T(8,128)S(1)} all-to-all(f32[32,8,128]{2,1,0:T(8,128)S(1)} %get-tuple-element.15), channel_id=1, replica_groups=mesh['row'=16,'col'=2] {'row','col'}, dimensions={0} | all-to-all | bytes 262144 | tf_op jit(solution)/shard_map/all_to_all | solution.py:290
  69.9 0.0 collective-permute-done.8.refs_1_
  69.9 0.0 collective-permute-done.9.refs_3_
  69.9 0.0 collective-permute-done.10.refs_5_
  69.9 0.0 collective-permute-done.11.refs_7_
  69.9 11.2 %covariance.1 = (f32[768,6144]{1,0:T(8,128)}, f32[3,3,32]{2,1,0:T(4,128)}) custom-call(s32[1]{0:T(128)} %bitcast.row, s32[1]{0:T(128)} %bitcast.1.col, f32[32,8,128]{2,1,0:T(8,128)S(1)} %all_to_all.11.fits_ref, bf16[3,64,768]{2,1,0:T(8,128)(2,1)S(1)} %get-tuple-element.16.rows_ref, f32[3,768]{1,0:T(4,128)S(1)} %get-tuple-element.17.rows_centre_ref, ...), custom_call_target="tpu_custom_call" | custom-call | flops 1811939328 | bytes 18874368 | tf_op jit(solution)/shard_map/covariance/pallas_call | solution.py:295
  (2 shorter events, 0.0 us)
Async XLA Ops:
  2.4 10.8 %collective-permute-start.3 = (bf16[3,32,768]{2,1,0:T(8,128)(2,1)}, bf16[3,32,768]{2,1,0:T(8,128)(2,1)S(1)}, u32[]{:S(2)}, u32[]{:S(2)}) collective-permute-start(bf16[3,32,768]{2,1,0:T(8,128)(2,1)} %bitcast.4), channel_id=1, source_target_pairs={{1,0},{17,1},{3,2},{19,3},{5,4},{21,5},{7,6},{23,7},{9,8},{25,9},{... | collective-permute-start | bytes 442376 | tf_op jit(solution)/shard_map/ppermute | solution.py:220
  6.4 6.8 %collective-permute-start.2 = (bf16[3,32,768]{2,1,0:T(8,128)(2,1)}, bf16[3,32,768]{2,1,0:T(8,128)(2,1)S(1)}, u32[]{:S(2)}, u32[]{:S(2)}) collective-permute-start(bf16[3,32,768]{2,1,0:T(8,128)(2,1)} %bitcast.5), channel_id=1, source_target_pairs={{0,0},{16,1},{2,2},{18,3},{4,4},{20,5},{6,6},{22,7},{8,8},{24,9},{... | collective-permute-start | bytes 442376 | tf_op jit(solution)/shard_map/ppermute | solution.py:220
  8.0 5.2 %collective-permute-start.1 = (f32[3,768]{1,0:T(4,128)}, f32[3,768]{1,0:T(4,128)S(1)}, u32[]{:S(2)}, u32[]{:S(2)}) collective-permute-start(f32[3,768]{1,0:T(4,128)} %partial_centre.1), channel_id=1, source_target_pairs={{1,0},{17,1},{3,2},{19,3},{5,4},{21,5},{7,6},{23,7},{9,8},{25,9},{... | collective-permute-start | bytes 27656 | tf_op jit(solution)/shard_map/ppermute | solution.py:220
  9.9 3.3 %collective-permute-start = (f32[3,768]{1,0:T(4,128)}, f32[3,768]{1,0:T(4,128)S(1)}, u32[]{:S(2)}, u32[]{:S(2)}) collective-permute-start(f32[3,768]{1,0:T(4,128)} %partial_centre.1), channel_id=1, source_target_pairs={{0,0},{16,1},{2,2},{18,3},{4,4},{20,5},{6,6},{22,7},{8,8},{24,9},{... | collective-permute-start | bytes 27656 | tf_op jit(solution)/shard_map/ppermute | solution.py:220
  13.3 0.7 copy-start.3
  13.3 0.7 copy-start.4
  15.7 37.1 %collective-permute-start.7 = (bf16[3,64,768]{2,1,0:T(8,128)(2,1)}, bf16[3,64,768]{2,1,0:T(8,128)(2,1)S(1)}, u32[]{:S(2)}, u32[]{:S(2)}) collective-permute-start(bf16[3,64,768]{2,1,0:T(8,128)(2,1)} %assemble.1.panel_ref.refs_0_), channel_id=1, source_target_pairs={{12,0},{13,1},{14,2},{15,3},{8,4},{9,5},{10,6},{11,7},{4,8},{5,9},... | collective-permute-start | bytes 884744 | tf_op jit(solution)/shard_map/ppermute | solution.py:220
  18.3 34.5 %collective-permute-start.6 = (bf16[3,64,768]{2,1,0:T(8,128)(2,1)}, bf16[3,64,768]{2,1,0:T(8,128)(2,1)S(1)}, u32[]{:S(2)}, u32[]{:S(2)}) collective-permute-start(bf16[3,64,768]{2,1,0:T(8,128)(2,1)} %assemble.1.panel_ref.refs_0_), channel_id=1, source_target_pairs={{8,0},{9,1},{10,2},{11,3},{12,4},{13,5},{14,6},{15,7},{0,8},{1,9},... | collective-permute-start | bytes 884744 | tf_op jit(solution)/shard_map/ppermute | solution.py:220
  18.7 34.1 %collective-permute-start.5 = (bf16[3,64,768]{2,1,0:T(8,128)(2,1)}, bf16[3,64,768]{2,1,0:T(8,128)(2,1)S(1)}, u32[]{:S(2)}, u32[]{:S(2)}) collective-permute-start(bf16[3,64,768]{2,1,0:T(8,128)(2,1)} %assemble.1.panel_ref.refs_0_), channel_id=1, source_target_pairs={{4,0},{5,1},{6,2},{7,3},{0,4},{1,5},{2,6},{3,7},{12,8},{13,9},{14,... | collective-permute-start | bytes 884744 | tf_op jit(solution)/shard_map/ppermute | solution.py:220
  19.2 16.2 %collective-permute-start.4 = (bf16[3,32,768]{2,1,0:T(8,128)(2,1)}, bf16[3,32,768]{2,1,0:T(8,128)(2,1)S(1)}, u32[]{:S(2)}, u32[]{:S(2)}) collective-permute-start(bf16[3,32,768]{2,1,0:T(8,128)(2,1)} %bitcast.6), channel_id=1, source_target_pairs={{0,1},{2,3},{4,5},{6,7},{8,9},{10,11},{12,13},{14,15},{17,16},{19,... | collective-permute-start | bytes 442376 | tf_op jit(solution)/shard_map/ppermute | solution.py:220
  35.4 1.0 %copy-start = (bf16[3,64,768]{2,1,0:T(8,128)(2,1)S(1)}, bf16[3,64,768]{2,1,0:T(8,128)(2,1)}, u32[]{:S(2)}) copy-start(bf16[3,64,768]{2,1,0:T(8,128)(2,1)} %assemble.1.panel_ref.refs_0_) | copy-start | bytes 884740
  36.3 0.9 %copy-start.1 = (bf16[32,3,768]{2,0,1:T(8,128)(2,1)S(1)}, bf16[32,3,768]{2,0,1:T(8,128)(2,1)}, u32[]{:S(2)}) copy-start(bf16[32,3,768]{2,0,1:T(8,128)(2,1)} %param.3) | copy-start | bytes 442372
  37.2 0.7 copy-start.2
  52.8 17.1 %collective-permute-start.8 = (bf16[3,64,768]{2,1,0:T(8,128)(2,1)S(1)}, bf16[3,64,768]{2,1,0:T(8,128)(2,1)S(1)}, u32[]{:S(2)}, u32[]{:S(2)}) collective-permute-start(bf16[3,64,768]{2,1,0:T(8,128)(2,1)S(1)} %copy-done), channel_id=1, source_target_pairs={{2,0},{3,1},{0,2},{1,3},{6,4},{7,5},{4,6},{5,7},{10,8},{11,9},{8,1... | collective-permute-start | bytes 884744 | tf_op jit(solution)/shard_map/ppermute | solution.py:220
  52.9 17.0 %collective-permute-start.9 = (bf16[3,64,768]{2,1,0:T(8,128)(2,1)S(1)}, bf16[3,64,768]{2,1,0:T(8,128)(2,1)S(1)}, u32[]{:S(2)}, u32[]{:S(2)}) collective-permute-start(bf16[3,64,768]{2,1,0:T(8,128)(2,1)S(1)} %collective-permute-done.5.refs_2_), channel_id=1, source_target_pairs={{2,0},{3,1},{0,2},{1,3},{6,4},{7,5},{4,6},{5,7},{10,8},{11,9},{8,1... | collective-permute-start | bytes 884744 | tf_op jit(solution)/shard_map/ppermute | solution.py:220
  53.4 16.5 %collective-permute-start.10 = (bf16[3,64,768]{2,1,0:T(8,128)(2,1)S(1)}, bf16[3,64,768]{2,1,0:T(8,128)(2,1)S(1)}, u32[]{:S(2)}, u32[]{:S(2)}) collective-permute-start(bf16[3,64,768]{2,1,0:T(8,128)(2,1)S(1)} %collective-permute-done.6.refs_4_), channel_id=1, source_target_pairs={{2,0},{3,1},{0,2},{1,3},{6,4},{7,5},{4,6},{5,7},{10,8},{11,9},{8,1... | collective-permute-start | bytes 884744 | tf_op jit(solution)/shard_map/ppermute | solution.py:220
  53.5 16.4 %collective-permute-start.11 = (bf16[3,64,768]{2,1,0:T(8,128)(2,1)S(1)}, bf16[3,64,768]{2,1,0:T(8,128)(2,1)S(1)}, u32[]{:S(2)}, u32[]{:S(2)}) collective-permute-start(bf16[3,64,768]{2,1,0:T(8,128)(2,1)S(1)} %collective-permute-done.7.refs_6_), channel_id=1, source_target_pairs={{2,0},{3,1},{0,2},{1,3},{6,4},{7,5},{4,6},{5,7},{10,8},{11,9},{8,1... | collective-permute-start | bytes 884744 | tf_op jit(solution)/shard_map/ppermute | solution.py:220

commit v4 on v3

v4 whole, which is shorter than its diff:
```python
import functools

import jax
import jax.numpy as jnp
from jax import lax
from jax.experimental import pallas as pl
from jax.experimental.pallas import tpu as pltpu
from jax.sharding import PartitionSpec as P

POLAR = 12
LANES = 128
F32 = jnp.float32
BF16 = jnp.bfloat16
MIB = 1 << 20


def vmem():
    return pl.BlockSpec(memory_space=pltpu.VMEM)


def smem():
    return pl.BlockSpec(memory_space=pltpu.SMEM)


def three_pieces(value):
    high = value.astype(BF16)
    rest = value - high.astype(F32)
    mid = rest.astype(BF16)
    low = (rest - mid.astype(F32)).astype(BF16)
    return high, mid, low


def rotated_sum(rot, coords):
    depth = coords.shape[0] * coords.shape[1]
    flat = jnp.concatenate([rot[:, part, :] for part in range(3)], axis=1)
    padded = jnp.concatenate([flat, jnp.zeros((5, depth), F32)], axis=0)
    stacked = jnp.concatenate(three_pieces(padded), axis=0)
    product = jnp.dot(stacked, coords.reshape(depth, coords.shape[2]), preferred_element_type=F32)
    return (product[16:19] + product[8:11]) + product[0:3]


def put_block(out_ref, block, value):
    local = value.shape[1]
    out_ref[:, pl.ds(pl.multiple_of(block * local, local), local), :] = value


def assemble_kernel(members, row, rot_ref, *refs):
    blocks, (out_ref, centre_ref) = refs[:-2], refs[-2:]
    for step, ref in enumerate(blocks):
        put_block(out_ref, lax.rem(row[0] // members + step, len(blocks)), ref[...])
    centre = rotated_sum(rot_ref[...], out_ref[...]) * (1.0 / out_ref.shape[1])
    centre_ref[...] = jnp.broadcast_to(centre[None], centre_ref.shape)


def weighted_fit_kernel(members, row, col, inv_ref, centre_ref, rot_ref, own_ref, panel_ref, *refs):
    others, (out_ref, rows_ref, rows_centre_ref, wide_ref, weighted_ref) = refs[:-5], refs[-5:]
    step = pl.program_id(0)
    height, col_width = inv_ref.shape
    width = centre_ref.shape[2]

    @pl.when(step == 0)
    def _():
        for block in range(members):
            for comp in range(3):
                factor = jnp.broadcast_to(centre_ref[block, comp : comp + 1, :], (8, width))
                wide_ref[comp, :, block * width : (block + 1) * width] = factor

    def body(chunk, sums):
        span = pl.ds(pl.multiple_of(chunk * LANES, LANES), LANES)
        value = inv_ref[:, span].reshape(height // 8, 8, LANES)
        return tuple(sums[comp] + value * wide_ref[comp, :, span][None] for comp in range(3))

    zero = jnp.zeros((height // 8, 8, LANES), F32)
    chunks = col_width // LANES
    sums = lax.fori_loop(0, chunks, body, (zero,) * 3, unroll=12 if chunks % 12 == 0 else 1)
    lane = lax.broadcasted_iota(jnp.int32, (height, LANES), 1)
    packed = jnp.zeros((height, LANES), F32)
    for comp in range(3):
        total = jnp.sum(sums[comp].reshape(height, LANES), axis=1, keepdims=True)
        packed = jnp.where(lane == comp, total, packed)
    weighted_ref[pl.ds(pl.multiple_of(step * height, height), height), :] = packed

    @pl.when(step == 0)
    def _():
        at_home = row[0] // members == col[0]

        @pl.when(at_home)
        def _():
            rows_ref[...] = panel_ref[...]

        @pl.when(jnp.logical_not(at_home))
        def _():
            for shift, ref in enumerate((own_ref, *others)):
                put_block(rows_ref, lax.rem(col[0] + shift, len(others) + 1), ref[...])

        rows_centre_ref[...] = rotated_sum(rot_ref[...], rows_ref[...]) * (1.0 / rows_ref.shape[1])

    @pl.when(step == pl.num_programs(0) - 1)
    def _():
        frame_total = rows_ref.shape[1]
        rows = rows_ref[...].reshape(3 * frame_total, width)
        high, mid, low = (
            jnp.dot(rows, piece, preferred_element_type=F32) for piece in three_pieces(weighted_ref[...])
        )
        fits = ((low + mid) + high).T
        entries = [
            fits[comp : comp + 1, part * frame_total : (part + 1) * frame_total]
            for part in range(3)
            for comp in range(3)
        ]
        first = jnp.concatenate(entries[:8], axis=0)
        last = jnp.concatenate([entries[8], jnp.zeros((7, frame_total), F32)], axis=0)
        message = jnp.concatenate([first, last], axis=1)
        out_ref[...] = jnp.broadcast_to(message[None], out_ref.shape)


def add_parts_kernel(parts_ref, out_ref):
    out_ref[...] = jnp.broadcast_to(jnp.sum(parts_ref[...], axis=0)[None], out_ref.shape)


def orthogonalized(message, frame_total):
    fitted = [message[entry : entry + 1, :frame_total] for entry in range(8)]
    fitted.append(message[0:1, frame_total:])
    norm = functools.reduce(lambda a, b: a + b, [value * value for value in fitted])
    scaling = jnp.sqrt(1.0 + norm)
    current = [[fitted[3 * col + row] / scaling for col in range(3)] for row in range(3)]
    for _ in range(POLAR):
        square = [[None] * 3 for _ in range(3)]
        for a in range(3):
            for b in range(a, 3):
                x, y = current[a], current[b]
                square[a][b] = square[b][a] = x[0] * y[0] + x[1] * y[1] + x[2] * y[2]
        cubed = [
            [square[a][0] * current[0][b] + square[a][1] * current[1][b] + square[a][2] * current[2][b] for b in range(3)]
            for a in range(3)
        ]
        current = [[1.5 * current[a][b] - 0.5 * cubed[a][b] for b in range(3)] for a in range(3)]
    return current


def put_deviations(wide_ref, coords_ref, centre, chunk, dev_ref):
    frame_total = coords_ref.shape[1]
    span = slice(chunk * LANES, (chunk + 1) * LANES)
    coords = [coords_ref[part, :, span].astype(F32) for part in range(3)]
    for comp in range(3):
        moved = wide_ref[3 * comp] * coords[0]
        moved = moved + wide_ref[3 * comp + 1] * coords[1]
        moved = moved + wide_ref[3 * comp + 2] * coords[2]
        value = moved - centre[comp : comp + 1, span]
        dev_ref[comp * frame_total : (comp + 1) * frame_total, span] = value.astype(BF16)


def covariance_kernel(members, row, col, fits_ref, rows_ref, rows_centre_ref, centre_ref, *refs):
    panel_refs = refs[:members]
    out_ref, rot_out_ref, wide_ref, rows_dev_ref, dev_ref, tile_ref, sems = refs[members:]
    frame_total = rows_ref.shape[1]
    local = rot_out_ref.shape[2]
    slots, strip, width = tile_ref.shape
    strips = slots // 2
    scale = 1.0 / (3 * frame_total)

    current = orthogonalized(jnp.sum(fits_ref[...], axis=0), frame_total)
    for a in range(3):
        flat = jnp.concatenate(current[a], axis=0)
        kept = flat[:, :local]
        for block in range(1, frame_total // local):
            kept = jnp.where(col[0] == block, flat[:, block * local : (block + 1) * local], kept)
        rot_out_ref[a] = kept
    entries = [current[a][b] for a in range(3) for b in range(3)]
    columns = jnp.concatenate(entries + [jnp.zeros((7, frame_total), F32)], axis=0).T
    for entry in range(9):
        wide_ref[entry] = jnp.broadcast_to(columns[:, entry : entry + 1], (frame_total, LANES))
    centre = rows_centre_ref[...]
    for chunk in range(width // LANES):
        put_deviations(wide_ref, rows_ref, centre, chunk, dev_ref.at[0])
    rows_dev_ref[...] = dev_ref[0].T

    member = lax.rem(row[0], members)

    def write(step, part):
        start = pl.multiple_of((member ^ step) * width, LANES)
        slot = (step % 2) * strips + part
        span = pl.ds(part * strip, strip)
        return pltpu.make_async_copy(tile_ref.at[slot], out_ref.at[span, pl.ds(start, width)], sems.at[slot])

    for step in range(members):
        dev = dev_ref.at[step % 2]
        centre = centre_ref[member ^ step]
        for chunk in range(width // LANES):
            put_deviations(wide_ref, panel_refs[step], centre, chunk, dev)
        for part in range(strips):
            product = jnp.dot(
                rows_dev_ref[part * strip : (part + 1) * strip, :], dev[...], preferred_element_type=F32
            )
            if step >= 2:
                write(step - 2, part).wait()
            tile_ref[(step % 2) * strips + part] = product * scale
            write(step, part).start()
    for step in range(max(members - 2, 0), members):
        for part in range(strips):
            write(step, part).wait()


def per_device(frames, rotations, inverse_cov):
    row_count, col_count = lax.axis_size("row"), lax.axis_size("col")
    members = row_count // col_count
    row = lax.axis_index("row").astype(jnp.int32).reshape(1)
    col = lax.axis_index("col").astype(jnp.int32).reshape(1)
    local, _, width = frames.shape
    frame_total = local * col_count
    col_width = inverse_cov.shape[1]
    coords = jnp.transpose(frames, (1, 0, 2))

    def move(value, source_of, receives=lambda group, col: True):
        pairs = []
        for group in range(col_count):
            for member in range(members):
                for place in range(col_count):
                    if receives(group, place):
                        from_group, from_member, from_col = source_of(group, member, place)
                        source = (from_group * members + from_member) * col_count + from_col
                        pairs.append((source, (group * members + member) * col_count + place))
        return lax.ppermute(value, ("row", "col"), pairs)

    def from_panel_row(value, step):
        return move(value, lambda g, m, c: (c, m, (g + step) % col_count))

    def from_member(value, mask):
        return move(value, lambda g, m, c: (g, m ^ mask, c))

    panel_parts = [from_panel_row(coords, step) for step in range(col_count)]
    others = [
        move(coords, lambda g, m, c, s=step: (g, m, (c + s) % col_count), lambda g, c: g != c)
        for step in range(1, col_count)
    ]
    panel_parts, others = lax.optimization_barrier((panel_parts, others))
    own_block, repeated = pl.pallas_call(
        functools.partial(assemble_kernel, members),
        out_shape=(
            jax.ShapeDtypeStruct((3, frame_total, width), BF16),
            jax.ShapeDtypeStruct((members, 3, width), F32),
        ),
        in_specs=[smem()] + [vmem()] * (1 + col_count),
        out_specs=(vmem(), vmem()),
        name="assemble",
    )(row, rotations, *panel_parts)
    groups = [[group * members + member for member in range(members)] for group in range(col_count)]
    centres = lax.all_to_all(repeated, "row", split_axis=0, concat_axis=0, axis_index_groups=groups, tiled=True)
    _, own_block = lax.optimization_barrier((centres, own_block))
    even_panel = [own_block] + [from_member(own_block, 2 * step) for step in range(1, members // 2)]

    height = 64 if width % 64 == 0 else 8
    message, rows_all, rows_centre = pl.pallas_call(
        functools.partial(weighted_fit_kernel, members),
        grid_spec=pltpu.PrefetchScalarGridSpec(
            num_scalar_prefetch=2,
            grid=(width // height,),
            in_specs=[pl.BlockSpec((height, col_width), lambda i, *_: (i, 0))] + [vmem()] * (3 + col_count),
            out_specs=(vmem(), vmem(), vmem()),
            scratch_shapes=[pltpu.VMEM((3, 8, col_width), F32), pltpu.VMEM((width, LANES), F32)],
        ),
        out_shape=(
            jax.ShapeDtypeStruct((members, 8, 2 * frame_total), F32),
            jax.ShapeDtypeStruct((3, frame_total, width), BF16),
            jax.ShapeDtypeStruct((3, width), F32),
        ),
        compiler_params=pltpu.CompilerParams(vmem_limit_bytes=16 * MIB),
        cost_estimate=pl.CostEstimate(
            flops=6 * width * col_width, bytes_accessed=4 * width * col_width, transcendentals=0
        ),
        name="weighted_fit",
    )(
        row,
        col,
        pltpu.with_memory_space_constraint(inverse_cov, pltpu.HBM),
        centres,
        rotations,
        coords,
        own_block,
        *others,
    )
    parts = lax.all_to_all(message, "row", split_axis=0, concat_axis=0, axis_index_groups=groups, tiled=True)
    summed = pl.pallas_call(
        add_parts_kernel,
        out_shape=jax.ShapeDtypeStruct((col_count * col_count, 8, 2 * frame_total), F32),
        in_specs=[vmem()],
        out_specs=vmem(),
        name="add_parts",
    )(parts)
    _, even_panel = lax.optimization_barrier((summed, even_panel))
    peers = [
        [(group * members + member) * col_count + place for group in range(col_count) for place in range(col_count)]
        for member in range(members)
    ]
    fits = lax.all_to_all(summed, ("row", "col"), split_axis=0, concat_axis=0, axis_index_groups=peers, tiled=True)
    panel = [None] * members
    panel[0::2] = even_panel
    panel[1::2] = [from_member(block, 1) for block in even_panel]

    strips = 4 if width % 64 == 0 else 1
    covariance, transforms = pl.pallas_call(
        functools.partial(covariance_kernel, members),
        grid_spec=pltpu.PrefetchScalarGridSpec(
            num_scalar_prefetch=2,
            grid=(1,),
            in_specs=[vmem()] * (4 + members),
            out_specs=(pl.BlockSpec(memory_space=pl.ANY), vmem()),
            scratch_shapes=[
                pltpu.VMEM((9, frame_total, LANES), F32),
                pltpu.VMEM((width, 3 * frame_total), BF16),
                pltpu.VMEM((2, 3 * frame_total, width), BF16),
                pltpu.VMEM((2 * strips, width // strips, width), F32),
                pltpu.SemaphoreType.DMA((2 * strips,)),
            ],
        ),
        out_shape=(
            jax.ShapeDtypeStruct((width, col_width), F32),
            jax.ShapeDtypeStruct((3, 3, local), F32),
        ),
        compiler_params=pltpu.CompilerParams(vmem_limit_bytes=24 * MIB),
        cost_estimate=pl.CostEstimate(
            flops=6 * frame_total * width * col_width, bytes_accessed=4 * width * col_width, transcendentals=0
        ),
        name="covariance",
    )(row, col, fits, rows_all, rows_centre, centres, *panel)
    return (covariance, transforms)


def solution(mesh):
    placed = (P("col", None, "row"), P(), P("row", "col"))
    return jax.shard_map(
        per_device,
        mesh=mesh,
        in_specs=placed,
        out_specs=(P("row", "col"), P(None, None, "col")),
        check_vma=False,
    )
```

time: 81.8 us -> 80.7 us (0.987)
  starting transfers between devices: 21 us -> 11.5 us
  blocking collectives: 24.5 us -> 32.9 us
  Pallas kernels: 29.6 us -> 28.1 us
  waiting for transfers between devices: 2.01 us -> 3.5 us
    ppermute x12 -> x10, starting transfers between devices: 21 us -> 11.5 us  [move(): return lax.ppermute(value, ('row', 'col'), pairs)]
    all_to_all x1 -> x2, blocking collectives: 16 us -> 22.8 us  [the longest x1 15 us: per_device(): lax.all_to_all(summed, ('row', 'col'), split_axis=0, concat_axis=0, axis_...]
    pallas_call x3, Pallas kernels: 18.3 us -> 16.2 us  [the longest x1 13 us: per_device(): pl.pallas_call(functools.partial(weighted_fit_kernel, members), grid_spec...]
    all_to_all x1, blocking collectives: 8.54 us -> 10.2 us  [per_device(): lax.all_to_all(repeated, 'row', split_axis=0, concat_axis=0, axis_index_g...]
    ppermute x12 -> x10, waiting for transfers between devices: 2.01 us -> 3.5 us  [move(): return lax.ppermute(value, ('row', 'col'), pairs)]
    unnamed x10 -> x12, local copies, waits for them, and re-layouts: 3.24 us -> 3.32 us
  transfers between devices with their start and end apart: 12 -> 10, of which waited for: 1 -> 2; matrix products, arithmetic and copies ran while one was open for 0% -> 0% of each run, Pallas kernels for 18% -> 18%
where the time goes in v4:
time: 80.7 us; the launch traced here: 80 us
  blocking collectives  32.9 us (41%)
  Pallas kernels  28.1 us (35%)
  starting transfers between devices  11.5 us (14%)
  waiting for transfers between devices  3.5 us (4%)
  local copies, waits for them, and re-layouts  3.32 us (4%)
    all_to_all x1, blocking collectives, per_device(): lax.all_to_all(summed, ('row', 'col'), split_axis=0, concat_axis=0, axis_...  15 us
    pallas_call x1, Pallas kernels, per_device(): pl.pallas_call(functools.partial(weighted_fit_kernel, members), grid_spec...  13 us
    pallas_call x1, Pallas kernels, per_device(): pl.pallas_call(functools.partial(covariance_kernel, members), grid_spec=p...  11.8 us
    ppermute x10, starting transfers between devices, move(): return lax.ppermute(value, ('row', 'col'), pairs)  11.5 us
    all_to_all x1, blocking collectives, per_device(): lax.all_to_all(repeated, 'row', split_axis=0, concat_axis=0, axis_index_g...  10.2 us
    all_to_all x1, blocking collectives, per_device(): lax.all_to_all(message, 'row', split_axis=0, concat_axis=0, axis_index_gr...  7.81 us
    ppermute x10, waiting for transfers between devices, move(): return lax.ppermute(value, ('row', 'col'), pairs)  3.5 us
    unnamed x12, local copies, waits for them, and re-layouts  3.32 us
  transfers between devices with their start and end apart: 10, of which 2 were waited for; matrix products, arithmetic and copies ran while one was open for 0% of the time, Pallas kernels for 18%

profile of v4, /device:TPU:0, one launch (start us, length us, event | category | flops | bytes accessed | tf_op | source)
XLA Modules:
  0.0 80.0 jit_solution(2563133567151795848)
XLA Ops:
  0.6 4.9 %collective-permute-start.2 = (bf16[3,32,768]{2,1,0:T(8,128)(2,1)}, bf16[3,32,768]{2,1,0:T(8,128)(2,1)S(1)}, u32[]{:S(2)}, u32[]{:S(2)}) collective-permute-start(bf16[3,32,768]{2,1,0:T(8,128)(2,1)} %bitcast.3), channel_id=1, source_target_pairs={{0,1},{2,3},{4,5},{6,7},{8,9},{10,11},{12,13},{14,15},{17,16},{19,... | collective-permute-start | bytes 442376 | tf_op jit(solution)/shard_map/ppermute | solution.py:223
  5.5 0.5 collective-permute-start.1
  6.0 1.6 %collective-permute-start = (bf16[3,32,768]{2,1,0:T(8,128)(2,1)}, bf16[3,32,768]{2,1,0:T(8,128)(2,1)S(1)}, u32[]{:S(2)}, u32[]{:S(2)}) collective-permute-start(bf16[3,32,768]{2,1,0:T(8,128)(2,1)} %bitcast.5), channel_id=1, source_target_pairs={{0,0},{16,1},{2,2},{18,3},{4,4},{20,5},{6,6},{22,7},{8,8},{24,9},{... | collective-permute-start | bytes 442376 | tf_op jit(solution)/shard_map/ppermute | solution.py:223
  7.6 1.3 %collective-permute-done.2.refs_0_ = bf16[3,32,768]{2,1,0:T(8,128)(2,1)S(1)} collective-permute-done((bf16[3,32,768]{2,1,0:T(8,128)(2,1)}, bf16[3,32,768]{2,1,0:T(8,128)(2,1)S(1)}, u32[]{:S(2)}, u32[]{:S(2)}) %collective-permute-start.2) | collective-permute-done | bytes 147488 | tf_op jit(solution)/shard_map/ppermute | solution.py:223
  8.9 2.2 %collective-permute-done.1.refs_1_ = bf16[3,32,768]{2,1,0:T(8,128)(2,1)S(1)} collective-permute-done((bf16[3,32,768]{2,1,0:T(8,128)(2,1)}, bf16[3,32,768]{2,1,0:T(8,128)(2,1)S(1)}, u32[]{:S(2)}, u32[]{:S(2)}) %collective-permute-start.1) | collective-permute-done | bytes 147488 | tf_op jit(solution)/shard_map/ppermute | solution.py:223
  11.1 0.0 copy-start.4
  11.1 0.0 collective-permute-done.refs_0_
  11.1 0.0 copy-start.5
  11.1 0.6 copy-done.4
  11.7 0.1 copy-done.5
  11.8 1.9 %assemble.1 = (bf16[3,64,768]{2,1,0:T(8,128)(2,1)}, f32[8,3,768]{2,1,0:T(4,128)}) custom-call(s32[1]{0:T(128)} %bitcast.row, f32[3,3,64]{2,1,0:T(4,128)} %rot_ref.3, bf16[3,32,768]{2,1,0:T(8,128)(2,1)} %copy-done.5, bf16[3,32,768]{2,1,0:T(8,128)(2,1)} %copy-done.4), custom_call_target="tpu_custom_call" | custom-call | tf_op jit(solution)/shard_map/assemble/pallas_call | solution.py:237
  13.7 10.2 %all_to_all.15.centre_ref = f32[8,3,768]{2,1,0:T(4,128)S(1)} all-to-all(f32[8,3,768]{2,1,0:T(4,128)} %get-tuple-element.17), channel_id=1, replica_groups={{0,2,4,6,8,10,12,14},{16,18,20,22,24,26,28,30},{1,3,5,7,9,11,13,15},{17..., dimensions={0} | all-to-all | bytes 147456 | tf_op jit(solution)/shard_map/all_to_all | solution.py:248
  23.8 0.8 %collective-permute-start.5 = (bf16[3,64,768]{2,1,0:T(8,128)(2,1)}, bf16[3,64,768]{2,1,0:T(8,128)(2,1)S(1)}, u32[]{:S(2)}, u32[]{:S(2)}) collective-permute-start(bf16[3,64,768]{2,1,0:T(8,128)(2,1)} %get-tuple-element.24.panel_ref.refs_0_), channel_id=1, source_target_pairs={{12,0},{13,1},{14,2},{15,3},{8,4},{9,5},{10,6},{11,7},{4,8},{5,9},... | collective-permute-start | bytes 884744 | tf_op jit(solution)/shard_map/ppermute | solution.py:223
  24.6 1.5 %collective-permute-start.4 = (bf16[3,64,768]{2,1,0:T(8,128)(2,1)}, bf16[3,64,768]{2,1,0:T(8,128)(2,1)S(1)}, u32[]{:S(2)}, u32[]{:S(2)}) collective-permute-start(bf16[3,64,768]{2,1,0:T(8,128)(2,1)} %get-tuple-element.24.panel_ref.refs_0_), channel_id=1, source_target_pairs={{8,0},{9,1},{10,2},{11,3},{12,4},{13,5},{14,6},{15,7},{0,8},{1,9},... | collective-permute-start | bytes 884744 | tf_op jit(solution)/shard_map/ppermute | solution.py:223
  26.1 1.2 %collective-permute-start.3 = (bf16[3,64,768]{2,1,0:T(8,128)(2,1)}, bf16[3,64,768]{2,1,0:T(8,128)(2,1)S(1)}, u32[]{:S(2)}, u32[]{:S(2)}) collective-permute-start(bf16[3,64,768]{2,1,0:T(8,128)(2,1)} %get-tuple-element.24.panel_ref.refs_0_), channel_id=1, source_target_pairs={{4,0},{5,1},{6,2},{7,3},{0,4},{1,5},{2,6},{3,7},{12,8},{13,9},{14,... | collective-permute-start | bytes 884744 | tf_op jit(solution)/shard_map/ppermute | solution.py:223
  27.3 0.0 copy-start
  27.3 1.0 %copy-done = bf16[3,64,768]{2,1,0:T(8,128)(2,1)S(1)} copy-done((bf16[3,64,768]{2,1,0:T(8,128)(2,1)S(1)}, bf16[3,64,768]{2,1,0:T(8,128)(2,1)}, u32[]{:S(2)}) %copy-start) | copy-done | bytes 294936
  28.3 0.0 copy-start.2
  28.3 0.9 %copy-done.2 = bf16[32,3,768]{2,0,1:T(8,128)(2,1)S(1)} copy-done((bf16[32,3,768]{2,0,1:T(8,128)(2,1)S(1)}, bf16[32,3,768]{2,0,1:T(8,128)(2,1)}, u32[]{:S(2)}) %copy-start.2) | copy-done | bytes 147480
  29.2 0.0 copy-start.3
  29.2 0.7 copy-done.3
  29.9 0.0 copy-start.1
  29.9 13.0 %weighted_fit.1 = (f32[8,8,128]{2,1,0:T(8,128)S(1)}, bf16[3,64,768]{2,1,0:T(8,128)(2,1)S(1)}, f32[3,768]{1,0:T(4,128)S(1)}) custom-call(s32[1]{0:T(128)} %bitcast.row, s32[1]{0:T(128)} %bitcast.1.col, f32[768,6144]{1,0:T(8,128)} %inv_ref.1, f32[8,3,768]{2,1,0:T(4,128)S(1)} %all_to_all.15.centre_ref, f32[3,3,64]{2,1,0:T(4,128)S(1)} %copy-done.3, ...), custom_call_target="tpu_custom_call" | custom-call | flops 28311552 | bytes 18874368 | tf_op jit(solution)/shard_map/weighted_fit/pallas_call | solution.py:253
  42.9 7.8 %all_to_all.16.parts_ref = f32[8,8,128]{2,1,0:T(8,128)} all-to-all(f32[8,8,128]{2,1,0:T(8,128)S(1)} %get-tuple-element.21), channel_id=1, replica_groups={{0,2,4,6,8,10,12,14},{16,18,20,22,24,26,28,30},{1,3,5,7,9,11,13,15},{17..., dimensions={0} | all-to-all | bytes 65536 | tf_op jit(solution)/shard_map/all_to_all | solution.py:282
  50.7 1.4 %add_parts.1 = f32[4,8,128]{2,1,0:T(8,128)} custom-call(f32[8,8,128]{2,1,0:T(8,128)} %all_to_all.16.parts_ref), custom_call_target="tpu_custom_call" | custom-call | tf_op jit(solution)/shard_map/add_parts/pallas_call | solution.py:283
  52.1 0.0 collective-permute-done.5.refs_6_
  52.1 0.0 collective-permute-done.4.refs_4_
  52.1 0.0 collective-permute-done.3.refs_2_
  52.1 0.0 copy-done.1
  52.1 0.1 collective-permute-start.6
  52.2 0.5 collective-permute-start.7
  52.7 0.1 collective-permute-start.8
  52.8 0.4 collective-permute-start.9
  53.2 15.0 %all_to_all.17.fits_ref = f32[4,8,128]{2,1,0:T(8,128)S(1)} all-to-all(f32[4,8,128]{2,1,0:T(8,128)} %add_parts.1), channel_id=1, replica_groups={{0,1,16,17},{2,3,18,19},{4,5,20,21},{6,7,22,23},{8,9,24,25},{10,11,26,2..., dimensions={0} | all-to-all | bytes 32768 | tf_op jit(solution)/shard_map/all_to_all | solution.py:295
  68.2 0.0 collective-permute-done.6.refs_1_
  68.2 0.0 collective-permute-done.7.refs_3_
  68.2 0.0 collective-permute-done.8.refs_5_
  68.2 0.0 collective-permute-done.9.refs_7_
  68.2 11.8 %covariance.1 = (f32[768,6144]{1,0:T(8,128)}, f32[3,3,32]{2,1,0:T(4,128)}) custom-call(s32[1]{0:T(128)} %bitcast.row, s32[1]{0:T(128)} %bitcast.1.col, f32[4,8,128]{2,1,0:T(8,128)S(1)} %all_to_all.17.fits_ref, bf16[3,64,768]{2,1,0:T(8,128)(2,1)S(1)} %get-tuple-element.22.rows_ref, f32[3,768]{1,0:T(4,128)S(1)} %get-tuple-element.23.rows_centre_ref, ...), custom_call_target="tpu_custom_call" | custom-call | flops 1811939328 | bytes 18874368 | tf_op jit(solution)/shard_map/covariance/pallas_call | solution.py:301
Async XLA Ops:
  0.6 8.3 %collective-permute-start.2 = (bf16[3,32,768]{2,1,0:T(8,128)(2,1)}, bf16[3,32,768]{2,1,0:T(8,128)(2,1)S(1)}, u32[]{:S(2)}, u32[]{:S(2)}) collective-permute-start(bf16[3,32,768]{2,1,0:T(8,128)(2,1)} %bitcast.3), channel_id=1, source_target_pairs={{0,1},{2,3},{4,5},{6,7},{8,9},{10,11},{12,13},{14,15},{17,16},{19,... | collective-permute-start | bytes 442376 | tf_op jit(solution)/shard_map/ppermute | solution.py:223
  5.5 5.6 %collective-permute-start.1 = (bf16[3,32,768]{2,1,0:T(8,128)(2,1)}, bf16[3,32,768]{2,1,0:T(8,128)(2,1)S(1)}, u32[]{:S(2)}, u32[]{:S(2)}) collective-permute-start(bf16[3,32,768]{2,1,0:T(8,128)(2,1)} %bitcast.4), channel_id=1, source_target_pairs={{1,0},{17,1},{3,2},{19,3},{5,4},{21,5},{7,6},{23,7},{9,8},{25,9},{... | collective-permute-start | bytes 442376 | tf_op jit(solution)/shard_map/ppermute | solution.py:223
  6.0 5.0 %collective-permute-start = (bf16[3,32,768]{2,1,0:T(8,128)(2,1)}, bf16[3,32,768]{2,1,0:T(8,128)(2,1)S(1)}, u32[]{:S(2)}, u32[]{:S(2)}) collective-permute-start(bf16[3,32,768]{2,1,0:T(8,128)(2,1)} %bitcast.5), channel_id=1, source_target_pairs={{0,0},{16,1},{2,2},{18,3},{4,4},{20,5},{6,6},{22,7},{8,8},{24,9},{... | collective-permute-start | bytes 442376 | tf_op jit(solution)/shard_map/ppermute | solution.py:223
  11.1 0.7 copy-start.4
  11.1 0.7 copy-start.5
  23.8 28.3 %collective-permute-start.5 = (bf16[3,64,768]{2,1,0:T(8,128)(2,1)}, bf16[3,64,768]{2,1,0:T(8,128)(2,1)S(1)}, u32[]{:S(2)}, u32[]{:S(2)}) collective-permute-start(bf16[3,64,768]{2,1,0:T(8,128)(2,1)} %get-tuple-element.24.panel_ref.refs_0_), channel_id=1, source_target_pairs={{12,0},{13,1},{14,2},{15,3},{8,4},{9,5},{10,6},{11,7},{4,8},{5,9},... | collective-permute-start | bytes 884744 | tf_op jit(solution)/shard_map/ppermute | solution.py:223
  24.6 27.5 %collective-permute-start.4 = (bf16[3,64,768]{2,1,0:T(8,128)(2,1)}, bf16[3,64,768]{2,1,0:T(8,128)(2,1)S(1)}, u32[]{:S(2)}, u32[]{:S(2)}) collective-permute-start(bf16[3,64,768]{2,1,0:T(8,128)(2,1)} %get-tuple-element.24.panel_ref.refs_0_), channel_id=1, source_target_pairs={{8,0},{9,1},{10,2},{11,3},{12,4},{13,5},{14,6},{15,7},{0,8},{1,9},... | collective-permute-start | bytes 884744 | tf_op jit(solution)/shard_map/ppermute | solution.py:223
  26.1 26.0 %collective-permute-start.3 = (bf16[3,64,768]{2,1,0:T(8,128)(2,1)}, bf16[3,64,768]{2,1,0:T(8,128)(2,1)S(1)}, u32[]{:S(2)}, u32[]{:S(2)}) collective-permute-start(bf16[3,64,768]{2,1,0:T(8,128)(2,1)} %get-tuple-element.24.panel_ref.refs_0_), channel_id=1, source_target_pairs={{4,0},{5,1},{6,2},{7,3},{0,4},{1,5},{2,6},{3,7},{12,8},{13,9},{14,... | collective-permute-start | bytes 884744 | tf_op jit(solution)/shard_map/ppermute | solution.py:223
  27.3 1.0 %copy-start = (bf16[3,64,768]{2,1,0:T(8,128)(2,1)S(1)}, bf16[3,64,768]{2,1,0:T(8,128)(2,1)}, u32[]{:S(2)}) copy-start(bf16[3,64,768]{2,1,0:T(8,128)(2,1)} %get-tuple-element.24.panel_ref.refs_0_) | copy-start | bytes 884740
  28.3 0.9 %copy-start.2 = (bf16[32,3,768]{2,0,1:T(8,128)(2,1)S(1)}, bf16[32,3,768]{2,0,1:T(8,128)(2,1)}, u32[]{:S(2)}) copy-start(bf16[32,3,768]{2,0,1:T(8,128)(2,1)} %param.3) | copy-start | bytes 442372
  29.2 0.7 copy-start.3
  29.9 22.2 %copy-start.1 = (bf16[3,64,768]{2,1,0:T(8,128)(2,1)S(1)}, bf16[3,64,768]{2,1,0:T(8,128)(2,1)}, u32[]{:S(2)}) copy-start(bf16[3,64,768]{2,1,0:T(8,128)(2,1)} %get-tuple-element.24.panel_ref.refs_0_) | copy-start | bytes 884740
  52.1 16.1 %collective-permute-start.6 = (bf16[3,64,768]{2,1,0:T(8,128)(2,1)S(1)}, bf16[3,64,768]{2,1,0:T(8,128)(2,1)S(1)}, u32[]{:S(2)}, u32[]{:S(2)}) collective-permute-start(bf16[3,64,768]{2,1,0:T(8,128)(2,1)S(1)} %copy-done.1), channel_id=1, source_target_pairs={{2,0},{3,1},{0,2},{1,3},{6,4},{7,5},{4,6},{5,7},{10,8},{11,9},{8,1... | collective-permute-start | bytes 884744 | tf_op jit(solution)/shard_map/ppermute | solution.py:223
  52.2 16.0 %collective-permute-start.7 = (bf16[3,64,768]{2,1,0:T(8,128)(2,1)S(1)}, bf16[3,64,768]{2,1,0:T(8,128)(2,1)S(1)}, u32[]{:S(2)}, u32[]{:S(2)}) collective-permute-start(bf16[3,64,768]{2,1,0:T(8,128)(2,1)S(1)} %collective-permute-done.3.refs_2_), channel_id=1, source_target_pairs={{2,0},{3,1},{0,2},{1,3},{6,4},{7,5},{4,6},{5,7},{10,8},{11,9},{8,1... | collective-permute-start | bytes 884744 | tf_op jit(solution)/shard_map/ppermute | solution.py:223
  52.7 15.5 %collective-permute-start.8 = (bf16[3,64,768]{2,1,0:T(8,128)(2,1)S(1)}, bf16[3,64,768]{2,1,0:T(8,128)(2,1)S(1)}, u32[]{:S(2)}, u32[]{:S(2)}) collective-permute-start(bf16[3,64,768]{2,1,0:T(8,128)(2,1)S(1)} %collective-permute-done.4.refs_4_), channel_id=1, source_target_pairs={{2,0},{3,1},{0,2},{1,3},{6,4},{7,5},{4,6},{5,7},{10,8},{11,9},{8,1... | collective-permute-start | bytes 884744 | tf_op jit(solution)/shard_map/ppermute | solution.py:223
  52.8 15.4 %collective-permute-start.9 = (bf16[3,64,768]{2,1,0:T(8,128)(2,1)S(1)}, bf16[3,64,768]{2,1,0:T(8,128)(2,1)S(1)}, u32[]{:S(2)}, u32[]{:S(2)}) collective-permute-start(bf16[3,64,768]{2,1,0:T(8,128)(2,1)S(1)} %collective-permute-done.5.refs_6_), channel_id=1, source_target_pairs={{2,0},{3,1},{0,2},{1,3},{6,4},{7,5},{4,6},{5,7},{10,8},{11,9},{8,1... | collective-permute-start | bytes 884744 | tf_op jit(solution)/shard_map/ppermute | solution.py:223

commit v5 on v2

v5 whole, which is shorter than its diff:
```python
import functools

import jax
import jax.numpy as jnp
from jax import lax
from jax.experimental import pallas as pl
from jax.experimental.pallas import tpu as pltpu
from jax.sharding import PartitionSpec as P

POLAR = 12
LANES = 128
F32 = jnp.float32
BF16 = jnp.bfloat16
MIB = 1 << 20


def vmem():
    return pl.BlockSpec(memory_space=pltpu.VMEM)


def smem():
    return pl.BlockSpec(memory_space=pltpu.SMEM)


def three_pieces(value):
    high = value.astype(BF16)
    rest = value - high.astype(F32)
    mid = rest.astype(BF16)
    low = (rest - mid.astype(F32)).astype(BF16)
    return high, mid, low


def rotated_sum(rot, coords):
    depth = coords.shape[0] * coords.shape[1]
    flat = jnp.concatenate([rot[:, part, :] for part in range(3)], axis=1)
    padded = jnp.concatenate([flat, jnp.zeros((5, depth), F32)], axis=0)
    stacked = jnp.concatenate(three_pieces(padded), axis=0)
    product = jnp.dot(stacked, coords.reshape(depth, coords.shape[2]), preferred_element_type=F32)
    return (product[16:19] + product[8:11]) + product[0:3]


def partial_centre_kernel(frame_total, col, rot_ref, coords_ref, out_ref):
    local = coords_ref.shape[1]
    block = lax.broadcasted_iota(jnp.int32, rot_ref.shape, 2) // local
    rot = jnp.where(block == col[0], rot_ref[...], 0.0)
    coords = jnp.concatenate([coords_ref[...]] * (frame_total // local), axis=1)
    centre = rotated_sum(rot, coords) * (1.0 / frame_total)
    out_ref[...] = jnp.broadcast_to(centre[None], out_ref.shape)


def centre_of(parts_ref, row, col_count):
    total = parts_ref[row * col_count]
    for place in range(1, col_count):
        total = total + parts_ref[row * col_count + place]
    return total


def put_block(out_ref, block, value):
    local = value.shape[1]
    out_ref[:, pl.ds(pl.multiple_of(block * local, local), local), :] = value


def assemble_kernel(members, row, *refs):
    blocks, out_ref = refs[:-1], refs[-1]
    for step, ref in enumerate(blocks):
        put_block(out_ref, lax.rem(row[0] // members + step, len(blocks)), ref[...])


def weighted_fit_kernel(members, row, col, inv_ref, parts_ref, *refs):
    coords_refs, (out_ref, rows_ref, strips_ref, wide_ref, weighted_ref, sems) = refs[:-6], refs[-6:]
    strips, height, col_width = strips_ref.shape
    width = parts_ref.shape[2]

    def fetch(strip):
        rows = pl.ds(pl.multiple_of(strip * height, height), height)
        return pltpu.make_async_copy(inv_ref.at[rows, :], strips_ref.at[strip], sems.at[strip])

    for strip in range(strips):
        fetch(strip).start()
    for block in range(members):
        centre = centre_of(parts_ref, col[0] * members + block, len(coords_refs))
        for comp in range(3):
            factor = jnp.broadcast_to(centre[comp : comp + 1, :], (8, width))
            wide_ref[comp, :, block * width : (block + 1) * width] = factor
    for shift, ref in enumerate(coords_refs):
        put_block(rows_ref, lax.rem(col[0] + shift, len(coords_refs)), ref[...])
    lane = lax.broadcasted_iota(jnp.int32, (height, LANES), 1)
    chunks = col_width // LANES

    def strip_body(strip, carry):
        fetch(strip).wait()

        def body(chunk, sums):
            span = pl.ds(pl.multiple_of(chunk * LANES, LANES), LANES)
            value = strips_ref[strip, :, span].reshape(height // 8, 8, LANES)
            return tuple(sums[comp] + value * wide_ref[comp, :, span][None] for comp in range(3))

        sums = (jnp.zeros((height // 8, 8, LANES), F32),) * 3
        sums = lax.fori_loop(0, chunks, body, sums, unroll=12 if chunks % 12 == 0 else 1)
        packed = jnp.zeros((height, LANES), F32)
        for comp in range(3):
            total = jnp.sum(sums[comp].reshape(height, LANES), axis=1, keepdims=True)
            packed = jnp.where(lane == comp, total, packed)
        weighted_ref[pl.ds(pl.multiple_of(strip * height, height), height), :] = packed
        return carry

    lax.fori_loop(0, strips, strip_body, 0)
    frame_total = rows_ref.shape[1]
    rows = rows_ref[...].reshape(3 * frame_total, width)
    high, mid, low = (jnp.dot(rows, piece, preferred_element_type=F32) for piece in three_pieces(weighted_ref[...]))
    fits = ((low + mid) + high).T
    entries = [
        fits[comp : comp + 1, part * frame_total : (part + 1) * frame_total] for part in range(3) for comp in range(3)
    ]
    first = jnp.concatenate(entries[:8], axis=0)
    last = jnp.concatenate([entries[8], jnp.zeros((7, frame_total), F32)], axis=0)
    message = jnp.concatenate([first, last], axis=1)
    out_ref[...] = jnp.broadcast_to(message[None], out_ref.shape)


def orthogonalized(message, frame_total):
    fitted = [message[entry : entry + 1, :frame_total] for entry in range(8)]
    fitted.append(message[0:1, frame_total:])
    norm = functools.reduce(lambda a, b: a + b, [value * value for value in fitted])
    scaling = jnp.sqrt(1.0 + norm)
    current = [[fitted[3 * col + row] / scaling for col in range(3)] for row in range(3)]
    for _ in range(POLAR):
        square = [[None] * 3 for _ in range(3)]
        for a in range(3):
            for b in range(a, 3):
                x, y = current[a], current[b]
                square[a][b] = square[b][a] = x[0] * y[0] + x[1] * y[1] + x[2] * y[2]
        cubed = [
            [square[a][0] * current[0][b] + square[a][1] * current[1][b] + square[a][2] * current[2][b] for b in range(3)]
            for a in range(3)
        ]
        current = [[1.5 * current[a][b] - 0.5 * cubed[a][b] for b in range(3)] for a in range(3)]
    return current


def put_deviations(wide_ref, coords_ref, centre, chunk, dev_ref):
    frame_total = coords_ref.shape[1]
    span = slice(chunk * LANES, (chunk + 1) * LANES)
    coords = [coords_ref[part, :, span].astype(F32) for part in range(3)]
    for comp in range(3):
        moved = wide_ref[3 * comp] * coords[0]
        moved = moved + wide_ref[3 * comp + 1] * coords[1]
        moved = moved + wide_ref[3 * comp + 2] * coords[2]
        value = moved - centre[comp : comp + 1, span]
        dev_ref[comp * frame_total : (comp + 1) * frame_total, span] = value.astype(BF16)


def put_tile(wide_ref, coords_ref, centre, rows_dev_ref, dev_ref, out_ref):
    width = coords_ref.shape[2]
    scale = 1.0 / (3 * coords_ref.shape[1])
    stride = 2 * LANES if width % (2 * LANES) == 0 else LANES
    for start in range(0, width, stride):
        for chunk in range(start // LANES, (start + stride) // LANES):
            put_deviations(wide_ref, coords_ref, centre, chunk, dev_ref)
        product = jnp.dot(rows_dev_ref[...], dev_ref[:, start : start + stride], preferred_element_type=F32)
        out_ref[:, start : start + stride] = product * scale


def panel_centre(parts_ref, row, col, count, mask, col_count):
    members = 2 * count
    return centre_of(parts_ref, col[0] * members + (lax.rem(row[0], members) ^ mask), col_count)


def first_tiles_kernel(count, row, col, fits_ref, rows_ref, parts_ref, *refs):
    panel_refs = refs[:count]
    out_ref, rot_out_ref, wide_ref, rows_dev_ref, dev_ref = refs[count:]
    frame_total = rows_ref.shape[1]
    local = rot_out_ref.shape[2]

    @pl.when(pl.program_id(0) == 0)
    def _():
        current = orthogonalized(jnp.sum(fits_ref[...], axis=0), frame_total)
        for a in range(3):
            flat = jnp.concatenate(current[a], axis=0)
            kept = flat[:, :local]
            for block in range(1, frame_total // local):
                kept = jnp.where(col[0] == block, flat[:, block * local : (block + 1) * local], kept)
            rot_out_ref[a] = kept
        entries = [current[a][b] for a in range(3) for b in range(3)]
        columns = jnp.concatenate(entries + [jnp.zeros((7, frame_total), F32)], axis=0).T
        for entry in range(9):
            wide_ref[entry] = jnp.broadcast_to(columns[:, entry : entry + 1], (frame_total, LANES))
        centre = centre_of(parts_ref, row[0], frame_total // local)
        for chunk in range(rows_ref.shape[2] // LANES):
            put_deviations(wide_ref, rows_ref, centre, chunk, dev_ref)
        rows_dev_ref[...] = dev_ref[...].T

    for step in range(count):

        @pl.when(pl.program_id(0) == step)
        def _(step=step):
            centre = panel_centre(parts_ref, row, col, count, 2 * step, frame_total // local)
            put_tile(wide_ref, panel_refs[step], centre, rows_dev_ref, dev_ref, out_ref)


def last_tiles_kernel(count, col_count, row, col, before_ref, wide_ref, rows_dev_ref, parts_ref, *refs):
    panel_refs = refs[:count]
    out_ref, dev_ref = refs[count:]
    for step in range(count):

        @pl.when(pl.program_id(0) == step)
        def _(step=step):
            centre = panel_centre(parts_ref, row, col, count, 2 * step + 1, col_count)
            put_tile(wide_ref, panel_refs[step], centre, rows_dev_ref, dev_ref, out_ref)


def per_device(frames, rotations, inverse_cov):
    row_count, col_count = lax.axis_size("row"), lax.axis_size("col")
    members = row_count // col_count
    row = lax.axis_index("row").astype(jnp.int32).reshape(1)
    col = lax.axis_index("col").astype(jnp.int32).reshape(1)
    local, _, width = frames.shape
    frame_total = local * col_count
    device_total = row_count * col_count
    col_width = inverse_cov.shape[1]
    half = members // 2
    coords = jnp.transpose(frames, (1, 0, 2))

    def move(value, source_of, receives=lambda group, col: True):
        pairs = []
        for group in range(col_count):
            for member in range(members):
                for place in range(col_count):
                    if receives(group, place):
                        from_group, from_member, from_col = source_of(group, member, place)
                        source = (from_group * members + from_member) * col_count + from_col
                        pairs.append((source, (group * members + member) * col_count + place))
        return lax.ppermute(value, ("row", "col"), pairs)

    def from_panel_row(value, step):
        return move(value, lambda g, m, c: (c, m, (g + step) % col_count))

    def from_member(value, mask):
        return move(value, lambda g, m, c: (g, m ^ mask, c))

    def limit(mib):
        return pltpu.CompilerParams(vmem_limit_bytes=mib * MIB)

    panel_parts = [from_panel_row(coords, step) for step in range(col_count)]
    others = [move(coords, lambda g, m, c, s=step: (g, m, (c + s) % col_count)) for step in range(1, col_count)]
    repeated = pl.pallas_call(
        functools.partial(partial_centre_kernel, frame_total),
        out_shape=jax.ShapeDtypeStruct((device_total, 3, width), F32),
        in_specs=[smem(), vmem(), vmem()],
        out_specs=vmem(),
        compiler_params=limit(8),
        name="partial_centre",
    )(col, rotations, coords)
    parts = lax.all_to_all(repeated, ("row", "col"), split_axis=0, concat_axis=0, tiled=True)

    _, panel_parts = lax.optimization_barrier((parts, panel_parts))
    own_block = pl.pallas_call(
        functools.partial(assemble_kernel, members),
        out_shape=jax.ShapeDtypeStruct((3, frame_total, width), BF16),
        in_specs=[smem()] + [vmem()] * col_count,
        out_specs=vmem(),
        compiler_params=limit(4),
        name="assemble",
    )(row, *panel_parts)
    even_panel = [own_block] + [from_member(own_block, 2 * step) for step in range(1, members // 2)]

    height = 64 if width % 64 == 0 else 8
    inverse_cov = pltpu.with_memory_space_constraint(inverse_cov, pltpu.HBM)
    message, rows_all = pl.pallas_call(
        functools.partial(weighted_fit_kernel, members),
        in_specs=[smem(), smem(), pl.BlockSpec(memory_space=pl.ANY)] + [vmem()] * (1 + col_count),
        out_specs=(vmem(), vmem()),
        scratch_shapes=[
            pltpu.VMEM((width // height, height, col_width), F32),
            pltpu.VMEM((3, 8, col_width), F32),
            pltpu.VMEM((width, LANES), F32),
            pltpu.SemaphoreType.DMA((width // height,)),
        ],
        out_shape=(
            jax.ShapeDtypeStruct((device_total, 8, 2 * frame_total), F32),
            jax.ShapeDtypeStruct((3, frame_total, width), BF16),
        ),
        compiler_params=limit(28),
        cost_estimate=pl.CostEstimate(
            flops=6 * width * col_width, bytes_accessed=4 * width * col_width, transcendentals=0
        ),
        name="weighted_fit",
    )(row, col, inverse_cov, parts, coords, *others)
    fits = lax.all_to_all(message, ("row", "col"), split_axis=0, concat_axis=0, tiled=True)
    fits, even_panel = lax.optimization_barrier((fits, even_panel))
    odd_panel = [from_member(block, 1) for block in even_panel]

    def tile_spec(odd):
        return pl.BlockSpec((width, width), lambda i, row, *_: (0, lax.rem(row[0], members) ^ (2 * i + odd)))

    tiles_cost = pl.CostEstimate(
        flops=3 * frame_total * width * col_width, bytes_accessed=2 * width * col_width, transcendentals=0
    )
    dev_scratch = pltpu.VMEM((3 * frame_total, width), BF16)
    half_done, transforms, wide, rows_dev = pl.pallas_call(
        functools.partial(first_tiles_kernel, half),
        grid_spec=pltpu.PrefetchScalarGridSpec(
            num_scalar_prefetch=2,
            grid=(half,),
            in_specs=[vmem()] * (3 + half),
            out_specs=(tile_spec(0), vmem(), vmem(), vmem()),
            scratch_shapes=[dev_scratch],
        ),
        out_shape=(
            jax.ShapeDtypeStruct((width, col_width), F32),
            jax.ShapeDtypeStruct((3, 3, local), F32),
            jax.ShapeDtypeStruct((9, frame_total, LANES), F32),
            jax.ShapeDtypeStruct((width, 3 * frame_total), BF16),
        ),
        compiler_params=limit(16),
        cost_estimate=tiles_cost,
        name="steps_and_even_tiles",
    )(row, col, fits, rows_all, parts, *even_panel)
    covariance = pl.pallas_call(
        functools.partial(last_tiles_kernel, half, col_count),
        grid_spec=pltpu.PrefetchScalarGridSpec(
            num_scalar_prefetch=2,
            grid=(half,),
            in_specs=[pl.BlockSpec(memory_space=pl.ANY)] + [vmem()] * (3 + half),
            out_specs=tile_spec(1),
            scratch_shapes=[dev_scratch],
        ),
        out_shape=jax.ShapeDtypeStruct((width, col_width), F32),
        input_output_aliases={2: 0},
        compiler_params=limit(16),
        cost_estimate=tiles_cost,
        name="odd_tiles",
    )(row, col, half_done, wide, rows_dev, parts, *odd_panel)
    return (covariance, transforms)


def solution(mesh):
    placed = (P("col", None, "row"), P(), P("row", "col"))
    return jax.shard_map(
        per_device,
        mesh=mesh,
        in_specs=placed,
        out_specs=(P("row", "col"), P(None, None, "col")),
        check_vma=False,
    )
```

time: 83.7 us -> 66.7 us (0.80)
  blocking collectives: 0 us -> 14.8 us
  local copies, waits for them, and re-layouts: 15 us -> 2.51 us
  starting transfers between devices: 27.6 us -> 19.6 us
  Pallas kernels: 26.1 us -> 20.5 us
  waiting for transfers between devices: 13.8 us -> 8.22 us
    all_to_all x0 -> x1, blocking collectives: none -> 14.8 us  [per_device(): lax.all_to_all(message, ('row', 'col'), split_axis=0, concat_axis=0, tile...]
    unnamed x18 -> x6, local copies, waits for them, and re-layouts: 15 us -> 2.51 us
    ppermute x16 -> x10, starting transfers between devices: 24.6 us -> 12.3 us  [move(): return lax.ppermute(value, ('row', 'col'), pairs)]
    all_to_all x1, starting transfers between devices: 3.01 us -> 7.3 us  [per_device(): lax.all_to_all(repeated, ('row', 'col'), split_axis=0, concat_axis=0, til...]
    all_to_all x1, waiting for transfers between devices: 8.59 us -> 5.5 us  [per_device(): lax.all_to_all(repeated, ('row', 'col'), split_axis=0, concat_axis=0, til...]
    pallas_call x5 -> x3, Pallas kernels: 22.6 us -> 19.5 us  [the longest x1 7.48 us: per_device(): pl.pallas_call(functools.partial(weighted_fit_kernel, members), in_specs=...]
    ppermute x16 -> x10, waiting for transfers between devices: 5.2 us -> 2.72 us  [move(): return lax.ppermute(value, ('row', 'col'), pairs)]
    pallas_call x1, Pallas kernels: 1.72 us -> 0.03 us  [per_device(): pl.pallas_call(functools.partial(assemble_kernel, members), out_shape=jax...]
  transfers between devices with their start and end apart: 17 -> 11, of which waited for: 5 -> 2; matrix products, arithmetic and copies ran while one was open for 0% -> 0% of each run, Pallas kernels for 24% -> 22%
where the time goes in v5:
time: 66.7 us; the launch traced here: 66.3 us
  Pallas kernels  20.5 us (31%)
  starting transfers between devices  19.6 us (29%)
  blocking collectives  14.8 us (22%)
  waiting for transfers between devices  8.22 us (12%)
  local copies, waits for them, and re-layouts  2.51 us (4%)
  between operations  0.7 us (1%)
    all_to_all x1, blocking collectives, per_device(): lax.all_to_all(message, ('row', 'col'), split_axis=0, concat_axis=0, tile...  14.8 us
    ppermute x10, starting transfers between devices, move(): return lax.ppermute(value, ('row', 'col'), pairs)  12.3 us
    pallas_call x1, Pallas kernels, per_device(): pl.pallas_call(functools.partial(weighted_fit_kernel, members), in_specs=...  7.48 us
    all_to_all x1, starting transfers between devices, per_device(): lax.all_to_all(repeated, ('row', 'col'), split_axis=0, concat_axis=0, til...  7.3 us
    pallas_call x1, Pallas kernels, per_device(): pl.pallas_call(functools.partial(first_tiles_kernel, half), grid_spec=plt...  7.23 us
    all_to_all x1, waiting for transfers between devices, per_device(): lax.all_to_all(repeated, ('row', 'col'), split_axis=0, concat_axis=0, til...  5.5 us
    pallas_call x1, Pallas kernels, per_device(): pl.pallas_call(functools.partial(last_tiles_kernel, half, col_count), gri...  4.77 us
    ppermute x10, waiting for transfers between devices, move(): return lax.ppermute(value, ('row', 'col'), pairs)  2.72 us
  transfers between devices with their start and end apart: 11, of which 2 were waited for; matrix products, arithmetic and copies ran while one was open for 0% of the time, Pallas kernels for 22%

profile of v5, /device:TPU:0, one launch (start us, length us, event | category | flops | bytes accessed | tf_op | source)
XLA Modules:
  0.0 66.3 jit_solution(6175347404863174022)
XLA Ops:
  0.6 0.0 copy-start
  0.6 0.9 %copy-done = bf16[32,3,768]{2,0,1:T(8,128)(2,1)S(1)} copy-done((bf16[32,3,768]{2,0,1:T(8,128)(2,1)S(1)}, bf16[32,3,768]{2,0,1:T(8,128)(2,1)}, u32[]{:S(2)}) %copy-start) | copy-done | bytes 147480
  1.5 0.0 copy-start.2
  1.6 0.7 %copy-done.2 = f32[3,3,64]{2,1,0:T(4,128)S(1)} copy-done((f32[3,3,64]{2,1,0:T(4,128)S(1)}, f32[3,3,64]{2,1,0:T(4,128)}, u32[]{:S(2)}) %copy-start.2) | copy-done | bytes 2328
  2.2 1.0 %partial_centre.1 = f32[32,3,768]{2,1,0:T(4,128)} custom-call(s32[1]{0:T(128)} %bitcast.1.col, f32[3,3,64]{2,1,0:T(4,128)S(1)} %copy-done.2, bf16[3,32,768]{2,1,0:T(8,128)(2,1)S(1)} %bitcast.6), custom_call_target="tpu_custom_call" | custom-call | tf_op jit(solution)/shard_map/partial_centre/pallas_call | solution.py:246
  3.2 7.3 %all-to-all-start = ((f32[32,3,768]{2,1,0:T(4,128)}), f32[32,3,768]{2,1,0:T(4,128)S(1)}, u32[]{:S(2)}, u32[]{:S(2)}) async-start(f32[32,3,768]{2,1,0:T(4,128)} %partial_centre.1), calls=%async_computation | async-start | bytes 786432 | tf_op jit(solution)/shard_map/all_to_all | solution.py:254
  10.5 2.7 %collective-permute-start.2 = (bf16[3,32,768]{2,1,0:T(8,128)(2,1)}, bf16[3,32,768]{2,1,0:T(8,128)(2,1)S(1)}, u32[]{:S(2)}, u32[]{:S(2)}) collective-permute-start(bf16[3,32,768]{2,1,0:T(8,128)(2,1)} %bitcast.3), channel_id=1, source_target_pairs={{1,0},{17,1},{3,2},{19,3},{5,4},{21,5},{7,6},{23,7},{9,8},{25,9},{... | collective-permute-start | bytes 442376 | tf_op jit(solution)/shard_map/ppermute | solution.py:233
  13.3 1.6 %collective-permute-start.1 = (bf16[3,32,768]{2,1,0:T(8,128)(2,1)}, bf16[3,32,768]{2,1,0:T(8,128)(2,1)S(1)}, u32[]{:S(2)}, u32[]{:S(2)}) collective-permute-start(bf16[3,32,768]{2,1,0:T(8,128)(2,1)} %bitcast.4), channel_id=1, source_target_pairs={{0,0},{16,1},{2,2},{18,3},{4,4},{20,5},{6,6},{22,7},{8,8},{24,9},{... | collective-permute-start | bytes 442376 | tf_op jit(solution)/shard_map/ppermute | solution.py:233
  14.8 3.3 %collective-permute-start = (bf16[3,32,768]{2,1,0:T(8,128)(2,1)}, bf16[3,32,768]{2,1,0:T(8,128)(2,1)S(1)}, u32[]{:S(2)}, u32[]{:S(2)}) collective-permute-start(bf16[3,32,768]{2,1,0:T(8,128)(2,1)} %bitcast.5), channel_id=1, source_target_pairs={{1,0},{0,1},{3,2},{2,3},{5,4},{4,5},{7,6},{6,7},{9,8},{8,9},{11,10... | collective-permute-start | bytes 442376 | tf_op jit(solution)/shard_map/ppermute | solution.py:233
  18.2 2.7 %collective-permute-done.2.refs_1_ = bf16[3,32,768]{2,1,0:T(8,128)(2,1)S(1)} collective-permute-done((bf16[3,32,768]{2,1,0:T(8,128)(2,1)}, bf16[3,32,768]{2,1,0:T(8,128)(2,1)S(1)}, u32[]{:S(2)}, u32[]{:S(2)}) %collective-permute-start.2) | collective-permute-done | bytes 147488 | tf_op jit(solution)/shard_map/ppermute | solution.py:233
  20.9 0.0 collective-permute-done.1.refs_0_
  20.9 5.5 %all-to-all-done.parts_ref = f32[32,3,768]{2,1,0:T(4,128)S(1)} async-done(((f32[32,3,768]{2,1,0:T(4,128)}), f32[32,3,768]{2,1,0:T(4,128)S(1)}, u32[]{:S(2)}, u32[]{:S(2)}) %all-to-all-start) | async-done | bytes 294944 | tf_op jit(solution)/shard_map/all_to_all | solution.py:254
  26.4 2.4 %collective-permute-start.5 = (bf16[3,64,768]{2,1,0:T(8,128)(2,1)S(1)}, bf16[3,64,768]{2,1,0:T(8,128)(2,1)S(1)}, u32[]{:S(2)}, u32[]{:S(2)}) collective-permute-start(bf16[3,64,768]{2,1,0:T(8,128)(2,1)S(1)} %assemble.1.refs_0_), channel_id=1, source_target_pairs={{12,0},{13,1},{14,2},{15,3},{8,4},{9,5},{10,6},{11,7},{4,8},{5,9},... | collective-permute-start | bytes 884744 | tf_op jit(solution)/shard_map/ppermute | solution.py:233
  28.8 0.6 collective-permute-start.4
  29.4 0.5 collective-permute-start.3
  30.0 0.0 collective-permute-done.refs_1_
  30.0 0.0 copy-start.1
  30.0 0.9 %copy-done.1 = bf16[32,3,768]{2,0,1:T(8,128)(2,1)S(1)} copy-done((bf16[32,3,768]{2,0,1:T(8,128)(2,1)S(1)}, bf16[32,3,768]{2,0,1:T(8,128)(2,1)}, u32[]{:S(2)}) %copy-start.1) | copy-done | bytes 147480
  30.9 7.5 %weighted_fit.1 = (f32[32,8,128]{2,1,0:T(8,128)S(1)}, bf16[3,64,768]{2,1,0:T(8,128)(2,1)S(1)}) custom-call(s32[1]{0:T(128)} %bitcast.row, s32[1]{0:T(128)} %bitcast.1.col, f32[768,6144]{1,0:T(8,128)} %inv_ref.1, f32[32,3,768]{2,1,0:T(4,128)S(1)} %all-to-all-done.parts_ref, bf16[3,32,768]{2,1,0:T(8,128)(2,1)S(1)} %bitcast.7, ...), custom_call_target="tpu_custom_call" | custom-call | flops 28311552 | bytes 18874368 | tf_op jit(solution)/shard_map/weighted_fit/pallas_call | solution.py:269
  38.4 14.8 %all_to_all.10.fits_ref = f32[32,8,128]{2,1,0:T(8,128)S(1)} all-to-all(f32[32,8,128]{2,1,0:T(8,128)S(1)} %get-tuple-element.15), channel_id=1, replica_groups=mesh['row'=16,'col'=2] {'row','col'}, dimensions={0} | all-to-all | bytes 262144 | tf_op jit(solution)/shard_map/all_to_all | solution.py:289
  53.2 0.0 collective-permute-done.5.refs_3_
  53.2 0.0 collective-permute-done.4.refs_2_
  53.2 0.0 collective-permute-done.3.refs_1_
  53.2 0.1 collective-permute-start.6
  53.3 0.5 collective-permute-start.7
  53.8 0.1 collective-permute-start.8
  53.9 0.4 collective-permute-start.9
  54.3 7.2 %steps_and_even_tiles.1 = (f32[768,6144]{1,0:T(8,128)}, f32[3,3,32]{2,1,0:T(4,128)}, f32[9,64,128]{2,1,0:T(8,128)S(1)}, bf16[768,192]{1,0:T(8,128)(2,1)S(1)}) custom-call(s32[1]{0:T(128)} %bitcast.row, s32[1]{0:T(128)} %bitcast.1.col, f32[32,8,128]{2,1,0:T(8,128)S(1)} %all_to_all.10.fits_ref, bf16[3,64,768]{2,1,0:T(8,128)(2,1)S(1)} %get-tuple-element.19.rows_ref, ...), custom_call_target="tpu_custom_call" | custom-call | flops 905969664 | bytes 9437184 | tf_op jit(solution)/shard_map/steps_and_even_tiles/pallas_call | solution.py:300
  61.5 0.0 collective-permute-done.6.refs_0_
  61.5 0.0 collective-permute-done.7.refs_1_
  61.5 0.0 collective-permute-done.8.refs_2_
  61.5 0.0 collective-permute-done.9.refs_3_
  61.6 4.8 %odd_tiles.1 = f32[768,6144]{1,0:T(8,128)} custom-call(s32[1]{0:T(128)} %bitcast.row, s32[1]{0:T(128)} %bitcast.1.col, f32[768,6144]{1,0:T(8,128)} %get-tuple-element.24.before_ref, f32[9,64,128]{2,1,0:T(8,128)S(1)} %get-tuple-element.25.wide_ref, bf16[768,192]{1,0:T(8,128)(2,1)S(1)} %get-tuple-element.26.rows_dev_ref, ...), custom_call_target="tpu_custom_call", output_to_operand_aliasing={{}: (2, {})} | custom-call | flops 905969664 | bytes 9437184 | tf_op jit(solution)/shard_map/odd_tiles/pallas_call | solution.py:319
  (1 shorter events, 0.0 us)
Async XLA Ops:
  0.6 0.9 %copy-start = (bf16[32,3,768]{2,0,1:T(8,128)(2,1)S(1)}, bf16[32,3,768]{2,0,1:T(8,128)(2,1)}, u32[]{:S(2)}) copy-start(bf16[32,3,768]{2,0,1:T(8,128)(2,1)} %param.3) | copy-start | bytes 442372
  1.5 0.7 %copy-start.2 = (f32[3,3,64]{2,1,0:T(4,128)S(1)}, f32[3,3,64]{2,1,0:T(4,128)}, u32[]{:S(2)}) copy-start(f32[3,3,64]{2,1,0:T(4,128)} %rot_ref.1) | copy-start | bytes 6916
  3.2 23.1 %all-to-all-start = ((f32[32,3,768]{2,1,0:T(4,128)}), f32[32,3,768]{2,1,0:T(4,128)S(1)}, u32[]{:S(2)}, u32[]{:S(2)}) async-start(f32[32,3,768]{2,1,0:T(4,128)} %partial_centre.1), calls=%async_computation | async-start | bytes 786432 | tf_op jit(solution)/shard_map/all_to_all | solution.py:254
  10.5 10.3 %collective-permute-start.2 = (bf16[3,32,768]{2,1,0:T(8,128)(2,1)}, bf16[3,32,768]{2,1,0:T(8,128)(2,1)S(1)}, u32[]{:S(2)}, u32[]{:S(2)}) collective-permute-start(bf16[3,32,768]{2,1,0:T(8,128)(2,1)} %bitcast.3), channel_id=1, source_target_pairs={{1,0},{17,1},{3,2},{19,3},{5,4},{21,5},{7,6},{23,7},{9,8},{25,9},{... | collective-permute-start | bytes 442376 | tf_op jit(solution)/shard_map/ppermute | solution.py:233
  13.3 7.6 %collective-permute-start.1 = (bf16[3,32,768]{2,1,0:T(8,128)(2,1)}, bf16[3,32,768]{2,1,0:T(8,128)(2,1)S(1)}, u32[]{:S(2)}, u32[]{:S(2)}) collective-permute-start(bf16[3,32,768]{2,1,0:T(8,128)(2,1)} %bitcast.4), channel_id=1, source_target_pairs={{0,0},{16,1},{2,2},{18,3},{4,4},{20,5},{6,6},{22,7},{8,8},{24,9},{... | collective-permute-start | bytes 442376 | tf_op jit(solution)/shard_map/ppermute | solution.py:233
  14.8 15.1 %collective-permute-start = (bf16[3,32,768]{2,1,0:T(8,128)(2,1)}, bf16[3,32,768]{2,1,0:T(8,128)(2,1)S(1)}, u32[]{:S(2)}, u32[]{:S(2)}) collective-permute-start(bf16[3,32,768]{2,1,0:T(8,128)(2,1)} %bitcast.5), channel_id=1, source_target_pairs={{1,0},{0,1},{3,2},{2,3},{5,4},{4,5},{7,6},{6,7},{9,8},{8,9},{11,10... | collective-permute-start | bytes 442376 | tf_op jit(solution)/shard_map/ppermute | solution.py:233
  26.4 26.8 %collective-permute-start.5 = (bf16[3,64,768]{2,1,0:T(8,128)(2,1)S(1)}, bf16[3,64,768]{2,1,0:T(8,128)(2,1)S(1)}, u32[]{:S(2)}, u32[]{:S(2)}) collective-permute-start(bf16[3,64,768]{2,1,0:T(8,128)(2,1)S(1)} %assemble.1.refs_0_), channel_id=1, source_target_pairs={{12,0},{13,1},{14,2},{15,3},{8,4},{9,5},{10,6},{11,7},{4,8},{5,9},... | collective-permute-start | bytes 884744 | tf_op jit(solution)/shard_map/ppermute | solution.py:233
  28.8 24.4 %collective-permute-start.4 = (bf16[3,64,768]{2,1,0:T(8,128)(2,1)S(1)}, bf16[3,64,768]{2,1,0:T(8,128)(2,1)S(1)}, u32[]{:S(2)}, u32[]{:S(2)}) collective-permute-start(bf16[3,64,768]{2,1,0:T(8,128)(2,1)S(1)} %assemble.1.refs_0_), channel_id=1, source_target_pairs={{8,0},{9,1},{10,2},{11,3},{12,4},{13,5},{14,6},{15,7},{0,8},{1,9},... | collective-permute-start | bytes 884744 | tf_op jit(solution)/shard_map/ppermute | solution.py:233
  29.4 23.8 %collective-permute-start.3 = (bf16[3,64,768]{2,1,0:T(8,128)(2,1)S(1)}, bf16[3,64,768]{2,1,0:T(8,128)(2,1)S(1)}, u32[]{:S(2)}, u32[]{:S(2)}) collective-permute-start(bf16[3,64,768]{2,1,0:T(8,128)(2,1)S(1)} %assemble.1.refs_0_), channel_id=1, source_target_pairs={{4,0},{5,1},{6,2},{7,3},{0,4},{1,5},{2,6},{3,7},{12,8},{13,9},{14,... | collective-permute-start | bytes 884744 | tf_op jit(solution)/shard_map/ppermute | solution.py:233
  30.0 0.9 %copy-start.1 = (bf16[32,3,768]{2,0,1:T(8,128)(2,1)S(1)}, bf16[32,3,768]{2,0,1:T(8,128)(2,1)}, u32[]{:S(2)}) copy-start(bf16[32,3,768]{2,0,1:T(8,128)(2,1)} %param.3) | copy-start | bytes 442372
  53.2 8.3 %collective-permute-start.6 = (bf16[3,64,768]{2,1,0:T(8,128)(2,1)S(1)}, bf16[3,64,768]{2,1,0:T(8,128)(2,1)S(1)}, u32[]{:S(2)}, u32[]{:S(2)}) collective-permute-start(bf16[3,64,768]{2,1,0:T(8,128)(2,1)S(1)} %assemble.1.refs_0_), channel_id=1, source_target_pairs={{2,0},{3,1},{0,2},{1,3},{6,4},{7,5},{4,6},{5,7},{10,8},{11,9},{8,1... | collective-permute-start | bytes 884744 | tf_op jit(solution)/shard_map/ppermute | solution.py:233
  53.3 8.2 %collective-permute-start.7 = (bf16[3,64,768]{2,1,0:T(8,128)(2,1)S(1)}, bf16[3,64,768]{2,1,0:T(8,128)(2,1)S(1)}, u32[]{:S(2)}, u32[]{:S(2)}) collective-permute-start(bf16[3,64,768]{2,1,0:T(8,128)(2,1)S(1)} %collective-permute-done.3.refs_1_), channel_id=1, source_target_pairs={{2,0},{3,1},{0,2},{1,3},{6,4},{7,5},{4,6},{5,7},{10,8},{11,9},{8,1... | collective-permute-start | bytes 884744 | tf_op jit(solution)/shard_map/ppermute | solution.py:233
  53.8 7.8 %collective-permute-start.8 = (bf16[3,64,768]{2,1,0:T(8,128)(2,1)S(1)}, bf16[3,64,768]{2,1,0:T(8,128)(2,1)S(1)}, u32[]{:S(2)}, u32[]{:S(2)}) collective-permute-start(bf16[3,64,768]{2,1,0:T(8,128)(2,1)S(1)} %collective-permute-done.4.refs_2_), channel_id=1, source_target_pairs={{2,0},{3,1},{0,2},{1,3},{6,4},{7,5},{4,6},{5,7},{10,8},{11,9},{8,1... | collective-permute-start | bytes 884744 | tf_op jit(solution)/shard_map/ppermute | solution.py:233
  53.9 7.7 %collective-permute-start.9 = (bf16[3,64,768]{2,1,0:T(8,128)(2,1)S(1)}, bf16[3,64,768]{2,1,0:T(8,128)(2,1)S(1)}, u32[]{:S(2)}, u32[]{:S(2)}) collective-permute-start(bf16[3,64,768]{2,1,0:T(8,128)(2,1)S(1)} %collective-permute-done.5.refs_3_), channel_id=1, source_target_pairs={{2,0},{3,1},{0,2},{1,3},{6,4},{7,5},{4,6},{5,7},{10,8},{11,9},{8,1... | collective-permute-start | bytes 884744 | tf_op jit(solution)/shard_map/ppermute | solution.py:233

commit v6 on v5

v6 whole, which is shorter than its diff:
```python
import functools

import jax
import jax.numpy as jnp
from jax import lax
from jax.experimental import pallas as pl
from jax.experimental.pallas import tpu as pltpu
from jax.sharding import PartitionSpec as P

POLAR = 12
LANES = 128
F32 = jnp.float32
BF16 = jnp.bfloat16
MIB = 1 << 20


def vmem():
    return pl.BlockSpec(memory_space=pltpu.VMEM)


def hbm():
    return pl.BlockSpec(memory_space=pl.ANY)


def smem():
    return pl.BlockSpec(memory_space=pltpu.SMEM)


def three_pieces(value):
    high = value.astype(BF16)
    rest = value - high.astype(F32)
    mid = rest.astype(BF16)
    low = (rest - mid.astype(F32)).astype(BF16)
    return high, mid, low


def rotated_sum(rot, coords):
    depth = coords.shape[0] * coords.shape[1]
    flat = jnp.concatenate([rot[:, part, :] for part in range(3)], axis=1)
    padded = jnp.concatenate([flat, jnp.zeros((5, depth), F32)], axis=0)
    stacked = jnp.concatenate(three_pieces(padded), axis=0)
    product = jnp.dot(stacked, coords.reshape(depth, coords.shape[2]), preferred_element_type=F32)
    return (product[16:19] + product[8:11]) + product[0:3]


def fetch_all(sources, targets, sems):
    copies = [pltpu.make_async_copy(source, target, sems.at[k]) for k, (source, target) in enumerate(zip(sources, targets))]
    for copy in copies:
        copy.start()
    for copy in copies:
        copy.wait()


def partial_centre_kernel(frame_total, col, rot_hbm, coords_hbm, out_ref, rot_ref, coords_ref, sems):
    fetch_all((rot_hbm, coords_hbm), (rot_ref, coords_ref), sems)
    local = coords_ref.shape[1]
    block = lax.broadcasted_iota(jnp.int32, rot_ref.shape, 2) // local
    rot = jnp.where(block == col[0], rot_ref[...], 0.0)
    coords = jnp.concatenate([coords_ref[...]] * (frame_total // local), axis=1)
    out_ref[...] = rotated_sum(rot, coords) * (1.0 / frame_total)


def stack_kernel(*refs):
    for index, ref in enumerate(refs[:-1]):
        refs[-1][index] = ref[...]


def sum_kernel(*refs):
    total = refs[0][...]
    for ref in refs[1:-1]:
        total = total + ref[...]
    refs[-1][...] = total


def put_block(out_ref, block, value):
    local = value.shape[1]
    out_ref[:, pl.ds(pl.multiple_of(block * local, local), local), :] = value


def assemble_kernel(members, row, col, rows_ref, *refs):
    far_refs, across_refs, out_ref = refs[: len(refs) // 2], refs[len(refs) // 2 : -1], refs[-1]
    col_count = len(far_refs) + 1
    distance = lax.rem(col[0] + col_count - row[0] // members, col_count)

    @pl.when(distance == 0)
    def _():
        out_ref[...] = rows_ref[...]

    for step, ref in enumerate(far_refs):

        @pl.when(distance == step + 1)
        def _(ref=ref):
            put_block(out_ref, col[0], ref[...])
            for shift, across_ref in enumerate(across_refs):
                put_block(out_ref, lax.rem(col[0] + 1 + shift, col_count), across_ref[...])


def weighted_fit_kernel(members, row, col, inv_ref, rot_hbm, coords_hbm, even_ref, odd_ref, *refs):
    others, (out_ref, rows_ref, rows_centre_ref) = refs[:-9], refs[-9:-6]
    strips_ref, wide_ref, weighted_ref, rot_ref, sems, small_sems = refs[-6:]
    strips, height, col_width = strips_ref.shape
    width = even_ref.shape[2]
    local = coords_hbm.shape[1]

    def fetch(strip):
        rows = pl.ds(pl.multiple_of(strip * height, height), height)
        return pltpu.make_async_copy(inv_ref.at[rows, :], strips_ref.at[strip], sems.at[strip])

    own_rows = rows_ref.at[:, pl.ds(pl.multiple_of(col[0] * local, local), local), :]
    small = [
        pltpu.make_async_copy(rot_hbm, rot_ref, small_sems.at[0]),
        pltpu.make_async_copy(coords_hbm, own_rows, small_sems.at[1]),
    ]
    for copy in small:
        copy.start()
    for strip in range(strips):
        fetch(strip).start()
    member = lax.rem(row[0], members)
    for mask in range(members):
        centre_ref = odd_ref if mask % 2 else even_ref
        start = pl.multiple_of((member ^ mask) * width, LANES)
        for comp in range(3):
            factor = jnp.broadcast_to(centre_ref[mask // 2, comp : comp + 1, :], (8, width))
            wide_ref[comp, :, pl.ds(start, width)] = factor
    for shift, ref in enumerate(others):
        put_block(rows_ref, lax.rem(col[0] + 1 + shift, len(others) + 1), ref[...])
    for copy in small:
        copy.wait()
    rows_centre_ref[...] = rotated_sum(rot_ref[...], rows_ref[...]) * (1.0 / rows_ref.shape[1])
    lane = lax.broadcasted_iota(jnp.int32, (height, LANES), 1)
    chunks = col_width // LANES

    def strip_body(strip, carry):
        fetch(strip).wait()

        def body(chunk, sums):
            span = pl.ds(pl.multiple_of(chunk * LANES, LANES), LANES)
            value = strips_ref[strip, :, span].reshape(height // 8, 8, LANES)
            return tuple(sums[comp] + value * wide_ref[comp, :, span][None] for comp in range(3))

        sums = (jnp.zeros((height // 8, 8, LANES), F32),) * 3
        sums = lax.fori_loop(0, chunks, body, sums, unroll=12 if chunks % 12 == 0 else 1)
        packed = jnp.zeros((height, LANES), F32)
        for comp in range(3):
            total = jnp.sum(sums[comp].reshape(height, LANES), axis=1, keepdims=True)
            packed = jnp.where(lane == comp, total, packed)
        weighted_ref[pl.ds(pl.multiple_of(strip * height, height), height), :] = packed
        return carry

    lax.fori_loop(0, strips, strip_body, 0)
    frame_total = rows_ref.shape[1]
    rows = rows_ref[...].reshape(3 * frame_total, width)
    high, mid, low = (jnp.dot(rows, piece, preferred_element_type=F32) for piece in three_pieces(weighted_ref[...]))
    fits = ((low + mid) + high).T
    entries = [
        fits[comp : comp + 1, part * frame_total : (part + 1) * frame_total] for part in range(3) for comp in range(3)
    ]
    spare = out_ref.shape[2] - 9 * frame_total
    if spare:
        entries.append(jnp.zeros((1, spare), F32))
    message = jnp.concatenate(entries, axis=1)
    out_ref[...] = jnp.broadcast_to(message[None], out_ref.shape)


def orthogonalized(message, frame_total):
    fitted = [message[:, entry * frame_total : (entry + 1) * frame_total] for entry in range(9)]
    norm = functools.reduce(lambda a, b: a + b, [value * value for value in fitted])
    scaling = jnp.sqrt(1.0 + norm)
    current = [[fitted[3 * col + row] / scaling for col in range(3)] for row in range(3)]
    for _ in range(POLAR):
        square = [[None] * 3 for _ in range(3)]
        for a in range(3):
            for b in range(a, 3):
                x, y = current[a], current[b]
                square[a][b] = square[b][a] = x[0] * y[0] + x[1] * y[1] + x[2] * y[2]
        cubed = [
            [square[a][0] * current[0][b] + square[a][1] * current[1][b] + square[a][2] * current[2][b] for b in range(3)]
            for a in range(3)
        ]
        current = [[1.5 * current[a][b] - 0.5 * cubed[a][b] for b in range(3)] for a in range(3)]
    return current


def put_deviations(wide_ref, coords_ref, centre, chunk, dev_ref):
    frame_total = coords_ref.shape[1]
    span = slice(chunk * LANES, (chunk + 1) * LANES)
    coords = [coords_ref[part, :, span].astype(F32) for part in range(3)]
    for comp in range(3):
        moved = wide_ref[3 * comp] * coords[0]
        moved = moved + wide_ref[3 * comp + 1] * coords[1]
        moved = moved + wide_ref[3 * comp + 2] * coords[2]
        value = moved - centre[comp : comp + 1, span]
        dev_ref[comp * frame_total : (comp + 1) * frame_total, span] = value.astype(BF16)


def put_tile(wide_ref, coords_ref, centre, rows_dev_ref, dev_ref, out_ref):
    width = coords_ref.shape[2]
    scale = 1.0 / (3 * coords_ref.shape[1])
    stride = 2 * LANES if width % (2 * LANES) == 0 else LANES
    for start in range(0, width, stride):
        for chunk in range(start // LANES, (start + stride) // LANES):
            put_deviations(wide_ref, coords_ref, centre, chunk, dev_ref)
        product = jnp.dot(rows_dev_ref[...], dev_ref[:, start : start + stride], preferred_element_type=F32)
        out_ref[:, start : start + stride] = product * scale


def put_tiles(masks, wide_ref, even_ref, odd_ref, panel_refs, rows_dev_ref, dev_ref, out_ref):
    for step, mask in enumerate(masks):

        @pl.when(pl.program_id(0) == step)
        def _(step=step, mask=mask):
            centre = (odd_ref if mask % 2 else even_ref)[mask // 2]
            put_tile(wide_ref, panel_refs[step], centre, rows_dev_ref, dev_ref, out_ref)


def first_tiles_kernel(masks, row, col, fits_ref, rows_ref, rows_centre_ref, even_ref, odd_ref, *refs):
    panel_refs = refs[: len(masks)]
    out_ref, rot_out_ref, wide_ref, rows_dev_ref, dev_ref = refs[len(masks) :]
    frame_total = rows_ref.shape[1]
    local = rot_out_ref.shape[2]

    @pl.when(pl.program_id(0) == 0)
    def _():
        current = orthogonalized(jnp.sum(fits_ref[...], axis=0), frame_total)
        for a in range(3):
            flat = jnp.concatenate(current[a], axis=0)
            kept = flat[:, :local]
            for block in range(1, frame_total // local):
                kept = jnp.where(col[0] == block, flat[:, block * local : (block + 1) * local], kept)
            rot_out_ref[a] = kept
        entries = [current[a][b] for a in range(3) for b in range(3)]
        columns = jnp.concatenate(entries + [jnp.zeros((7, frame_total), F32)], axis=0).T
        for entry in range(9):
            wide_ref[entry] = jnp.broadcast_to(columns[:, entry : entry + 1], (frame_total, LANES))
        centre = rows_centre_ref[...]
        for chunk in range(rows_ref.shape[2] // LANES):
            put_deviations(wide_ref, rows_ref, centre, chunk, dev_ref)
        rows_dev_ref[...] = dev_ref[...].T

    put_tiles(masks, wide_ref, even_ref, odd_ref, panel_refs, rows_dev_ref, dev_ref, out_ref)


def more_tiles_kernel(masks, row, before_ref, wide_ref, rows_dev_ref, even_ref, odd_ref, *refs):
    panel_refs, (out_ref, dev_ref) = refs[: len(masks)], refs[len(masks) :]
    put_tiles(masks, wide_ref, even_ref, odd_ref, panel_refs, rows_dev_ref, dev_ref, out_ref)


def per_device(frames, rotations, inverse_cov):
    row_count, col_count = lax.axis_size("row"), lax.axis_size("col")
    members = row_count // col_count
    row = lax.axis_index("row").astype(jnp.int32).reshape(1)
    col = lax.axis_index("col").astype(jnp.int32).reshape(1)
    local, _, width = frames.shape
    frame_total = local * col_count
    device_total = row_count * col_count
    col_width = inverse_cov.shape[1]
    half = members // 2
    coords = jnp.transpose(frames, (1, 0, 2))

    def limit(mib):
        return pltpu.CompilerParams(vmem_limit_bytes=mib * MIB)

    def move(value, source_of, receives=lambda group, col: True):
        pairs = []
        for group in range(col_count):
            for member in range(members):
                for place in range(col_count):
                    if receives(group, place):
                        from_group, from_member, from_col = source_of(group, member, place)
                        source = (from_group * members + from_member) * col_count + from_col
                        pairs.append((source, (group * members + member) * col_count + place))
        return lax.ppermute(value, ("row", "col"), pairs)

    def from_panel_row(value, step):
        return move(value, lambda g, m, c: (c, m, (g + step) % col_count))

    def from_member(value, mask):
        return move(value, lambda g, m, c: (g, m ^ mask, c))

    def limit(mib):
        return pltpu.CompilerParams(vmem_limit_bytes=mib * MIB)

    def after(first, value):
        return lax.optimization_barrier((first, value))[1]

    def small_kernel(kernel, shape, name, *values):
        return pl.pallas_call(
            kernel,
            out_shape=jax.ShapeDtypeStruct(shape, F32),
            in_specs=[vmem()] * len(values),
            out_specs=vmem(),
            compiler_params=limit(4),
            name=name,
        )(*values)

    partial = pl.pallas_call(
        functools.partial(partial_centre_kernel, frame_total),
        out_shape=jax.ShapeDtypeStruct((3, width), F32),
        in_specs=[smem(), hbm(), hbm()],
        out_specs=vmem(),
        scratch_shapes=[
            pltpu.VMEM(rotations.shape, F32),
            pltpu.VMEM(coords.shape, BF16),
            pltpu.SemaphoreType.DMA((2,)),
        ],
        compiler_params=limit(8),
        name="partial_centre",
    )(col, rotations, coords)
    parts = [from_panel_row(partial, step) for step in range(col_count)]

    late_coords = after(partial, coords)
    others = [move(late_coords, lambda g, m, c, s=step: (g, m, (c + s) % col_count)) for step in range(1, col_count)]
    far = [
        move(late_coords, lambda g, m, c, s=step: ((g + s) % col_count, m, c)) for step in range(1, col_count)
    ]

    own_centre = small_kernel(sum_kernel, (3, width), "add_centre", *parts)
    centres = [own_centre] + [from_member(own_centre, 2 * step) for step in range(1, half)]
    centres, others = lax.optimization_barrier((centres, others))
    even_centres = small_kernel(stack_kernel, (half, 3, width), "stack_centres", *centres)
    odd_centres = from_member(even_centres, 1)

    far = after(odd_centres, far)
    distance = lax.rem(col[0] + col_count - row[0] // members, col_count)
    across = []
    for step in range(1, col_count):
        held = far[0]
        if col_count > 2:
            held = lax.select_n(lax.rem(distance + col_count - step, col_count), late_coords, *far)
        across.append(move(held, lambda g, m, c, s=step: (g, m, (c + s) % col_count), lambda g, c: g != c))

    height = 64 if width % 64 == 0 else 8
    message_width = -(-9 * frame_total // LANES) * LANES
    message, rows_all, rows_centre = pl.pallas_call(
        functools.partial(weighted_fit_kernel, members),
        in_specs=[smem(), smem()] + [hbm()] * 3 + [vmem()] * (1 + col_count),
        out_specs=(vmem(), vmem(), vmem()),
        scratch_shapes=[
            pltpu.VMEM((width // height, height, col_width), F32),
            pltpu.VMEM((3, 8, col_width), F32),
            pltpu.VMEM((width, LANES), F32),
            pltpu.VMEM(rotations.shape, F32),
            pltpu.SemaphoreType.DMA((width // height,)),
            pltpu.SemaphoreType.DMA((2,)),
        ],
        out_shape=(
            jax.ShapeDtypeStruct((device_total, 1, message_width), F32),
            jax.ShapeDtypeStruct((3, frame_total, width), BF16),
            jax.ShapeDtypeStruct((3, width), F32),
        ),
        compiler_params=limit(28),
        cost_estimate=pl.CostEstimate(
            flops=6 * width * col_width, bytes_accessed=4 * width * col_width, transcendentals=0
        ),
        name="weighted_fit",
    )(
        row,
        col,
        pltpu.with_memory_space_constraint(inverse_cov, pltpu.HBM),
        rotations,
        coords,
        even_centres,
        odd_centres,
        *others,
    )
    fits = lax.all_to_all(message, ("row", "col"), split_axis=0, concat_axis=0, tiled=True)

    own_block = pl.pallas_call(
        functools.partial(assemble_kernel, members),
        out_shape=jax.ShapeDtypeStruct((3, frame_total, width), BF16),
        in_specs=[smem(), smem()] + [vmem()] * (2 * col_count - 1),
        out_specs=vmem(),
        compiler_params=limit(4),
        name="assemble",
    )(row, col, rows_all, *far, *across)
    panel = [own_block, from_member(own_block, 1)]
    evens = [from_member(own_block, mask) for mask in range(2, members, 2)]

    def tile_spec(masks):
        def index(i, row, *_):
            mask = masks[-1]
            for step, value in enumerate(masks[:-1]):
                mask = jnp.where(i == step, value, mask)
            return (0, lax.rem(row[0], members) ^ mask)

        return pl.BlockSpec((width, width), index)

    def tiles_cost(masks):
        return pl.CostEstimate(
            flops=6 * frame_total * width * width * len(masks),
            bytes_accessed=4 * width * width * len(masks),
            transcendentals=0,
        )

    dev_scratch = pltpu.VMEM((3 * frame_total, width), BF16)
    masks = (0, 1)
    covariance, transforms, wide, rows_dev = pl.pallas_call(
        functools.partial(first_tiles_kernel, masks),
        grid_spec=pltpu.PrefetchScalarGridSpec(
            num_scalar_prefetch=2,
            grid=(len(masks),),
            in_specs=[vmem()] * (5 + len(masks)),
            out_specs=(tile_spec(masks), vmem(), vmem(), vmem()),
            scratch_shapes=[dev_scratch],
        ),
        out_shape=(
            jax.ShapeDtypeStruct((width, col_width), F32),
            jax.ShapeDtypeStruct((3, 3, local), F32),
            jax.ShapeDtypeStruct((9, frame_total, LANES), F32),
            jax.ShapeDtypeStruct((width, 3 * frame_total), BF16),
        ),
        compiler_params=limit(16),
        cost_estimate=tiles_cost(masks),
        name="steps_and_first_tiles",
    )(row, col, fits, rows_all, rows_centre, even_centres, odd_centres, *panel)

    def more_tiles(covariance, masks, blocks, name):
        return pl.pallas_call(
            functools.partial(more_tiles_kernel, masks),
            grid_spec=pltpu.PrefetchScalarGridSpec(
                num_scalar_prefetch=1,
                grid=(len(masks),),
                in_specs=[pl.BlockSpec(memory_space=pl.ANY)] + [vmem()] * (4 + len(masks)),
                out_specs=tile_spec(masks),
                scratch_shapes=[dev_scratch],
            ),
            out_shape=jax.ShapeDtypeStruct((width, col_width), F32),
            input_output_aliases={1: 0},
            compiler_params=limit(16),
            cost_estimate=tiles_cost(masks),
            name=name,
        )(row, covariance, wide, rows_dev, even_centres, odd_centres, *blocks)

    if members > 2:
        evens = after(wide, evens)
        odds = [from_member(block, 1) for block in evens]
        covariance = more_tiles(covariance, tuple(range(2, members, 2)), evens, "even_tiles")
        covariance = more_tiles(covariance, tuple(range(3, members, 2)), odds, "odd_tiles")
    return (covariance, transforms)


def solution(mesh):
    placed = (P("col", None, "row"), P(), P("row", "col"))
    return jax.shard_map(
        per_device,
        mesh=mesh,
        in_specs=placed,
        out_specs=(P("row", "col"), P(None, None, "col")),
        check_vma=False,
    )
```

time: 66.7 us -> 71.5 us (1.072)
  starting transfers between devices: 19.6 us -> 22.1 us
  Pallas kernels: 20.5 us -> 22.9 us
  waiting for transfers between devices: 8.22 us -> 7 us
    ppermute x10 -> x16, starting transfers between devices: 12.3 us -> 22.1 us  [move(): return lax.ppermute(value, ('row', 'col'), pairs)]
    all_to_all x1 -> x0, starting transfers between devices: 7.3 us -> none  [per_device(): lax.all_to_all(repeated, ('row', 'col'), split_axis=0, concat_axis=0, til...]
    all_to_all x1 -> x0, waiting for transfers between devices: 5.5 us -> none  [per_device(): lax.all_to_all(repeated, ('row', 'col'), split_axis=0, concat_axis=0, til...]
    ppermute x10 -> x16, waiting for transfers between devices: 2.72 us -> 7 us  [move(): return lax.ppermute(value, ('row', 'col'), pairs)]
    pallas_call x2 -> x5, Pallas kernels: 12 us -> 14.8 us  [the longest x2 7.94 us: more_tiles(): pl.pallas_call(functools.partial(more_tiles_kernel, masks), grid_spec=plt...]
    unnamed x6 -> x8, local copies, waits for them, and re-layouts: 2.51 us -> 3.19 us
  transfers between devices with their start and end apart: 11 -> 16, of which waited for: 2 -> 4; matrix products, arithmetic and copies ran while one was open for 0% -> 0% of each run, Pallas kernels for 22% -> 26%
where the time goes in v6:
time: 71.5 us; the launch traced here: 71.2 us
  Pallas kernels  22.9 us (32%)
  starting transfers between devices  22.1 us (31%)
  blocking collectives  15.3 us (21%)
  waiting for transfers between devices  7 us (10%)
  local copies, waits for them, and re-layouts  3.19 us (4%)
  between operations  0.76 us (1%)
    ppermute x16, starting transfers between devices, move(): return lax.ppermute(value, ('row', 'col'), pairs)  22.1 us
    all_to_all x1, blocking collectives, per_device(): lax.all_to_all(message, ('row', 'col'), split_axis=0, concat_axis=0, tile...  15.3 us
    pallas_call x2, Pallas kernels, more_tiles(): pl.pallas_call(functools.partial(more_tiles_kernel, masks), grid_spec=plt...  7.94 us
    pallas_call x1, Pallas kernels, per_device(): pl.pallas_call(functools.partial(weighted_fit_kernel, members), in_specs=...  7.57 us
    ppermute x16, waiting for transfers between devices, move(): return lax.ppermute(value, ('row', 'col'), pairs)  7 us
    pallas_call x1, Pallas kernels, per_device(): pl.pallas_call(functools.partial(first_tiles_kernel, masks), grid_spec=pl...  6.87 us
    unnamed x8, local copies, waits for them, and re-layouts  3.19 us
  transfers between devices with their start and end apart: 16, of which 4 were waited for; matrix products, arithmetic and copies ran while one was open for 0% of the time, Pallas kernels for 26%

profile of v6, /device:TPU:0, one launch (start us, length us, event | category | flops | bytes accessed | tf_op | source)
XLA Modules:
  0.0 71.2 jit_solution(13320951901618988384)
XLA Ops:
  0.6 0.0 copy-start
  0.6 0.9 %copy-done = bf16[32,3,768]{2,0,1:T(8,128)(2,1)S(1)} copy-done((bf16[32,3,768]{2,0,1:T(8,128)(2,1)S(1)}, bf16[32,3,768]{2,0,1:T(8,128)(2,1)}, u32[]{:S(2)}) %copy-start) | copy-done | bytes 147480
  1.5 0.0 copy-start.2
  1.5 0.7 copy-done.2
  2.2 0.4 partial_centre.1
  2.7 3.0 %collective-permute-start.5 = (bf16[3,32,768]{2,1,0:T(8,128)(2,1)S(1)}, bf16[3,32,768]{2,1,0:T(8,128)(2,1)S(1)}, u32[]{:S(2)}, u32[]{:S(2)}) collective-permute-start(bf16[3,32,768]{2,1,0:T(8,128)(2,1)S(1)} %bitcast.4), channel_id=1, source_target_pairs={{1,0},{0,1},{3,2},{2,3},{5,4},{4,5},{7,6},{6,7},{9,8},{8,9},{11,10... | collective-permute-start | bytes 442376 | tf_op jit(solution)/shard_map/ppermute | solution.py:272
  5.7 2.6 %collective-permute-start.7 = (bf16[3,32,768]{2,1,0:T(8,128)(2,1)S(1)}, bf16[3,32,768]{2,1,0:T(8,128)(2,1)S(1)}, u32[]{:S(2)}, u32[]{:S(2)}) collective-permute-start(bf16[3,32,768]{2,1,0:T(8,128)(2,1)S(1)} %bitcast.5), channel_id=1, source_target_pairs={{16,0},{17,1},{18,2},{19,3},{20,4},{21,5},{22,6},{23,7},{24,8},{25... | collective-permute-start | bytes 442376 | tf_op jit(solution)/shard_map/ppermute | solution.py:272
  8.3 0.3 collective-permute-start.1
  8.6 0.7 collective-permute-start
  9.3 2.7 %collective-permute-done.1.refs_1_ = f32[3,768]{1,0:T(4,128)S(1)} collective-permute-done((f32[3,768]{1,0:T(4,128)S(1)}, f32[3,768]{1,0:T(4,128)S(1)}, u32[]{:S(2)}, u32[]{:S(2)}) %collective-permute-start.1) | collective-permute-done | bytes 9248 | tf_op jit(solution)/shard_map/ppermute | solution.py:272
  12.0 0.0 collective-permute-done.refs_0_
  12.0 5.2 %collective-permute-start.4 = (f32[3,768]{1,0:T(4,128)S(1)}, f32[3,768]{1,0:T(4,128)S(1)}, u32[]{:S(2)}, u32[]{:S(2)}) collective-permute-start(f32[3,768]{1,0:T(4,128)S(1)} %add_centre.1.refs_0_), channel_id=1, source_target_pairs={{12,0},{13,1},{14,2},{15,3},{8,4},{9,5},{10,6},{11,7},{4,8},{5,9},... | collective-permute-start | bytes 27656 | tf_op jit(solution)/shard_map/ppermute | solution.py:272
  17.2 0.0 collective-permute-start.3
  17.2 0.6 collective-permute-start.2
  17.8 1.0 %collective-permute-done.4.refs_3_ = f32[3,768]{1,0:T(4,128)S(1)} collective-permute-done((f32[3,768]{1,0:T(4,128)S(1)}, f32[3,768]{1,0:T(4,128)S(1)}, u32[]{:S(2)}, u32[]{:S(2)}) %collective-permute-start.4) | collective-permute-done | bytes 9248 | tf_op jit(solution)/shard_map/ppermute | solution.py:272
  18.9 2.0 %collective-permute-done.3.refs_2_ = f32[3,768]{1,0:T(4,128)S(1)} collective-permute-done((f32[3,768]{1,0:T(4,128)S(1)}, f32[3,768]{1,0:T(4,128)S(1)}, u32[]{:S(2)}, u32[]{:S(2)}) %collective-permute-start.3) | collective-permute-done | bytes 9248 | tf_op jit(solution)/shard_map/ppermute | solution.py:272
  20.9 0.0 collective-permute-done.2.refs_1_
  20.9 0.0 collective-permute-done.5.refs_0_
  20.9 0.1 collective-permute-start.6
  21.0 0.0 collective-permute-done.7.refs_0_
  21.0 1.2 %collective-permute-done.6.odd_ref = f32[4,3,768]{2,1,0:T(4,128)S(1)} collective-permute-done((f32[4,3,768]{2,1,0:T(4,128)S(1)}, f32[4,3,768]{2,1,0:T(4,128)S(1)}, u32[]{:S(2)}, u32[]{:S(2)}) %collective-permute-start.6) | collective-permute-done | bytes 36896 | tf_op jit(solution)/shard_map/ppermute | solution.py:272
  22.2 5.3 %collective-permute-start.8 = (bf16[3,32,768]{2,1,0:T(8,128)(2,1)S(1)}, bf16[3,32,768]{2,1,0:T(8,128)(2,1)S(1)}, u32[]{:S(2)}, u32[]{:S(2)}) collective-permute-start(bf16[3,32,768]{2,1,0:T(8,128)(2,1)S(1)} %collective-permute-done.7.refs_0_), channel_id=1, source_target_pairs={{0,1},{2,3},{4,5},{6,7},{8,9},{10,11},{12,13},{14,15},{17,16},{19,... | collective-permute-start | bytes 442376 | tf_op jit(solution)/shard_map/ppermute | solution.py:272
  27.6 0.0 copy-start.1
  27.6 0.9 %copy-done.1 = bf16[32,3,768]{2,0,1:T(8,128)(2,1)S(1)} copy-done((bf16[32,3,768]{2,0,1:T(8,128)(2,1)S(1)}, bf16[32,3,768]{2,0,1:T(8,128)(2,1)}, u32[]{:S(2)}) %copy-start.1) | copy-done | bytes 147480
  28.5 0.0 copy-start.3
  28.5 0.7 copy-done.3
  29.2 7.6 %weighted_fit.1 = (f32[32,1,640]{2,1,0:T(1,128)S(1)}, bf16[3,64,768]{2,1,0:T(8,128)(2,1)S(1)}, f32[3,768]{1,0:T(4,128)S(1)}) custom-call(s32[1]{0:T(128)} %bitcast.row, s32[1]{0:T(128)} %bitcast.1.col, f32[768,6144]{1,0:T(8,128)} %inv_ref.1, f32[3,3,64]{2,1,0:T(4,128)S(1)} %copy-done.3, bf16[3,32,768]{2,1,0:T(8,128)(2,1)S(1)} %bitcast.6, ...), custom_call_target="tpu_custom_call" | custom-call | flops 28311552 | bytes 18874368 | tf_op jit(solution)/shard_map/weighted_fit/pallas_call | solution.py:334
  36.8 0.0 collective-permute-done.8.refs_1_
  36.8 0.1 collective-permute-start.9
  36.9 1.6 %collective-permute-start.12 = (bf16[3,64,768]{2,1,0:T(8,128)(2,1)S(1)}, bf16[3,64,768]{2,1,0:T(8,128)(2,1)S(1)}, u32[]{:S(2)}, u32[]{:S(2)}) collective-permute-start(bf16[3,64,768]{2,1,0:T(8,128)(2,1)S(1)} %assemble.1.refs_0_), channel_id=1, source_target_pairs={{12,0},{13,1},{14,2},{15,3},{8,4},{9,5},{10,6},{11,7},{4,8},{5,9},... | collective-permute-start | bytes 884744 | tf_op jit(solution)/shard_map/ppermute | solution.py:272
  38.5 0.4 collective-permute-start.11
  38.9 1.5 %collective-permute-start.10 = (bf16[3,64,768]{2,1,0:T(8,128)(2,1)S(1)}, bf16[3,64,768]{2,1,0:T(8,128)(2,1)S(1)}, u32[]{:S(2)}, u32[]{:S(2)}) collective-permute-start(bf16[3,64,768]{2,1,0:T(8,128)(2,1)S(1)} %assemble.1.refs_0_), channel_id=1, source_target_pairs={{4,0},{5,1},{6,2},{7,3},{0,4},{1,5},{2,6},{3,7},{12,8},{13,9},{14,... | collective-permute-start | bytes 884744 | tf_op jit(solution)/shard_map/ppermute | solution.py:272
  40.4 15.3 %all_to_all.5.fits_ref = f32[32,1,640]{2,1,0:T(1,128)S(1)} all-to-all(f32[32,1,640]{2,1,0:T(1,128)S(1)} %get-tuple-element.25), channel_id=1, replica_groups=mesh['row'=16,'col'=2] {'row','col'}, dimensions={0} | all-to-all | bytes 163840 | tf_op jit(solution)/shard_map/all_to_all | solution.py:366
  55.7 0.0 collective-permute-done.9.refs_1_
  55.7 6.9 %steps_and_first_tiles.1 = (f32[768,6144]{1,0:T(8,128)}, f32[3,3,32]{2,1,0:T(4,128)}, f32[9,64,128]{2,1,0:T(8,128)S(1)}, bf16[768,192]{1,0:T(8,128)(2,1)S(1)}) custom-call(s32[1]{0:T(128)} %bitcast.row, s32[1]{0:T(128)} %bitcast.1.col, f32[32,1,640]{2,1,0:T(1,128)S(1)} %all_to_all.5.fits_ref, bf16[3,64,768]{2,1,0:T(8,128)(2,1)S(1)} %get-tuple-element.26.rows_ref, ...), custom_call_target="tpu_custom_call" | custom-call | flops 452984832 | bytes 4718592 | tf_op jit(solution)/shard_map/steps_and_first_tiles/pallas_call | solution.py:397
  62.6 0.0 collective-permute-done.12.refs_2_
  62.6 0.0 collective-permute-done.11.refs_1_
  62.6 0.0 collective-permute-done.10.refs_0_
  62.6 0.1 collective-permute-start.13
  62.7 0.5 collective-permute-start.14
  63.2 0.1 collective-permute-start.15
  63.3 4.0 %even_tiles.1.before_ref = f32[768,6144]{1,0:T(8,128)} custom-call(s32[1]{0:T(128)} %bitcast.row, f32[768,6144]{1,0:T(8,128)} %get-tuple-element.29.before_ref, f32[9,64,128]{2,1,0:T(8,128)S(1)} %get-tuple-element.30.wide_ref, bf16[768,192]{1,0:T(8,128)(2,1)S(1)} %get-tuple-element.31.rows_dev_ref, ...), custom_call_target="tpu_custom_call", output_to_operand_aliasing={{}: (1, {})} | custom-call | flops 679477248 | bytes 7077888 | tf_op jit(solution)/shard_map/even_tiles/pallas_call | solution.py:418
  67.2 0.0 collective-permute-done.13.refs_0_
  67.2 0.0 collective-permute-done.14.refs_1_
  67.2 0.0 collective-permute-done.15.refs_2_
  67.2 4.0 %odd_tiles.1 = f32[768,6144]{1,0:T(8,128)} custom-call(s32[1]{0:T(128)} %bitcast.row, f32[768,6144]{1,0:T(8,128)} %even_tiles.1.before_ref, f32[9,64,128]{2,1,0:T(8,128)S(1)} %get-tuple-element.30.wide_ref, bf16[768,192]{1,0:T(8,128)(2,1)S(1)} %get-tuple-element.31.rows_dev_ref, ...), custom_call_target="tpu_custom_call", output_to_operand_aliasing={{}: (1, {})} | custom-call | flops 679477248 | bytes 7077888 | tf_op jit(solution)/shard_map/odd_tiles/pallas_call | solution.py:418
  (3 shorter events, 0.0 us)
Async XLA Ops:
  0.6 0.9 %copy-start = (bf16[32,3,768]{2,0,1:T(8,128)(2,1)S(1)}, bf16[32,3,768]{2,0,1:T(8,128)(2,1)}, u32[]{:S(2)}) copy-start(bf16[32,3,768]{2,0,1:T(8,128)(2,1)} %param.3) | copy-start | bytes 442372
  1.5 0.7 copy-start.2
  2.7 18.2 %collective-permute-start.5 = (bf16[3,32,768]{2,1,0:T(8,128)(2,1)S(1)}, bf16[3,32,768]{2,1,0:T(8,128)(2,1)S(1)}, u32[]{:S(2)}, u32[]{:S(2)}) collective-permute-start(bf16[3,32,768]{2,1,0:T(8,128)(2,1)S(1)} %bitcast.4), channel_id=1, source_target_pairs={{1,0},{0,1},{3,2},{2,3},{5,4},{4,5},{7,6},{6,7},{9,8},{8,9},{11,10... | collective-permute-start | bytes 442376 | tf_op jit(solution)/shard_map/ppermute | solution.py:272
  5.7 15.3 %collective-permute-start.7 = (bf16[3,32,768]{2,1,0:T(8,128)(2,1)S(1)}, bf16[3,32,768]{2,1,0:T(8,128)(2,1)S(1)}, u32[]{:S(2)}, u32[]{:S(2)}) collective-permute-start(bf16[3,32,768]{2,1,0:T(8,128)(2,1)S(1)} %bitcast.5), channel_id=1, source_target_pairs={{16,0},{17,1},{18,2},{19,3},{20,4},{21,5},{22,6},{23,7},{24,8},{25... | collective-permute-start | bytes 442376 | tf_op jit(solution)/shard_map/ppermute | solution.py:272
  8.3 3.7 %collective-permute-start.1 = (f32[3,768]{1,0:T(4,128)S(1)}, f32[3,768]{1,0:T(4,128)S(1)}, u32[]{:S(2)}, u32[]{:S(2)}) collective-permute-start(f32[3,768]{1,0:T(4,128)S(1)} %partial_centre.1), channel_id=1, source_target_pairs={{1,0},{17,1},{3,2},{19,3},{5,4},{21,5},{7,6},{23,7},{9,8},{25,9},{... | collective-permute-start | bytes 27656 | tf_op jit(solution)/shard_map/ppermute | solution.py:272
  8.6 3.4 %collective-permute-start = (f32[3,768]{1,0:T(4,128)S(1)}, f32[3,768]{1,0:T(4,128)S(1)}, u32[]{:S(2)}, u32[]{:S(2)}) collective-permute-start(f32[3,768]{1,0:T(4,128)S(1)} %partial_centre.1), channel_id=1, source_target_pairs={{0,0},{16,1},{2,2},{18,3},{4,4},{20,5},{6,6},{22,7},{8,8},{24,9},{... | collective-permute-start | bytes 27656 | tf_op jit(solution)/shard_map/ppermute | solution.py:272
  12.0 6.9 %collective-permute-start.4 = (f32[3,768]{1,0:T(4,128)S(1)}, f32[3,768]{1,0:T(4,128)S(1)}, u32[]{:S(2)}, u32[]{:S(2)}) collective-permute-start(f32[3,768]{1,0:T(4,128)S(1)} %add_centre.1.refs_0_), channel_id=1, source_target_pairs={{12,0},{13,1},{14,2},{15,3},{8,4},{9,5},{10,6},{11,7},{4,8},{5,9},... | collective-permute-start | bytes 27656 | tf_op jit(solution)/shard_map/ppermute | solution.py:272
  17.2 3.7 %collective-permute-start.3 = (f32[3,768]{1,0:T(4,128)S(1)}, f32[3,768]{1,0:T(4,128)S(1)}, u32[]{:S(2)}, u32[]{:S(2)}) collective-permute-start(f32[3,768]{1,0:T(4,128)S(1)} %add_centre.1.refs_0_), channel_id=1, source_target_pairs={{8,0},{9,1},{10,2},{11,3},{12,4},{13,5},{14,6},{15,7},{0,8},{1,9},... | collective-permute-start | bytes 27656 | tf_op jit(solution)/shard_map/ppermute | solution.py:272
  17.2 3.7 %collective-permute-start.2 = (f32[3,768]{1,0:T(4,128)S(1)}, f32[3,768]{1,0:T(4,128)S(1)}, u32[]{:S(2)}, u32[]{:S(2)}) collective-permute-start(f32[3,768]{1,0:T(4,128)S(1)} %add_centre.1.refs_0_), channel_id=1, source_target_pairs={{4,0},{5,1},{6,2},{7,3},{0,4},{1,5},{2,6},{3,7},{12,8},{13,9},{14,... | collective-permute-start | bytes 27656 | tf_op jit(solution)/shard_map/ppermute | solution.py:272
  20.9 1.3 %collective-permute-start.6 = (f32[4,3,768]{2,1,0:T(4,128)S(1)}, f32[4,3,768]{2,1,0:T(4,128)S(1)}, u32[]{:S(2)}, u32[]{:S(2)}) collective-permute-start(f32[4,3,768]{2,1,0:T(4,128)S(1)} %stack_centres.1.even_ref), channel_id=1, source_target_pairs={{2,0},{3,1},{0,2},{1,3},{6,4},{7,5},{4,6},{5,7},{10,8},{11,9},{8,1... | collective-permute-start | bytes 110600 | tf_op jit(solution)/shard_map/ppermute | solution.py:272
  22.2 14.5 %collective-permute-start.8 = (bf16[3,32,768]{2,1,0:T(8,128)(2,1)S(1)}, bf16[3,32,768]{2,1,0:T(8,128)(2,1)S(1)}, u32[]{:S(2)}, u32[]{:S(2)}) collective-permute-start(bf16[3,32,768]{2,1,0:T(8,128)(2,1)S(1)} %collective-permute-done.7.refs_0_), channel_id=1, source_target_pairs={{0,1},{2,3},{4,5},{6,7},{8,9},{10,11},{12,13},{14,15},{17,16},{19,... | collective-permute-start | bytes 442376 | tf_op jit(solution)/shard_map/ppermute | solution.py:272
  27.6 0.9 %copy-start.1 = (bf16[32,3,768]{2,0,1:T(8,128)(2,1)S(1)}, bf16[32,3,768]{2,0,1:T(8,128)(2,1)}, u32[]{:S(2)}) copy-start(bf16[32,3,768]{2,0,1:T(8,128)(2,1)} %param.3) | copy-start | bytes 442372
  28.5 0.7 copy-start.3
  36.8 18.9 %collective-permute-start.9 = (bf16[3,64,768]{2,1,0:T(8,128)(2,1)S(1)}, bf16[3,64,768]{2,1,0:T(8,128)(2,1)S(1)}, u32[]{:S(2)}, u32[]{:S(2)}) collective-permute-start(bf16[3,64,768]{2,1,0:T(8,128)(2,1)S(1)} %assemble.1.refs_0_), channel_id=1, source_target_pairs={{2,0},{3,1},{0,2},{1,3},{6,4},{7,5},{4,6},{5,7},{10,8},{11,9},{8,1... | collective-permute-start | bytes 884744 | tf_op jit(solution)/shard_map/ppermute | solution.py:272
  36.9 25.7 %collective-permute-start.12 = (bf16[3,64,768]{2,1,0:T(8,128)(2,1)S(1)}, bf16[3,64,768]{2,1,0:T(8,128)(2,1)S(1)}, u32[]{:S(2)}, u32[]{:S(2)}) collective-permute-start(bf16[3,64,768]{2,1,0:T(8,128)(2,1)S(1)} %assemble.1.refs_0_), channel_id=1, source_target_pairs={{12,0},{13,1},{14,2},{15,3},{8,4},{9,5},{10,6},{11,7},{4,8},{5,9},... | collective-permute-start | bytes 884744 | tf_op jit(solution)/shard_map/ppermute | solution.py:272
  38.5 24.1 %collective-permute-start.11 = (bf16[3,64,768]{2,1,0:T(8,128)(2,1)S(1)}, bf16[3,64,768]{2,1,0:T(8,128)(2,1)S(1)}, u32[]{:S(2)}, u32[]{:S(2)}) collective-permute-start(bf16[3,64,768]{2,1,0:T(8,128)(2,1)S(1)} %assemble.1.refs_0_), channel_id=1, source_target_pairs={{8,0},{9,1},{10,2},{11,3},{12,4},{13,5},{14,6},{15,7},{0,8},{1,9},... | collective-permute-start | bytes 884744 | tf_op jit(solution)/shard_map/ppermute | solution.py:272
  38.9 23.7 %collective-permute-start.10 = (bf16[3,64,768]{2,1,0:T(8,128)(2,1)S(1)}, bf16[3,64,768]{2,1,0:T(8,128)(2,1)S(1)}, u32[]{:S(2)}, u32[]{:S(2)}) collective-permute-start(bf16[3,64,768]{2,1,0:T(8,128)(2,1)S(1)} %assemble.1.refs_0_), channel_id=1, source_target_pairs={{4,0},{5,1},{6,2},{7,3},{0,4},{1,5},{2,6},{3,7},{12,8},{13,9},{14,... | collective-permute-start | bytes 884744 | tf_op jit(solution)/shard_map/ppermute | solution.py:272
  62.6 4.6 %collective-permute-start.13 = (bf16[3,64,768]{2,1,0:T(8,128)(2,1)S(1)}, bf16[3,64,768]{2,1,0:T(8,128)(2,1)S(1)}, u32[]{:S(2)}, u32[]{:S(2)}) collective-permute-start(bf16[3,64,768]{2,1,0:T(8,128)(2,1)S(1)} %collective-permute-done.10.refs_0_), channel_id=1, source_target_pairs={{2,0},{3,1},{0,2},{1,3},{6,4},{7,5},{4,6},{5,7},{10,8},{11,9},{8,1... | collective-permute-start | bytes 884744 | tf_op jit(solution)/shard_map/ppermute | solution.py:272
  62.7 4.5 %collective-permute-start.14 = (bf16[3,64,768]{2,1,0:T(8,128)(2,1)S(1)}, bf16[3,64,768]{2,1,0:T(8,128)(2,1)S(1)}, u32[]{:S(2)}, u32[]{:S(2)}) collective-permute-start(bf16[3,64,768]{2,1,0:T(8,128)(2,1)S(1)} %collective-permute-done.11.refs_1_), channel_id=1, source_target_pairs={{2,0},{3,1},{0,2},{1,3},{6,4},{7,5},{4,6},{5,7},{10,8},{11,9},{8,1... | collective-permute-start | bytes 884744 | tf_op jit(solution)/shard_map/ppermute | solution.py:272
  63.2 4.0 %collective-permute-start.15 = (bf16[3,64,768]{2,1,0:T(8,128)(2,1)S(1)}, bf16[3,64,768]{2,1,0:T(8,128)(2,1)S(1)}, u32[]{:S(2)}, u32[]{:S(2)}) collective-permute-start(bf16[3,64,768]{2,1,0:T(8,128)(2,1)S(1)} %collective-permute-done.12.refs_2_), channel_id=1, source_target_pairs={{2,0},{3,1},{0,2},{1,3},{6,4},{7,5},{4,6},{5,7},{10,8},{11,9},{8,1... | collective-permute-start | bytes 884744 | tf_op jit(solution)/shard_map/ppermute | solution.py:272

commit v7 on v5

v7 whole, which is shorter than its diff:
```python
import functools

import jax
import jax.numpy as jnp
from jax import lax
from jax.experimental import pallas as pl
from jax.experimental.pallas import tpu as pltpu
from jax.sharding import PartitionSpec as P

POLAR = 12
LANES = 128
F32 = jnp.float32
BF16 = jnp.bfloat16
MIB = 1 << 20


def vmem():
    return pl.BlockSpec(memory_space=pltpu.VMEM)


def hbm():
    return pl.BlockSpec(memory_space=pl.ANY)


def smem():
    return pl.BlockSpec(memory_space=pltpu.SMEM)


def three_pieces(value):
    high = value.astype(BF16)
    rest = value - high.astype(F32)
    mid = rest.astype(BF16)
    low = (rest - mid.astype(F32)).astype(BF16)
    return high, mid, low


def rotated_sum(rot, coords):
    depth = coords.shape[0] * coords.shape[1]
    flat = jnp.concatenate([rot[:, part, :] for part in range(3)], axis=1)
    padded = jnp.concatenate([flat, jnp.zeros((5, depth), F32)], axis=0)
    stacked = jnp.concatenate(three_pieces(padded), axis=0)
    product = jnp.dot(stacked, coords.reshape(depth, coords.shape[2]), preferred_element_type=F32)
    return (product[16:19] + product[8:11]) + product[0:3]


def stack_kernel(*refs):
    for index, ref in enumerate(refs[:-1]):
        refs[-1][index] = ref[...]


def put_block(out_ref, block, value):
    local = value.shape[1]
    out_ref[:, pl.ds(pl.multiple_of(block * local, local), local), :] = value


def rows_kernel(col, rot_hbm, coords_hbm, *refs):
    others, (rows_ref, centre_ref, rot_ref, sems) = refs[:-4], refs[-4:]
    local = coords_hbm.shape[1]
    own_rows = rows_ref.at[:, pl.ds(pl.multiple_of(col[0] * local, local), local), :]
    copies = [
        pltpu.make_async_copy(rot_hbm, rot_ref, sems.at[0]),
        pltpu.make_async_copy(coords_hbm, own_rows, sems.at[1]),
    ]
    for copy in copies:
        copy.start()
    for shift, ref in enumerate(others):
        put_block(rows_ref, lax.rem(col[0] + 1 + shift, len(others) + 1), ref[...])
    for copy in copies:
        copy.wait()
    centre_ref[...] = rotated_sum(rot_ref[...], rows_ref[...]) * (1.0 / rows_ref.shape[1])


def assemble_kernel(members, row, col, rot_ref, rows_ref, *refs):
    sources, (out_ref, centre_ref) = refs[:-2], refs[-2:]
    far_refs, across_refs = sources[: len(sources) // 2], sources[len(sources) // 2 :]
    col_count = len(far_refs) + 1
    distance = lax.rem(col[0] + col_count - row[0] // members, col_count)

    @pl.when(distance == 0)
    def _():
        out_ref[...] = rows_ref[...]

    for step, ref in enumerate(far_refs):

        @pl.when(distance == step + 1)
        def _(ref=ref):
            put_block(out_ref, col[0], ref[...])
            for shift, across_ref in enumerate(across_refs):
                put_block(out_ref, lax.rem(col[0] + 1 + shift, col_count), across_ref[...])

    centre_ref[...] = rotated_sum(rot_ref[...], out_ref[...]) * (1.0 / out_ref.shape[1])


def weighted_fit_kernel(members, row, inv_ref, even_ref, odd_ref, rows_ref, out_ref, strips_ref, wide_ref, weighted_ref, sems):
    strips, height, col_width = strips_ref.shape
    width = even_ref.shape[2]

    def fetch(strip):
        rows = pl.ds(pl.multiple_of(strip * height, height), height)
        return pltpu.make_async_copy(inv_ref.at[rows, :], strips_ref.at[strip], sems.at[strip])

    for strip in range(strips):
        fetch(strip).start()
    member = lax.rem(row[0], members)
    for mask in range(members):
        centre_ref = odd_ref if mask % 2 else even_ref
        start = pl.multiple_of((member ^ mask) * width, LANES)
        for comp in range(3):
            factor = jnp.broadcast_to(centre_ref[mask // 2, comp : comp + 1, :], (8, width))
            wide_ref[comp, :, pl.ds(start, width)] = factor
    lane = lax.broadcasted_iota(jnp.int32, (height, LANES), 1)
    chunks = col_width // LANES

    def strip_body(strip, carry):
        fetch(strip).wait()

        def body(chunk, sums):
            span = pl.ds(pl.multiple_of(chunk * LANES, LANES), LANES)
            value = strips_ref[strip, :, span].reshape(height // 8, 8, LANES)
            return tuple(sums[comp] + value * wide_ref[comp, :, span][None] for comp in range(3))

        sums = (jnp.zeros((height // 8, 8, LANES), F32),) * 3
        sums = lax.fori_loop(0, chunks, body, sums, unroll=12 if chunks % 12 == 0 else 1)
        packed = jnp.zeros((height, LANES), F32)
        for comp in range(3):
            total = jnp.sum(sums[comp].reshape(height, LANES), axis=1, keepdims=True)
            packed = jnp.where(lane == comp, total, packed)
        weighted_ref[pl.ds(pl.multiple_of(strip * height, height), height), :] = packed
        return carry

    lax.fori_loop(0, strips, strip_body, 0)
    frame_total = rows_ref.shape[1]
    rows = rows_ref[...].reshape(3 * frame_total, width)
    high, mid, low = (jnp.dot(rows, piece, preferred_element_type=F32) for piece in three_pieces(weighted_ref[...]))
    fits = ((low + mid) + high).T
    entries = [
        fits[comp : comp + 1, part * frame_total : (part + 1) * frame_total] for part in range(3) for comp in range(3)
    ]
    first = jnp.concatenate(entries[:8], axis=0)
    last = jnp.concatenate([entries[8], jnp.zeros((7, frame_total), F32)], axis=0)
    message = jnp.concatenate([first, last], axis=1)
    out_ref[...] = jnp.broadcast_to(message[None], out_ref.shape)


def orthogonalized(message, frame_total):
    fitted = [message[entry : entry + 1, :frame_total] for entry in range(8)]
    fitted.append(message[0:1, frame_total:])
    norm = functools.reduce(lambda a, b: a + b, [value * value for value in fitted])
    scaling = jnp.sqrt(1.0 + norm)
    current = [[fitted[3 * col + row] / scaling for col in range(3)] for row in range(3)]
    for _ in range(POLAR):
        square = [[None] * 3 for _ in range(3)]
        for a in range(3):
            for b in range(a, 3):
                x, y = current[a], current[b]
                square[a][b] = square[b][a] = x[0] * y[0] + x[1] * y[1] + x[2] * y[2]
        cubed = [
            [square[a][0] * current[0][b] + square[a][1] * current[1][b] + square[a][2] * current[2][b] for b in range(3)]
            for a in range(3)
        ]
        current = [[1.5 * current[a][b] - 0.5 * cubed[a][b] for b in range(3)] for a in range(3)]
    return current


def put_deviations(wide_ref, coords_ref, centre, source, dev_ref, target):
    frame_total = coords_ref.shape[1]
    span = slice(source, source + LANES)
    coords = [coords_ref[part, :, span].astype(F32) for part in range(3)]
    for comp in range(3):
        moved = wide_ref[3 * comp] * coords[0]
        moved = moved + wide_ref[3 * comp + 1] * coords[1]
        moved = moved + wide_ref[3 * comp + 2] * coords[2]
        value = moved - centre[comp : comp + 1, span]
        dev_ref[comp * frame_total : (comp + 1) * frame_total, target : target + LANES] = value.astype(BF16)


def put_tile(wide_ref, coords_ref, centre, first, rows_dev_ref, dev_ref, out_ref):
    width = out_ref.shape[1]
    scale = 1.0 / (3 * coords_ref.shape[1])
    for start in range(0, width, LANES):
        put_deviations(wide_ref, coords_ref, centre, first + start, dev_ref, start)
    product = jnp.dot(rows_dev_ref[...], dev_ref[:, :width], preferred_element_type=F32)
    out_ref[...] = product * scale


def put_tiles(wide_ref, centre_ref, panel_refs, rows_dev_ref, dev_ref, out_ref):
    width, pieces = out_ref.shape[1], centre_ref.shape[2] // out_ref.shape[1]
    for step in range(len(panel_refs) * pieces):

        @pl.when(pl.program_id(0) == step)
        def _(block=step // pieces, first=step % pieces * width):
            put_tile(wide_ref, panel_refs[block], centre_ref[block], first, rows_dev_ref, dev_ref, out_ref)


def first_tiles_kernel(half, row, col, fits_ref, rows_ref, rows_centre_ref, centre_ref, *refs):
    panel_refs = refs[:half]
    out_ref, rot_out_ref, wide_ref, rows_dev_ref, dev_ref = refs[half:]
    frame_total = rows_ref.shape[1]
    local = rot_out_ref.shape[2]

    @pl.when(pl.program_id(0) == 0)
    def _():
        current = orthogonalized(jnp.sum(fits_ref[...], axis=0), frame_total)
        for a in range(3):
            flat = jnp.concatenate(current[a], axis=0)
            kept = flat[:, :local]
            for block in range(1, frame_total // local):
                kept = jnp.where(col[0] == block, flat[:, block * local : (block + 1) * local], kept)
            rot_out_ref[a] = kept
        entries = [current[a][b] for a in range(3) for b in range(3)]
        columns = jnp.concatenate(entries + [jnp.zeros((7, frame_total), F32)], axis=0).T
        for entry in range(9):
            wide_ref[entry] = jnp.broadcast_to(columns[:, entry : entry + 1], (frame_total, LANES))
        centre = rows_centre_ref[...]
        for chunk in range(rows_ref.shape[2] // LANES):
            put_deviations(wide_ref, rows_ref, centre, chunk * LANES, dev_ref, chunk * LANES)
        rows_dev_ref[...] = dev_ref[...].T

    put_tiles(wide_ref, centre_ref, panel_refs, rows_dev_ref, dev_ref, out_ref)


def more_tiles_kernel(half, row, before_ref, wide_ref, rows_dev_ref, centre_ref, *refs):
    panel_refs, (out_ref, dev_ref) = refs[:half], refs[half:]
    put_tiles(wide_ref, centre_ref, panel_refs, rows_dev_ref, dev_ref, out_ref)


def per_device(frames, rotations, inverse_cov):
    row_count, col_count = lax.axis_size("row"), lax.axis_size("col")
    members = row_count // col_count
    row = lax.axis_index("row").astype(jnp.int32).reshape(1)
    col = lax.axis_index("col").astype(jnp.int32).reshape(1)
    local, _, width = frames.shape
    frame_total = local * col_count
    device_total = row_count * col_count
    col_width = inverse_cov.shape[1]
    half = members // 2
    coords = jnp.transpose(frames, (1, 0, 2))

    def limit(mib):
        return pltpu.CompilerParams(vmem_limit_bytes=mib * MIB)

    def move(value, source_of, receives=lambda group, col: True):
        pairs = []
        for group in range(col_count):
            for member in range(members):
                for place in range(col_count):
                    if receives(group, place):
                        from_group, from_member, from_col = source_of(group, member, place)
                        source = (from_group * members + from_member) * col_count + from_col
                        pairs.append((source, (group * members + member) * col_count + place))
        return lax.ppermute(value, ("row", "col"), pairs)

    def from_panel_row(value, step):
        return move(value, lambda g, m, c: (c, m, (g + step) % col_count))

    def from_member(value, mask):
        return move(value, lambda g, m, c: (g, m ^ mask, c))

    def limit(mib):
        return pltpu.CompilerParams(vmem_limit_bytes=mib * MIB)

    def after(first, value):
        return lax.optimization_barrier((first, value))[1]

    def small_kernel(kernel, shape, name, *values):
        return pl.pallas_call(
            kernel,
            out_shape=jax.ShapeDtypeStruct(shape, F32),
            in_specs=[vmem()] * len(values),
            out_specs=vmem(),
            compiler_params=limit(4),
            name=name,
        )(*values)

    def in_hbm(value):
        return pltpu.with_memory_space_constraint(value, pltpu.HBM)

    far = [move(coords, lambda g, m, c, s=step: ((g + s) % col_count, m, c)) for step in range(1, col_count)]
    others = [move(coords, lambda g, m, c, s=step: (g, m, (c + s) % col_count)) for step in range(1, col_count)]
    rows_all, rows_centre, rot = pl.pallas_call(
        rows_kernel,
        out_shape=(
            jax.ShapeDtypeStruct((3, frame_total, width), BF16),
            jax.ShapeDtypeStruct((3, width), F32),
            jax.ShapeDtypeStruct(rotations.shape, F32),
        ),
        in_specs=[smem(), hbm(), hbm()] + [vmem()] * (col_count - 1),
        out_specs=(vmem(), vmem(), vmem()),
        scratch_shapes=[pltpu.SemaphoreType.DMA((2,))],
        compiler_params=limit(8),
        name="rows",
    )(col, in_hbm(rotations), in_hbm(coords), *others)

    distance = lax.rem(col[0] + col_count - row[0] // members, col_count)
    across = []
    for step in range(1, col_count):
        held = far[0]
        if col_count > 2:
            held = lax.select_n(lax.rem(distance + col_count - step, col_count), coords, *far)
        across.append(move(held, lambda g, m, c, s=step: (g, m, (c + s) % col_count), lambda g, c: g != c))
    own_block, own_centre = pl.pallas_call(
        functools.partial(assemble_kernel, members),
        out_shape=(
            jax.ShapeDtypeStruct((3, frame_total, width), BF16),
            jax.ShapeDtypeStruct((3, width), F32),
        ),
        in_specs=[smem(), smem()] + [vmem()] * (2 * col_count),
        out_specs=(vmem(), vmem()),
        compiler_params=limit(8),
        name="assemble",
    )(row, col, rot, rows_all, *far, *across)

    centres = [own_centre] + [from_member(own_centre, 2 * step) for step in range(1, half)]
    evens = [own_block] + [from_member(own_block, 2 * step) for step in range(1, half)]
    even_centres = small_kernel(stack_kernel, (half, 3, width), "stack_centres", *centres)
    odd_centres = from_member(even_centres, 1)

    height = 64 if width % 64 == 0 else 8
    message = pl.pallas_call(
        functools.partial(weighted_fit_kernel, members),
        in_specs=[smem(), hbm()] + [vmem()] * 3,
        out_specs=vmem(),
        scratch_shapes=[
            pltpu.VMEM((width // height, height, col_width), F32),
            pltpu.VMEM((3, 8, col_width), F32),
            pltpu.VMEM((width, LANES), F32),
            pltpu.SemaphoreType.DMA((width // height,)),
        ],
        out_shape=jax.ShapeDtypeStruct((device_total, 8, 2 * frame_total), F32),
        compiler_params=limit(28),
        cost_estimate=pl.CostEstimate(
            flops=6 * width * col_width, bytes_accessed=4 * width * col_width, transcendentals=0
        ),
        name="weighted_fit",
    )(row, in_hbm(inverse_cov), even_centres, odd_centres, rows_all)
    fits = lax.all_to_all(message, ("row", "col"), split_axis=0, concat_axis=0, tiled=True)
    evens = after(fits, evens)
    odds = [from_member(block, 1) for block in evens]

    pieces = 2 if width % (2 * LANES) == 0 else 1

    def tile_spec(odd):
        def index(i, row, *_):
            return (0, (lax.rem(row[0], members) ^ (2 * (i // pieces) + odd)) * pieces + lax.rem(i, pieces))

        return pl.BlockSpec((width, width // pieces), index)

    tiles_cost = pl.CostEstimate(
        flops=3 * frame_total * width * col_width, bytes_accessed=2 * width * col_width, transcendentals=0
    )
    dev_scratch = pltpu.VMEM((3 * frame_total, width), BF16)
    covariance, transforms, wide, rows_dev = pl.pallas_call(
        functools.partial(first_tiles_kernel, half),
        grid_spec=pltpu.PrefetchScalarGridSpec(
            num_scalar_prefetch=2,
            grid=(half * pieces,),
            in_specs=[vmem()] * (4 + half),
            out_specs=(tile_spec(0), vmem(), vmem(), vmem()),
            scratch_shapes=[dev_scratch],
        ),
        out_shape=(
            jax.ShapeDtypeStruct((width, col_width), F32),
            jax.ShapeDtypeStruct((3, 3, local), F32),
            jax.ShapeDtypeStruct((9, frame_total, LANES), F32),
            jax.ShapeDtypeStruct((width, 3 * frame_total), BF16),
        ),
        compiler_params=limit(16),
        cost_estimate=tiles_cost,
        name="steps_and_even_tiles",
    )(row, col, fits, rows_all, rows_centre, even_centres, *evens)
    covariance = pl.pallas_call(
        functools.partial(more_tiles_kernel, half),
        grid_spec=pltpu.PrefetchScalarGridSpec(
            num_scalar_prefetch=1,
            grid=(half * pieces,),
            in_specs=[hbm()] + [vmem()] * (3 + half),
            out_specs=tile_spec(1),
            scratch_shapes=[dev_scratch],
        ),
        out_shape=jax.ShapeDtypeStruct((width, col_width), F32),
        input_output_aliases={1: 0},
        compiler_params=limit(16),
        cost_estimate=tiles_cost,
        name="odd_tiles",
    )(row, covariance, wide, rows_dev, odd_centres, *odds)
    return (covariance, transforms)


def solution(mesh):
    placed = (P("col", None, "row"), P(), P("row", "col"))
    return jax.shard_map(
        per_device,
        mesh=mesh,
        in_specs=placed,
        out_specs=(P("row", "col"), P(None, None, "col")),
        check_vma=False,
    )
```

time: 66.7 us -> 68.8 us (1.031)
  blocking collectives: 14.8 us -> 0 us
  waiting for transfers between devices: 8.22 us -> 19.2 us
  Pallas kernels: 20.5 us -> 24.9 us
  starting transfers between devices: 19.6 us -> 23.7 us
  local copies, waits for them, and re-layouts: 2.51 us -> 0 us
    all_to_all x1 -> x0, blocking collectives: 14.8 us -> none  [per_device(): lax.all_to_all(message, ('row', 'col'), split_axis=0, concat_axis=0, tile...]
    ppermute x10 -> x14, waiting for transfers between devices: 2.72 us -> 10.7 us  [move(): return lax.ppermute(value, ('row', 'col'), pairs)]
    ppermute x10 -> x14, starting transfers between devices: 12.3 us -> 17.1 us  [move(): return lax.ppermute(value, ('row', 'col'), pairs)]
    all_to_all x1, waiting for transfers between devices: 5.5 us -> 8.59 us  [per_device(): lax.all_to_all(message, ('row', 'col'), split_axis=0, concat_axis=0, tile...]
    unnamed x6 -> x0, local copies, waits for them, and re-layouts: 2.51 us -> none
    pallas_call x3 -> x4, Pallas kernels: 5.79 us -> 7.94 us  [the longest x1 6.53 us: per_device(): pl.pallas_call(functools.partial(more_tiles_kernel, half), grid_spec=pltp...]
    pallas_call x1, Pallas kernels: 7.23 us -> 8.86 us  [per_device(): pl.pallas_call(functools.partial(first_tiles_kernel, half), grid_spec=plt...]
    all_to_all x1, starting transfers between devices: 7.3 us -> 6.6 us  [per_device(): lax.all_to_all(message, ('row', 'col'), split_axis=0, concat_axis=0, tile...]
  transfers between devices with their start and end apart: 11 -> 15, of which waited for: 2 -> 5; matrix products, arithmetic and copies ran while one was open for 0% -> 0% of each run, Pallas kernels for 22% -> 27%
where the time goes in v7:
time: 68.8 us; the launch traced here: 68.6 us
  Pallas kernels  24.9 us (36%)
  starting transfers between devices  23.7 us (34%)
  waiting for transfers between devices  19.2 us (28%)
  between operations  0.74 us (1%)
    ppermute x14, starting transfers between devices, move(): return lax.ppermute(value, ('row', 'col'), pairs)  17.1 us
    ppermute x14, waiting for transfers between devices, move(): return lax.ppermute(value, ('row', 'col'), pairs)  10.7 us
    pallas_call x1, Pallas kernels, per_device(): pl.pallas_call(functools.partial(first_tiles_kernel, half), grid_spec=plt...  8.86 us
    all_to_all x1, waiting for transfers between devices, per_device(): lax.all_to_all(message, ('row', 'col'), split_axis=0, concat_axis=0, tile...  8.59 us
    pallas_call x1, Pallas kernels, per_device(): pl.pallas_call(functools.partial(weighted_fit_kernel, members), in_specs=...  8.14 us
    all_to_all x1, starting transfers between devices, per_device(): lax.all_to_all(message, ('row', 'col'), split_axis=0, concat_axis=0, tile...  6.6 us
    pallas_call x1, Pallas kernels, per_device(): pl.pallas_call(functools.partial(more_tiles_kernel, half), grid_spec=pltp...  6.53 us
  transfers between devices with their start and end apart: 15, of which 5 were waited for; matrix products, arithmetic and copies ran while one was open for 0% of the time, Pallas kernels for 27%

profile of v7, /device:TPU:0, one launch (start us, length us, event | category | flops | bytes accessed | tf_op | source)
XLA Modules:
  0.0 68.6 jit_solution(13093194594347131537)
XLA Ops:
  0.6 4.1 %collective-permute-start.1 = (bf16[3,32,768]{2,1,0:T(8,128)(2,1)}, bf16[3,32,768]{2,1,0:T(8,128)(2,1)S(1)}, u32[]{:S(2)}, u32[]{:S(2)}) collective-permute-start(bf16[3,32,768]{2,1,0:T(8,128)(2,1)} %bitcast.3), channel_id=1, source_target_pairs={{16,0},{17,1},{18,2},{19,3},{20,4},{21,5},{22,6},{23,7},{24,8},{25... | collective-permute-start | bytes 442376 | tf_op jit(solution)/shard_map/ppermute | solution.py:251
  4.7 1.5 %collective-permute-start = (bf16[3,32,768]{2,1,0:T(8,128)(2,1)}, bf16[3,32,768]{2,1,0:T(8,128)(2,1)S(1)}, u32[]{:S(2)}, u32[]{:S(2)}) collective-permute-start(bf16[3,32,768]{2,1,0:T(8,128)(2,1)} %bitcast.4), channel_id=1, source_target_pairs={{1,0},{0,1},{3,2},{2,3},{5,4},{4,5},{7,6},{6,7},{9,8},{8,9},{11,10... | collective-permute-start | bytes 442376 | tf_op jit(solution)/shard_map/ppermute | solution.py:251
  6.2 5.7 %collective-permute-done.1.refs_0_ = bf16[3,32,768]{2,1,0:T(8,128)(2,1)S(1)} collective-permute-done((bf16[3,32,768]{2,1,0:T(8,128)(2,1)}, bf16[3,32,768]{2,1,0:T(8,128)(2,1)S(1)}, u32[]{:S(2)}, u32[]{:S(2)}) %collective-permute-start.1) | collective-permute-done | bytes 147488 | tf_op jit(solution)/shard_map/ppermute | solution.py:251
  11.9 3.4 %collective-permute-start.2 = (bf16[3,32,768]{2,1,0:T(8,128)(2,1)S(1)}, bf16[3,32,768]{2,1,0:T(8,128)(2,1)S(1)}, u32[]{:S(2)}, u32[]{:S(2)}) collective-permute-start(bf16[3,32,768]{2,1,0:T(8,128)(2,1)S(1)} %collective-permute-done.1.refs_0_), channel_id=1, source_target_pairs={{0,1},{2,3},{4,5},{6,7},{8,9},{10,11},{12,13},{14,15},{17,16},{19,... | collective-permute-start | bytes 442376 | tf_op jit(solution)/shard_map/ppermute | solution.py:251
  15.4 0.0 collective-permute-done.refs_0_
  15.4 1.2 %rows.1 = (bf16[3,64,768]{2,1,0:T(8,128)(2,1)S(1)}, f32[3,768]{1,0:T(4,128)S(1)}, f32[3,3,64]{2,1,0:T(4,128)S(1)}) custom-call(s32[1]{0:T(128)} %bitcast.1.col, f32[3,3,64]{2,1,0:T(4,128)} %rot_hbm.1, bf16[3,32,768]{2,1,0:T(8,128)(2,1)} %bitcast.5, bf16[3,32,768]{2,1,0:T(8,128)(2,1)S(1)} %collective-permute-done.refs_0_), custom_call_target="tpu_custom_call" | custom-call | tf_op jit(solution)/shard_map/rows/pallas_call | solution.py:280
  16.6 1.4 %collective-permute-done.2.refs_1_ = bf16[3,32,768]{2,1,0:T(8,128)(2,1)S(1)} collective-permute-done((bf16[3,32,768]{2,1,0:T(8,128)(2,1)S(1)}, bf16[3,32,768]{2,1,0:T(8,128)(2,1)S(1)}, u32[]{:S(2)}, u32[]{:S(2)}) %collective-permute-start.2) | collective-permute-done | bytes 147488 | tf_op jit(solution)/shard_map/ppermute | solution.py:251
  18.0 0.2 assemble.1
  18.3 2.4 %collective-permute-start.5 = (f32[3,768]{1,0:T(4,128)S(1)}, f32[3,768]{1,0:T(4,128)S(1)}, u32[]{:S(2)}, u32[]{:S(2)}) collective-permute-start(f32[3,768]{1,0:T(4,128)S(1)} %get-tuple-element.17.refs_0_), channel_id=1, source_target_pairs={{12,0},{13,1},{14,2},{15,3},{8,4},{9,5},{10,6},{11,7},{4,8},{5,9},... | collective-permute-start | bytes 27656 | tf_op jit(solution)/shard_map/ppermute | solution.py:251
  20.7 0.6 collective-permute-start.4
  21.3 0.5 collective-permute-start.3
  21.8 2.3 %collective-permute-start.9 = (bf16[3,64,768]{2,1,0:T(8,128)(2,1)S(1)}, bf16[3,64,768]{2,1,0:T(8,128)(2,1)S(1)}, u32[]{:S(2)}, u32[]{:S(2)}) collective-permute-start(bf16[3,64,768]{2,1,0:T(8,128)(2,1)S(1)} %get-tuple-element.20.refs_0_), channel_id=1, source_target_pairs={{12,0},{13,1},{14,2},{15,3},{8,4},{9,5},{10,6},{11,7},{4,8},{5,9},... | collective-permute-start | bytes 884744 | tf_op jit(solution)/shard_map/ppermute | solution.py:251
  24.2 0.6 collective-permute-start.8
  24.8 0.0 collective-permute-done.5.refs_3_
  24.8 0.5 collective-permute-start.7
  25.3 0.0 collective-permute-done.4.refs_2_
  25.3 2.2 %collective-permute-done.3.refs_1_ = f32[3,768]{1,0:T(4,128)S(1)} collective-permute-done((f32[3,768]{1,0:T(4,128)S(1)}, f32[3,768]{1,0:T(4,128)S(1)}, u32[]{:S(2)}, u32[]{:S(2)}) %collective-permute-start.3) | collective-permute-done | bytes 9248 | tf_op jit(solution)/shard_map/ppermute | solution.py:251
  27.6 0.0 collective-permute-start.6
  27.6 1.2 %collective-permute-done.6.odd_ref.centre_ref = f32[4,3,768]{2,1,0:T(4,128)S(1)} collective-permute-done((f32[4,3,768]{2,1,0:T(4,128)S(1)}, f32[4,3,768]{2,1,0:T(4,128)S(1)}, u32[]{:S(2)}, u32[]{:S(2)}) %collective-permute-start.6) | collective-permute-done | bytes 36896 | tf_op jit(solution)/shard_map/ppermute | solution.py:251
  28.8 8.1 %weighted_fit.1 = f32[32,8,128]{2,1,0:T(8,128)} custom-call(s32[1]{0:T(128)} %bitcast.row, f32[768,6144]{1,0:T(8,128)} %inv_ref.1, f32[4,3,768]{2,1,0:T(4,128)S(1)} %stack_centres.1.even_ref.centre_ref, f32[4,3,768]{2,1,0:T(4,128)S(1)} %collective-permute-done.6.odd_ref.centre_ref, bf16[3,64,768]{2,1,0:T(8,128)(2,1)S(1)} %get-tuple-element.16.rows_ref), custom_call_target="tpu_custom_call" | custom-call | flops 28311552 | bytes 18874368 | tf_op jit(solution)/shard_map/weighted_fit/pallas_call | solution.py:319
  37.0 6.6 %all-to-all-start = ((f32[32,8,128]{2,1,0:T(8,128)}), f32[32,8,128]{2,1,0:T(8,128)S(1)}, u32[]{:S(2)}, u32[]{:S(2)}) async-start(f32[32,8,128]{2,1,0:T(8,128)} %weighted_fit.1), calls=%async_computation | async-start | bytes 262144 | tf_op jit(solution)/shard_map/all_to_all | solution.py:336
  43.6 0.0 collective-permute-done.9.refs_3_
  43.6 0.0 collective-permute-done.8.refs_2_
  43.6 0.0 collective-permute-done.7.refs_1_
  43.6 8.6 %all-to-all-done.fits_ref = f32[32,8,128]{2,1,0:T(8,128)S(1)} async-done(((f32[32,8,128]{2,1,0:T(8,128)}), f32[32,8,128]{2,1,0:T(8,128)S(1)}, u32[]{:S(2)}, u32[]{:S(2)}) %all-to-all-start) | async-done | bytes 131104 | tf_op jit(solution)/shard_map/all_to_all | solution.py:336
  52.2 0.0 collective-permute-start.10
  52.2 0.5 collective-permute-start.11
  52.7 0.0 collective-permute-start.12
  52.7 0.5 collective-permute-start.13
  53.2 8.9 %steps_and_even_tiles.1 = (f32[768,6144]{1,0:T(8,128)}, f32[3,3,32]{2,1,0:T(4,128)}, f32[9,64,128]{2,1,0:T(8,128)S(1)}, bf16[768,192]{1,0:T(8,128)(2,1)S(1)}) custom-call(s32[1]{0:T(128)} %bitcast.row, s32[1]{0:T(128)} %bitcast.1.col, f32[32,8,128]{2,1,0:T(8,128)S(1)} %all-to-all-done.fits_ref, bf16[3,64,768]{2,1,0:T(8,128)(2,1)S(1)} %get-tuple-element.16.rows_ref, ...), custom_call_target="tpu_custom_call" | custom-call | flops 905969664 | bytes 9437184 | tf_op jit(solution)/shard_map/steps_and_even_tiles/pallas_call | solution.py:352
  62.1 0.0 collective-permute-done.10.refs_0_
  62.1 0.0 collective-permute-done.11.refs_1_
  62.1 0.0 collective-permute-done.12.refs_2_
  62.1 0.0 collective-permute-done.13.refs_3_
  62.1 6.5 %odd_tiles.1 = f32[768,6144]{1,0:T(8,128)} custom-call(s32[1]{0:T(128)} %bitcast.row, f32[768,6144]{1,0:T(8,128)} %get-tuple-element.24.before_ref, f32[9,64,128]{2,1,0:T(8,128)S(1)} %get-tuple-element.25.wide_ref, bf16[768,192]{1,0:T(8,128)(2,1)S(1)} %get-tuple-element.26.rows_dev_ref, ...), custom_call_target="tpu_custom_call", output_to_operand_aliasing={{}: (1, {})} | custom-call | flops 905969664 | bytes 9437184 | tf_op jit(solution)/shard_map/odd_tiles/pallas_call | solution.py:371
  (1 shorter events, 0.0 us)
Async XLA Ops:
  0.6 11.3 %collective-permute-start.1 = (bf16[3,32,768]{2,1,0:T(8,128)(2,1)}, bf16[3,32,768]{2,1,0:T(8,128)(2,1)S(1)}, u32[]{:S(2)}, u32[]{:S(2)}) collective-permute-start(bf16[3,32,768]{2,1,0:T(8,128)(2,1)} %bitcast.3), channel_id=1, source_target_pairs={{16,0},{17,1},{18,2},{19,3},{20,4},{21,5},{22,6},{23,7},{24,8},{25... | collective-permute-start | bytes 442376 | tf_op jit(solution)/shard_map/ppermute | solution.py:251
  4.7 10.7 %collective-permute-start = (bf16[3,32,768]{2,1,0:T(8,128)(2,1)}, bf16[3,32,768]{2,1,0:T(8,128)(2,1)S(1)}, u32[]{:S(2)}, u32[]{:S(2)}) collective-permute-start(bf16[3,32,768]{2,1,0:T(8,128)(2,1)} %bitcast.4), channel_id=1, source_target_pairs={{1,0},{0,1},{3,2},{2,3},{5,4},{4,5},{7,6},{6,7},{9,8},{8,9},{11,10... | collective-permute-start | bytes 442376 | tf_op jit(solution)/shard_map/ppermute | solution.py:251
  11.9 6.1 %collective-permute-start.2 = (bf16[3,32,768]{2,1,0:T(8,128)(2,1)S(1)}, bf16[3,32,768]{2,1,0:T(8,128)(2,1)S(1)}, u32[]{:S(2)}, u32[]{:S(2)}) collective-permute-start(bf16[3,32,768]{2,1,0:T(8,128)(2,1)S(1)} %collective-permute-done.1.refs_0_), channel_id=1, source_target_pairs={{0,1},{2,3},{4,5},{6,7},{8,9},{10,11},{12,13},{14,15},{17,16},{19,... | collective-permute-start | bytes 442376 | tf_op jit(solution)/shard_map/ppermute | solution.py:251
  18.3 6.5 %collective-permute-start.5 = (f32[3,768]{1,0:T(4,128)S(1)}, f32[3,768]{1,0:T(4,128)S(1)}, u32[]{:S(2)}, u32[]{:S(2)}) collective-permute-start(f32[3,768]{1,0:T(4,128)S(1)} %get-tuple-element.17.refs_0_), channel_id=1, source_target_pairs={{12,0},{13,1},{14,2},{15,3},{8,4},{9,5},{10,6},{11,7},{4,8},{5,9},... | collective-permute-start | bytes 27656 | tf_op jit(solution)/shard_map/ppermute | solution.py:251
  20.7 4.6 %collective-permute-start.4 = (f32[3,768]{1,0:T(4,128)S(1)}, f32[3,768]{1,0:T(4,128)S(1)}, u32[]{:S(2)}, u32[]{:S(2)}) collective-permute-start(f32[3,768]{1,0:T(4,128)S(1)} %get-tuple-element.17.refs_0_), channel_id=1, source_target_pairs={{8,0},{9,1},{10,2},{11,3},{12,4},{13,5},{14,6},{15,7},{0,8},{1,9},... | collective-permute-start | bytes 27656 | tf_op jit(solution)/shard_map/ppermute | solution.py:251
  21.3 6.2 %collective-permute-start.3 = (f32[3,768]{1,0:T(4,128)S(1)}, f32[3,768]{1,0:T(4,128)S(1)}, u32[]{:S(2)}, u32[]{:S(2)}) collective-permute-start(f32[3,768]{1,0:T(4,128)S(1)} %get-tuple-element.17.refs_0_), channel_id=1, source_target_pairs={{4,0},{5,1},{6,2},{7,3},{0,4},{1,5},{2,6},{3,7},{12,8},{13,9},{14,... | collective-permute-start | bytes 27656 | tf_op jit(solution)/shard_map/ppermute | solution.py:251
  21.8 21.7 %collective-permute-start.9 = (bf16[3,64,768]{2,1,0:T(8,128)(2,1)S(1)}, bf16[3,64,768]{2,1,0:T(8,128)(2,1)S(1)}, u32[]{:S(2)}, u32[]{:S(2)}) collective-permute-start(bf16[3,64,768]{2,1,0:T(8,128)(2,1)S(1)} %get-tuple-element.20.refs_0_), channel_id=1, source_target_pairs={{12,0},{13,1},{14,2},{15,3},{8,4},{9,5},{10,6},{11,7},{4,8},{5,9},... | collective-permute-start | bytes 884744 | tf_op jit(solution)/shard_map/ppermute | solution.py:251
  24.2 19.4 %collective-permute-start.8 = (bf16[3,64,768]{2,1,0:T(8,128)(2,1)S(1)}, bf16[3,64,768]{2,1,0:T(8,128)(2,1)S(1)}, u32[]{:S(2)}, u32[]{:S(2)}) collective-permute-start(bf16[3,64,768]{2,1,0:T(8,128)(2,1)S(1)} %get-tuple-element.20.refs_0_), channel_id=1, source_target_pairs={{8,0},{9,1},{10,2},{11,3},{12,4},{13,5},{14,6},{15,7},{0,8},{1,9},... | collective-permute-start | bytes 884744 | tf_op jit(solution)/shard_map/ppermute | solution.py:251
  24.8 18.8 %collective-permute-start.7 = (bf16[3,64,768]{2,1,0:T(8,128)(2,1)S(1)}, bf16[3,64,768]{2,1,0:T(8,128)(2,1)S(1)}, u32[]{:S(2)}, u32[]{:S(2)}) collective-permute-start(bf16[3,64,768]{2,1,0:T(8,128)(2,1)S(1)} %get-tuple-element.20.refs_0_), channel_id=1, source_target_pairs={{4,0},{5,1},{6,2},{7,3},{0,4},{1,5},{2,6},{3,7},{12,8},{13,9},{14,... | collective-permute-start | bytes 884744 | tf_op jit(solution)/shard_map/ppermute | solution.py:251
  27.6 1.2 %collective-permute-start.6 = (f32[4,3,768]{2,1,0:T(4,128)S(1)}, f32[4,3,768]{2,1,0:T(4,128)S(1)}, u32[]{:S(2)}, u32[]{:S(2)}) collective-permute-start(f32[4,3,768]{2,1,0:T(4,128)S(1)} %stack_centres.1.even_ref.centre_ref), channel_id=1, source_target_pairs={{2,0},{3,1},{0,2},{1,3},{6,4},{7,5},{4,6},{5,7},{10,8},{11,9},{8,1... | collective-permute-start | bytes 110600 | tf_op jit(solution)/shard_map/ppermute | solution.py:251
  37.0 15.2 %all-to-all-start = ((f32[32,8,128]{2,1,0:T(8,128)}), f32[32,8,128]{2,1,0:T(8,128)S(1)}, u32[]{:S(2)}, u32[]{:S(2)}) async-start(f32[32,8,128]{2,1,0:T(8,128)} %weighted_fit.1), calls=%async_computation | async-start | bytes 262144 | tf_op jit(solution)/shard_map/all_to_all | solution.py:336
  52.2 9.9 %collective-permute-start.10 = (bf16[3,64,768]{2,1,0:T(8,128)(2,1)S(1)}, bf16[3,64,768]{2,1,0:T(8,128)(2,1)S(1)}, u32[]{:S(2)}, u32[]{:S(2)}) collective-permute-start(bf16[3,64,768]{2,1,0:T(8,128)(2,1)S(1)} %get-tuple-element.20.refs_0_), channel_id=1, source_target_pairs={{2,0},{3,1},{0,2},{1,3},{6,4},{7,5},{4,6},{5,7},{10,8},{11,9},{8,1... | collective-permute-start | bytes 884744 | tf_op jit(solution)/shard_map/ppermute | solution.py:251
  52.2 9.9 %collective-permute-start.11 = (bf16[3,64,768]{2,1,0:T(8,128)(2,1)S(1)}, bf16[3,64,768]{2,1,0:T(8,128)(2,1)S(1)}, u32[]{:S(2)}, u32[]{:S(2)}) collective-permute-start(bf16[3,64,768]{2,1,0:T(8,128)(2,1)S(1)} %collective-permute-done.7.refs_1_), channel_id=1, source_target_pairs={{2,0},{3,1},{0,2},{1,3},{6,4},{7,5},{4,6},{5,7},{10,8},{11,9},{8,1... | collective-permute-start | bytes 884744 | tf_op jit(solution)/shard_map/ppermute | solution.py:251
  52.7 9.4 %collective-permute-start.12 = (bf16[3,64,768]{2,1,0:T(8,128)(2,1)S(1)}, bf16[3,64,768]{2,1,0:T(8,128)(2,1)S(1)}, u32[]{:S(2)}, u32[]{:S(2)}) collective-permute-start(bf16[3,64,768]{2,1,0:T(8,128)(2,1)S(1)} %collective-permute-done.8.refs_2_), channel_id=1, source_target_pairs={{2,0},{3,1},{0,2},{1,3},{6,4},{7,5},{4,6},{5,7},{10,8},{11,9},{8,1... | collective-permute-start | bytes 884744 | tf_op jit(solution)/shard_map/ppermute | solution.py:251
  52.7 9.4 %collective-permute-start.13 = (bf16[3,64,768]{2,1,0:T(8,128)(2,1)S(1)}, bf16[3,64,768]{2,1,0:T(8,128)(2,1)S(1)}, u32[]{:S(2)}, u32[]{:S(2)}) collective-permute-start(bf16[3,64,768]{2,1,0:T(8,128)(2,1)S(1)} %collective-permute-done.9.refs_3_), channel_id=1, source_target_pairs={{2,0},{3,1},{0,2},{1,3},{6,4},{7,5},{4,6},{5,7},{10,8},{11,9},{8,1... | collective-permute-start | bytes 884744 | tf_op jit(solution)/shard_map/ppermute | solution.py:251

commit v8 on v7

--- a/solution.py
+++ b/solution.py
@@ -53,7 +53,7 @@
     out_ref[:, pl.ds(pl.multiple_of(block * local, local), local), :] = value
 
 
-def rows_kernel(col, rot_hbm, coords_hbm, *refs):
+def rows_kernel(col, token_ref, rot_hbm, coords_hbm, *refs):
     others, (rows_ref, centre_ref, rot_ref, sems) = refs[:-4], refs[-4:]
     local = coords_hbm.shape[1]
     own_rows = rows_ref.at[:, pl.ds(pl.multiple_of(col[0] * local, local), local), :]
@@ -91,44 +91,50 @@
     centre_ref[...] = rotated_sum(rot_ref[...], out_ref[...]) * (1.0 / out_ref.shape[1])
 
 
-def weighted_fit_kernel(members, row, inv_ref, even_ref, odd_ref, rows_ref, out_ref, strips_ref, wide_ref, weighted_ref, sems):
-    strips, height, col_width = strips_ref.shape
+def fetch_kernel(source_ref, target_ref, token_ref, sems):
+    height = source_ref.shape[0] // sems.shape[0]
+    copies = []
+    for strip in range(sems.shape[0]):
+        span = pl.ds(strip * height, height)
+        copies.append(pltpu.make_async_copy(source_ref.at[span, :], target_ref.at[span, :], sems.at[strip]))
+        copies[-1].start()
+    for copy in copies:
+        copy.wait()
+    token_ref[...] = jnp.zeros_like(token_ref)
+
+
+def weighted_fit_kernel(members, height, row, inv_ref, even_ref, odd_ref, rows_ref, out_ref, wide_ref, weighted_ref):
     width = even_ref.shape[2]
-
-    def fetch(strip):
-        rows = pl.ds(pl.multiple_of(strip * height, height), height)
-        return pltpu.make_async_copy(inv_ref.at[rows, :], strips_ref.at[strip], sems.at[strip])
-
-    for strip in range(strips):
-        fetch(strip).start()
     member = lax.rem(row[0], members)
     for mask in range(members):
         centre_ref = odd_ref if mask % 2 else even_ref
-        start = pl.multiple_of((member ^ mask) * width, LANES)
         for comp in range(3):
             factor = jnp.broadcast_to(centre_ref[mask // 2, comp : comp + 1, :], (8, width))
-            wide_ref[comp, :, pl.ds(start, width)] = factor
+            wide_ref[comp, :, mask * width : (mask + 1) * width] = factor
     lane = lax.broadcasted_iota(jnp.int32, (height, LANES), 1)
-    chunks = col_width // LANES
 
     def strip_body(strip, carry):
-        fetch(strip).wait()
-
-        def body(chunk, sums):
-            span = pl.ds(pl.multiple_of(chunk * LANES, LANES), LANES)
-            value = strips_ref[strip, :, span].reshape(height // 8, 8, LANES)
-            return tuple(sums[comp] + value * wide_ref[comp, :, span][None] for comp in range(3))
+        strip_rows = pl.ds(pl.multiple_of(strip * height, height), height)
+
+        def body(mask, sums):
+            block = member ^ mask
+            for start in range(0, width, LANES):
+                span = pl.ds(pl.multiple_of(block * width + start, LANES), LANES)
+                value = inv_ref[strip_rows, span].reshape(height // 8, 8, LANES)
+                span = pl.ds(pl.multiple_of(mask * width + start, LANES), LANES)
+                sums = tuple(sums[comp] + value * wide_ref[comp, :, span][None] for comp in range(3))
+            return sums
 
         sums = (jnp.zeros((height // 8, 8, LANES), F32),) * 3
-        sums = lax.fori_loop(0, chunks, body, sums, unroll=12 if chunks % 12 == 0 else 1)
+        sums = lax.fori_loop(0, members, body, sums)
         packed = jnp.zeros((height, LANES), F32)
         for comp in range(3):
             total = jnp.sum(sums[comp].reshape(height, LANES), axis=1, keepdims=True)
             packed = jnp.where(lane == comp, total, packed)
-        weighted_ref[pl.ds(pl.multiple_of(strip * height, height), height), :] = packed
+        weighted_ref[strip_rows, :] = packed
         return carry
 
-    lax.fori_loop(0, strips, strip_body, 0)
+    lax.fori_loop(0, width // height, strip_body, 0)
     frame_total = rows_ref.shape[1]
     rows = rows_ref[...].reshape(3 * frame_total, width)
     high, mid, low = (jnp.dot(rows, piece, preferred_element_type=F32) for piece in three_pieces(weighted_ref[...]))
@@ -162,34 +168,36 @@
     return current
 
 
-def put_deviations(wide_ref, coords_ref, centre, source, dev_ref, target):
-    frame_total = coords_ref.shape[1]
-    span = slice(source, source + LANES)
-    coords = [coords_ref[part, :, span].astype(F32) for part in range(3)]
-    for comp in range(3):
-        moved = wide_ref[3 * comp] * coords[0]
-        moved = moved + wide_ref[3 * comp + 1] * coords[1]
-        moved = moved + wide_ref[3 * comp + 2] * coords[2]
-        value = moved - centre[comp : comp + 1, span]
-        dev_ref[comp * frame_total : (comp + 1) * frame_total, target : target + LANES] = value.astype(BF16)
-
-
-def put_tile(wide_ref, coords_ref, centre, first, rows_dev_ref, dev_ref, out_ref):
-    width = out_ref.shape[1]
-    scale = 1.0 / (3 * coords_ref.shape[1])
+def put_deviations(wide_ref, coords_ref, centre_ref, dev_ref):
+    frame_total, width = coords_ref.shape[1:]
     for start in range(0, width, LANES):
-        put_deviations(wide_ref, coords_ref, centre, first + start, dev_ref, start)
-    product = jnp.dot(rows_dev_ref[...], dev_ref[:, :width], preferred_element_type=F32)
-    out_ref[...] = product * scale
+        span = slice(start, start + LANES)
+        coords = [coords_ref[part, :, span].astype(F32) for part in range(3)]
+        for comp in range(3):
+            moved = wide_ref[3 * comp] * coords[0]
+            moved = moved + wide_ref[3 * comp + 1] * coords[1]
+            moved = moved + wide_ref[3 * comp + 2] * coords[2]
+            value = moved - centre_ref[comp : comp + 1, span]
+            dev_ref[comp * frame_total : (comp + 1) * frame_total, span] = value.astype(BF16)
+
+
+def clear_spare(dev_ref, frame_total):
+    depth, width = dev_ref.shape[1:]
+    if depth > 3 * frame_total:
+        dev_ref[:, 3 * frame_total :, :] = jnp.zeros((2, depth - 3 * frame_total, width), BF16)
 
 
 def put_tiles(wide_ref, centre_ref, panel_refs, rows_dev_ref, dev_ref, out_ref):
-    width, pieces = out_ref.shape[1], centre_ref.shape[2] // out_ref.shape[1]
-    for step in range(len(panel_refs) * pieces):
+    scale = 1.0 / (3 * wide_ref.shape[1])
+    for step in range(len(panel_refs)):
 
         @pl.when(pl.program_id(0) == step)
-        def _(block=step // pieces, first=step % pieces * width):
-            put_tile(wide_ref, panel_refs[block], centre_ref[block], first, rows_dev_ref, dev_ref, out_ref)
+        def _(step=step):
+            product = jnp.dot(rows_dev_ref[...], dev_ref[step % 2], preferred_element_type=F32)
+            if step + 1 < len(panel_refs):
+                later = dev_ref.at[(step + 1) % 2]
+                put_deviations(wide_ref, panel_refs[step + 1], centre_ref.at[step + 1], later)
+            out_ref[...] = product * scale
 
 
 def first_tiles_kernel(half, row, col, fits_ref, rows_ref, rows_centre_ref, centre_ref, *refs):
@@ -211,16 +219,22 @@
         columns = jnp.concatenate(entries + [jnp.zeros((7, frame_total), F32)], axis=0).T
         for entry in range(9):
             wide_ref[entry] = jnp.broadcast_to(columns[:, entry : entry + 1], (frame_total, LANES))
-        centre = rows_centre_ref[...]
-        for chunk in range(rows_ref.shape[2] // LANES):
-            put_deviations(wide_ref, rows_ref, centre, chunk * LANES, dev_ref, chunk * LANES)
-        rows_dev_ref[...] = dev_ref[...].T
+        clear_spare(dev_ref, frame_total)
+        put_deviations(wide_ref, rows_ref, rows_centre_ref, dev_ref.at[1])
+        rows_dev_ref[...] = dev_ref[1].T
+        put_deviations(wide_ref, panel_refs[0], centre_ref.at[0], dev_ref.at[0])
 
     put_tiles(wide_ref, centre_ref, panel_refs, rows_dev_ref, dev_ref, out_ref)
 
 
 def more_tiles_kernel(half, row, before_ref, wide_ref, rows_dev_ref, centre_ref, *refs):
     panel_refs, (out_ref, dev_ref) = refs[:half], refs[half:]
+
+    @pl.when(pl.program_id(0) == 0)
+    def _():
+        clear_spare(dev_ref, wide_ref.shape[1])
+        put_deviations(wide_ref, panel_refs[0], centre_ref.at[0], dev_ref.at[0])
+
     put_tiles(wide_ref, centre_ref, panel_refs, rows_dev_ref, dev_ref, out_ref)
 
 
@@ -277,6 +291,16 @@
 
     far = [move(coords, lambda g, m, c, s=step: ((g + s) % col_count, m, c)) for step in range(1, col_count)]
     others = [move(coords, lambda g, m, c, s=step: (g, m, (c + s) % col_count)) for step in range(1, col_count)]
+    inverse_here, token = pl.pallas_call(
+        fetch_kernel,
+        out_shape=(jax.ShapeDtypeStruct(inverse_cov.shape, F32), jax.ShapeDtypeStruct((8, LANES), F32)),
+        in_specs=[hbm()],
+        out_specs=(vmem(), vmem()),
+        scratch_shapes=[pltpu.SemaphoreType.DMA((12,))],
+        compiler_params=limit(4),
+        cost_estimate=pl.CostEstimate(flops=0, bytes_accessed=4 * width * col_width, transcendentals=0),
+        name="fetch_inverse",
+    )(in_hbm(inverse_cov))
     rows_all, rows_centre, rot = pl.pallas_call(
         rows_kernel,
         out_shape=(
@@ -284,12 +308,12 @@
             jax.ShapeDtypeStruct((3, width), F32),
             jax.ShapeDtypeStruct(rotations.shape, F32),
         ),
-        in_specs=[smem(), hbm(), hbm()] + [vmem()] * (col_count - 1),
+        in_specs=[smem(), vmem(), hbm(), hbm()] + [vmem()] * (col_count - 1),
         out_specs=(vmem(), vmem(), vmem()),
         scratch_shapes=[pltpu.SemaphoreType.DMA((2,))],
         compiler_params=limit(8),
         name="rows",
-    )(col, in_hbm(rotations), in_hbm(coords), *others)
+    )(col, token, in_hbm(rotations), in_hbm(coords), *others)
 
     distance = lax.rem(col[0] + col_count - row[0] // members, col_count)
     across = []
@@ -311,49 +335,45 @@
     )(row, col, rot, rows_all, *far, *across)
 
     centres = [own_centre] + [from_member(own_centre, 2 * step) for step in range(1, half)]
-    evens = [own_block] + [from_member(own_block, 2 * step) for step in range(1, half)]
     even_centres = small_kernel(stack_kernel, (half, 3, width), "stack_centres", *centres)
     odd_centres = from_member(even_centres, 1)
+    own_block = after(odd_centres, own_block)
+    evens = [own_block] + [from_member(own_block, 2 * step) for step in range(1, half)]
 
     height = 64 if width % 64 == 0 else 8
     message = pl.pallas_call(
-        functools.partial(weighted_fit_kernel, members),
-        in_specs=[smem(), hbm()] + [vmem()] * 3,
+        functools.partial(weighted_fit_kernel, members, height),
+        in_specs=[smem()] + [vmem()] * 4,
         out_specs=vmem(),
-        scratch_shapes=[
-            pltpu.VMEM((width // height, height, col_width), F32),
-            pltpu.VMEM((3, 8, col_width), F32),
-            pltpu.VMEM((width, LANES), F32),
-            pltpu.SemaphoreType.DMA((width // height,)),
-        ],
+        scratch_shapes=[pltpu.VMEM((3, 8, col_width), F32), pltpu.VMEM((width, LANES), F32)],
         out_shape=jax.ShapeDtypeStruct((device_total, 8, 2 * frame_total), F32),
-        compiler_params=limit(28),
+        compiler_params=limit(8),
         cost_estimate=pl.CostEstimate(
             flops=6 * width * col_width, bytes_accessed=4 * width * col_width, transcendentals=0
         ),
         name="weighted_fit",
-    )(row, in_hbm(inverse_cov), even_centres, odd_centres, rows_all)
+    )(row, inverse_here, even_centres, odd_centres, rows_all)
     fits = lax.all_to_all(message, ("row", "col"), split_axis=0, concat_axis=0, tiled=True)
     evens = after(fits, evens)
     odds = [from_member(block, 1) for block in evens]
 
-    pieces = 2 if width % (2 * LANES) == 0 else 1
+    depth = -(-3 * frame_total // 256) * 256
 
     def tile_spec(odd):
         def index(i, row, *_):
-            return (0, (lax.rem(row[0], members) ^ (2 * (i // pieces) + odd)) * pieces + lax.rem(i, pieces))
-
-        return pl.BlockSpec((width, width // pieces), index)
+            return (0, lax.rem(row[0], members) ^ (2 * i + odd))
+
+        return pl.BlockSpec((width, width), index)
 
     tiles_cost = pl.CostEstimate(
         flops=3 * frame_total * width * col_width, bytes_accessed=2 * width * col_width, transcendentals=0
     )
-    dev_scratch = pltpu.VMEM((3 * frame_total, width), BF16)
+    dev_scratch = pltpu.VMEM((2, depth, width), BF16)
     covariance, transforms, wide, rows_dev = pl.pallas_call(
         functools.partial(first_tiles_kernel, half),
         grid_spec=pltpu.PrefetchScalarGridSpec(
             num_scalar_prefetch=2,
-            grid=(half * pieces,),
+            grid=(half,),
             in_specs=[vmem()] * (4 + half),
             out_specs=(tile_spec(0), vmem(), vmem(), vmem()),
             scratch_shapes=[dev_scratch],
@@ -362,7 +382,7 @@
             jax.ShapeDtypeStruct((width, col_width), F32),
             jax.ShapeDtypeStruct((3, 3, local), F32),
             jax.ShapeDtypeStruct((9, frame_total, LANES), F32),
-            jax.ShapeDtypeStruct((width, 3 * frame_total), BF16),
+            jax.ShapeDtypeStruct((width, depth), BF16),
         ),
         compiler_params=limit(16),
         cost_estimate=tiles_cost,
@@ -372,7 +392,7 @@
         functools.partial(more_tiles_kernel, half),
         grid_spec=pltpu.PrefetchScalarGridSpec(
             num_scalar_prefetch=1,
-            grid=(half * pieces,),
+            grid=(half,),
             in_specs=[hbm()] + [vmem()] * (3 + half),
             out_specs=tile_spec(1),
             scratch_shapes=[dev_scratch],

time: 68.8 us -> 67.1 us (0.975)
  blocking collectives: 0 us -> 12.3 us
  waiting for transfers between devices: 19.2 us -> 10.2 us
  starting transfers between devices: 23.7 us -> 17.2 us
  Pallas kernels: 24.9 us -> 26.6 us
    all_to_all x0 -> x1, blocking collectives: none -> 12.3 us  [per_device(): lax.all_to_all(message, ('row', 'col'), split_axis=0, concat_axis=0, tile...]
    all_to_all x1 -> x0, waiting for transfers between devices: 8.59 us -> none  [per_device(): lax.all_to_all(message, ('row', 'col'), split_axis=0, concat_axis=0, tile...]
    all_to_all x1 -> x0, starting transfers between devices: 6.6 us -> none  [per_device(): lax.all_to_all(message, ('row', 'col'), split_axis=0, concat_axis=0, tile...]
    pallas_call x1 -> x2, Pallas kernels: 8.14 us -> 13 us  [the longest x1 6.53 us: per_device(): pl.pallas_call(fetch_kernel, out_shape=(jax.ShapeDtypeStruct(inverse_cov....]
    pallas_call x1, Pallas kernels: 6.53 us -> 4.89 us  [per_device(): pl.pallas_call(functools.partial(more_tiles_kernel, half), grid_spec=pltp...]
    pallas_call x1, Pallas kernels: 8.86 us -> 7.35 us  [per_device(): pl.pallas_call(functools.partial(first_tiles_kernel, half), grid_spec=plt...]
  transfers between devices with their start and end apart: 15 -> 14, of which waited for: 5 -> 5; matrix products, arithmetic and copies ran while one was open for 0% -> 0% of each run, Pallas kernels for 27% -> 32%
where the time goes in v8:
time: 67.1 us; the launch traced here: 66.9 us
  Pallas kernels  26.6 us (40%)
  starting transfers between devices  17.2 us (26%)
  blocking collectives  12.3 us (18%)
  waiting for transfers between devices  10.2 us (15%)
  between operations  0.73 us (1%)
    ppermute x14, starting transfers between devices, move(): return lax.ppermute(value, ('row', 'col'), pairs)  17.2 us
    all_to_all x1, blocking collectives, per_device(): lax.all_to_all(message, ('row', 'col'), split_axis=0, concat_axis=0, tile...  12.3 us
    ppermute x14, waiting for transfers between devices, move(): return lax.ppermute(value, ('row', 'col'), pairs)  10.2 us
    pallas_call x1, Pallas kernels, per_device(): pl.pallas_call(functools.partial(first_tiles_kernel, half), grid_spec=plt...  7.35 us
    pallas_call x1, Pallas kernels, per_device(): pl.pallas_call(fetch_kernel, out_shape=(jax.ShapeDtypeStruct(inverse_cov....  6.53 us
    pallas_call x1, Pallas kernels, per_device(): pl.pallas_call(functools.partial(weighted_fit_kernel, members, height), i...  6.42 us
    pallas_call x1, Pallas kernels, per_device(): pl.pallas_call(functools.partial(more_tiles_kernel, half), grid_spec=pltp...  4.89 us
  transfers between devices with their start and end apart: 14, of which 5 were waited for; matrix products, arithmetic and copies ran while one was open for 0% of the time, Pallas kernels for 32%

profile of v8, /device:TPU:0, one launch (start us, length us, event | category | flops | bytes accessed | tf_op | source)
XLA Modules:
  0.0 66.9 jit_solution(4181293780304469576)
XLA Ops:
  0.6 4.1 %collective-permute-start.1 = (bf16[3,32,768]{2,1,0:T(8,128)(2,1)}, bf16[3,32,768]{2,1,0:T(8,128)(2,1)S(1)}, u32[]{:S(2)}, u32[]{:S(2)}) collective-permute-start(bf16[3,32,768]{2,1,0:T(8,128)(2,1)} %bitcast.3), channel_id=1, source_target_pairs={{16,0},{17,1},{18,2},{19,3},{20,4},{21,5},{22,6},{23,7},{24,8},{25... | collective-permute-start | bytes 442376 | tf_op jit(solution)/shard_map/ppermute | solution.py:265
  4.7 1.5 %collective-permute-start = (bf16[3,32,768]{2,1,0:T(8,128)(2,1)}, bf16[3,32,768]{2,1,0:T(8,128)(2,1)S(1)}, u32[]{:S(2)}, u32[]{:S(2)}) collective-permute-start(bf16[3,32,768]{2,1,0:T(8,128)(2,1)} %bitcast.4), channel_id=1, source_target_pairs={{1,0},{0,1},{3,2},{2,3},{5,4},{4,5},{7,6},{6,7},{9,8},{8,9},{11,10... | collective-permute-start | bytes 442376 | tf_op jit(solution)/shard_map/ppermute | solution.py:265
  6.2 5.7 %collective-permute-done.1.refs_0_ = bf16[3,32,768]{2,1,0:T(8,128)(2,1)S(1)} collective-permute-done((bf16[3,32,768]{2,1,0:T(8,128)(2,1)}, bf16[3,32,768]{2,1,0:T(8,128)(2,1)S(1)}, u32[]{:S(2)}, u32[]{:S(2)}) %collective-permute-start.1) | collective-permute-done | bytes 147488 | tf_op jit(solution)/shard_map/ppermute | solution.py:265
  12.0 3.4 %collective-permute-start.2 = (bf16[3,32,768]{2,1,0:T(8,128)(2,1)S(1)}, bf16[3,32,768]{2,1,0:T(8,128)(2,1)S(1)}, u32[]{:S(2)}, u32[]{:S(2)}) collective-permute-start(bf16[3,32,768]{2,1,0:T(8,128)(2,1)S(1)} %collective-permute-done.1.refs_0_), channel_id=1, source_target_pairs={{0,1},{2,3},{4,5},{6,7},{8,9},{10,11},{12,13},{14,15},{17,16},{19,... | collective-permute-start | bytes 442376 | tf_op jit(solution)/shard_map/ppermute | solution.py:265
  15.4 6.5 %fetch_inverse.1 = (f32[768,6144]{1,0:T(8,128)S(1)}, f32[8,128]{1,0:T(8,128)S(1)}) custom-call(f32[768,6144]{1,0:T(8,128)} %source_ref.1), custom_call_target="tpu_custom_call" | custom-call | bytes 18874368 | tf_op jit(solution)/shard_map/fetch_inverse/pallas_call | solution.py:294
  21.9 0.0 collective-permute-done.refs_0_
  22.0 1.2 %rows.1 = (bf16[3,64,768]{2,1,0:T(8,128)(2,1)S(1)}, f32[3,768]{1,0:T(4,128)S(1)}, f32[3,3,64]{2,1,0:T(4,128)S(1)}) custom-call(s32[1]{0:T(128)} %bitcast.1.col, f32[8,128]{1,0:T(8,128)S(1)} %get-tuple-element.19.token_ref, f32[3,3,64]{2,1,0:T(4,128)} %rot_hbm.1, bf16[3,32,768]{2,1,0:T(8,128)(2,1)} %bitcast.5, ...), custom_call_target="tpu_custom_call" | custom-call | tf_op jit(solution)/shard_map/rows/pallas_call | solution.py:304
  23.1 0.0 collective-permute-done.2.refs_1_
  23.2 0.2 assemble.1
  23.4 1.8 %collective-permute-start.5 = (f32[3,768]{1,0:T(4,128)S(1)}, f32[3,768]{1,0:T(4,128)S(1)}, u32[]{:S(2)}, u32[]{:S(2)}) collective-permute-start(f32[3,768]{1,0:T(4,128)S(1)} %get-tuple-element.22.refs_0_), channel_id=1, source_target_pairs={{12,0},{13,1},{14,2},{15,3},{8,4},{9,5},{10,6},{11,7},{4,8},{5,9},... | collective-permute-start | bytes 27656 | tf_op jit(solution)/shard_map/ppermute | solution.py:265
  25.2 1.2 %collective-permute-start.4 = (f32[3,768]{1,0:T(4,128)S(1)}, f32[3,768]{1,0:T(4,128)S(1)}, u32[]{:S(2)}, u32[]{:S(2)}) collective-permute-start(f32[3,768]{1,0:T(4,128)S(1)} %get-tuple-element.22.refs_0_), channel_id=1, source_target_pairs={{8,0},{9,1},{10,2},{11,3},{12,4},{13,5},{14,6},{15,7},{0,8},{1,9},... | collective-permute-start | bytes 27656 | tf_op jit(solution)/shard_map/ppermute | solution.py:265
  26.4 0.5 collective-permute-start.3
  27.0 1.1 %collective-permute-done.5.refs_3_ = f32[3,768]{1,0:T(4,128)S(1)} collective-permute-done((f32[3,768]{1,0:T(4,128)S(1)}, f32[3,768]{1,0:T(4,128)S(1)}, u32[]{:S(2)}, u32[]{:S(2)}) %collective-permute-start.5) | collective-permute-done | bytes 9248 | tf_op jit(solution)/shard_map/ppermute | solution.py:265
  28.1 0.8 %collective-permute-done.4.refs_2_ = f32[3,768]{1,0:T(4,128)S(1)} collective-permute-done((f32[3,768]{1,0:T(4,128)S(1)}, f32[3,768]{1,0:T(4,128)S(1)}, u32[]{:S(2)}, u32[]{:S(2)}) %collective-permute-start.4) | collective-permute-done | bytes 9248 | tf_op jit(solution)/shard_map/ppermute | solution.py:265
  28.9 1.2 %collective-permute-done.3.refs_1_ = f32[3,768]{1,0:T(4,128)S(1)} collective-permute-done((f32[3,768]{1,0:T(4,128)S(1)}, f32[3,768]{1,0:T(4,128)S(1)}, u32[]{:S(2)}, u32[]{:S(2)}) %collective-permute-start.3) | collective-permute-done | bytes 9248 | tf_op jit(solution)/shard_map/ppermute | solution.py:265
  30.1 0.0 collective-permute-start.6
  30.2 1.2 %collective-permute-done.6.odd_ref.centre_ref = f32[4,3,768]{2,1,0:T(4,128)S(1)} collective-permute-done((f32[4,3,768]{2,1,0:T(4,128)S(1)}, f32[4,3,768]{2,1,0:T(4,128)S(1)}, u32[]{:S(2)}, u32[]{:S(2)}) %collective-permute-start.6) | collective-permute-done | bytes 36896 | tf_op jit(solution)/shard_map/ppermute | solution.py:265
  31.4 0.7 %collective-permute-start.9 = (bf16[3,64,768]{2,1,0:T(8,128)(2,1)S(1)}, bf16[3,64,768]{2,1,0:T(8,128)(2,1)S(1)}, u32[]{:S(2)}, u32[]{:S(2)}) collective-permute-start(bf16[3,64,768]{2,1,0:T(8,128)(2,1)S(1)} %get-tuple-element.26.refs_0_), channel_id=1, source_target_pairs={{12,0},{13,1},{14,2},{15,3},{8,4},{9,5},{10,6},{11,7},{4,8},{5,9},... | collective-permute-start | bytes 884744 | tf_op jit(solution)/shard_map/ppermute | solution.py:265
  32.1 1.2 %collective-permute-start.8 = (bf16[3,64,768]{2,1,0:T(8,128)(2,1)S(1)}, bf16[3,64,768]{2,1,0:T(8,128)(2,1)S(1)}, u32[]{:S(2)}, u32[]{:S(2)}) collective-permute-start(bf16[3,64,768]{2,1,0:T(8,128)(2,1)S(1)} %get-tuple-element.26.refs_0_), channel_id=1, source_target_pairs={{8,0},{9,1},{10,2},{11,3},{12,4},{13,5},{14,6},{15,7},{0,8},{1,9},... | collective-permute-start | bytes 884744 | tf_op jit(solution)/shard_map/ppermute | solution.py:265
  33.3 1.5 %collective-permute-start.7 = (bf16[3,64,768]{2,1,0:T(8,128)(2,1)S(1)}, bf16[3,64,768]{2,1,0:T(8,128)(2,1)S(1)}, u32[]{:S(2)}, u32[]{:S(2)}) collective-permute-start(bf16[3,64,768]{2,1,0:T(8,128)(2,1)S(1)} %get-tuple-element.26.refs_0_), channel_id=1, source_target_pairs={{4,0},{5,1},{6,2},{7,3},{0,4},{1,5},{2,6},{3,7},{12,8},{13,9},{14,... | collective-permute-start | bytes 884744 | tf_op jit(solution)/shard_map/ppermute | solution.py:265
  34.9 6.4 %weighted_fit.1 = f32[32,8,128]{2,1,0:T(8,128)S(1)} custom-call(s32[1]{0:T(128)} %bitcast.row, f32[768,6144]{1,0:T(8,128)S(1)} %get-tuple-element.18.inv_ref, f32[4,3,768]{2,1,0:T(4,128)S(1)} %stack_centres.1.even_ref.centre_ref, f32[4,3,768]{2,1,0:T(4,128)S(1)} %collective-permute-done.6.odd_ref.centre_ref, bf16[3,64,768]{2,1,0:T(8,128)(2,1)S(1)} %get-tuple-element.21.rows_ref), custom_call_target="tpu_custom_call" | custom-call | flops 28311552 | bytes 18874368 | tf_op jit(solution)/shard_map/weighted_fit/pallas_call | solution.py:344
  41.3 12.3 %all_to_all.5.fits_ref = f32[32,8,128]{2,1,0:T(8,128)S(1)} all-to-all(f32[32,8,128]{2,1,0:T(8,128)S(1)} %weighted_fit.1), channel_id=1, replica_groups=mesh['row'=16,'col'=2] {'row','col'}, dimensions={0} | all-to-all | bytes 262144 | tf_op jit(solution)/shard_map/all_to_all | solution.py:356
  53.5 0.0 collective-permute-done.9.refs_3_
  53.6 0.0 collective-permute-done.8.refs_2_
  53.6 0.0 collective-permute-done.7.refs_1_
  53.6 0.1 collective-permute-start.10
  53.6 0.5 collective-permute-start.11
  54.1 0.1 collective-permute-start.12
  54.2 0.4 collective-permute-start.13
  54.6 7.4 %steps_and_even_tiles.1 = (f32[768,6144]{1,0:T(8,128)}, f32[3,3,32]{2,1,0:T(4,128)}, f32[9,64,128]{2,1,0:T(8,128)S(1)}, bf16[768,256]{1,0:T(8,128)(2,1)S(1)}) custom-call(s32[1]{0:T(128)} %bitcast.row, s32[1]{0:T(128)} %bitcast.1.col, f32[32,8,128]{2,1,0:T(8,128)S(1)} %all_to_all.5.fits_ref, bf16[3,64,768]{2,1,0:T(8,128)(2,1)S(1)} %get-tuple-element.21.rows_ref, ...), custom_call_target="tpu_custom_call" | custom-call | flops 905969664 | bytes 9437184 | tf_op jit(solution)/shard_map/steps_and_even_tiles/pallas_call | solution.py:372
  62.0 0.0 collective-permute-done.10.refs_0_
  62.0 0.0 collective-permute-done.11.refs_1_
  62.0 0.0 collective-permute-done.12.refs_2_
  62.0 0.0 collective-permute-done.13.refs_3_
  62.0 4.9 %odd_tiles.1 = f32[768,6144]{1,0:T(8,128)} custom-call(s32[1]{0:T(128)} %bitcast.row, f32[768,6144]{1,0:T(8,128)} %get-tuple-element.30.before_ref, f32[9,64,128]{2,1,0:T(8,128)S(1)} %get-tuple-element.31.wide_ref, bf16[768,256]{1,0:T(8,128)(2,1)S(1)} %get-tuple-element.32.rows_dev_ref, ...), custom_call_target="tpu_custom_call", output_to_operand_aliasing={{}: (1, {})} | custom-call | flops 905969664 | bytes 9437184 | tf_op jit(solution)/shard_map/odd_tiles/pallas_call | solution.py:391
  (1 shorter events, 0.0 us)
Async XLA Ops:
  0.6 11.3 %collective-permute-start.1 = (bf16[3,32,768]{2,1,0:T(8,128)(2,1)}, bf16[3,32,768]{2,1,0:T(8,128)(2,1)S(1)}, u32[]{:S(2)}, u32[]{:S(2)}) collective-permute-start(bf16[3,32,768]{2,1,0:T(8,128)(2,1)} %bitcast.3), channel_id=1, source_target_pairs={{16,0},{17,1},{18,2},{19,3},{20,4},{21,5},{22,6},{23,7},{24,8},{25... | collective-permute-start | bytes 442376 | tf_op jit(solution)/shard_map/ppermute | solution.py:265
  4.7 17.2 %collective-permute-start = (bf16[3,32,768]{2,1,0:T(8,128)(2,1)}, bf16[3,32,768]{2,1,0:T(8,128)(2,1)S(1)}, u32[]{:S(2)}, u32[]{:S(2)}) collective-permute-start(bf16[3,32,768]{2,1,0:T(8,128)(2,1)} %bitcast.4), channel_id=1, source_target_pairs={{1,0},{0,1},{3,2},{2,3},{5,4},{4,5},{7,6},{6,7},{9,8},{8,9},{11,10... | collective-permute-start | bytes 442376 | tf_op jit(solution)/shard_map/ppermute | solution.py:265
  12.0 11.2 %collective-permute-start.2 = (bf16[3,32,768]{2,1,0:T(8,128)(2,1)S(1)}, bf16[3,32,768]{2,1,0:T(8,128)(2,1)S(1)}, u32[]{:S(2)}, u32[]{:S(2)}) collective-permute-start(bf16[3,32,768]{2,1,0:T(8,128)(2,1)S(1)} %collective-permute-done.1.refs_0_), channel_id=1, source_target_pairs={{0,1},{2,3},{4,5},{6,7},{8,9},{10,11},{12,13},{14,15},{17,16},{19,... | collective-permute-start | bytes 442376 | tf_op jit(solution)/shard_map/ppermute | solution.py:265
  23.4 4.7 %collective-permute-start.5 = (f32[3,768]{1,0:T(4,128)S(1)}, f32[3,768]{1,0:T(4,128)S(1)}, u32[]{:S(2)}, u32[]{:S(2)}) collective-permute-start(f32[3,768]{1,0:T(4,128)S(1)} %get-tuple-element.22.refs_0_), channel_id=1, source_target_pairs={{12,0},{13,1},{14,2},{15,3},{8,4},{9,5},{10,6},{11,7},{4,8},{5,9},... | collective-permute-start | bytes 27656 | tf_op jit(solution)/shard_map/ppermute | solution.py:265
  25.2 3.7 %collective-permute-start.4 = (f32[3,768]{1,0:T(4,128)S(1)}, f32[3,768]{1,0:T(4,128)S(1)}, u32[]{:S(2)}, u32[]{:S(2)}) collective-permute-start(f32[3,768]{1,0:T(4,128)S(1)} %get-tuple-element.22.refs_0_), channel_id=1, source_target_pairs={{8,0},{9,1},{10,2},{11,3},{12,4},{13,5},{14,6},{15,7},{0,8},{1,9},... | collective-permute-start | bytes 27656 | tf_op jit(solution)/shard_map/ppermute | solution.py:265
  26.4 3.7 %collective-permute-start.3 = (f32[3,768]{1,0:T(4,128)S(1)}, f32[3,768]{1,0:T(4,128)S(1)}, u32[]{:S(2)}, u32[]{:S(2)}) collective-permute-start(f32[3,768]{1,0:T(4,128)S(1)} %get-tuple-element.22.refs_0_), channel_id=1, source_target_pairs={{4,0},{5,1},{6,2},{7,3},{0,4},{1,5},{2,6},{3,7},{12,8},{13,9},{14,... | collective-permute-start | bytes 27656 | tf_op jit(solution)/shard_map/ppermute | solution.py:265
  30.1 1.2 %collective-permute-start.6 = (f32[4,3,768]{2,1,0:T(4,128)S(1)}, f32[4,3,768]{2,1,0:T(4,128)S(1)}, u32[]{:S(2)}, u32[]{:S(2)}) collective-permute-start(f32[4,3,768]{2,1,0:T(4,128)S(1)} %stack_centres.1.even_ref.centre_ref), channel_id=1, source_target_pairs={{2,0},{3,1},{0,2},{1,3},{6,4},{7,5},{4,6},{5,7},{10,8},{11,9},{8,1... | collective-permute-start | bytes 110600 | tf_op jit(solution)/shard_map/ppermute | solution.py:265
  31.4 22.2 %collective-permute-start.9 = (bf16[3,64,768]{2,1,0:T(8,128)(2,1)S(1)}, bf16[3,64,768]{2,1,0:T(8,128)(2,1)S(1)}, u32[]{:S(2)}, u32[]{:S(2)}) collective-permute-start(bf16[3,64,768]{2,1,0:T(8,128)(2,1)S(1)} %get-tuple-element.26.refs_0_), channel_id=1, source_target_pairs={{12,0},{13,1},{14,2},{15,3},{8,4},{9,5},{10,6},{11,7},{4,8},{5,9},... | collective-permute-start | bytes 884744 | tf_op jit(solution)/shard_map/ppermute | solution.py:265
  32.1 21.5 %collective-permute-start.8 = (bf16[3,64,768]{2,1,0:T(8,128)(2,1)S(1)}, bf16[3,64,768]{2,1,0:T(8,128)(2,1)S(1)}, u32[]{:S(2)}, u32[]{:S(2)}) collective-permute-start(bf16[3,64,768]{2,1,0:T(8,128)(2,1)S(1)} %get-tuple-element.26.refs_0_), channel_id=1, source_target_pairs={{8,0},{9,1},{10,2},{11,3},{12,4},{13,5},{14,6},{15,7},{0,8},{1,9},... | collective-permute-start | bytes 884744 | tf_op jit(solution)/shard_map/ppermute | solution.py:265
  33.3 20.2 %collective-permute-start.7 = (bf16[3,64,768]{2,1,0:T(8,128)(2,1)S(1)}, bf16[3,64,768]{2,1,0:T(8,128)(2,1)S(1)}, u32[]{:S(2)}, u32[]{:S(2)}) collective-permute-start(bf16[3,64,768]{2,1,0:T(8,128)(2,1)S(1)} %get-tuple-element.26.refs_0_), channel_id=1, source_target_pairs={{4,0},{5,1},{6,2},{7,3},{0,4},{1,5},{2,6},{3,7},{12,8},{13,9},{14,... | collective-permute-start | bytes 884744 | tf_op jit(solution)/shard_map/ppermute | solution.py:265
  53.6 8.4 %collective-permute-start.10 = (bf16[3,64,768]{2,1,0:T(8,128)(2,1)S(1)}, bf16[3,64,768]{2,1,0:T(8,128)(2,1)S(1)}, u32[]{:S(2)}, u32[]{:S(2)}) collective-permute-start(bf16[3,64,768]{2,1,0:T(8,128)(2,1)S(1)} %get-tuple-element.26.refs_0_), channel_id=1, source_target_pairs={{2,0},{3,1},{0,2},{1,3},{6,4},{7,5},{4,6},{5,7},{10,8},{11,9},{8,1... | collective-permute-start | bytes 884744 | tf_op jit(solution)/shard_map/ppermute | solution.py:265
  53.6 8.4 %collective-permute-start.11 = (bf16[3,64,768]{2,1,0:T(8,128)(2,1)S(1)}, bf16[3,64,768]{2,1,0:T(8,128)(2,1)S(1)}, u32[]{:S(2)}, u32[]{:S(2)}) collective-permute-start(bf16[3,64,768]{2,1,0:T(8,128)(2,1)S(1)} %collective-permute-done.7.refs_1_), channel_id=1, source_target_pairs={{2,0},{3,1},{0,2},{1,3},{6,4},{7,5},{4,6},{5,7},{10,8},{11,9},{8,1... | collective-permute-start | bytes 884744 | tf_op jit(solution)/shard_map/ppermute | solution.py:265
  54.1 7.9 %collective-permute-start.12 = (bf16[3,64,768]{2,1,0:T(8,128)(2,1)S(1)}, bf16[3,64,768]{2,1,0:T(8,128)(2,1)S(1)}, u32[]{:S(2)}, u32[]{:S(2)}) collective-permute-start(bf16[3,64,768]{2,1,0:T(8,128)(2,1)S(1)} %collective-permute-done.8.refs_2_), channel_id=1, source_target_pairs={{2,0},{3,1},{0,2},{1,3},{6,4},{7,5},{4,6},{5,7},{10,8},{11,9},{8,1... | collective-permute-start | bytes 884744 | tf_op jit(solution)/shard_map/ppermute | solution.py:265
  54.2 7.8 %collective-permute-start.13 = (bf16[3,64,768]{2,1,0:T(8,128)(2,1)S(1)}, bf16[3,64,768]{2,1,0:T(8,128)(2,1)S(1)}, u32[]{:S(2)}, u32[]{:S(2)}) collective-permute-start(bf16[3,64,768]{2,1,0:T(8,128)(2,1)S(1)} %collective-permute-done.9.refs_3_), channel_id=1, source_target_pairs={{2,0},{3,1},{0,2},{1,3},{6,4},{7,5},{4,6},{5,7},{10,8},{11,9},{8,1... | collective-permute-start | bytes 884744 | tf_op jit(solution)/shard_map/ppermute | solution.py:265

commit v9 on v8

v9 whole, which is shorter than its diff:
```python
import functools

import jax
import jax.numpy as jnp
from jax import lax
from jax.experimental import pallas as pl
from jax.experimental.pallas import tpu as pltpu
from jax.sharding import PartitionSpec as P

POLAR = 12
LANES = 128
F32 = jnp.float32
BF16 = jnp.bfloat16
MIB = 1 << 20


def vmem():
    return pl.BlockSpec(memory_space=pltpu.VMEM)


def hbm():
    return pl.BlockSpec(memory_space=pl.ANY)


def smem():
    return pl.BlockSpec(memory_space=pltpu.SMEM)


def three_pieces(value):
    high = value.astype(BF16)
    rest = value - high.astype(F32)
    mid = rest.astype(BF16)
    low = (rest - mid.astype(F32)).astype(BF16)
    return high, mid, low


def rotated_sum(rot, coords):
    depth = coords.shape[0] * coords.shape[1]
    flat = jnp.concatenate([rot[:, part, :] for part in range(3)], axis=1)
    padded = jnp.concatenate([flat, jnp.zeros((5, depth), F32)], axis=0)
    stacked = jnp.concatenate(three_pieces(padded), axis=0)
    product = jnp.dot(stacked, coords.reshape(depth, coords.shape[2]), preferred_element_type=F32)
    return (product[16:19] + product[8:11]) + product[0:3]


def partial_centre_kernel(frame_total, col, rot_hbm, coords_hbm, out_ref, coords_ref, rot_ref, sems):
    copies = [
        pltpu.make_async_copy(rot_hbm, rot_ref, sems.at[0]),
        pltpu.make_async_copy(coords_hbm, coords_ref, sems.at[1]),
    ]
    for copy in copies:
        copy.start()
    for copy in copies:
        copy.wait()
    local = coords_ref.shape[1]
    block = lax.broadcasted_iota(jnp.int32, rot_ref.shape, 2) // local
    rot = jnp.where(block == col[0], rot_ref[...], 0.0)
    coords = jnp.concatenate([coords_ref[...]] * (frame_total // local), axis=1)
    centre = rotated_sum(rot, coords) * (1.0 / frame_total)
    flat = jnp.concatenate([centre[comp : comp + 1, :] for comp in range(3)], axis=1)
    out_ref[...] = jnp.broadcast_to(flat[None], out_ref.shape)


def put_centre(parts_ref, row, col_count, centre_ref):
    total = parts_ref[row * col_count]
    for place in range(1, col_count):
        total = total + parts_ref[row * col_count + place]
    width = centre_ref.shape[1]
    for comp in range(3):
        centre_ref[comp : comp + 1, :] = total[:, comp * width : (comp + 1) * width]


def put_block(out_ref, block, value):
    local = value.shape[1]
    out_ref[:, pl.ds(pl.multiple_of(block * local, local), local), :] = value


def assemble_kernel(members, row, col, rows_ref, *refs):
    sources, out_ref = refs[:-1], refs[-1]
    far_refs, across_refs = sources[: len(sources) // 2], sources[len(sources) // 2 :]
    col_count = len(far_refs) + 1
    distance = lax.rem(col[0] + col_count - row[0] // members, col_count)

    @pl.when(distance == 0)
    def _():
        out_ref[...] = rows_ref[...]

    for step, ref in enumerate(far_refs):

        @pl.when(distance == step + 1)
        def _(ref=ref):
            put_block(out_ref, col[0], ref[...])
            for shift, across_ref in enumerate(across_refs):
                put_block(out_ref, lax.rem(col[0] + 1 + shift, col_count), across_ref[...])


def fetch_kernel(source_ref, target_ref, sems):
    height = source_ref.shape[0] // sems.shape[0]
    copies = []
    for strip in range(sems.shape[0]):
        span = pl.ds(strip * height, height)
        copies.append(pltpu.make_async_copy(source_ref.at[span, :], target_ref.at[span, :], sems.at[strip]))
        copies[-1].start()
    for copy in copies:
        copy.wait()


def weighted_kernel(members, col_count, height, row, col, inv_ref, parts_ref, out_ref, even_ref, odd_ref, rows_centre_ref, wide_ref):
    width = even_ref.shape[2]
    member = lax.rem(row[0], members)
    for mask in range(members):
        centre_ref = (odd_ref if mask % 2 else even_ref).at[mask // 2]
        put_centre(parts_ref, col[0] * members + (member ^ mask), col_count, centre_ref)
        for comp in range(3):
            factor = jnp.broadcast_to(centre_ref[comp : comp + 1, :], (8, width))
            wide_ref[comp, :, mask * width : (mask + 1) * width] = factor
    put_centre(parts_ref, row[0], col_count, rows_centre_ref)
    lane = lax.broadcasted_iota(jnp.int32, (height, LANES), 1)

    def strip_body(strip, carry):
        strip_rows = pl.ds(pl.multiple_of(strip * height, height), height)
        sums = [jnp.zeros((height // 8, 8, LANES), F32)] * 3
        for mask in range(members):
            block = member ^ mask
            for start in range(0, width, LANES):
                span = pl.ds(pl.multiple_of(block * width + start, LANES), LANES)
                value = inv_ref[strip_rows, span].reshape(height // 8, 8, LANES)
                place = mask * width + start
                for comp in range(3):
                    sums[comp] = sums[comp] + value * wide_ref[comp, :, place : place + LANES][None]
        packed = jnp.zeros((height, LANES), F32)
        for comp in range(3):
            total = jnp.sum(sums[comp].reshape(height, LANES), axis=1, keepdims=True)
            packed = jnp.where(lane == comp, total, packed)
        out_ref[strip_rows, :] = packed
        return carry

    lax.fori_loop(0, inv_ref.shape[0] // height, strip_body, 0)


def fit_kernel(col, weighted_ref, own_ref, *refs):
    others, (out_ref, rows_ref) = refs[:-2], refs[-2:]
    for shift, ref in enumerate((own_ref, *others)):
        put_block(rows_ref, lax.rem(col[0] + shift, len(others) + 1), ref[...])
    frame_total, width = rows_ref.shape[1:]
    rows = rows_ref[...].reshape(3 * frame_total, width)
    high, mid, low = (jnp.dot(rows, piece, preferred_element_type=F32) for piece in three_pieces(weighted_ref[...]))
    fits = ((low + mid) + high).T
    entries = [
        fits[comp : comp + 1, part * frame_total : (part + 1) * frame_total] for part in range(3) for comp in range(3)
    ]
    first = jnp.concatenate(entries[:8], axis=0)
    last = jnp.concatenate([entries[8], jnp.zeros((7, frame_total), F32)], axis=0)
    message = jnp.concatenate([first, last], axis=1)
    out_ref[...] = jnp.broadcast_to(message[None], out_ref.shape)


def orthogonalized(message, frame_total):
    fitted = [message[entry : entry + 1, :frame_total] for entry in range(8)]
    fitted.append(message[0:1, frame_total:])
    norm = functools.reduce(lambda a, b: a + b, [value * value for value in fitted])
    scaling = jnp.sqrt(1.0 + norm)
    current = [[fitted[3 * col + row] / scaling for col in range(3)] for row in range(3)]
    for _ in range(POLAR):
        square = [[None] * 3 for _ in range(3)]
        for a in range(3):
            for b in range(a, 3):
                x, y = current[a], current[b]
                square[a][b] = square[b][a] = x[0] * y[0] + x[1] * y[1] + x[2] * y[2]
        cubed = [
            [square[a][0] * current[0][b] + square[a][1] * current[1][b] + square[a][2] * current[2][b] for b in range(3)]
            for a in range(3)
        ]
        current = [[1.5 * current[a][b] - 0.5 * cubed[a][b] for b in range(3)] for a in range(3)]
    return current


def put_deviations(wide_ref, coords_ref, centre_ref, first, dev_ref):
    frame_total = coords_ref.shape[1]
    for start in range(0, dev_ref.shape[1], LANES):
        span = slice(first + start, first + start + LANES)
        coords = [coords_ref[part, :, span].astype(F32) for part in range(3)]
        for comp in range(3):
            moved = wide_ref[3 * comp] * coords[0]
            moved = moved + wide_ref[3 * comp + 1] * coords[1]
            moved = moved + wide_ref[3 * comp + 2] * coords[2]
            value = moved - centre_ref[comp : comp + 1, span]
            dev_ref[comp * frame_total : (comp + 1) * frame_total, start : start + LANES] = value.astype(BF16)


def put_tiles(masks, row, wide_ref, centre_ref, panel_refs, rows_dev_ref, dev_ref, tile_ref, sems, out_ref):
    slots, _, tile = tile_ref.shape
    width = centre_ref.shape[2]
    members = out_ref.shape[1] // width
    scale = 1.0 / (3 * wide_ref.shape[1])
    writes = []
    for step, mask in enumerate(masks):
        block = lax.rem(row[0], members) ^ mask
        for first in range(0, width, tile):
            count = len(writes)
            dev = dev_ref.at[count % 2]
            put_deviations(wide_ref, panel_refs[step], centre_ref.at[step], first, dev)
            product = jnp.dot(rows_dev_ref[...], dev[...], preferred_element_type=F32)
            if count >= slots:
                writes[count - slots].wait()
            tile_ref[count % slots] = product * scale
            target = out_ref.at[:, pl.ds(pl.multiple_of(block * width + first, LANES), tile)]
            writes.append(pltpu.make_async_copy(tile_ref.at[count % slots], target, sems.at[count % slots]))
            writes[-1].start()
    for write in writes[-slots:]:
        write.wait()


def first_tiles_kernel(masks, row, col, fits_ref, rows_ref, rows_centre_ref, centre_ref, *refs):
    panel_refs = refs[: len(masks)]
    out_ref, rot_out_ref, wide_ref, rows_dev_ref, rows_ref_t, dev_ref, tile_ref, sems = refs[len(masks) :]
    frame_total = rows_ref.shape[1]
    local = rot_out_ref.shape[2]
    current = orthogonalized(jnp.sum(fits_ref[...], axis=0), frame_total)
    for a in range(3):
        flat = jnp.concatenate(current[a], axis=0)
        kept = flat[:, :local]
        for block in range(1, frame_total // local):
            kept = jnp.where(col[0] == block, flat[:, block * local : (block + 1) * local], kept)
        rot_out_ref[a] = kept
    entries = [current[a][b] for a in range(3) for b in range(3)]
    columns = jnp.concatenate(entries + [jnp.zeros((7, frame_total), F32)], axis=0).T
    for entry in range(9):
        wide_ref[entry] = jnp.broadcast_to(columns[:, entry : entry + 1], (frame_total, LANES))
    put_deviations(wide_ref, rows_ref, rows_centre_ref, 0, rows_ref_t)
    rows_dev_ref[...] = rows_ref_t[...].T
    put_tiles(masks, row, wide_ref, centre_ref, panel_refs, rows_dev_ref, dev_ref, tile_ref, sems, out_ref)


def more_tiles_kernel(masks, row, before_ref, wide_ref, rows_dev_ref, centre_ref, *refs):
    panel_refs, (out_ref, dev_ref, tile_ref, sems) = refs[: len(masks)], refs[len(masks) :]
    put_tiles(masks, row, wide_ref, centre_ref, panel_refs, rows_dev_ref, dev_ref, tile_ref, sems, out_ref)


def per_device(frames, rotations, inverse_cov):
    row_count, col_count = lax.axis_size("row"), lax.axis_size("col")
    members = row_count // col_count
    row = lax.axis_index("row").astype(jnp.int32).reshape(1)
    col = lax.axis_index("col").astype(jnp.int32).reshape(1)
    local, _, width = frames.shape
    frame_total = local * col_count
    device_total = row_count * col_count
    col_width = inverse_cov.shape[1]
    half = members // 2
    coords = jnp.transpose(frames, (1, 0, 2))

    def limit(mib):
        return pltpu.CompilerParams(vmem_limit_bytes=mib * MIB)

    def move(value, source_of, receives=lambda group, col: True):
        pairs = []
        for group in range(col_count):
            for member in range(members):
                for place in range(col_count):
                    if receives(group, place):
                        from_group, from_member, from_col = source_of(group, member, place)
                        source = (from_group * members + from_member) * col_count + from_col
                        pairs.append((source, (group * members + member) * col_count + place))
        return lax.ppermute(value, ("row", "col"), pairs)

    def from_panel_row(value, step):
        return move(value, lambda g, m, c: (c, m, (g + step) % col_count))

    def from_member(value, mask):
        return move(value, lambda g, m, c: (g, m ^ mask, c))

    def limit(mib):
        return pltpu.CompilerParams(vmem_limit_bytes=mib * MIB)

    def in_hbm(value):
        return pltpu.with_memory_space_constraint(value, pltpu.HBM)

    repeated, coords_here = pl.pallas_call(
        functools.partial(partial_centre_kernel, frame_total),
        out_shape=(
            jax.ShapeDtypeStruct((device_total, 1, 3 * width), F32),
            jax.ShapeDtypeStruct(coords.shape, BF16),
        ),
        in_specs=[smem(), hbm(), hbm()],
        out_specs=(vmem(), vmem()),
        scratch_shapes=[pltpu.VMEM(rotations.shape, F32), pltpu.SemaphoreType.DMA((2,))],
        compiler_params=limit(8),
        name="partial_centre",
    )(col, in_hbm(rotations), in_hbm(coords))
    parts = lax.all_to_all(repeated, ("row", "col"), split_axis=0, concat_axis=0, tiled=True)

    far = [move(coords_here, lambda g, m, c, s=step: ((g + s) % col_count, m, c)) for step in range(1, col_count)]
    others = [
        move(coords_here, lambda g, m, c, s=step: (g, m, (c + s) % col_count)) for step in range(1, col_count)
    ]
    inverse_here = pl.pallas_call(
        fetch_kernel,
        out_shape=jax.ShapeDtypeStruct(inverse_cov.shape, F32),
        in_specs=[hbm()],
        out_specs=vmem(),
        scratch_shapes=[pltpu.SemaphoreType.DMA((12,))],
        compiler_params=limit(4),
        cost_estimate=pl.CostEstimate(flops=0, bytes_accessed=4 * width * col_width, transcendentals=0),
        name="fetch_inverse",
    )(in_hbm(inverse_cov))

    height = 64 if width % 64 == 0 else 8
    weighted, even_centres, odd_centres, rows_centre = pl.pallas_call(
        functools.partial(weighted_kernel, members, col_count, height),
        out_shape=(
            jax.ShapeDtypeStruct((width, LANES), F32),
            jax.ShapeDtypeStruct((half, 3, width), F32),
            jax.ShapeDtypeStruct((half, 3, width), F32),
            jax.ShapeDtypeStruct((3, width), F32),
        ),
        in_specs=[smem(), smem(), vmem(), vmem()],
        out_specs=(vmem(),) * 4,
        scratch_shapes=[pltpu.VMEM((3, 8, col_width), F32)],
        compiler_params=limit(8),
        cost_estimate=pl.CostEstimate(
            flops=6 * width * col_width, bytes_accessed=4 * width * col_width, transcendentals=0
        ),
        name="weighted",
    )(row, col, inverse_here, parts)
    message, rows_all = pl.pallas_call(
        fit_kernel,
        out_shape=(
            jax.ShapeDtypeStruct((device_total, 8, 2 * frame_total), F32),
            jax.ShapeDtypeStruct((3, frame_total, width), BF16),
        ),
        in_specs=[smem()] + [vmem()] * (1 + col_count),
        out_specs=(vmem(), vmem()),
        compiler_params=limit(8),
        name="fit",
    )(col, weighted, coords_here, *others)

    distance = lax.rem(col[0] + col_count - row[0] // members, col_count)
    across = []
    for step in range(1, col_count):
        held = far[0]
        if col_count > 2:
            held = lax.select_n(lax.rem(distance + col_count - step, col_count), coords_here, *far)
        across.append(move(held, lambda g, m, c, s=step: (g, m, (c + s) % col_count), lambda g, c: g != c))
    own_block = pl.pallas_call(
        functools.partial(assemble_kernel, members),
        out_shape=jax.ShapeDtypeStruct((3, frame_total, width), BF16),
        in_specs=[smem(), smem()] + [vmem()] * (2 * col_count - 1),
        out_specs=vmem(),
        compiler_params=limit(8),
        name="assemble",
    )(row, col, rows_all, *far, *across)
    evens = [own_block] + [from_member(own_block, 2 * step) for step in range(1, half)]
    fits = lax.all_to_all(message, ("row", "col"), split_axis=0, concat_axis=0, tiled=True)
    fits, evens = lax.optimization_barrier((fits, evens))
    odds = [from_member(block, 1) for block in evens]

    depth = 3 * frame_total
    tile = 2 * LANES if width % (2 * LANES) == 0 else LANES
    tile_scratch = [
        pltpu.VMEM((2, depth, tile), BF16),
        pltpu.VMEM((4, width, tile), F32),
        pltpu.SemaphoreType.DMA((4,)),
    ]
    tiles_cost = pl.CostEstimate(
        flops=3 * frame_total * width * col_width, bytes_accessed=2 * width * col_width, transcendentals=0
    )
    covariance, transforms, wide, rows_dev = pl.pallas_call(
        functools.partial(first_tiles_kernel, tuple(range(0, members, 2))),
        in_specs=[smem(), smem()] + [vmem()] * (4 + half),
        out_specs=(hbm(), vmem(), vmem(), vmem()),
        scratch_shapes=[pltpu.VMEM((depth, width), BF16)] + tile_scratch,
        out_shape=(
            jax.ShapeDtypeStruct((width, col_width), F32),
            jax.ShapeDtypeStruct((3, 3, local), F32),
            jax.ShapeDtypeStruct((9, frame_total, LANES), F32),
            jax.ShapeDtypeStruct((width, depth), BF16),
        ),
        compiler_params=limit(16),
        cost_estimate=tiles_cost,
        name="steps_and_even_tiles",
    )(row, col, fits, rows_all, rows_centre, even_centres, *evens)
    covariance = pl.pallas_call(
        functools.partial(more_tiles_kernel, tuple(range(1, members, 2))),
        in_specs=[smem(), hbm()] + [vmem()] * (3 + half),
        out_specs=hbm(),
        scratch_shapes=tile_scratch,
        out_shape=jax.ShapeDtypeStruct((width, col_width), F32),
        input_output_aliases={1: 0},
        compiler_params=limit(16),
        cost_estimate=tiles_cost,
        name="odd_tiles",
    )(row, covariance, wide, rows_dev, odd_centres, *odds)
    return (covariance, transforms)


def solution(mesh):
    placed = (P("col", None, "row"), P(), P("row", "col"))
    return jax.shard_map(
        per_device,
        mesh=mesh,
        in_specs=placed,
        out_specs=(P("row", "col"), P(None, None, "col")),
        check_vma=False,
    )
```

time: 67.1 us -> 92.7 us (1.38)
  local copies, waits for them, and re-layouts: 0 us -> 13.2 us
  Pallas kernels: 26.6 us -> 32.6 us
  starting transfers between devices: 17.2 us -> 19.5 us
  waiting for transfers between devices: 10.2 us -> 12.2 us
  blocking collectives: 12.3 us -> 14.1 us
    unnamed x0 -> x4, local copies, waits for them, and re-layouts: none -> 13.2 us
    all_to_all x0 -> x1, starting transfers between devices: none -> 7.3 us  [per_device(): lax.all_to_all(repeated, ('row', 'col'), split_axis=0, concat_axis=0, til...]
    pallas_call x7, Pallas kernels: 26.6 us -> 32.6 us  [the longest x1 9.54 us: per_device(): pl.pallas_call(functools.partial(weighted_kernel, members, col_count, hei...]
    ppermute x14 -> x10, starting transfers between devices: 17.2 us -> 12.2 us  [move(): return lax.ppermute(value, ('row', 'col'), pairs)]
    ppermute x14 -> x10, waiting for transfers between devices: 10.2 us -> 12.2 us  [move(): return lax.ppermute(value, ('row', 'col'), pairs)]
    all_to_all x1, blocking collectives: 12.3 us -> 14.1 us  [per_device(): lax.all_to_all(message, ('row', 'col'), split_axis=0, concat_axis=0, tile...]
  transfers between devices with their start and end apart: 14 -> 11, of which waited for: 5 -> 1; matrix products, arithmetic and copies ran while one was open for 0% -> 0% of each run, Pallas kernels for 32% -> 27%
where the time goes in v9:
time: 92.7 us; the launch traced here: 92.4 us
  Pallas kernels  32.6 us (35%)
  starting transfers between devices  19.5 us (21%)
  blocking collectives  14.1 us (15%)
  local copies, waits for them, and re-layouts  13.2 us (14%)
  waiting for transfers between devices  12.2 us (13%)
    all_to_all x1, blocking collectives, per_device(): lax.all_to_all(message, ('row', 'col'), split_axis=0, concat_axis=0, tile...  14.1 us
    unnamed x4, local copies, waits for them, and re-layouts  13.2 us
    ppermute x10, waiting for transfers between devices, move(): return lax.ppermute(value, ('row', 'col'), pairs)  12.2 us
    ppermute x10, starting transfers between devices, move(): return lax.ppermute(value, ('row', 'col'), pairs)  12.2 us
    pallas_call x1, Pallas kernels, per_device(): pl.pallas_call(functools.partial(weighted_kernel, members, col_count, hei...  9.54 us
    pallas_call x1, Pallas kernels, per_device(): pl.pallas_call(functools.partial(first_tiles_kernel, tuple(range(0, membe...  8.52 us
    all_to_all x1, starting transfers between devices, per_device(): lax.all_to_all(repeated, ('row', 'col'), split_axis=0, concat_axis=0, til...  7.3 us
    pallas_call x1, Pallas kernels, per_device(): pl.pallas_call(fetch_kernel, out_shape=jax.ShapeDtypeStruct(inverse_cov.s...  6.53 us
  transfers between devices with their start and end apart: 11, of which 1 were waited for; matrix products, arithmetic and copies ran while one was open for 0% of the time, Pallas kernels for 27%

profile of v9, /device:TPU:0, one launch (start us, length us, event | category | flops | bytes accessed | tf_op | source)
XLA Modules:
  0.0 92.4 jit_solution(6582794947705569840)
XLA Ops:
  0.6 1.9 %partial_centre.1 = (f32[32,1,2304]{2,1,0:T(1,128)}, bf16[3,32,768]{2,1,0:T(8,128)(2,1)S(1)}) custom-call(s32[1]{0:T(128)} %bitcast.1.col, f32[3,3,64]{2,1,0:T(4,128)} %rot_hbm.1, bf16[3,32,768]{2,1,0:T(8,128)(2,1)} %bitcast.3), custom_call_target="tpu_custom_call" | custom-call | tf_op jit(solution)/shard_map/partial_centre/pallas_call | solution.py:278
  2.6 7.3 %all-to-all-start = ((f32[32,1,2304]{2,1,0:T(1,128)}), f32[32,1,2304]{2,1,0:T(1,128)S(1)}, u32[]{:S(2)}, u32[]{:S(2)}) async-start(f32[32,1,2304]{2,1,0:T(1,128)} %get-tuple-element.19), calls=%async_computation | async-start | bytes 589824 | tf_op jit(solution)/shard_map/all_to_all | solution.py:290
  9.9 2.7 %collective-permute-start.1 = (bf16[3,32,768]{2,1,0:T(8,128)(2,1)S(1)}, bf16[3,32,768]{2,1,0:T(8,128)(2,1)S(1)}, u32[]{:S(2)}, u32[]{:S(2)}) collective-permute-start(bf16[3,32,768]{2,1,0:T(8,128)(2,1)S(1)} %get-tuple-element.21.own_ref), channel_id=1, source_target_pairs={{16,0},{17,1},{18,2},{19,3},{20,4},{21,5},{22,6},{23,7},{24,8},{25... | collective-permute-start | bytes 442376 | tf_op jit(solution)/shard_map/ppermute | solution.py:264
  12.6 1.5 %collective-permute-start = (bf16[3,32,768]{2,1,0:T(8,128)(2,1)S(1)}, bf16[3,32,768]{2,1,0:T(8,128)(2,1)S(1)}, u32[]{:S(2)}, u32[]{:S(2)}) collective-permute-start(bf16[3,32,768]{2,1,0:T(8,128)(2,1)S(1)} %get-tuple-element.21.own_ref), channel_id=1, source_target_pairs={{1,0},{0,1},{3,2},{2,3},{5,4},{4,5},{7,6},{6,7},{9,8},{8,9},{11,10... | collective-permute-start | bytes 442376 | tf_op jit(solution)/shard_map/ppermute | solution.py:264
  14.1 12.2 %collective-permute-done.1.refs_0_ = bf16[3,32,768]{2,1,0:T(8,128)(2,1)S(1)} collective-permute-done((bf16[3,32,768]{2,1,0:T(8,128)(2,1)S(1)}, bf16[3,32,768]{2,1,0:T(8,128)(2,1)S(1)}, u32[]{:S(2)}, u32[]{:S(2)}) %collective-permute-start.1) | collective-permute-done | bytes 147488 | tf_op jit(solution)/shard_map/ppermute | solution.py:264
  26.3 3.4 %collective-permute-start.2 = (bf16[3,32,768]{2,1,0:T(8,128)(2,1)S(1)}, bf16[3,32,768]{2,1,0:T(8,128)(2,1)S(1)}, u32[]{:S(2)}, u32[]{:S(2)}) collective-permute-start(bf16[3,32,768]{2,1,0:T(8,128)(2,1)S(1)} %collective-permute-done.1.refs_0_), channel_id=1, source_target_pairs={{0,1},{2,3},{4,5},{6,7},{8,9},{10,11},{12,13},{14,15},{17,16},{19,... | collective-permute-start | bytes 442376 | tf_op jit(solution)/shard_map/ppermute | solution.py:264
  29.7 6.5 %fetch_inverse.1.inv_ref = f32[768,6144]{1,0:T(8,128)S(1)} custom-call(f32[768,6144]{1,0:T(8,128)} %source_ref.1), custom_call_target="tpu_custom_call" | custom-call | bytes 18874368 | tf_op jit(solution)/shard_map/fetch_inverse/pallas_call | solution.py:296
  36.2 0.0 copy-start
  36.2 6.8 %copy-done = f32[768,6144]{1,0:T(8,128)} copy-done((f32[768,6144]{1,0:T(8,128)}, f32[768,6144]{1,0:T(8,128)S(1)}, u32[]{:S(2)}) %copy-start) | copy-done | bytes 18874392
  43.0 0.0 all-to-all-done.parts_ref
  43.0 0.0 copy-start.1
  43.1 6.4 %copy-done.1 = f32[768,6144]{1,0:T(8,128)S(1)} copy-done((f32[768,6144]{1,0:T(8,128)S(1)}, f32[768,6144]{1,0:T(8,128)}, u32[]{:S(2)}) %copy-start.1) | copy-done | bytes 18874392
  49.4 9.5 %weighted.1 = (f32[768,128]{1,0:T(8,128)S(1)}, f32[4,3,768]{2,1,0:T(4,128)S(1)}, f32[4,3,768]{2,1,0:T(4,128)S(1)}, f32[3,768]{1,0:T(4,128)S(1)}) custom-call(s32[1]{0:T(128)} %bitcast.row, s32[1]{0:T(128)} %bitcast.1.col, f32[768,6144]{1,0:T(8,128)S(1)} %copy-done.1, f32[32,1,2304]{2,1,0:T(1,128)S(1)} %all-to-all-done.parts_ref), custom_call_target="tpu_custom_call" | custom-call | flops 28311552 | bytes 18874368 | tf_op jit(solution)/shard_map/weighted/pallas_call | solution.py:308
  59.0 0.0 collective-permute-done.refs_0_
  59.0 0.5 fit.1
  59.5 0.0 collective-permute-done.2.refs_1_
  59.6 0.1 collective-permute-start.5
  59.6 2.9 %collective-permute-start.4 = (bf16[3,64,768]{2,1,0:T(8,128)(2,1)S(1)}, bf16[3,64,768]{2,1,0:T(8,128)(2,1)S(1)}, u32[]{:S(2)}, u32[]{:S(2)}) collective-permute-start(bf16[3,64,768]{2,1,0:T(8,128)(2,1)S(1)} %assemble.1.refs_0_), channel_id=1, source_target_pairs={{8,0},{9,1},{10,2},{11,3},{12,4},{13,5},{14,6},{15,7},{0,8},{1,9},... | collective-permute-start | bytes 884744 | tf_op jit(solution)/shard_map/ppermute | solution.py:264
  62.6 0.5 collective-permute-start.3
  63.1 14.1 %all_to_all.10.fits_ref = f32[32,8,128]{2,1,0:T(8,128)S(1)} all-to-all(f32[32,8,128]{2,1,0:T(8,128)S(1)} %get-tuple-element.22), channel_id=1, replica_groups=mesh['row'=16,'col'=2] {'row','col'}, dimensions={0} | all-to-all | bytes 262144 | tf_op jit(solution)/shard_map/all_to_all | solution.py:353
  77.2 0.0 collective-permute-done.5.refs_3_
  77.2 0.0 collective-permute-done.4.refs_2_
  77.2 0.0 collective-permute-done.3.refs_1_
  77.3 0.2 collective-permute-start.6
  77.4 0.4 collective-permute-start.7
  77.8 0.1 collective-permute-start.8
  77.9 0.4 collective-permute-start.9
  78.3 8.5 %steps_and_even_tiles.1 = (f32[768,6144]{1,0:T(8,128)}, f32[3,3,32]{2,1,0:T(4,128)}, f32[9,64,128]{2,1,0:T(8,128)S(1)}, bf16[768,192]{1,0:T(8,128)(2,1)S(1)}) custom-call(s32[1]{0:T(128)} %bitcast.row, s32[1]{0:T(128)} %bitcast.1.col, f32[32,8,128]{2,1,0:T(8,128)S(1)} %all_to_all.10.fits_ref, bf16[3,64,768]{2,1,0:T(8,128)(2,1)S(1)} %get-tuple-element.23.rows_ref, ...), custom_call_target="tpu_custom_call" | custom-call | flops 905969664 | bytes 9437184 | tf_op jit(solution)/shard_map/steps_and_even_tiles/pallas_call | solution.py:367
  86.9 0.0 collective-permute-done.6.refs_0_
  86.9 0.0 collective-permute-done.7.refs_1_
  86.9 0.0 collective-permute-done.8.refs_2_
  86.9 0.0 collective-permute-done.9.refs_3_
  86.9 5.5 %odd_tiles.1 = f32[768,6144]{1,0:T(8,128)} custom-call(s32[1]{0:T(128)} %bitcast.row, f32[768,6144]{1,0:T(8,128)} %get-tuple-element.31.before_ref, f32[9,64,128]{2,1,0:T(8,128)S(1)} %get-tuple-element.32.wide_ref, bf16[768,192]{1,0:T(8,128)(2,1)S(1)} %get-tuple-element.33.rows_dev_ref, ...), custom_call_target="tpu_custom_call", output_to_operand_aliasing={{}: (1, {})} | custom-call | flops 905969664 | bytes 9437184 | tf_op jit(solution)/shard_map/odd_tiles/pallas_call | solution.py:382
  (1 shorter events, 0.0 us)
Async XLA Ops:
  2.6 40.5 %all-to-all-start = ((f32[32,1,2304]{2,1,0:T(1,128)}), f32[32,1,2304]{2,1,0:T(1,128)S(1)}, u32[]{:S(2)}, u32[]{:S(2)}) async-start(f32[32,1,2304]{2,1,0:T(1,128)} %get-tuple-element.19), calls=%async_computation | async-start | bytes 589824 | tf_op jit(solution)/shard_map/all_to_all | solution.py:290
  9.9 16.4 %collective-permute-start.1 = (bf16[3,32,768]{2,1,0:T(8,128)(2,1)S(1)}, bf16[3,32,768]{2,1,0:T(8,128)(2,1)S(1)}, u32[]{:S(2)}, u32[]{:S(2)}) collective-permute-start(bf16[3,32,768]{2,1,0:T(8,128)(2,1)S(1)} %get-tuple-element.21.own_ref), channel_id=1, source_target_pairs={{16,0},{17,1},{18,2},{19,3},{20,4},{21,5},{22,6},{23,7},{24,8},{25... | collective-permute-start | bytes 442376 | tf_op jit(solution)/shard_map/ppermute | solution.py:264
  12.6 46.4 %collective-permute-start = (bf16[3,32,768]{2,1,0:T(8,128)(2,1)S(1)}, bf16[3,32,768]{2,1,0:T(8,128)(2,1)S(1)}, u32[]{:S(2)}, u32[]{:S(2)}) collective-permute-start(bf16[3,32,768]{2,1,0:T(8,128)(2,1)S(1)} %get-tuple-element.21.own_ref), channel_id=1, source_target_pairs={{1,0},{0,1},{3,2},{2,3},{5,4},{4,5},{7,6},{6,7},{9,8},{8,9},{11,10... | collective-permute-start | bytes 442376 | tf_op jit(solution)/shard_map/ppermute | solution.py:264
  26.3 33.2 %collective-permute-start.2 = (bf16[3,32,768]{2,1,0:T(8,128)(2,1)S(1)}, bf16[3,32,768]{2,1,0:T(8,128)(2,1)S(1)}, u32[]{:S(2)}, u32[]{:S(2)}) collective-permute-start(bf16[3,32,768]{2,1,0:T(8,128)(2,1)S(1)} %collective-permute-done.1.refs_0_), channel_id=1, source_target_pairs={{0,1},{2,3},{4,5},{6,7},{8,9},{10,11},{12,13},{14,15},{17,16},{19,... | collective-permute-start | bytes 442376 | tf_op jit(solution)/shard_map/ppermute | solution.py:264
  36.2 6.9 %copy-start = (f32[768,6144]{1,0:T(8,128)}, f32[768,6144]{1,0:T(8,128)S(1)}, u32[]{:S(2)}) copy-start(f32[768,6144]{1,0:T(8,128)S(1)} %fetch_inverse.1.inv_ref) | copy-start | bytes 56623108
  43.0 6.4 %copy-start.1 = (f32[768,6144]{1,0:T(8,128)S(1)}, f32[768,6144]{1,0:T(8,128)}, u32[]{:S(2)}) copy-start(f32[768,6144]{1,0:T(8,128)} %copy-done) | copy-start | bytes 56623108
  59.6 17.7 %collective-permute-start.5 = (bf16[3,64,768]{2,1,0:T(8,128)(2,1)S(1)}, bf16[3,64,768]{2,1,0:T(8,128)(2,1)S(1)}, u32[]{:S(2)}, u32[]{:S(2)}) collective-permute-start(bf16[3,64,768]{2,1,0:T(8,128)(2,1)S(1)} %assemble.1.refs_0_), channel_id=1, source_target_pairs={{12,0},{13,1},{14,2},{15,3},{8,4},{9,5},{10,6},{11,7},{4,8},{5,9},... | collective-permute-start | bytes 884744 | tf_op jit(solution)/shard_map/ppermute | solution.py:264
  59.6 17.6 %collective-permute-start.4 = (bf16[3,64,768]{2,1,0:T(8,128)(2,1)S(1)}, bf16[3,64,768]{2,1,0:T(8,128)(2,1)S(1)}, u32[]{:S(2)}, u32[]{:S(2)}) collective-permute-start(bf16[3,64,768]{2,1,0:T(8,128)(2,1)S(1)} %assemble.1.refs_0_), channel_id=1, source_target_pairs={{8,0},{9,1},{10,2},{11,3},{12,4},{13,5},{14,6},{15,7},{0,8},{1,9},... | collective-permute-start | bytes 884744 | tf_op jit(solution)/shard_map/ppermute | solution.py:264
  62.6 14.7 %collective-permute-start.3 = (bf16[3,64,768]{2,1,0:T(8,128)(2,1)S(1)}, bf16[3,64,768]{2,1,0:T(8,128)(2,1)S(1)}, u32[]{:S(2)}, u32[]{:S(2)}) collective-permute-start(bf16[3,64,768]{2,1,0:T(8,128)(2,1)S(1)} %assemble.1.refs_0_), channel_id=1, source_target_pairs={{4,0},{5,1},{6,2},{7,3},{0,4},{1,5},{2,6},{3,7},{12,8},{13,9},{14,... | collective-permute-start | bytes 884744 | tf_op jit(solution)/shard_map/ppermute | solution.py:264
  77.3 9.6 %collective-permute-start.6 = (bf16[3,64,768]{2,1,0:T(8,128)(2,1)S(1)}, bf16[3,64,768]{2,1,0:T(8,128)(2,1)S(1)}, u32[]{:S(2)}, u32[]{:S(2)}) collective-permute-start(bf16[3,64,768]{2,1,0:T(8,128)(2,1)S(1)} %assemble.1.refs_0_), channel_id=1, source_target_pairs={{2,0},{3,1},{0,2},{1,3},{6,4},{7,5},{4,6},{5,7},{10,8},{11,9},{8,1... | collective-permute-start | bytes 884744 | tf_op jit(solution)/shard_map/ppermute | solution.py:264
  77.4 9.4 %collective-permute-start.7 = (bf16[3,64,768]{2,1,0:T(8,128)(2,1)S(1)}, bf16[3,64,768]{2,1,0:T(8,128)(2,1)S(1)}, u32[]{:S(2)}, u32[]{:S(2)}) collective-permute-start(bf16[3,64,768]{2,1,0:T(8,128)(2,1)S(1)} %collective-permute-done.3.refs_1_), channel_id=1, source_target_pairs={{2,0},{3,1},{0,2},{1,3},{6,4},{7,5},{4,6},{5,7},{10,8},{11,9},{8,1... | collective-permute-start | bytes 884744 | tf_op jit(solution)/shard_map/ppermute | solution.py:264
  77.8 9.1 %collective-permute-start.8 = (bf16[3,64,768]{2,1,0:T(8,128)(2,1)S(1)}, bf16[3,64,768]{2,1,0:T(8,128)(2,1)S(1)}, u32[]{:S(2)}, u32[]{:S(2)}) collective-permute-start(bf16[3,64,768]{2,1,0:T(8,128)(2,1)S(1)} %collective-permute-done.4.refs_2_), channel_id=1, source_target_pairs={{2,0},{3,1},{0,2},{1,3},{6,4},{7,5},{4,6},{5,7},{10,8},{11,9},{8,1... | collective-permute-start | bytes 884744 | tf_op jit(solution)/shard_map/ppermute | solution.py:264
  77.9 9.0 %collective-permute-start.9 = (bf16[3,64,768]{2,1,0:T(8,128)(2,1)S(1)}, bf16[3,64,768]{2,1,0:T(8,128)(2,1)S(1)}, u32[]{:S(2)}, u32[]{:S(2)}) collective-permute-start(bf16[3,64,768]{2,1,0:T(8,128)(2,1)S(1)} %collective-permute-done.5.refs_3_), channel_id=1, source_target_pairs={{2,0},{3,1},{0,2},{1,3},{6,4},{7,5},{4,6},{5,7},{10,8},{11,9},{8,1... | collective-permute-start | bytes 884744 | tf_op jit(solution)/shard_map/ppermute | solution.py:264

commit v10 on v5

--- a/solution.py
+++ b/solution.py
@@ -16,6 +16,10 @@
 
 def vmem():
     return pl.BlockSpec(memory_space=pltpu.VMEM)
+
+
+def hbm():
+    return pl.BlockSpec(memory_space=pl.ANY)
 
 
 def smem():
@@ -39,37 +43,68 @@
     return (product[16:19] + product[8:11]) + product[0:3]
 
 
-def partial_centre_kernel(frame_total, col, rot_ref, coords_ref, out_ref):
-    local = coords_ref.shape[1]
-    block = lax.broadcasted_iota(jnp.int32, rot_ref.shape, 2) // local
-    rot = jnp.where(block == col[0], rot_ref[...], 0.0)
-    coords = jnp.concatenate([coords_ref[...]] * (frame_total // local), axis=1)
-    centre = rotated_sum(rot, coords) * (1.0 / frame_total)
-    out_ref[...] = jnp.broadcast_to(centre[None], out_ref.shape)
-
-
-def centre_of(parts_ref, row, col_count):
-    total = parts_ref[row * col_count]
-    for place in range(1, col_count):
-        total = total + parts_ref[row * col_count + place]
-    return total
-
-
 def put_block(out_ref, block, value):
     local = value.shape[1]
     out_ref[:, pl.ds(pl.multiple_of(block * local, local), local), :] = value
 
 
-def assemble_kernel(members, row, *refs):
-    blocks, out_ref = refs[:-1], refs[-1]
-    for step, ref in enumerate(blocks):
-        put_block(out_ref, lax.rem(row[0] // members + step, len(blocks)), ref[...])
-
-
-def weighted_fit_kernel(members, row, col, inv_ref, parts_ref, *refs):
-    coords_refs, (out_ref, rows_ref, strips_ref, wide_ref, weighted_ref, sems) = refs[:-6], refs[-6:]
+def rows_kernel(col, rot_hbm, coords_hbm, *refs):
+    others, (rows_ref, centre_ref, rot_ref, sems) = refs[:-4], refs[-4:]
+    local = coords_hbm.shape[1]
+    own_rows = rows_ref.at[:, pl.ds(pl.multiple_of(col[0] * local, local), local), :]
+    copies = [
+        pltpu.make_async_copy(rot_hbm, rot_ref, sems.at[0]),
+        pltpu.make_async_copy(coords_hbm, own_rows, sems.at[1]),
+    ]
+    for copy in copies:
+        copy.start()
+    for shift, ref in enumerate(others):
+        put_block(rows_ref, lax.rem(col[0] + 1 + shift, len(others) + 1), ref[...])
+    for copy in copies:
+        copy.wait()
+    centre = rotated_sum(rot_ref[...], rows_ref[...]) * (1.0 / rows_ref.shape[1])
+    flat = jnp.concatenate([centre[comp : comp + 1, :] for comp in range(3)], axis=1)
+    centre_ref[...] = jnp.broadcast_to(flat[None], centre_ref.shape)
+
+
+def pick_kernel(members, step, row, col, rows_ref, *refs):
+    far_refs, out_ref = refs[:-1], refs[-1]
+    col_count, local = len(far_refs) + 1, out_ref.shape[1]
+    index = lax.rem(col[0] + 2 * col_count - row[0] // members - step, col_count)
+
+    @pl.when(index == 0)
+    def _():
+        out_ref[...] = rows_ref[:, pl.ds(pl.multiple_of(col[0] * local, local), local), :]
+
+    for shift, ref in enumerate(far_refs):
+
+        @pl.when(index == shift + 1)
+        def _(ref=ref):
+            out_ref[...] = ref[...]
+
+
+def assemble_kernel(members, row, col, centres_ref, rows_ref, *refs):
+    sources, out_ref = refs[:-1], refs[-1]
+    far_refs, across_refs = sources[: len(sources) // 2], sources[len(sources) // 2 :]
+    col_count = len(far_refs) + 1
+    distance = lax.rem(col[0] + col_count - row[0] // members, col_count)
+
+    @pl.when(distance == 0)
+    def _():
+        out_ref[...] = rows_ref[...]
+
+    for step, ref in enumerate(far_refs):
+
+        @pl.when(distance == step + 1)
+        def _(ref=ref):
+            put_block(out_ref, col[0], ref[...])
+            for shift, across_ref in enumerate(across_refs):
+                put_block(out_ref, lax.rem(col[0] + 1 + shift, col_count), across_ref[...])
+
+
+def weighted_fit_kernel(members, row, col, inv_ref, centres_ref, rows_ref, out_ref, strips_ref, wide_ref, weighted_ref, sems):
     strips, height, col_width = strips_ref.shape
-    width = parts_ref.shape[2]
+    width = rows_ref.shape[2]
 
     def fetch(strip):
         rows = pl.ds(pl.multiple_of(strip * height, height), height)
@@ -78,12 +113,10 @@
     for strip in range(strips):
         fetch(strip).start()
     for block in range(members):
-        centre = centre_of(parts_ref, col[0] * members + block, len(coords_refs))
+        centre = centres_ref[col[0] * members + block]
         for comp in range(3):
-            factor = jnp.broadcast_to(centre[comp : comp + 1, :], (8, width))
+            factor = jnp.broadcast_to(centre[:, comp * width : (comp + 1) * width], (8, width))
             wide_ref[comp, :, block * width : (block + 1) * width] = factor
-    for shift, ref in enumerate(coords_refs):
-        put_block(rows_ref, lax.rem(col[0] + shift, len(coords_refs)), ref[...])
     lane = lax.broadcasted_iota(jnp.int32, (height, LANES), 1)
     chunks = col_width // LANES
 
@@ -138,35 +171,31 @@
     return current
 
 
-def put_deviations(wide_ref, coords_ref, centre, chunk, dev_ref):
-    frame_total = coords_ref.shape[1]
+def put_deviations(wide_ref, coords_ref, centres_ref, row, chunk, dev_ref):
+    frame_total, width = coords_ref.shape[1:]
     span = slice(chunk * LANES, (chunk + 1) * LANES)
     coords = [coords_ref[part, :, span].astype(F32) for part in range(3)]
     for comp in range(3):
         moved = wide_ref[3 * comp] * coords[0]
         moved = moved + wide_ref[3 * comp + 1] * coords[1]
         moved = moved + wide_ref[3 * comp + 2] * coords[2]
-        value = moved - centre[comp : comp + 1, span]
+        start = comp * width + chunk * LANES
+        value = moved - centres_ref[row, :, start : start + LANES]
         dev_ref[comp * frame_total : (comp + 1) * frame_total, span] = value.astype(BF16)
 
 
-def put_tile(wide_ref, coords_ref, centre, rows_dev_ref, dev_ref, out_ref):
+def put_tile(wide_ref, coords_ref, centres_ref, row, rows_dev_ref, dev_ref, out_ref):
     width = coords_ref.shape[2]
     scale = 1.0 / (3 * coords_ref.shape[1])
     stride = 2 * LANES if width % (2 * LANES) == 0 else LANES
     for start in range(0, width, stride):
         for chunk in range(start // LANES, (start + stride) // LANES):
-            put_deviations(wide_ref, coords_ref, centre, chunk, dev_ref)
+            put_deviations(wide_ref, coords_ref, centres_ref, row, chunk, dev_ref)
         product = jnp.dot(rows_dev_ref[...], dev_ref[:, start : start + stride], preferred_element_type=F32)
         out_ref[:, start : start + stride] = product * scale
 
 
-def panel_centre(parts_ref, row, col, count, mask, col_count):
-    members = 2 * count
-    return centre_of(parts_ref, col[0] * members + (lax.rem(row[0], members) ^ mask), col_count)
-
-
-def first_tiles_kernel(count, row, col, fits_ref, rows_ref, parts_ref, *refs):
+def first_tiles_kernel(count, row, col, fits_ref, rows_ref, centres_ref, *refs):
     panel_refs = refs[:count]
     out_ref, rot_out_ref, wide_ref, rows_dev_ref, dev_ref = refs[count:]
     frame_total = rows_ref.shape[1]
@@ -185,28 +214,27 @@
         columns = jnp.concatenate(entries + [jnp.zeros((7, frame_total), F32)], axis=0).T
         for entry in range(9):
             wide_ref[entry] = jnp.broadcast_to(columns[:, entry : entry + 1], (frame_total, LANES))
-        centre = centre_of(parts_ref, row[0], frame_total // local)
         for chunk in range(rows_ref.shape[2] // LANES):
-            put_deviations(wide_ref, rows_ref, centre, chunk, dev_ref)
+            put_deviations(wide_ref, rows_ref, centres_ref, row[0], chunk, dev_ref)
         rows_dev_ref[...] = dev_ref[...].T
 
     for step in range(count):
 
         @pl.when(pl.program_id(0) == step)
         def _(step=step):
-            centre = panel_centre(parts_ref, row, col, count, 2 * step, frame_total // local)
-            put_tile(wide_ref, panel_refs[step], centre, rows_dev_ref, dev_ref, out_ref)
-
-
-def last_tiles_kernel(count, col_count, row, col, before_ref, wide_ref, rows_dev_ref, parts_ref, *refs):
+            block = col[0] * 2 * count + (lax.rem(row[0], 2 * count) ^ (2 * step))
+            put_tile(wide_ref, panel_refs[step], centres_ref, block, rows_dev_ref, dev_ref, out_ref)
+
+
+def last_tiles_kernel(count, row, col, before_ref, wide_ref, rows_dev_ref, centres_ref, *refs):
     panel_refs = refs[:count]
     out_ref, dev_ref = refs[count:]
     for step in range(count):
 
         @pl.when(pl.program_id(0) == step)
         def _(step=step):
-            centre = panel_centre(parts_ref, row, col, count, 2 * step + 1, col_count)
-            put_tile(wide_ref, panel_refs[step], centre, rows_dev_ref, dev_ref, out_ref)
+            block = col[0] * 2 * count + (lax.rem(row[0], 2 * count) ^ (2 * step + 1))
+            put_tile(wide_ref, panel_refs[step], centres_ref, block, rows_dev_ref, dev_ref, out_ref)
 
 
 def per_device(frames, rotations, inverse_cov):
@@ -221,6 +249,9 @@
     half = members // 2
     coords = jnp.transpose(frames, (1, 0, 2))
 
+    def limit(mib):
+        return pltpu.CompilerParams(vmem_limit_bytes=mib * MIB)
+
     def move(value, source_of, receives=lambda group, col: True):
         pairs = []
         for group in range(col_count):
@@ -241,54 +272,67 @@
     def limit(mib):
         return pltpu.CompilerParams(vmem_limit_bytes=mib * MIB)
 
-    panel_parts = [from_panel_row(coords, step) for step in range(col_count)]
+    def in_hbm(value):
+        return pltpu.with_memory_space_constraint(value, pltpu.HBM)
+
+    far = [move(coords, lambda g, m, c, s=step: ((g + s) % col_count, m, c)) for step in range(1, col_count)]
     others = [move(coords, lambda g, m, c, s=step: (g, m, (c + s) % col_count)) for step in range(1, col_count)]
-    repeated = pl.pallas_call(
-        functools.partial(partial_centre_kernel, frame_total),
-        out_shape=jax.ShapeDtypeStruct((device_total, 3, width), F32),
-        in_specs=[smem(), vmem(), vmem()],
-        out_specs=vmem(),
+    rows_all, repeated = pl.pallas_call(
+        rows_kernel,
+        out_shape=(
+            jax.ShapeDtypeStruct((3, frame_total, width), BF16),
+            jax.ShapeDtypeStruct((row_count, 1, 3 * width), F32),
+        ),
+        in_specs=[smem(), hbm(), hbm()] + [vmem()] * (col_count - 1),
+        out_specs=(vmem(), vmem()),
+        scratch_shapes=[pltpu.VMEM(rotations.shape, F32), pltpu.SemaphoreType.DMA((2,))],
         compiler_params=limit(8),
-        name="partial_centre",
-    )(col, rotations, coords)
-    parts = lax.all_to_all(repeated, ("row", "col"), split_axis=0, concat_axis=0, tiled=True)
-
-    _, panel_parts = lax.optimization_barrier((parts, panel_parts))
+        name="rows",
+    )(col, in_hbm(rotations), in_hbm(coords), *others)
+    centres = lax.all_to_all(repeated, "row", split_axis=0, concat_axis=0, tiled=True)
+
+    across = []
+    for step in range(1, col_count):
+        held = pl.pallas_call(
+            functools.partial(pick_kernel, members, step),
+            out_shape=jax.ShapeDtypeStruct((3, local, width), BF16),
+            in_specs=[smem(), smem()] + [vmem()] * col_count,
+            out_specs=vmem(),
+            compiler_params=limit(4),
+            name="pick",
+        )(row, col, rows_all, *far)
+        across.append(move(held, lambda g, m, c, s=step: (g, m, (c + s) % col_count), lambda g, c: g != c))
     own_block = pl.pallas_call(
         functools.partial(assemble_kernel, members),
         out_shape=jax.ShapeDtypeStruct((3, frame_total, width), BF16),
-        in_specs=[smem()] + [vmem()] * col_count,
+        in_specs=[smem(), smem()] + [vmem()] * (2 * col_count),
         out_specs=vmem(),
-        compiler_params=limit(4),
+        compiler_params=limit(8),
         name="assemble",
-    )(row, *panel_parts)
-    even_panel = [own_block] + [from_member(own_block, 2 * step) for step in range(1, members // 2)]
+    )(row, col, centres, rows_all, *far, *across)
+    evens = [own_block] + [from_member(own_block, 2 * step) for step in range(1, half)]
 
     height = 64 if width % 64 == 0 else 8
-    inverse_cov = pltpu.with_memory_space_constraint(inverse_cov, pltpu.HBM)
-    message, rows_all = pl.pallas_call(
+    message = pl.pallas_call(
         functools.partial(weighted_fit_kernel, members),
-        in_specs=[smem(), smem(), pl.BlockSpec(memory_space=pl.ANY)] + [vmem()] * (1 + col_count),
-        out_specs=(vmem(), vmem()),
+        in_specs=[smem(), smem(), hbm(), vmem(), vmem()],
+        out_specs=vmem(),
         scratch_shapes=[
             pltpu.VMEM((width // height, height, col_width), F32),
             pltpu.VMEM((3, 8, col_width), F32),
             pltpu.VMEM((width, LANES), F32),
             pltpu.SemaphoreType.DMA((width // height,)),
         ],
-        out_shape=(
-            jax.ShapeDtypeStruct((device_total, 8, 2 * frame_total), F32),
-            jax.ShapeDtypeStruct((3, frame_total, width), BF16),
-        ),
+        out_shape=jax.ShapeDtypeStruct((device_total, 8, 2 * frame_total), F32),
         compiler_params=limit(28),
         cost_estimate=pl.CostEstimate(
             flops=6 * width * col_width, bytes_accessed=4 * width * col_width, transcendentals=0
         ),
         name="weighted_fit",
-    )(row, col, inverse_cov, parts, coords, *others)
+    )(row, col, in_hbm(inverse_cov), centres, rows_all)
     fits = lax.all_to_all(message, ("row", "col"), split_axis=0, concat_axis=0, tiled=True)
-    fits, even_panel = lax.optimization_barrier((fits, even_panel))
-    odd_panel = [from_member(block, 1) for block in even_panel]
+    fits, evens = lax.optimization_barrier((fits, evens))
+    odds = [from_member(block, 1) for block in evens]
 
     def tile_spec(odd):
         return pl.BlockSpec((width, width), lambda i, row, *_: (0, lax.rem(row[0], members) ^ (2 * i + odd)))
@@ -315,9 +359,9 @@
         compiler_params=limit(16),
         cost_estimate=tiles_cost,
         name="steps_and_even_tiles",
-    )(row, col, fits, rows_all, parts, *even_panel)
+    )(row, col, fits, rows_all, centres, *evens)
     covariance = pl.pallas_call(
-        functools.partial(last_tiles_kernel, half, col_count),
+        functools.partial(last_tiles_kernel, half),
         grid_spec=pltpu.PrefetchScalarGridSpec(
             num_scalar_prefetch=2,
             grid=(half,),
@@ -330,7 +374,7 @@
         compiler_params=limit(16),
         cost_estimate=tiles_cost,
         name="odd_tiles",
-    )(row, col, half_done, wide, rows_dev, parts, *odd_panel)
+    )(row, col, half_done, wide, rows_dev, centres, *odds)
     return (covariance, transforms)
 
 

time: 66.7 us -> 61.5 us (0.922)
  local copies, waits for them, and re-layouts: 2.51 us -> 0 us
  waiting for transfers between devices: 8.22 us -> 6.22 us
  blocking collectives: 14.8 us -> 13.1 us
  Pallas kernels: 20.5 us -> 21.4 us
    all_to_all x1, waiting for transfers between devices: 5.5 us -> 1.05 us  [per_device(): lax.all_to_all(repeated, 'row', split_axis=0, concat_axis=0, tiled=True)]
    unnamed x6 -> x0, local copies, waits for them, and re-layouts: 2.51 us -> none
    ppermute x10, waiting for transfers between devices: 2.72 us -> 5.16 us  [move(): return lax.ppermute(value, ('row', 'col'), pairs)]
    all_to_all x1, blocking collectives: 14.8 us -> 13.1 us  [per_device(): lax.all_to_all(message, ('row', 'col'), split_axis=0, concat_axis=0, tile...]
    ppermute x10, starting transfers between devices: 12.3 us -> 13.6 us  [move(): return lax.ppermute(value, ('row', 'col'), pairs)]
    all_to_all x1, starting transfers between devices: 7.3 us -> 6.2 us  [per_device(): lax.all_to_all(repeated, 'row', split_axis=0, concat_axis=0, tiled=True)]
    pallas_call x2 -> x3, Pallas kernels: 5.76 us -> 6.65 us  [the longest x1 4.77 us: per_device(): pl.pallas_call(functools.partial(last_tiles_kernel, half), grid_spec=pltp...]
  transfers between devices with their start and end apart: 11 -> 11, of which waited for: 2 -> 3; matrix products, arithmetic and copies ran while one was open for 0% -> 0% of each run, Pallas kernels for 22% -> 27%
where the time goes in v10:
time: 61.5 us; the launch traced here: 61.2 us
  Pallas kernels  21.4 us (35%)
  starting transfers between devices  19.8 us (32%)
  blocking collectives  13.1 us (21%)
  waiting for transfers between devices  6.22 us (10%)
  between operations  0.72 us (1%)
    ppermute x10, starting transfers between devices, move(): return lax.ppermute(value, ('row', 'col'), pairs)  13.6 us
    all_to_all x1, blocking collectives, per_device(): lax.all_to_all(message, ('row', 'col'), split_axis=0, concat_axis=0, tile...  13.1 us
    pallas_call x1, Pallas kernels, per_device(): pl.pallas_call(functools.partial(weighted_fit_kernel, members), in_specs=...  7.48 us
    pallas_call x1, Pallas kernels, per_device(): pl.pallas_call(functools.partial(first_tiles_kernel, half), grid_spec=plt...  7.24 us
    all_to_all x1, starting transfers between devices, per_device(): lax.all_to_all(repeated, 'row', split_axis=0, concat_axis=0, tiled=True)  6.2 us
    ppermute x10, waiting for transfers between devices, move(): return lax.ppermute(value, ('row', 'col'), pairs)  5.16 us
    pallas_call x1, Pallas kernels, per_device(): pl.pallas_call(functools.partial(last_tiles_kernel, half), grid_spec=pltp...  4.77 us
    pallas_call x1, Pallas kernels, per_device(): pl.pallas_call(rows_kernel, out_shape=(jax.ShapeDtypeStruct((3, frame_tot...  1.85 us
  transfers between devices with their start and end apart: 11, of which 3 were waited for; matrix products, arithmetic and copies ran while one was open for 0% of the time, Pallas kernels for 27%

profile of v10, /device:TPU:0, one launch (start us, length us, event | category | flops | bytes accessed | tf_op | source)
XLA Modules:
  0.0 61.2 jit_solution(8179501788826954592)
XLA Ops:
  0.6 3.0 %collective-permute-start = (bf16[3,32,768]{2,1,0:T(8,128)(2,1)}, bf16[3,32,768]{2,1,0:T(8,128)(2,1)S(1)}, u32[]{:S(2)}, u32[]{:S(2)}) collective-permute-start(bf16[3,32,768]{2,1,0:T(8,128)(2,1)} %bitcast.3), channel_id=1, source_target_pairs={{1,0},{0,1},{3,2},{2,3},{5,4},{4,5},{7,6},{6,7},{9,8},{8,9},{11,10... | collective-permute-start | bytes 442376 | tf_op jit(solution)/shard_map/ppermute | solution.py:264
  3.6 2.6 %collective-permute-start.1 = (bf16[3,32,768]{2,1,0:T(8,128)(2,1)}, bf16[3,32,768]{2,1,0:T(8,128)(2,1)S(1)}, u32[]{:S(2)}, u32[]{:S(2)}) collective-permute-start(bf16[3,32,768]{2,1,0:T(8,128)(2,1)} %bitcast.4), channel_id=1, source_target_pairs={{16,0},{17,1},{18,2},{19,3},{20,4},{21,5},{22,6},{23,7},{24,8},{25... | collective-permute-start | bytes 442376 | tf_op jit(solution)/shard_map/ppermute | solution.py:264
  6.2 1.5 %collective-permute-done.refs_0_ = bf16[3,32,768]{2,1,0:T(8,128)(2,1)S(1)} collective-permute-done((bf16[3,32,768]{2,1,0:T(8,128)(2,1)}, bf16[3,32,768]{2,1,0:T(8,128)(2,1)S(1)}, u32[]{:S(2)}, u32[]{:S(2)}) %collective-permute-start) | collective-permute-done | bytes 147488 | tf_op jit(solution)/shard_map/ppermute | solution.py:264
  7.7 1.9 %rows.1 = (bf16[3,64,768]{2,1,0:T(8,128)(2,1)S(1)}, f32[16,1,2304]{2,1,0:T(1,128)}) custom-call(s32[1]{0:T(128)} %bitcast.1.col, f32[3,3,64]{2,1,0:T(4,128)} %rot_hbm.1, bf16[3,32,768]{2,1,0:T(8,128)(2,1)} %bitcast.5, bf16[3,32,768]{2,1,0:T(8,128)(2,1)S(1)} %collective-permute-done.refs_0_), custom_call_target="tpu_custom_call" | custom-call | tf_op jit(solution)/shard_map/rows/pallas_call | solution.py:280
  9.6 6.2 %all-to-all-start = ((f32[16,1,2304]{2,1,0:T(1,128)}), f32[16,1,2304]{2,1,0:T(1,128)S(1)}, u32[]{:S(2)}, u32[]{:S(2)}) async-start(f32[16,1,2304]{2,1,0:T(1,128)} %get-tuple-element.13), calls=%async_computation | async-start | bytes 294912 | tf_op jit(solution)/shard_map/all_to_all | solution.py:292
  15.8 0.0 collective-permute-done.1.refs_0_
  15.8 3.4 %collective-permute-start.2 = (bf16[3,32,768]{2,1,0:T(8,128)(2,1)S(1)}, bf16[3,32,768]{2,1,0:T(8,128)(2,1)S(1)}, u32[]{:S(2)}, u32[]{:S(2)}) collective-permute-start(bf16[3,32,768]{2,1,0:T(8,128)(2,1)S(1)} %pick.1), channel_id=1, source_target_pairs={{0,1},{2,3},{4,5},{6,7},{8,9},{10,11},{12,13},{14,15},{17,16},{19,... | collective-permute-start | bytes 442376 | tf_op jit(solution)/shard_map/ppermute | solution.py:264
  19.2 3.7 %collective-permute-done.2.refs_1_ = bf16[3,32,768]{2,1,0:T(8,128)(2,1)S(1)} collective-permute-done((bf16[3,32,768]{2,1,0:T(8,128)(2,1)S(1)}, bf16[3,32,768]{2,1,0:T(8,128)(2,1)S(1)}, u32[]{:S(2)}, u32[]{:S(2)}) %collective-permute-start.2) | collective-permute-done | bytes 147488 | tf_op jit(solution)/shard_map/ppermute | solution.py:264
  22.9 1.1 %all-to-all-done.centres_ref = f32[16,1,2304]{2,1,0:T(1,128)S(1)} async-done(((f32[16,1,2304]{2,1,0:T(1,128)}), f32[16,1,2304]{2,1,0:T(1,128)S(1)}, u32[]{:S(2)}, u32[]{:S(2)}) %all-to-all-start) | async-done | bytes 147488 | tf_op jit(solution)/shard_map/all_to_all | solution.py:292
  24.0 1.6 %collective-permute-start.5 = (bf16[3,64,768]{2,1,0:T(8,128)(2,1)S(1)}, bf16[3,64,768]{2,1,0:T(8,128)(2,1)S(1)}, u32[]{:S(2)}, u32[]{:S(2)}) collective-permute-start(bf16[3,64,768]{2,1,0:T(8,128)(2,1)S(1)} %assemble.1.refs_0_), channel_id=1, source_target_pairs={{12,0},{13,1},{14,2},{15,3},{8,4},{9,5},{10,6},{11,7},{4,8},{5,9},... | collective-permute-start | bytes 884744 | tf_op jit(solution)/shard_map/ppermute | solution.py:264
  25.5 0.6 collective-permute-start.4
  26.1 1.4 %collective-permute-start.3 = (bf16[3,64,768]{2,1,0:T(8,128)(2,1)S(1)}, bf16[3,64,768]{2,1,0:T(8,128)(2,1)S(1)}, u32[]{:S(2)}, u32[]{:S(2)}) collective-permute-start(bf16[3,64,768]{2,1,0:T(8,128)(2,1)S(1)} %assemble.1.refs_0_), channel_id=1, source_target_pairs={{4,0},{5,1},{6,2},{7,3},{0,4},{1,5},{2,6},{3,7},{12,8},{13,9},{14,... | collective-permute-start | bytes 884744 | tf_op jit(solution)/shard_map/ppermute | solution.py:264
  27.5 7.5 %weighted_fit.1 = f32[32,8,128]{2,1,0:T(8,128)S(1)} custom-call(s32[1]{0:T(128)} %bitcast.row, s32[1]{0:T(128)} %bitcast.1.col, f32[768,6144]{1,0:T(8,128)} %inv_ref.1, f32[16,1,2304]{2,1,0:T(1,128)S(1)} %all-to-all-done.centres_ref, bf16[3,64,768]{2,1,0:T(8,128)(2,1)S(1)} %get-tuple-element.14.rows_ref), custom_call_target="tpu_custom_call" | custom-call | flops 28311552 | bytes 18874368 | tf_op jit(solution)/shard_map/weighted_fit/pallas_call | solution.py:316
  35.0 13.1 %all_to_all.10.fits_ref = f32[32,8,128]{2,1,0:T(8,128)S(1)} all-to-all(f32[32,8,128]{2,1,0:T(8,128)S(1)} %weighted_fit.1), channel_id=1, replica_groups=mesh['row'=16,'col'=2] {'row','col'}, dimensions={0} | all-to-all | bytes 262144 | tf_op jit(solution)/shard_map/all_to_all | solution.py:333
  48.1 0.0 collective-permute-done.5.refs_3_
  48.1 0.0 collective-permute-done.4.refs_2_
  48.1 0.0 collective-permute-done.3.refs_1_
  48.1 0.1 collective-permute-start.6
  48.2 0.5 collective-permute-start.7
  48.7 0.1 collective-permute-start.8
  48.8 0.4 collective-permute-start.9
  49.2 7.2 %steps_and_even_tiles.1 = (f32[768,6144]{1,0:T(8,128)}, f32[3,3,32]{2,1,0:T(4,128)}, f32[9,64,128]{2,1,0:T(8,128)S(1)}, bf16[768,192]{1,0:T(8,128)(2,1)S(1)}) custom-call(s32[1]{0:T(128)} %bitcast.row, s32[1]{0:T(128)} %bitcast.1.col, f32[32,8,128]{2,1,0:T(8,128)S(1)} %all_to_all.10.fits_ref, bf16[3,64,768]{2,1,0:T(8,128)(2,1)S(1)} %get-tuple-element.14.rows_ref, ...), custom_call_target="tpu_custom_call" | custom-call | flops 905969664 | bytes 9437184 | tf_op jit(solution)/shard_map/steps_and_even_tiles/pallas_call | solution.py:344
  56.4 0.0 collective-permute-done.6.refs_0_
  56.5 0.0 collective-permute-done.7.refs_1_
  56.5 0.0 collective-permute-done.8.refs_2_
  56.5 0.0 collective-permute-done.9.refs_3_
  56.5 4.8 %odd_tiles.1 = f32[768,6144]{1,0:T(8,128)} custom-call(s32[1]{0:T(128)} %bitcast.row, s32[1]{0:T(128)} %bitcast.1.col, f32[768,6144]{1,0:T(8,128)} %get-tuple-element.20.before_ref, f32[9,64,128]{2,1,0:T(8,128)S(1)} %get-tuple-element.21.wide_ref, bf16[768,192]{1,0:T(8,128)(2,1)S(1)} %get-tuple-element.22.rows_dev_ref, ...), custom_call_target="tpu_custom_call", output_to_operand_aliasing={{}: (2, {})} | custom-call | flops 905969664 | bytes 9437184 | tf_op jit(solution)/shard_map/odd_tiles/pallas_call | solution.py:363
  (2 shorter events, 0.1 us)
Async XLA Ops:
  0.6 7.1 %collective-permute-start = (bf16[3,32,768]{2,1,0:T(8,128)(2,1)}, bf16[3,32,768]{2,1,0:T(8,128)(2,1)S(1)}, u32[]{:S(2)}, u32[]{:S(2)}) collective-permute-start(bf16[3,32,768]{2,1,0:T(8,128)(2,1)} %bitcast.3), channel_id=1, source_target_pairs={{1,0},{0,1},{3,2},{2,3},{5,4},{4,5},{7,6},{6,7},{9,8},{8,9},{11,10... | collective-permute-start | bytes 442376 | tf_op jit(solution)/shard_map/ppermute | solution.py:264
  3.6 12.1 %collective-permute-start.1 = (bf16[3,32,768]{2,1,0:T(8,128)(2,1)}, bf16[3,32,768]{2,1,0:T(8,128)(2,1)S(1)}, u32[]{:S(2)}, u32[]{:S(2)}) collective-permute-start(bf16[3,32,768]{2,1,0:T(8,128)(2,1)} %bitcast.4), channel_id=1, source_target_pairs={{16,0},{17,1},{18,2},{19,3},{20,4},{21,5},{22,6},{23,7},{24,8},{25... | collective-permute-start | bytes 442376 | tf_op jit(solution)/shard_map/ppermute | solution.py:264
  9.6 14.4 %all-to-all-start = ((f32[16,1,2304]{2,1,0:T(1,128)}), f32[16,1,2304]{2,1,0:T(1,128)S(1)}, u32[]{:S(2)}, u32[]{:S(2)}) async-start(f32[16,1,2304]{2,1,0:T(1,128)} %get-tuple-element.13), calls=%async_computation | async-start | bytes 294912 | tf_op jit(solution)/shard_map/all_to_all | solution.py:292
  15.8 7.1 %collective-permute-start.2 = (bf16[3,32,768]{2,1,0:T(8,128)(2,1)S(1)}, bf16[3,32,768]{2,1,0:T(8,128)(2,1)S(1)}, u32[]{:S(2)}, u32[]{:S(2)}) collective-permute-start(bf16[3,32,768]{2,1,0:T(8,128)(2,1)S(1)} %pick.1), channel_id=1, source_target_pairs={{0,1},{2,3},{4,5},{6,7},{8,9},{10,11},{12,13},{14,15},{17,16},{19,... | collective-permute-start | bytes 442376 | tf_op jit(solution)/shard_map/ppermute | solution.py:264
  24.0 24.1 %collective-permute-start.5 = (bf16[3,64,768]{2,1,0:T(8,128)(2,1)S(1)}, bf16[3,64,768]{2,1,0:T(8,128)(2,1)S(1)}, u32[]{:S(2)}, u32[]{:S(2)}) collective-permute-start(bf16[3,64,768]{2,1,0:T(8,128)(2,1)S(1)} %assemble.1.refs_0_), channel_id=1, source_target_pairs={{12,0},{13,1},{14,2},{15,3},{8,4},{9,5},{10,6},{11,7},{4,8},{5,9},... | collective-permute-start | bytes 884744 | tf_op jit(solution)/shard_map/ppermute | solution.py:264
  25.5 22.6 %collective-permute-start.4 = (bf16[3,64,768]{2,1,0:T(8,128)(2,1)S(1)}, bf16[3,64,768]{2,1,0:T(8,128)(2,1)S(1)}, u32[]{:S(2)}, u32[]{:S(2)}) collective-permute-start(bf16[3,64,768]{2,1,0:T(8,128)(2,1)S(1)} %assemble.1.refs_0_), channel_id=1, source_target_pairs={{8,0},{9,1},{10,2},{11,3},{12,4},{13,5},{14,6},{15,7},{0,8},{1,9},... | collective-permute-start | bytes 884744 | tf_op jit(solution)/shard_map/ppermute | solution.py:264
  26.1 22.0 %collective-permute-start.3 = (bf16[3,64,768]{2,1,0:T(8,128)(2,1)S(1)}, bf16[3,64,768]{2,1,0:T(8,128)(2,1)S(1)}, u32[]{:S(2)}, u32[]{:S(2)}) collective-permute-start(bf16[3,64,768]{2,1,0:T(8,128)(2,1)S(1)} %assemble.1.refs_0_), channel_id=1, source_target_pairs={{4,0},{5,1},{6,2},{7,3},{0,4},{1,5},{2,6},{3,7},{12,8},{13,9},{14,... | collective-permute-start | bytes 884744 | tf_op jit(solution)/shard_map/ppermute | solution.py:264
  48.1 8.3 %collective-permute-start.6 = (bf16[3,64,768]{2,1,0:T(8,128)(2,1)S(1)}, bf16[3,64,768]{2,1,0:T(8,128)(2,1)S(1)}, u32[]{:S(2)}, u32[]{:S(2)}) collective-permute-start(bf16[3,64,768]{2,1,0:T(8,128)(2,1)S(1)} %assemble.1.refs_0_), channel_id=1, source_target_pairs={{2,0},{3,1},{0,2},{1,3},{6,4},{7,5},{4,6},{5,7},{10,8},{11,9},{8,1... | collective-permute-start | bytes 884744 | tf_op jit(solution)/shard_map/ppermute | solution.py:264
  48.2 8.3 %collective-permute-start.7 = (bf16[3,64,768]{2,1,0:T(8,128)(2,1)S(1)}, bf16[3,64,768]{2,1,0:T(8,128)(2,1)S(1)}, u32[]{:S(2)}, u32[]{:S(2)}) collective-permute-start(bf16[3,64,768]{2,1,0:T(8,128)(2,1)S(1)} %collective-permute-done.3.refs_1_), channel_id=1, source_target_pairs={{2,0},{3,1},{0,2},{1,3},{6,4},{7,5},{4,6},{5,7},{10,8},{11,9},{8,1... | collective-permute-start | bytes 884744 | tf_op jit(solution)/shard_map/ppermute | solution.py:264
  48.7 7.8 %collective-permute-start.8 = (bf16[3,64,768]{2,1,0:T(8,128)(2,1)S(1)}, bf16[3,64,768]{2,1,0:T(8,128)(2,1)S(1)}, u32[]{:S(2)}, u32[]{:S(2)}) collective-permute-start(bf16[3,64,768]{2,1,0:T(8,128)(2,1)S(1)} %collective-permute-done.4.refs_2_), channel_id=1, source_target_pairs={{2,0},{3,1},{0,2},{1,3},{6,4},{7,5},{4,6},{5,7},{10,8},{11,9},{8,1... | collective-permute-start | bytes 884744 | tf_op jit(solution)/shard_map/ppermute | solution.py:264
  48.8 7.7 %collective-permute-start.9 = (bf16[3,64,768]{2,1,0:T(8,128)(2,1)S(1)}, bf16[3,64,768]{2,1,0:T(8,128)(2,1)S(1)}, u32[]{:S(2)}, u32[]{:S(2)}) collective-permute-start(bf16[3,64,768]{2,1,0:T(8,128)(2,1)S(1)} %collective-permute-done.5.refs_3_), channel_id=1, source_target_pairs={{2,0},{3,1},{0,2},{1,3},{6,4},{7,5},{4,6},{5,7},{10,8},{11,9},{8,1... | collective-permute-start | bytes 884744 | tf_op jit(solution)/shard_map/ppermute | solution.py:264

commit v11 on v10

--- a/solution.py
+++ b/solution.py
@@ -48,58 +48,38 @@
     out_ref[:, pl.ds(pl.multiple_of(block * local, local), local), :] = value
 
 
-def rows_kernel(col, rot_hbm, coords_hbm, *refs):
-    others, (rows_ref, centre_ref, rot_ref, sems) = refs[:-4], refs[-4:]
-    local = coords_hbm.shape[1]
-    own_rows = rows_ref.at[:, pl.ds(pl.multiple_of(col[0] * local, local), local), :]
+def load_kernel(rot_hbm, coords_hbm, rot_ref, coords_ref, sems):
     copies = [
         pltpu.make_async_copy(rot_hbm, rot_ref, sems.at[0]),
-        pltpu.make_async_copy(coords_hbm, own_rows, sems.at[1]),
+        pltpu.make_async_copy(coords_hbm, coords_ref, sems.at[1]),
     ]
     for copy in copies:
         copy.start()
-    for shift, ref in enumerate(others):
-        put_block(rows_ref, lax.rem(col[0] + 1 + shift, len(others) + 1), ref[...])
     for copy in copies:
         copy.wait()
+
+
+def rows_kernel(col, rot_ref, *refs):
+    blocks, (rows_ref, centre_ref) = refs[:-2], refs[-2:]
+    for shift, ref in enumerate(blocks):
+        put_block(rows_ref, lax.rem(col[0] + shift, len(blocks)), ref[...])
     centre = rotated_sum(rot_ref[...], rows_ref[...]) * (1.0 / rows_ref.shape[1])
     flat = jnp.concatenate([centre[comp : comp + 1, :] for comp in range(3)], axis=1)
     centre_ref[...] = jnp.broadcast_to(flat[None], centre_ref.shape)
 
 
-def pick_kernel(members, step, row, col, rows_ref, *refs):
+def assemble_kernel(members, row, col, centres_ref, rows_ref, *refs):
     far_refs, out_ref = refs[:-1], refs[-1]
-    col_count, local = len(far_refs) + 1, out_ref.shape[1]
-    index = lax.rem(col[0] + 2 * col_count - row[0] // members - step, col_count)
-
-    @pl.when(index == 0)
-    def _():
-        out_ref[...] = rows_ref[:, pl.ds(pl.multiple_of(col[0] * local, local), local), :]
-
-    for shift, ref in enumerate(far_refs):
-
-        @pl.when(index == shift + 1)
-        def _(ref=ref):
-            out_ref[...] = ref[...]
-
-
-def assemble_kernel(members, row, col, centres_ref, rows_ref, *refs):
-    sources, out_ref = refs[:-1], refs[-1]
-    far_refs, across_refs = sources[: len(sources) // 2], sources[len(sources) // 2 :]
-    col_count = len(far_refs) + 1
-    distance = lax.rem(col[0] + col_count - row[0] // members, col_count)
-
-    @pl.when(distance == 0)
+    group = row[0] // members
+
+    @pl.when(group == col[0])
     def _():
         out_ref[...] = rows_ref[...]
 
-    for step, ref in enumerate(far_refs):
-
-        @pl.when(distance == step + 1)
-        def _(ref=ref):
-            put_block(out_ref, col[0], ref[...])
-            for shift, across_ref in enumerate(across_refs):
-                put_block(out_ref, lax.rem(col[0] + 1 + shift, col_count), across_ref[...])
+    @pl.when(group != col[0])
+    def _():
+        for shift, ref in enumerate(far_refs):
+            put_block(out_ref, lax.rem(group + shift, len(far_refs)), ref[...])
 
 
 def weighted_fit_kernel(members, row, col, inv_ref, centres_ref, rows_ref, out_ref, strips_ref, wide_ref, weighted_ref, sems):
@@ -191,8 +171,11 @@
     for start in range(0, width, stride):
         for chunk in range(start // LANES, (start + stride) // LANES):
             put_deviations(wide_ref, coords_ref, centres_ref, row, chunk, dev_ref)
-        product = jnp.dot(rows_dev_ref[...], dev_ref[:, start : start + stride], preferred_element_type=F32)
-        out_ref[:, start : start + stride] = product * scale
+        span = slice(start, start + stride)
+        for first in range(0, rows_dev_ref.shape[0], LANES):
+            strip = slice(first, first + LANES)
+            product = jnp.dot(rows_dev_ref[strip, :], dev_ref[:, span], preferred_element_type=F32)
+            out_ref[strip, span] = product * scale
 
 
 def first_tiles_kernel(count, row, col, fits_ref, rows_ref, centres_ref, *refs):
@@ -275,41 +258,41 @@
     def in_hbm(value):
         return pltpu.with_memory_space_constraint(value, pltpu.HBM)
 
-    far = [move(coords, lambda g, m, c, s=step: ((g + s) % col_count, m, c)) for step in range(1, col_count)]
     others = [move(coords, lambda g, m, c, s=step: (g, m, (c + s) % col_count)) for step in range(1, col_count)]
+    far = [
+        move(coords, lambda g, m, c, s=step: (c, m, (g + s) % col_count), lambda g, c: g != c)
+        for step in range(col_count)
+    ]
+    rot_here, coords_here = pl.pallas_call(
+        load_kernel,
+        out_shape=(jax.ShapeDtypeStruct(rotations.shape, F32), jax.ShapeDtypeStruct(coords.shape, BF16)),
+        in_specs=[hbm(), hbm()],
+        out_specs=(vmem(), vmem()),
+        scratch_shapes=[pltpu.SemaphoreType.DMA((2,))],
+        compiler_params=limit(4),
+        name="load",
+    )(in_hbm(rotations), in_hbm(coords))
     rows_all, repeated = pl.pallas_call(
         rows_kernel,
         out_shape=(
             jax.ShapeDtypeStruct((3, frame_total, width), BF16),
             jax.ShapeDtypeStruct((row_count, 1, 3 * width), F32),
         ),
-        in_specs=[smem(), hbm(), hbm()] + [vmem()] * (col_count - 1),
+        in_specs=[smem()] + [vmem()] * (1 + col_count),
         out_specs=(vmem(), vmem()),
-        scratch_shapes=[pltpu.VMEM(rotations.shape, F32), pltpu.SemaphoreType.DMA((2,))],
         compiler_params=limit(8),
         name="rows",
-    )(col, in_hbm(rotations), in_hbm(coords), *others)
+    )(col, rot_here, coords_here, *others)
     centres = lax.all_to_all(repeated, "row", split_axis=0, concat_axis=0, tiled=True)
 
-    across = []
-    for step in range(1, col_count):
-        held = pl.pallas_call(
-            functools.partial(pick_kernel, members, step),
-            out_shape=jax.ShapeDtypeStruct((3, local, width), BF16),
-            in_specs=[smem(), smem()] + [vmem()] * col_count,
-            out_specs=vmem(),
-            compiler_params=limit(4),
-            name="pick",
-        )(row, col, rows_all, *far)
-        across.append(move(held, lambda g, m, c, s=step: (g, m, (c + s) % col_count), lambda g, c: g != c))
     own_block = pl.pallas_call(
         functools.partial(assemble_kernel, members),
         out_shape=jax.ShapeDtypeStruct((3, frame_total, width), BF16),
-        in_specs=[smem(), smem()] + [vmem()] * (2 * col_count),
+        in_specs=[smem(), smem()] + [vmem()] * (2 + col_count),
         out_specs=vmem(),
         compiler_params=limit(8),
         name="assemble",
-    )(row, col, centres, rows_all, *far, *across)
+    )(row, col, centres, rows_all, *far)
     evens = [own_block] + [from_member(own_block, 2 * step) for step in range(1, half)]
 
     height = 64 if width % 64 == 0 else 8

time: 61.5 us -> 67 us (1.089)
  blocking collectives: 13.1 us -> 16.6 us
  starting transfers between devices: 19.8 us -> 21.9 us
    all_to_all x1, blocking collectives: 13.1 us -> 16.6 us  [per_device(): lax.all_to_all(message, ('row', 'col'), split_axis=0, concat_axis=0, tile...]
    ppermute x10, starting transfers between devices: 13.6 us -> 15.7 us  [move(): return lax.ppermute(value, ('row', 'col'), pairs)]
    all_to_all x1, waiting for transfers between devices: 1.05 us -> 0.01 us  [per_device(): lax.all_to_all(repeated, 'row', split_axis=0, concat_axis=0, tiled=True)]
    ppermute x10, waiting for transfers between devices: 5.16 us -> 6.18 us  [move(): return lax.ppermute(value, ('row', 'col'), pairs)]
    pallas_call x1, Pallas kernels: 1.85 us -> 0.91 us  [per_device(): pl.pallas_call(rows_kernel, out_shape=(jax.ShapeDtypeStruct((3, frame_tot...]
    pallas_call x1, Pallas kernels: 0.03 us -> 0.96 us  [per_device(): pl.pallas_call(load_kernel, out_shape=(jax.ShapeDtypeStruct(rotations.sha...]
  transfers between devices with their start and end apart: 11 -> 11, of which waited for: 3 -> 2; matrix products, arithmetic and copies ran while one was open for 0% -> 0% of each run, Pallas kernels for 27% -> 23%
where the time goes in v11:
time: 67 us; the launch traced here: 66.8 us
  starting transfers between devices  21.9 us (33%)
  Pallas kernels  21.4 us (32%)
  blocking collectives  16.6 us (25%)
  waiting for transfers between devices  6.19 us (9%)
  between operations  0.71 us (1%)
    all_to_all x1, blocking collectives, per_device(): lax.all_to_all(message, ('row', 'col'), split_axis=0, concat_axis=0, tile...  16.6 us
    ppermute x10, starting transfers between devices, move(): return lax.ppermute(value, ('row', 'col'), pairs)  15.7 us
    pallas_call x1, Pallas kernels, per_device(): pl.pallas_call(functools.partial(weighted_fit_kernel, members), in_specs=...  7.48 us
    pallas_call x1, Pallas kernels, per_device(): pl.pallas_call(functools.partial(first_tiles_kernel, half), grid_spec=plt...  7.22 us
    all_to_all x1, starting transfers between devices, per_device(): lax.all_to_all(repeated, 'row', split_axis=0, concat_axis=0, tiled=True)  6.18 us
    ppermute x10, waiting for transfers between devices, move(): return lax.ppermute(value, ('row', 'col'), pairs)  6.18 us
    pallas_call x1, Pallas kernels, per_device(): pl.pallas_call(functools.partial(last_tiles_kernel, half), grid_spec=pltp...  4.76 us
  transfers between devices with their start and end apart: 11, of which 2 were waited for; matrix products, arithmetic and copies ran while one was open for 0% of the time, Pallas kernels for 23%

profile of v11, /device:TPU:0, one launch (start us, length us, event | category | flops | bytes accessed | tf_op | source)
XLA Modules:
  0.0 66.8 jit_solution(2617969090847143731)
XLA Ops:
  0.6 3.0 %collective-permute-start = (bf16[3,32,768]{2,1,0:T(8,128)(2,1)}, bf16[3,32,768]{2,1,0:T(8,128)(2,1)S(1)}, u32[]{:S(2)}, u32[]{:S(2)}) collective-permute-start(bf16[3,32,768]{2,1,0:T(8,128)(2,1)} %bitcast.3), channel_id=1, source_target_pairs={{1,0},{0,1},{3,2},{2,3},{5,4},{4,5},{7,6},{6,7},{9,8},{8,9},{11,10... | collective-permute-start | bytes 442376 | tf_op jit(solution)/shard_map/ppermute | solution.py:247
  3.6 1.0 %load.1 = (f32[3,3,64]{2,1,0:T(4,128)S(1)}, bf16[3,32,768]{2,1,0:T(8,128)(2,1)S(1)}) custom-call(f32[3,3,64]{2,1,0:T(4,128)} %rot_hbm.1, bf16[3,32,768]{2,1,0:T(8,128)(2,1)} %bitcast.4), custom_call_target="tpu_custom_call" | custom-call | tf_op jit(solution)/shard_map/load/pallas_call | solution.py:266
  4.6 3.1 %collective-permute-done.refs_1_ = bf16[3,32,768]{2,1,0:T(8,128)(2,1)S(1)} collective-permute-done((bf16[3,32,768]{2,1,0:T(8,128)(2,1)}, bf16[3,32,768]{2,1,0:T(8,128)(2,1)S(1)}, u32[]{:S(2)}, u32[]{:S(2)}) %collective-permute-start) | collective-permute-done | bytes 147488 | tf_op jit(solution)/shard_map/ppermute | solution.py:247
  7.7 0.9 %rows.1 = (bf16[3,64,768]{2,1,0:T(8,128)(2,1)S(1)}, f32[16,1,2304]{2,1,0:T(1,128)}) custom-call(s32[1]{0:T(128)} %bitcast.1.col, f32[3,3,64]{2,1,0:T(4,128)S(1)} %get-tuple-element.15.rot_ref, bf16[3,32,768]{2,1,0:T(8,128)(2,1)S(1)} %get-tuple-element.16.refs_0_, bf16[3,32,768]{2,1,0:T(8,128)(2,1)S(1)} %collective-permute-done.refs_1_), custom_call_target="tpu_custom_call" | custom-call | tf_op jit(solution)/shard_map/rows/pallas_call | solution.py:275
  8.6 6.2 %all-to-all-start = ((f32[16,1,2304]{2,1,0:T(1,128)}), f32[16,1,2304]{2,1,0:T(1,128)S(1)}, u32[]{:S(2)}, u32[]{:S(2)}) async-start(f32[16,1,2304]{2,1,0:T(1,128)} %get-tuple-element.17), calls=%async_computation | async-start | bytes 294912 | tf_op jit(solution)/shard_map/all_to_all | solution.py:286
  14.8 4.7 %collective-permute-start.2 = (bf16[3,32,768]{2,1,0:T(8,128)(2,1)}, bf16[3,32,768]{2,1,0:T(8,128)(2,1)S(1)}, u32[]{:S(2)}, u32[]{:S(2)}) collective-permute-start(bf16[3,32,768]{2,1,0:T(8,128)(2,1)} %bitcast.5), channel_id=1, source_target_pairs={{17,1},{19,3},{21,5},{23,7},{25,9},{27,11},{29,13},{31,15},{0,16},... | collective-permute-start | bytes 442376 | tf_op jit(solution)/shard_map/ppermute | solution.py:247
  19.5 0.7 %collective-permute-start.1 = (bf16[3,32,768]{2,1,0:T(8,128)(2,1)}, bf16[3,32,768]{2,1,0:T(8,128)(2,1)S(1)}, u32[]{:S(2)}, u32[]{:S(2)}) collective-permute-start(bf16[3,32,768]{2,1,0:T(8,128)(2,1)} %bitcast.6), channel_id=1, source_target_pairs={{16,1},{18,3},{20,5},{22,7},{24,9},{26,11},{28,13},{30,15},{1,16},... | collective-permute-start | bytes 442376 | tf_op jit(solution)/shard_map/ppermute | solution.py:247
  20.2 3.1 %collective-permute-done.2.refs_1_ = bf16[3,32,768]{2,1,0:T(8,128)(2,1)S(1)} collective-permute-done((bf16[3,32,768]{2,1,0:T(8,128)(2,1)}, bf16[3,32,768]{2,1,0:T(8,128)(2,1)S(1)}, u32[]{:S(2)}, u32[]{:S(2)}) %collective-permute-start.2) | collective-permute-done | bytes 147488 | tf_op jit(solution)/shard_map/ppermute | solution.py:247
  23.3 0.0 collective-permute-done.1.refs_0_
  23.3 0.0 all-to-all-done.centres_ref
  23.3 5.5 %collective-permute-start.5 = (bf16[3,64,768]{2,1,0:T(8,128)(2,1)S(1)}, bf16[3,64,768]{2,1,0:T(8,128)(2,1)S(1)}, u32[]{:S(2)}, u32[]{:S(2)}) collective-permute-start(bf16[3,64,768]{2,1,0:T(8,128)(2,1)S(1)} %assemble.1.refs_0_), channel_id=1, source_target_pairs={{12,0},{13,1},{14,2},{15,3},{8,4},{9,5},{10,6},{11,7},{4,8},{5,9},... | collective-permute-start | bytes 884744 | tf_op jit(solution)/shard_map/ppermute | solution.py:247
  28.9 0.0 collective-permute-start.4
  28.9 0.6 collective-permute-start.3
  29.5 7.5 %weighted_fit.1 = f32[32,8,128]{2,1,0:T(8,128)S(1)} custom-call(s32[1]{0:T(128)} %bitcast.row, s32[1]{0:T(128)} %bitcast.1.col, f32[768,6144]{1,0:T(8,128)} %inv_ref.1, f32[16,1,2304]{2,1,0:T(1,128)S(1)} %all-to-all-done.centres_ref, bf16[3,64,768]{2,1,0:T(8,128)(2,1)S(1)} %get-tuple-element.18.rows_ref), custom_call_target="tpu_custom_call" | custom-call | flops 28311552 | bytes 18874368 | tf_op jit(solution)/shard_map/weighted_fit/pallas_call | solution.py:299
  37.0 16.6 %all_to_all.10.fits_ref = f32[32,8,128]{2,1,0:T(8,128)S(1)} all-to-all(f32[32,8,128]{2,1,0:T(8,128)S(1)} %weighted_fit.1), channel_id=1, replica_groups=mesh['row'=16,'col'=2] {'row','col'}, dimensions={0} | all-to-all | bytes 262144 | tf_op jit(solution)/shard_map/all_to_all | solution.py:316
  53.6 0.0 collective-permute-done.5.refs_3_
  53.7 0.0 collective-permute-done.4.refs_2_
  53.7 0.0 collective-permute-done.3.refs_1_
  53.7 0.1 collective-permute-start.6
  53.7 0.5 collective-permute-start.7
  54.2 0.1 collective-permute-start.8
  54.3 0.4 collective-permute-start.9
  54.7 7.2 %steps_and_even_tiles.1 = (f32[768,6144]{1,0:T(8,128)}, f32[3,3,32]{2,1,0:T(4,128)}, f32[9,64,128]{2,1,0:T(8,128)S(1)}, bf16[768,192]{1,0:T(8,128)(2,1)S(1)}) custom-call(s32[1]{0:T(128)} %bitcast.row, s32[1]{0:T(128)} %bitcast.1.col, f32[32,8,128]{2,1,0:T(8,128)S(1)} %all_to_all.10.fits_ref, bf16[3,64,768]{2,1,0:T(8,128)(2,1)S(1)} %get-tuple-element.18.rows_ref, ...), custom_call_target="tpu_custom_call" | custom-call | flops 905969664 | bytes 9437184 | tf_op jit(solution)/shard_map/steps_and_even_tiles/pallas_call | solution.py:327
  62.0 0.0 collective-permute-done.6.refs_0_
  62.0 0.0 collective-permute-done.7.refs_1_
  62.0 0.0 collective-permute-done.8.refs_2_
  62.0 0.0 collective-permute-done.9.refs_3_
  62.0 4.8 %odd_tiles.1 = f32[768,6144]{1,0:T(8,128)} custom-call(s32[1]{0:T(128)} %bitcast.row, s32[1]{0:T(128)} %bitcast.1.col, f32[768,6144]{1,0:T(8,128)} %get-tuple-element.24.before_ref, f32[9,64,128]{2,1,0:T(8,128)S(1)} %get-tuple-element.25.wide_ref, bf16[768,192]{1,0:T(8,128)(2,1)S(1)} %get-tuple-element.26.rows_dev_ref, ...), custom_call_target="tpu_custom_call", output_to_operand_aliasing={{}: (2, {})} | custom-call | flops 905969664 | bytes 9437184 | tf_op jit(solution)/shard_map/odd_tiles/pallas_call | solution.py:346
  (1 shorter events, 0.0 us)
Async XLA Ops:
  0.6 7.1 %collective-permute-start = (bf16[3,32,768]{2,1,0:T(8,128)(2,1)}, bf16[3,32,768]{2,1,0:T(8,128)(2,1)S(1)}, u32[]{:S(2)}, u32[]{:S(2)}) collective-permute-start(bf16[3,32,768]{2,1,0:T(8,128)(2,1)} %bitcast.3), channel_id=1, source_target_pairs={{1,0},{0,1},{3,2},{2,3},{5,4},{4,5},{7,6},{6,7},{9,8},{8,9},{11,10... | collective-permute-start | bytes 442376 | tf_op jit(solution)/shard_map/ppermute | solution.py:247
  8.6 14.7 %all-to-all-start = ((f32[16,1,2304]{2,1,0:T(1,128)}), f32[16,1,2304]{2,1,0:T(1,128)S(1)}, u32[]{:S(2)}, u32[]{:S(2)}) async-start(f32[16,1,2304]{2,1,0:T(1,128)} %get-tuple-element.17), calls=%async_computation | async-start | bytes 294912 | tf_op jit(solution)/shard_map/all_to_all | solution.py:286
  14.8 8.5 %collective-permute-start.2 = (bf16[3,32,768]{2,1,0:T(8,128)(2,1)}, bf16[3,32,768]{2,1,0:T(8,128)(2,1)S(1)}, u32[]{:S(2)}, u32[]{:S(2)}) collective-permute-start(bf16[3,32,768]{2,1,0:T(8,128)(2,1)} %bitcast.5), channel_id=1, source_target_pairs={{17,1},{19,3},{21,5},{23,7},{25,9},{27,11},{29,13},{31,15},{0,16},... | collective-permute-start | bytes 442376 | tf_op jit(solution)/shard_map/ppermute | solution.py:247
  19.5 3.8 %collective-permute-start.1 = (bf16[3,32,768]{2,1,0:T(8,128)(2,1)}, bf16[3,32,768]{2,1,0:T(8,128)(2,1)S(1)}, u32[]{:S(2)}, u32[]{:S(2)}) collective-permute-start(bf16[3,32,768]{2,1,0:T(8,128)(2,1)} %bitcast.6), channel_id=1, source_target_pairs={{16,1},{18,3},{20,5},{22,7},{24,9},{26,11},{28,13},{30,15},{1,16},... | collective-permute-start | bytes 442376 | tf_op jit(solution)/shard_map/ppermute | solution.py:247
  23.3 30.3 %collective-permute-start.5 = (bf16[3,64,768]{2,1,0:T(8,128)(2,1)S(1)}, bf16[3,64,768]{2,1,0:T(8,128)(2,1)S(1)}, u32[]{:S(2)}, u32[]{:S(2)}) collective-permute-start(bf16[3,64,768]{2,1,0:T(8,128)(2,1)S(1)} %assemble.1.refs_0_), channel_id=1, source_target_pairs={{12,0},{13,1},{14,2},{15,3},{8,4},{9,5},{10,6},{11,7},{4,8},{5,9},... | collective-permute-start | bytes 884744 | tf_op jit(solution)/shard_map/ppermute | solution.py:247
  28.9 24.8 %collective-permute-start.4 = (bf16[3,64,768]{2,1,0:T(8,128)(2,1)S(1)}, bf16[3,64,768]{2,1,0:T(8,128)(2,1)S(1)}, u32[]{:S(2)}, u32[]{:S(2)}) collective-permute-start(bf16[3,64,768]{2,1,0:T(8,128)(2,1)S(1)} %assemble.1.refs_0_), channel_id=1, source_target_pairs={{8,0},{9,1},{10,2},{11,3},{12,4},{13,5},{14,6},{15,7},{0,8},{1,9},... | collective-permute-start | bytes 884744 | tf_op jit(solution)/shard_map/ppermute | solution.py:247
  28.9 24.8 %collective-permute-start.3 = (bf16[3,64,768]{2,1,0:T(8,128)(2,1)S(1)}, bf16[3,64,768]{2,1,0:T(8,128)(2,1)S(1)}, u32[]{:S(2)}, u32[]{:S(2)}) collective-permute-start(bf16[3,64,768]{2,1,0:T(8,128)(2,1)S(1)} %assemble.1.refs_0_), channel_id=1, source_target_pairs={{4,0},{5,1},{6,2},{7,3},{0,4},{1,5},{2,6},{3,7},{12,8},{13,9},{14,... | collective-permute-start | bytes 884744 | tf_op jit(solution)/shard_map/ppermute | solution.py:247
  53.7 8.3 %collective-permute-start.6 = (bf16[3,64,768]{2,1,0:T(8,128)(2,1)S(1)}, bf16[3,64,768]{2,1,0:T(8,128)(2,1)S(1)}, u32[]{:S(2)}, u32[]{:S(2)}) collective-permute-start(bf16[3,64,768]{2,1,0:T(8,128)(2,1)S(1)} %assemble.1.refs_0_), channel_id=1, source_target_pairs={{2,0},{3,1},{0,2},{1,3},{6,4},{7,5},{4,6},{5,7},{10,8},{11,9},{8,1... | collective-permute-start | bytes 884744 | tf_op jit(solution)/shard_map/ppermute | solution.py:247
  53.7 8.2 %collective-permute-start.7 = (bf16[3,64,768]{2,1,0:T(8,128)(2,1)S(1)}, bf16[3,64,768]{2,1,0:T(8,128)(2,1)S(1)}, u32[]{:S(2)}, u32[]{:S(2)}) collective-permute-start(bf16[3,64,768]{2,1,0:T(8,128)(2,1)S(1)} %collective-permute-done.3.refs_1_), channel_id=1, source_target_pairs={{2,0},{3,1},{0,2},{1,3},{6,4},{7,5},{4,6},{5,7},{10,8},{11,9},{8,1... | collective-permute-start | bytes 884744 | tf_op jit(solution)/shard_map/ppermute | solution.py:247
  54.2 7.7 %collective-permute-start.8 = (bf16[3,64,768]{2,1,0:T(8,128)(2,1)S(1)}, bf16[3,64,768]{2,1,0:T(8,128)(2,1)S(1)}, u32[]{:S(2)}, u32[]{:S(2)}) collective-permute-start(bf16[3,64,768]{2,1,0:T(8,128)(2,1)S(1)} %collective-permute-done.4.refs_2_), channel_id=1, source_target_pairs={{2,0},{3,1},{0,2},{1,3},{6,4},{7,5},{4,6},{5,7},{10,8},{11,9},{8,1... | collective-permute-start | bytes 884744 | tf_op jit(solution)/shard_map/ppermute | solution.py:247
  54.3 7.7 %collective-permute-start.9 = (bf16[3,64,768]{2,1,0:T(8,128)(2,1)S(1)}, bf16[3,64,768]{2,1,0:T(8,128)(2,1)S(1)}, u32[]{:S(2)}, u32[]{:S(2)}) collective-permute-start(bf16[3,64,768]{2,1,0:T(8,128)(2,1)S(1)} %collective-permute-done.5.refs_3_), channel_id=1, source_target_pairs={{2,0},{3,1},{0,2},{1,3},{6,4},{7,5},{4,6},{5,7},{10,8},{11,9},{8,1... | collective-permute-start | bytes 884744 | tf_op jit(solution)/shard_map/ppermute | solution.py:247

commit v12 on v11

--- a/solution.py
+++ b/solution.py
@@ -68,18 +68,23 @@
     centre_ref[...] = jnp.broadcast_to(flat[None], centre_ref.shape)
 
 
-def assemble_kernel(members, row, col, centres_ref, rows_ref, *refs):
-    far_refs, out_ref = refs[:-1], refs[-1]
-    group = row[0] // members
-
-    @pl.when(group == col[0])
+def assemble_kernel(members, row, col, rows_ref, *refs):
+    sources, out_ref = refs[:-1], refs[-1]
+    far_refs, across_refs = sources[: len(sources) // 2], sources[len(sources) // 2 :]
+    col_count = len(far_refs) + 1
+    distance = lax.rem(col[0] + col_count - row[0] // members, col_count)
+
+    @pl.when(distance == 0)
     def _():
         out_ref[...] = rows_ref[...]
 
-    @pl.when(group != col[0])
-    def _():
-        for shift, ref in enumerate(far_refs):
-            put_block(out_ref, lax.rem(group + shift, len(far_refs)), ref[...])
+    for step, ref in enumerate(far_refs):
+
+        @pl.when(distance == step + 1)
+        def _(ref=ref):
+            put_block(out_ref, col[0], ref[...])
+            for shift, across_ref in enumerate(across_refs):
+                put_block(out_ref, lax.rem(col[0] + 1 + shift, col_count), across_ref[...])
 
 
 def weighted_fit_kernel(members, row, col, inv_ref, centres_ref, rows_ref, out_ref, strips_ref, wide_ref, weighted_ref, sems):
@@ -171,11 +176,8 @@
     for start in range(0, width, stride):
         for chunk in range(start // LANES, (start + stride) // LANES):
             put_deviations(wide_ref, coords_ref, centres_ref, row, chunk, dev_ref)
-        span = slice(start, start + stride)
-        for first in range(0, rows_dev_ref.shape[0], LANES):
-            strip = slice(first, first + LANES)
-            product = jnp.dot(rows_dev_ref[strip, :], dev_ref[:, span], preferred_element_type=F32)
-            out_ref[strip, span] = product * scale
+        product = jnp.dot(rows_dev_ref[...], dev_ref[:, start : start + stride], preferred_element_type=F32)
+        out_ref[:, start : start + stride] = product * scale
 
 
 def first_tiles_kernel(count, row, col, fits_ref, rows_ref, centres_ref, *refs):
@@ -258,11 +260,8 @@
     def in_hbm(value):
         return pltpu.with_memory_space_constraint(value, pltpu.HBM)
 
+    far = [move(coords, lambda g, m, c, s=step: ((g + s) % col_count, m, c)) for step in range(1, col_count)]
     others = [move(coords, lambda g, m, c, s=step: (g, m, (c + s) % col_count)) for step in range(1, col_count)]
-    far = [
-        move(coords, lambda g, m, c, s=step: (c, m, (g + s) % col_count), lambda g, c: g != c)
-        for step in range(col_count)
-    ]
     rot_here, coords_here = pl.pallas_call(
         load_kernel,
         out_shape=(jax.ShapeDtypeStruct(rotations.shape, F32), jax.ShapeDtypeStruct(coords.shape, BF16)),
@@ -285,14 +284,21 @@
     )(col, rot_here, coords_here, *others)
     centres = lax.all_to_all(repeated, "row", split_axis=0, concat_axis=0, tiled=True)
 
+    distance = lax.rem(col[0] + col_count - row[0] // members, col_count)
+    across = []
+    for step in range(1, col_count):
+        held = far[0]
+        if col_count > 2:
+            held = lax.select_n(lax.rem(distance + col_count - step, col_count), coords, *far)
+        across.append(move(held, lambda g, m, c, s=step: (g, m, (c + s) % col_count), lambda g, c: g != c))
     own_block = pl.pallas_call(
         functools.partial(assemble_kernel, members),
         out_shape=jax.ShapeDtypeStruct((3, frame_total, width), BF16),
-        in_specs=[smem(), smem()] + [vmem()] * (2 + col_count),
+        in_specs=[smem(), smem()] + [vmem()] * (2 * col_count - 1),
         out_specs=vmem(),
         compiler_params=limit(8),
         name="assemble",
-    )(row, col, centres, rows_all, *far)
+    )(row, col, rows_all, *far, *across)
     evens = [own_block] + [from_member(own_block, 2 * step) for step in range(1, half)]
 
     height = 64 if width % 64 == 0 else 8

time: 67 us -> 61.3 us (0.915)
  blocking collectives: 16.6 us -> 0 us
  waiting for transfers between devices: 6.19 us -> 12.8 us
  starting transfers between devices: 21.9 us -> 25.5 us
    all_to_all x1 -> x0, blocking collectives: 16.6 us -> none  [per_device(): lax.all_to_all(message, ('row', 'col'), split_axis=0, concat_axis=0, tile...]
    all_to_all x0 -> x1, waiting for transfers between devices: none -> 8.59 us  [per_device(): lax.all_to_all(message, ('row', 'col'), split_axis=0, concat_axis=0, tile...]
    all_to_all x0 -> x1, starting transfers between devices: none -> 5.71 us  [per_device(): lax.all_to_all(message, ('row', 'col'), split_axis=0, concat_axis=0, tile...]
    ppermute x10, starting transfers between devices: 15.7 us -> 13.6 us  [move(): return lax.ppermute(value, ('row', 'col'), pairs)]
    ppermute x10, waiting for transfers between devices: 6.18 us -> 4.19 us  [move(): return lax.ppermute(value, ('row', 'col'), pairs)]
  transfers between devices with their start and end apart: 11 -> 12, of which waited for: 2 -> 3; matrix products, arithmetic and copies ran while one was open for 0% -> 0% of each run, Pallas kernels for 23% -> 28%
where the time goes in v12:
time: 61.3 us; the launch traced here: 61 us
  starting transfers between devices  25.5 us (42%)
  Pallas kernels  22 us (36%)
  waiting for transfers between devices  12.8 us (21%)
  between operations  0.73 us (1%)
    ppermute x10, starting transfers between devices, move(): return lax.ppermute(value, ('row', 'col'), pairs)  13.6 us
    all_to_all x1, waiting for transfers between devices, per_device(): lax.all_to_all(message, ('row', 'col'), split_axis=0, concat_axis=0, tile...  8.59 us
    pallas_call x1, Pallas kernels, per_device(): pl.pallas_call(functools.partial(weighted_fit_kernel, members), in_specs=...  8.13 us
    pallas_call x1, Pallas kernels, per_device(): pl.pallas_call(functools.partial(first_tiles_kernel, half), grid_spec=plt...  7.24 us
    all_to_all x1, starting transfers between devices, per_device(): lax.all_to_all(repeated, 'row', split_axis=0, concat_axis=0, tiled=True)  6.19 us
    all_to_all x1, starting transfers between devices, per_device(): lax.all_to_all(message, ('row', 'col'), split_axis=0, concat_axis=0, tile...  5.71 us
    pallas_call x1, Pallas kernels, per_device(): pl.pallas_call(functools.partial(last_tiles_kernel, half), grid_spec=pltp...  4.77 us
    ppermute x10, waiting for transfers between devices, move(): return lax.ppermute(value, ('row', 'col'), pairs)  4.19 us
  transfers between devices with their start and end apart: 12, of which 3 were waited for; matrix products, arithmetic and copies ran while one was open for 0% of the time, Pallas kernels for 28%

profile of v12, /device:TPU:0, one launch (start us, length us, event | category | flops | bytes accessed | tf_op | source)
XLA Modules:
  0.0 61.0 jit_solution(5998666430784868084)
XLA Ops:
  0.6 3.0 %collective-permute-start = (bf16[3,32,768]{2,1,0:T(8,128)(2,1)}, bf16[3,32,768]{2,1,0:T(8,128)(2,1)S(1)}, u32[]{:S(2)}, u32[]{:S(2)}) collective-permute-start(bf16[3,32,768]{2,1,0:T(8,128)(2,1)} %bitcast.3), channel_id=1, source_target_pairs={{1,0},{0,1},{3,2},{2,3},{5,4},{4,5},{7,6},{6,7},{9,8},{8,9},{11,10... | collective-permute-start | bytes 442376 | tf_op jit(solution)/shard_map/ppermute | solution.py:249
  3.6 2.6 %collective-permute-start.1 = (bf16[3,32,768]{2,1,0:T(8,128)(2,1)}, bf16[3,32,768]{2,1,0:T(8,128)(2,1)S(1)}, u32[]{:S(2)}, u32[]{:S(2)}) collective-permute-start(bf16[3,32,768]{2,1,0:T(8,128)(2,1)} %bitcast.4), channel_id=1, source_target_pairs={{16,0},{17,1},{18,2},{19,3},{20,4},{21,5},{22,6},{23,7},{24,8},{25... | collective-permute-start | bytes 442376 | tf_op jit(solution)/shard_map/ppermute | solution.py:249
  6.2 1.0 %load.1 = (f32[3,3,64]{2,1,0:T(4,128)S(1)}, bf16[3,32,768]{2,1,0:T(8,128)(2,1)S(1)}) custom-call(f32[3,3,64]{2,1,0:T(4,128)} %rot_hbm.1, bf16[3,32,768]{2,1,0:T(8,128)(2,1)} %bitcast.5), custom_call_target="tpu_custom_call" | custom-call | tf_op jit(solution)/shard_map/load/pallas_call | solution.py:265
  7.2 0.5 collective-permute-done.refs_1_
  7.7 0.9 %rows.1 = (bf16[3,64,768]{2,1,0:T(8,128)(2,1)S(1)}, f32[16,1,2304]{2,1,0:T(1,128)}) custom-call(s32[1]{0:T(128)} %bitcast.1.col, f32[3,3,64]{2,1,0:T(4,128)S(1)} %get-tuple-element.15.rot_ref, bf16[3,32,768]{2,1,0:T(8,128)(2,1)S(1)} %get-tuple-element.16.refs_0_, bf16[3,32,768]{2,1,0:T(8,128)(2,1)S(1)} %collective-permute-done.refs_1_), custom_call_target="tpu_custom_call" | custom-call | tf_op jit(solution)/shard_map/rows/pallas_call | solution.py:274
  8.6 6.2 %all-to-all-start = ((f32[16,1,2304]{2,1,0:T(1,128)}), f32[16,1,2304]{2,1,0:T(1,128)S(1)}, u32[]{:S(2)}, u32[]{:S(2)}) async-start(f32[16,1,2304]{2,1,0:T(1,128)} %get-tuple-element.17), calls=%async_computation | async-start | bytes 294912 | tf_op jit(solution)/shard_map/all_to_all | solution.py:285
  14.8 0.0 collective-permute-done.1.refs_0_
  14.8 3.4 %collective-permute-start.2 = (bf16[3,32,768]{2,1,0:T(8,128)(2,1)S(1)}, bf16[3,32,768]{2,1,0:T(8,128)(2,1)S(1)}, u32[]{:S(2)}, u32[]{:S(2)}) collective-permute-start(bf16[3,32,768]{2,1,0:T(8,128)(2,1)S(1)} %collective-permute-done.1.refs_0_), channel_id=1, source_target_pairs={{0,1},{2,3},{4,5},{6,7},{8,9},{10,11},{12,13},{14,15},{17,16},{19,... | collective-permute-start | bytes 442376 | tf_op jit(solution)/shard_map/ppermute | solution.py:249
  18.2 3.7 %collective-permute-done.2.refs_1_ = bf16[3,32,768]{2,1,0:T(8,128)(2,1)S(1)} collective-permute-done((bf16[3,32,768]{2,1,0:T(8,128)(2,1)S(1)}, bf16[3,32,768]{2,1,0:T(8,128)(2,1)S(1)}, u32[]{:S(2)}, u32[]{:S(2)}) %collective-permute-start.2) | collective-permute-done | bytes 147488 | tf_op jit(solution)/shard_map/ppermute | solution.py:249
  21.9 2.6 %collective-permute-start.5 = (bf16[3,64,768]{2,1,0:T(8,128)(2,1)S(1)}, bf16[3,64,768]{2,1,0:T(8,128)(2,1)S(1)}, u32[]{:S(2)}, u32[]{:S(2)}) collective-permute-start(bf16[3,64,768]{2,1,0:T(8,128)(2,1)S(1)} %assemble.1.refs_0_), channel_id=1, source_target_pairs={{12,0},{13,1},{14,2},{15,3},{8,4},{9,5},{10,6},{11,7},{4,8},{5,9},... | collective-permute-start | bytes 884744 | tf_op jit(solution)/shard_map/ppermute | solution.py:249
  24.5 0.6 collective-permute-start.4
  25.1 0.4 collective-permute-start.3
  25.5 0.0 all-to-all-done.centres_ref
  25.5 8.1 %weighted_fit.1 = f32[32,8,128]{2,1,0:T(8,128)} custom-call(s32[1]{0:T(128)} %bitcast.row, s32[1]{0:T(128)} %bitcast.1.col, f32[768,6144]{1,0:T(8,128)} %inv_ref.1, f32[16,1,2304]{2,1,0:T(1,128)S(1)} %all-to-all-done.centres_ref, bf16[3,64,768]{2,1,0:T(8,128)(2,1)S(1)} %get-tuple-element.18.rows_ref), custom_call_target="tpu_custom_call" | custom-call | flops 28311552 | bytes 18874368 | tf_op jit(solution)/shard_map/weighted_fit/pallas_call | solution.py:305
  33.6 5.7 %all-to-all-start.1 = ((f32[32,8,128]{2,1,0:T(8,128)}), f32[32,8,128]{2,1,0:T(8,128)S(1)}, u32[]{:S(2)}, u32[]{:S(2)}) async-start(f32[32,8,128]{2,1,0:T(8,128)} %weighted_fit.1), calls=%async_computation.1 | async-start | bytes 262144 | tf_op jit(solution)/shard_map/all_to_all | solution.py:322
  39.3 0.0 collective-permute-done.5.refs_3_
  39.3 0.0 collective-permute-done.4.refs_2_
  39.4 0.0 collective-permute-done.3.refs_1_
  39.4 8.6 %all-to-all-done.1.fits_ref = f32[32,8,128]{2,1,0:T(8,128)S(1)} async-done(((f32[32,8,128]{2,1,0:T(8,128)}), f32[32,8,128]{2,1,0:T(8,128)S(1)}, u32[]{:S(2)}, u32[]{:S(2)}) %all-to-all-start.1) | async-done | bytes 131104 | tf_op jit(solution)/shard_map/all_to_all | solution.py:322
  48.0 0.0 collective-permute-start.6
  48.0 0.5 collective-permute-start.7
  48.5 0.0 collective-permute-start.8
  48.5 0.5 collective-permute-start.9
  49.0 7.2 %steps_and_even_tiles.1 = (f32[768,6144]{1,0:T(8,128)}, f32[3,3,32]{2,1,0:T(4,128)}, f32[9,64,128]{2,1,0:T(8,128)S(1)}, bf16[768,192]{1,0:T(8,128)(2,1)S(1)}) custom-call(s32[1]{0:T(128)} %bitcast.row, s32[1]{0:T(128)} %bitcast.1.col, f32[32,8,128]{2,1,0:T(8,128)S(1)} %all-to-all-done.1.fits_ref, bf16[3,64,768]{2,1,0:T(8,128)(2,1)S(1)} %get-tuple-element.18.rows_ref, ...), custom_call_target="tpu_custom_call" | custom-call | flops 905969664 | bytes 9437184 | tf_op jit(solution)/shard_map/steps_and_even_tiles/pallas_call | solution.py:333
  56.2 0.0 collective-permute-done.6.refs_0_
  56.2 0.0 collective-permute-done.7.refs_1_
  56.2 0.0 collective-permute-done.8.refs_2_
  56.2 0.0 collective-permute-done.9.refs_3_
  56.2 4.8 %odd_tiles.1 = f32[768,6144]{1,0:T(8,128)} custom-call(s32[1]{0:T(128)} %bitcast.row, s32[1]{0:T(128)} %bitcast.1.col, f32[768,6144]{1,0:T(8,128)} %get-tuple-element.24.before_ref, f32[9,64,128]{2,1,0:T(8,128)S(1)} %get-tuple-element.25.wide_ref, bf16[768,192]{1,0:T(8,128)(2,1)S(1)} %get-tuple-element.26.rows_dev_ref, ...), custom_call_target="tpu_custom_call", output_to_operand_aliasing={{}: (2, {})} | custom-call | flops 905969664 | bytes 9437184 | tf_op jit(solution)/shard_map/odd_tiles/pallas_call | solution.py:352
  (1 shorter events, 0.0 us)
Async XLA Ops:
  0.6 7.1 %collective-permute-start = (bf16[3,32,768]{2,1,0:T(8,128)(2,1)}, bf16[3,32,768]{2,1,0:T(8,128)(2,1)S(1)}, u32[]{:S(2)}, u32[]{:S(2)}) collective-permute-start(bf16[3,32,768]{2,1,0:T(8,128)(2,1)} %bitcast.3), channel_id=1, source_target_pairs={{1,0},{0,1},{3,2},{2,3},{5,4},{4,5},{7,6},{6,7},{9,8},{8,9},{11,10... | collective-permute-start | bytes 442376 | tf_op jit(solution)/shard_map/ppermute | solution.py:249
  3.6 11.2 %collective-permute-start.1 = (bf16[3,32,768]{2,1,0:T(8,128)(2,1)}, bf16[3,32,768]{2,1,0:T(8,128)(2,1)S(1)}, u32[]{:S(2)}, u32[]{:S(2)}) collective-permute-start(bf16[3,32,768]{2,1,0:T(8,128)(2,1)} %bitcast.4), channel_id=1, source_target_pairs={{16,0},{17,1},{18,2},{19,3},{20,4},{21,5},{22,6},{23,7},{24,8},{25... | collective-permute-start | bytes 442376 | tf_op jit(solution)/shard_map/ppermute | solution.py:249
  8.6 16.9 %all-to-all-start = ((f32[16,1,2304]{2,1,0:T(1,128)}), f32[16,1,2304]{2,1,0:T(1,128)S(1)}, u32[]{:S(2)}, u32[]{:S(2)}) async-start(f32[16,1,2304]{2,1,0:T(1,128)} %get-tuple-element.17), calls=%async_computation | async-start | bytes 294912 | tf_op jit(solution)/shard_map/all_to_all | solution.py:285
  14.8 7.1 %collective-permute-start.2 = (bf16[3,32,768]{2,1,0:T(8,128)(2,1)S(1)}, bf16[3,32,768]{2,1,0:T(8,128)(2,1)S(1)}, u32[]{:S(2)}, u32[]{:S(2)}) collective-permute-start(bf16[3,32,768]{2,1,0:T(8,128)(2,1)S(1)} %collective-permute-done.1.refs_0_), channel_id=1, source_target_pairs={{0,1},{2,3},{4,5},{6,7},{8,9},{10,11},{12,13},{14,15},{17,16},{19,... | collective-permute-start | bytes 442376 | tf_op jit(solution)/shard_map/ppermute | solution.py:249
  21.9 17.4 %collective-permute-start.5 = (bf16[3,64,768]{2,1,0:T(8,128)(2,1)S(1)}, bf16[3,64,768]{2,1,0:T(8,128)(2,1)S(1)}, u32[]{:S(2)}, u32[]{:S(2)}) collective-permute-start(bf16[3,64,768]{2,1,0:T(8,128)(2,1)S(1)} %assemble.1.refs_0_), channel_id=1, source_target_pairs={{12,0},{13,1},{14,2},{15,3},{8,4},{9,5},{10,6},{11,7},{4,8},{5,9},... | collective-permute-start | bytes 884744 | tf_op jit(solution)/shard_map/ppermute | solution.py:249
  24.5 14.8 %collective-permute-start.4 = (bf16[3,64,768]{2,1,0:T(8,128)(2,1)S(1)}, bf16[3,64,768]{2,1,0:T(8,128)(2,1)S(1)}, u32[]{:S(2)}, u32[]{:S(2)}) collective-permute-start(bf16[3,64,768]{2,1,0:T(8,128)(2,1)S(1)} %assemble.1.refs_0_), channel_id=1, source_target_pairs={{8,0},{9,1},{10,2},{11,3},{12,4},{13,5},{14,6},{15,7},{0,8},{1,9},... | collective-permute-start | bytes 884744 | tf_op jit(solution)/shard_map/ppermute | solution.py:249
  25.1 14.3 %collective-permute-start.3 = (bf16[3,64,768]{2,1,0:T(8,128)(2,1)S(1)}, bf16[3,64,768]{2,1,0:T(8,128)(2,1)S(1)}, u32[]{:S(2)}, u32[]{:S(2)}) collective-permute-start(bf16[3,64,768]{2,1,0:T(8,128)(2,1)S(1)} %assemble.1.refs_0_), channel_id=1, source_target_pairs={{4,0},{5,1},{6,2},{7,3},{0,4},{1,5},{2,6},{3,7},{12,8},{13,9},{14,... | collective-permute-start | bytes 884744 | tf_op jit(solution)/shard_map/ppermute | solution.py:249
  33.6 14.3 %all-to-all-start.1 = ((f32[32,8,128]{2,1,0:T(8,128)}), f32[32,8,128]{2,1,0:T(8,128)S(1)}, u32[]{:S(2)}, u32[]{:S(2)}) async-start(f32[32,8,128]{2,1,0:T(8,128)} %weighted_fit.1), calls=%async_computation.1 | async-start | bytes 262144 | tf_op jit(solution)/shard_map/all_to_all | solution.py:322
  48.0 8.3 %collective-permute-start.6 = (bf16[3,64,768]{2,1,0:T(8,128)(2,1)S(1)}, bf16[3,64,768]{2,1,0:T(8,128)(2,1)S(1)}, u32[]{:S(2)}, u32[]{:S(2)}) collective-permute-start(bf16[3,64,768]{2,1,0:T(8,128)(2,1)S(1)} %assemble.1.refs_0_), channel_id=1, source_target_pairs={{2,0},{3,1},{0,2},{1,3},{6,4},{7,5},{4,6},{5,7},{10,8},{11,9},{8,1... | collective-permute-start | bytes 884744 | tf_op jit(solution)/shard_map/ppermute | solution.py:249
  48.0 8.3 %collective-permute-start.7 = (bf16[3,64,768]{2,1,0:T(8,128)(2,1)S(1)}, bf16[3,64,768]{2,1,0:T(8,128)(2,1)S(1)}, u32[]{:S(2)}, u32[]{:S(2)}) collective-permute-start(bf16[3,64,768]{2,1,0:T(8,128)(2,1)S(1)} %collective-permute-done.3.refs_1_), channel_id=1, source_target_pairs={{2,0},{3,1},{0,2},{1,3},{6,4},{7,5},{4,6},{5,7},{10,8},{11,9},{8,1... | collective-permute-start | bytes 884744 | tf_op jit(solution)/shard_map/ppermute | solution.py:249
  48.5 7.8 %collective-permute-start.8 = (bf16[3,64,768]{2,1,0:T(8,128)(2,1)S(1)}, bf16[3,64,768]{2,1,0:T(8,128)(2,1)S(1)}, u32[]{:S(2)}, u32[]{:S(2)}) collective-permute-start(bf16[3,64,768]{2,1,0:T(8,128)(2,1)S(1)} %collective-permute-done.4.refs_2_), channel_id=1, source_target_pairs={{2,0},{3,1},{0,2},{1,3},{6,4},{7,5},{4,6},{5,7},{10,8},{11,9},{8,1... | collective-permute-start | bytes 884744 | tf_op jit(solution)/shard_map/ppermute | solution.py:249
  48.5 7.8 %collective-permute-start.9 = (bf16[3,64,768]{2,1,0:T(8,128)(2,1)S(1)}, bf16[3,64,768]{2,1,0:T(8,128)(2,1)S(1)}, u32[]{:S(2)}, u32[]{:S(2)}) collective-permute-start(bf16[3,64,768]{2,1,0:T(8,128)(2,1)S(1)} %collective-permute-done.5.refs_3_), channel_id=1, source_target_pairs={{2,0},{3,1},{0,2},{1,3},{6,4},{7,5},{4,6},{5,7},{10,8},{11,9},{8,1... | collective-permute-start | bytes 884744 | tf_op jit(solution)/shard_map/ppermute | solution.py:249

commit v13 on v12

--- a/solution.py
+++ b/solution.py
@@ -59,8 +59,8 @@
         copy.wait()
 
 
-def rows_kernel(col, rot_ref, *refs):
-    blocks, (rows_ref, centre_ref) = refs[:-2], refs[-2:]
+def rows_kernel(col_count, col, rot_ref, *refs):
+    blocks, (rows_ref, centre_ref) = refs[:col_count], refs[-2:]
     for shift, ref in enumerate(blocks):
         put_block(rows_ref, lax.rem(col[0] + shift, len(blocks)), ref[...])
     centre = rotated_sum(rot_ref[...], rows_ref[...]) * (1.0 / rows_ref.shape[1])
@@ -272,16 +272,16 @@
         name="load",
     )(in_hbm(rotations), in_hbm(coords))
     rows_all, repeated = pl.pallas_call(
-        rows_kernel,
+        functools.partial(rows_kernel, col_count),
         out_shape=(
             jax.ShapeDtypeStruct((3, frame_total, width), BF16),
             jax.ShapeDtypeStruct((row_count, 1, 3 * width), F32),
         ),
-        in_specs=[smem()] + [vmem()] * (1 + col_count),
+        in_specs=[smem()] + [vmem()] * (2 * col_count),
         out_specs=(vmem(), vmem()),
         compiler_params=limit(8),
         name="rows",
-    )(col, rot_here, coords_here, *others)
+    )(col, rot_here, coords_here, *others, *far)
     centres = lax.all_to_all(repeated, "row", split_axis=0, concat_axis=0, tiled=True)
 
     distance = lax.rem(col[0] + col_count - row[0] // members, col_count)

time: 61.3 us -> 65.3 us (1.065)
  waiting for transfers between devices: 12.8 us -> 17 us
    ppermute x10, waiting for transfers between devices: 4.19 us -> 8.45 us  [move(): return lax.ppermute(value, ('row', 'col'), pairs)]
  transfers between devices with their start and end apart: 12 -> 12, of which waited for: 3 -> 3; matrix products, arithmetic and copies ran while one was open for 0% -> 0% of each run, Pallas kernels for 28% -> 25%
where the time goes in v13:
time: 65.3 us; the launch traced here: 64.9 us
  starting transfers between devices  25.1 us (38%)
  Pallas kernels  22 us (34%)
  waiting for transfers between devices  17 us (26%)
  between operations  0.73 us (1%)
    ppermute x10, starting transfers between devices, move(): return lax.ppermute(value, ('row', 'col'), pairs)  13.6 us
    all_to_all x1, waiting for transfers between devices, per_device(): lax.all_to_all(message, ('row', 'col'), split_axis=0, concat_axis=0, tile...  8.59 us
    ppermute x10, waiting for transfers between devices, move(): return lax.ppermute(value, ('row', 'col'), pairs)  8.45 us
    pallas_call x1, Pallas kernels, per_device(): pl.pallas_call(functools.partial(weighted_fit_kernel, members), in_specs=...  8.13 us
    pallas_call x1, Pallas kernels, per_device(): pl.pallas_call(functools.partial(first_tiles_kernel, half), grid_spec=plt...  7.24 us
    all_to_all x1, starting transfers between devices, per_device(): lax.all_to_all(repeated, 'row', split_axis=0, concat_axis=0, tiled=True)  5.87 us
    all_to_all x1, starting transfers between devices, per_device(): lax.all_to_all(message, ('row', 'col'), split_axis=0, concat_axis=0, tile...  5.7 us
    pallas_call x1, Pallas kernels, per_device(): pl.pallas_call(functools.partial(last_tiles_kernel, half), grid_spec=pltp...  4.77 us
  transfers between devices with their start and end apart: 12, of which 3 were waited for; matrix products, arithmetic and copies ran while one was open for 0% of the time, Pallas kernels for 25%

profile of v13, /device:TPU:0, one launch (start us, length us, event | category | flops | bytes accessed | tf_op | source)
XLA Modules:
  0.0 64.9 jit_solution(9423411237824569650)
XLA Ops:
  0.6 4.1 %collective-permute-start.1 = (bf16[3,32,768]{2,1,0:T(8,128)(2,1)}, bf16[3,32,768]{2,1,0:T(8,128)(2,1)S(1)}, u32[]{:S(2)}, u32[]{:S(2)}) collective-permute-start(bf16[3,32,768]{2,1,0:T(8,128)(2,1)} %bitcast.3), channel_id=1, source_target_pairs={{16,0},{17,1},{18,2},{19,3},{20,4},{21,5},{22,6},{23,7},{24,8},{25... | collective-permute-start | bytes 442376 | tf_op jit(solution)/shard_map/ppermute | solution.py:249
  4.7 1.5 %collective-permute-start = (bf16[3,32,768]{2,1,0:T(8,128)(2,1)}, bf16[3,32,768]{2,1,0:T(8,128)(2,1)S(1)}, u32[]{:S(2)}, u32[]{:S(2)}) collective-permute-start(bf16[3,32,768]{2,1,0:T(8,128)(2,1)} %bitcast.4), channel_id=1, source_target_pairs={{1,0},{0,1},{3,2},{2,3},{5,4},{4,5},{7,6},{6,7},{9,8},{8,9},{11,10... | collective-permute-start | bytes 442376 | tf_op jit(solution)/shard_map/ppermute | solution.py:249
  6.2 1.0 %load.1 = (f32[3,3,64]{2,1,0:T(4,128)S(1)}, bf16[3,32,768]{2,1,0:T(8,128)(2,1)S(1)}) custom-call(f32[3,3,64]{2,1,0:T(4,128)} %rot_hbm.1, bf16[3,32,768]{2,1,0:T(8,128)(2,1)} %bitcast.5), custom_call_target="tpu_custom_call" | custom-call | tf_op jit(solution)/shard_map/load/pallas_call | solution.py:265
  7.2 4.8 %collective-permute-done.1.refs_2_.refs_0_ = bf16[3,32,768]{2,1,0:T(8,128)(2,1)S(1)} collective-permute-done((bf16[3,32,768]{2,1,0:T(8,128)(2,1)}, bf16[3,32,768]{2,1,0:T(8,128)(2,1)S(1)}, u32[]{:S(2)}, u32[]{:S(2)}) %collective-permute-start.1) | collective-permute-done | bytes 147488 | tf_op jit(solution)/shard_map/ppermute | solution.py:249
  11.9 0.0 collective-permute-done.refs_1_
  12.0 0.9 %rows.1 = (bf16[3,64,768]{2,1,0:T(8,128)(2,1)S(1)}, f32[16,1,2304]{2,1,0:T(1,128)}) custom-call(s32[1]{0:T(128)} %bitcast.1.col, f32[3,3,64]{2,1,0:T(4,128)S(1)} %get-tuple-element.15.rot_ref, bf16[3,32,768]{2,1,0:T(8,128)(2,1)S(1)} %get-tuple-element.16.refs_0_, bf16[3,32,768]{2,1,0:T(8,128)(2,1)S(1)} %collective-permute-done.refs_1_, ...), custom_call_target="tpu_custom_call" | custom-call | tf_op jit(solution)/shard_map/rows/pallas_call | solution.py:274
  12.9 5.9 %all-to-all-start = ((f32[16,1,2304]{2,1,0:T(1,128)}), f32[16,1,2304]{2,1,0:T(1,128)S(1)}, u32[]{:S(2)}, u32[]{:S(2)}) async-start(f32[16,1,2304]{2,1,0:T(1,128)} %get-tuple-element.17), calls=%async_computation | async-start | bytes 294912 | tf_op jit(solution)/shard_map/all_to_all | solution.py:285
  18.7 3.4 %collective-permute-start.2 = (bf16[3,32,768]{2,1,0:T(8,128)(2,1)S(1)}, bf16[3,32,768]{2,1,0:T(8,128)(2,1)S(1)}, u32[]{:S(2)}, u32[]{:S(2)}) collective-permute-start(bf16[3,32,768]{2,1,0:T(8,128)(2,1)S(1)} %collective-permute-done.1.refs_2_.refs_0_), channel_id=1, source_target_pairs={{0,1},{2,3},{4,5},{6,7},{8,9},{10,11},{12,13},{14,15},{17,16},{19,... | collective-permute-start | bytes 442376 | tf_op jit(solution)/shard_map/ppermute | solution.py:249
  22.2 3.7 %collective-permute-done.2.refs_1_ = bf16[3,32,768]{2,1,0:T(8,128)(2,1)S(1)} collective-permute-done((bf16[3,32,768]{2,1,0:T(8,128)(2,1)S(1)}, bf16[3,32,768]{2,1,0:T(8,128)(2,1)S(1)}, u32[]{:S(2)}, u32[]{:S(2)}) %collective-permute-start.2) | collective-permute-done | bytes 147488 | tf_op jit(solution)/shard_map/ppermute | solution.py:249
  25.9 2.6 %collective-permute-start.5 = (bf16[3,64,768]{2,1,0:T(8,128)(2,1)S(1)}, bf16[3,64,768]{2,1,0:T(8,128)(2,1)S(1)}, u32[]{:S(2)}, u32[]{:S(2)}) collective-permute-start(bf16[3,64,768]{2,1,0:T(8,128)(2,1)S(1)} %assemble.1.refs_0_), channel_id=1, source_target_pairs={{12,0},{13,1},{14,2},{15,3},{8,4},{9,5},{10,6},{11,7},{4,8},{5,9},... | collective-permute-start | bytes 884744 | tf_op jit(solution)/shard_map/ppermute | solution.py:249
  28.5 0.6 collective-permute-start.4
  29.0 0.4 collective-permute-start.3
  29.4 0.0 all-to-all-done.centres_ref
  29.4 8.1 %weighted_fit.1 = f32[32,8,128]{2,1,0:T(8,128)} custom-call(s32[1]{0:T(128)} %bitcast.row, s32[1]{0:T(128)} %bitcast.1.col, f32[768,6144]{1,0:T(8,128)} %inv_ref.1, f32[16,1,2304]{2,1,0:T(1,128)S(1)} %all-to-all-done.centres_ref, bf16[3,64,768]{2,1,0:T(8,128)(2,1)S(1)} %get-tuple-element.18.rows_ref), custom_call_target="tpu_custom_call" | custom-call | flops 28311552 | bytes 18874368 | tf_op jit(solution)/shard_map/weighted_fit/pallas_call | solution.py:305
  37.6 5.7 %all-to-all-start.1 = ((f32[32,8,128]{2,1,0:T(8,128)}), f32[32,8,128]{2,1,0:T(8,128)S(1)}, u32[]{:S(2)}, u32[]{:S(2)}) async-start(f32[32,8,128]{2,1,0:T(8,128)} %weighted_fit.1), calls=%async_computation.1 | async-start | bytes 262144 | tf_op jit(solution)/shard_map/all_to_all | solution.py:322
  43.3 0.0 collective-permute-done.5.refs_3_
  43.3 0.0 collective-permute-done.4.refs_2_
  43.3 0.0 collective-permute-done.3.refs_1_
  43.3 8.6 %all-to-all-done.1.fits_ref = f32[32,8,128]{2,1,0:T(8,128)S(1)} async-done(((f32[32,8,128]{2,1,0:T(8,128)}), f32[32,8,128]{2,1,0:T(8,128)S(1)}, u32[]{:S(2)}, u32[]{:S(2)}) %all-to-all-start.1) | async-done | bytes 131104 | tf_op jit(solution)/shard_map/all_to_all | solution.py:322
  51.9 0.0 collective-permute-start.6
  51.9 0.5 collective-permute-start.7
  52.4 0.0 collective-permute-start.8
  52.4 0.5 collective-permute-start.9
  52.9 7.2 %steps_and_even_tiles.1 = (f32[768,6144]{1,0:T(8,128)}, f32[3,3,32]{2,1,0:T(4,128)}, f32[9,64,128]{2,1,0:T(8,128)S(1)}, bf16[768,192]{1,0:T(8,128)(2,1)S(1)}) custom-call(s32[1]{0:T(128)} %bitcast.row, s32[1]{0:T(128)} %bitcast.1.col, f32[32,8,128]{2,1,0:T(8,128)S(1)} %all-to-all-done.1.fits_ref, bf16[3,64,768]{2,1,0:T(8,128)(2,1)S(1)} %get-tuple-element.18.rows_ref, ...), custom_call_target="tpu_custom_call" | custom-call | flops 905969664 | bytes 9437184 | tf_op jit(solution)/shard_map/steps_and_even_tiles/pallas_call | solution.py:333
  60.1 0.0 collective-permute-done.6.refs_0_
  60.2 0.0 collective-permute-done.7.refs_1_
  60.2 0.0 collective-permute-done.8.refs_2_
  60.2 0.0 collective-permute-done.9.refs_3_
  60.2 4.8 %odd_tiles.1 = f32[768,6144]{1,0:T(8,128)} custom-call(s32[1]{0:T(128)} %bitcast.row, s32[1]{0:T(128)} %bitcast.1.col, f32[768,6144]{1,0:T(8,128)} %get-tuple-element.24.before_ref, f32[9,64,128]{2,1,0:T(8,128)S(1)} %get-tuple-element.25.wide_ref, bf16[768,192]{1,0:T(8,128)(2,1)S(1)} %get-tuple-element.26.rows_dev_ref, ...), custom_call_target="tpu_custom_call", output_to_operand_aliasing={{}: (2, {})} | custom-call | flops 905969664 | bytes 9437184 | tf_op jit(solution)/shard_map/odd_tiles/pallas_call | solution.py:352
  (1 shorter events, 0.0 us)
Async XLA Ops:
  0.6 11.3 %collective-permute-start.1 = (bf16[3,32,768]{2,1,0:T(8,128)(2,1)}, bf16[3,32,768]{2,1,0:T(8,128)(2,1)S(1)}, u32[]{:S(2)}, u32[]{:S(2)}) collective-permute-start(bf16[3,32,768]{2,1,0:T(8,128)(2,1)} %bitcast.3), channel_id=1, source_target_pairs={{16,0},{17,1},{18,2},{19,3},{20,4},{21,5},{22,6},{23,7},{24,8},{25... | collective-permute-start | bytes 442376 | tf_op jit(solution)/shard_map/ppermute | solution.py:249
  4.7 7.2 %collective-permute-start = (bf16[3,32,768]{2,1,0:T(8,128)(2,1)}, bf16[3,32,768]{2,1,0:T(8,128)(2,1)S(1)}, u32[]{:S(2)}, u32[]{:S(2)}) collective-permute-start(bf16[3,32,768]{2,1,0:T(8,128)(2,1)} %bitcast.4), channel_id=1, source_target_pairs={{1,0},{0,1},{3,2},{2,3},{5,4},{4,5},{7,6},{6,7},{9,8},{8,9},{11,10... | collective-permute-start | bytes 442376 | tf_op jit(solution)/shard_map/ppermute | solution.py:249
  12.9 16.6 %all-to-all-start = ((f32[16,1,2304]{2,1,0:T(1,128)}), f32[16,1,2304]{2,1,0:T(1,128)S(1)}, u32[]{:S(2)}, u32[]{:S(2)}) async-start(f32[16,1,2304]{2,1,0:T(1,128)} %get-tuple-element.17), calls=%async_computation | async-start | bytes 294912 | tf_op jit(solution)/shard_map/all_to_all | solution.py:285
  18.7 7.1 %collective-permute-start.2 = (bf16[3,32,768]{2,1,0:T(8,128)(2,1)S(1)}, bf16[3,32,768]{2,1,0:T(8,128)(2,1)S(1)}, u32[]{:S(2)}, u32[]{:S(2)}) collective-permute-start(bf16[3,32,768]{2,1,0:T(8,128)(2,1)S(1)} %collective-permute-done.1.refs_2_.refs_0_), channel_id=1, source_target_pairs={{0,1},{2,3},{4,5},{6,7},{8,9},{10,11},{12,13},{14,15},{17,16},{19,... | collective-permute-start | bytes 442376 | tf_op jit(solution)/shard_map/ppermute | solution.py:249
  25.9 17.4 %collective-permute-start.5 = (bf16[3,64,768]{2,1,0:T(8,128)(2,1)S(1)}, bf16[3,64,768]{2,1,0:T(8,128)(2,1)S(1)}, u32[]{:S(2)}, u32[]{:S(2)}) collective-permute-start(bf16[3,64,768]{2,1,0:T(8,128)(2,1)S(1)} %assemble.1.refs_0_), channel_id=1, source_target_pairs={{12,0},{13,1},{14,2},{15,3},{8,4},{9,5},{10,6},{11,7},{4,8},{5,9},... | collective-permute-start | bytes 884744 | tf_op jit(solution)/shard_map/ppermute | solution.py:249
  28.5 14.8 %collective-permute-start.4 = (bf16[3,64,768]{2,1,0:T(8,128)(2,1)S(1)}, bf16[3,64,768]{2,1,0:T(8,128)(2,1)S(1)}, u32[]{:S(2)}, u32[]{:S(2)}) collective-permute-start(bf16[3,64,768]{2,1,0:T(8,128)(2,1)S(1)} %assemble.1.refs_0_), channel_id=1, source_target_pairs={{8,0},{9,1},{10,2},{11,3},{12,4},{13,5},{14,6},{15,7},{0,8},{1,9},... | collective-permute-start | bytes 884744 | tf_op jit(solution)/shard_map/ppermute | solution.py:249
  29.0 14.3 %collective-permute-start.3 = (bf16[3,64,768]{2,1,0:T(8,128)(2,1)S(1)}, bf16[3,64,768]{2,1,0:T(8,128)(2,1)S(1)}, u32[]{:S(2)}, u32[]{:S(2)}) collective-permute-start(bf16[3,64,768]{2,1,0:T(8,128)(2,1)S(1)} %assemble.1.refs_0_), channel_id=1, source_target_pairs={{4,0},{5,1},{6,2},{7,3},{0,4},{1,5},{2,6},{3,7},{12,8},{13,9},{14,... | collective-permute-start | bytes 884744 | tf_op jit(solution)/shard_map/ppermute | solution.py:249
  37.6 14.3 %all-to-all-start.1 = ((f32[32,8,128]{2,1,0:T(8,128)}), f32[32,8,128]{2,1,0:T(8,128)S(1)}, u32[]{:S(2)}, u32[]{:S(2)}) async-start(f32[32,8,128]{2,1,0:T(8,128)} %weighted_fit.1), calls=%async_computation.1 | async-start | bytes 262144 | tf_op jit(solution)/shard_map/all_to_all | solution.py:322
  51.9 8.3 %collective-permute-start.6 = (bf16[3,64,768]{2,1,0:T(8,128)(2,1)S(1)}, bf16[3,64,768]{2,1,0:T(8,128)(2,1)S(1)}, u32[]{:S(2)}, u32[]{:S(2)}) collective-permute-start(bf16[3,64,768]{2,1,0:T(8,128)(2,1)S(1)} %assemble.1.refs_0_), channel_id=1, source_target_pairs={{2,0},{3,1},{0,2},{1,3},{6,4},{7,5},{4,6},{5,7},{10,8},{11,9},{8,1... | collective-permute-start | bytes 884744 | tf_op jit(solution)/shard_map/ppermute | solution.py:249
  51.9 8.3 %collective-permute-start.7 = (bf16[3,64,768]{2,1,0:T(8,128)(2,1)S(1)}, bf16[3,64,768]{2,1,0:T(8,128)(2,1)S(1)}, u32[]{:S(2)}, u32[]{:S(2)}) collective-permute-start(bf16[3,64,768]{2,1,0:T(8,128)(2,1)S(1)} %collective-permute-done.3.refs_1_), channel_id=1, source_target_pairs={{2,0},{3,1},{0,2},{1,3},{6,4},{7,5},{4,6},{5,7},{10,8},{11,9},{8,1... | collective-permute-start | bytes 884744 | tf_op jit(solution)/shard_map/ppermute | solution.py:249
  52.4 7.8 %collective-permute-start.8 = (bf16[3,64,768]{2,1,0:T(8,128)(2,1)S(1)}, bf16[3,64,768]{2,1,0:T(8,128)(2,1)S(1)}, u32[]{:S(2)}, u32[]{:S(2)}) collective-permute-start(bf16[3,64,768]{2,1,0:T(8,128)(2,1)S(1)} %collective-permute-done.4.refs_2_), channel_id=1, source_target_pairs={{2,0},{3,1},{0,2},{1,3},{6,4},{7,5},{4,6},{5,7},{10,8},{11,9},{8,1... | collective-permute-start | bytes 884744 | tf_op jit(solution)/shard_map/ppermute | solution.py:249
  52.4 7.8 %collective-permute-start.9 = (bf16[3,64,768]{2,1,0:T(8,128)(2,1)S(1)}, bf16[3,64,768]{2,1,0:T(8,128)(2,1)S(1)}, u32[]{:S(2)}, u32[]{:S(2)}) collective-permute-start(bf16[3,64,768]{2,1,0:T(8,128)(2,1)S(1)} %collective-permute-done.5.refs_3_), channel_id=1, source_target_pairs={{2,0},{3,1},{0,2},{1,3},{6,4},{7,5},{4,6},{5,7},{10,8},{11,9},{8,1... | collective-permute-start | bytes 884744 | tf_op jit(solution)/shard_map/ppermute | solution.py:249

commit v14 on v11

--- a/solution.py
+++ b/solution.py
@@ -68,7 +68,7 @@
     centre_ref[...] = jnp.broadcast_to(flat[None], centre_ref.shape)
 
 
-def assemble_kernel(members, row, col, centres_ref, rows_ref, *refs):
+def assemble_kernel(members, row, col, rows_ref, *refs):
     far_refs, out_ref = refs[:-1], refs[-1]
     group = row[0] // members
 
@@ -171,11 +171,8 @@
     for start in range(0, width, stride):
         for chunk in range(start // LANES, (start + stride) // LANES):
             put_deviations(wide_ref, coords_ref, centres_ref, row, chunk, dev_ref)
-        span = slice(start, start + stride)
-        for first in range(0, rows_dev_ref.shape[0], LANES):
-            strip = slice(first, first + LANES)
-            product = jnp.dot(rows_dev_ref[strip, :], dev_ref[:, span], preferred_element_type=F32)
-            out_ref[strip, span] = product * scale
+        product = jnp.dot(rows_dev_ref[...], dev_ref[:, start : start + stride], preferred_element_type=F32)
+        out_ref[:, start : start + stride] = product * scale
 
 
 def first_tiles_kernel(count, row, col, fits_ref, rows_ref, centres_ref, *refs):
@@ -288,11 +285,12 @@
     own_block = pl.pallas_call(
         functools.partial(assemble_kernel, members),
         out_shape=jax.ShapeDtypeStruct((3, frame_total, width), BF16),
-        in_specs=[smem(), smem()] + [vmem()] * (2 + col_count),
+        in_specs=[smem(), smem()] + [vmem()] * (1 + col_count),
         out_specs=vmem(),
         compiler_params=limit(8),
+        cost_estimate=pl.CostEstimate(flops=0, bytes_accessed=100 * MIB, transcendentals=0),
         name="assemble",
-    )(row, col, centres, rows_all, *far)
+    )(row, col, rows_all, *far)
     evens = [own_block] + [from_member(own_block, 2 * step) for step in range(1, half)]
 
     height = 64 if width % 64 == 0 else 8

time: 67 us -> 67.9 us (1.013)
  blocking collectives: 16.6 us -> 0 us
  waiting for transfers between devices: 6.19 us -> 14.8 us
  starting transfers between devices: 21.9 us -> 30 us
    all_to_all x1 -> x0, blocking collectives: 16.6 us -> none  [per_device(): lax.all_to_all(message, ('row', 'col'), split_axis=0, concat_axis=0, tile...]
    all_to_all x0 -> x1, waiting for transfers between devices: none -> 8.59 us  [per_device(): lax.all_to_all(message, ('row', 'col'), split_axis=0, concat_axis=0, tile...]
    all_to_all x0 -> x1, starting transfers between devices: none -> 8.22 us  [per_device(): lax.all_to_all(message, ('row', 'col'), split_axis=0, concat_axis=0, tile...]
  transfers between devices with their start and end apart: 11 -> 12, of which waited for: 2 -> 3; matrix products, arithmetic and copies ran while one was open for 0% -> 0% of each run, Pallas kernels for 23% -> 24%
where the time goes in v14:
time: 67.9 us; the launch traced here: 67.6 us
  starting transfers between devices  30 us (44%)
  Pallas kernels  22 us (32%)
  waiting for transfers between devices  14.8 us (22%)
  between operations  0.73 us (1%)
    ppermute x10, starting transfers between devices, move(): return lax.ppermute(value, ('row', 'col'), pairs)  15.6 us
    all_to_all x1, waiting for transfers between devices, per_device(): lax.all_to_all(message, ('row', 'col'), split_axis=0, concat_axis=0, tile...  8.59 us
    all_to_all x1, starting transfers between devices, per_device(): lax.all_to_all(message, ('row', 'col'), split_axis=0, concat_axis=0, tile...  8.22 us
    pallas_call x1, Pallas kernels, per_device(): pl.pallas_call(functools.partial(weighted_fit_kernel, members), in_specs=...  8.13 us
    pallas_call x1, Pallas kernels, per_device(): pl.pallas_call(functools.partial(first_tiles_kernel, half), grid_spec=plt...  7.24 us
    all_to_all x1, starting transfers between devices, per_device(): lax.all_to_all(repeated, 'row', split_axis=0, concat_axis=0, tiled=True)  6.18 us
    ppermute x10, waiting for transfers between devices, move(): return lax.ppermute(value, ('row', 'col'), pairs)  6.18 us
    pallas_call x1, Pallas kernels, per_device(): pl.pallas_call(functools.partial(last_tiles_kernel, half), grid_spec=pltp...  4.77 us
  transfers between devices with their start and end apart: 12, of which 3 were waited for; matrix products, arithmetic and copies ran while one was open for 0% of the time, Pallas kernels for 24%

profile of v14, /device:TPU:0, one launch (start us, length us, event | category | flops | bytes accessed | tf_op | source)
XLA Modules:
  0.0 67.6 jit_solution(17215271638186087344)
XLA Ops:
  0.6 3.0 %collective-permute-start = (bf16[3,32,768]{2,1,0:T(8,128)(2,1)}, bf16[3,32,768]{2,1,0:T(8,128)(2,1)S(1)}, u32[]{:S(2)}, u32[]{:S(2)}) collective-permute-start(bf16[3,32,768]{2,1,0:T(8,128)(2,1)} %bitcast.3), channel_id=1, source_target_pairs={{1,0},{0,1},{3,2},{2,3},{5,4},{4,5},{7,6},{6,7},{9,8},{8,9},{11,10... | collective-permute-start | bytes 442376 | tf_op jit(solution)/shard_map/ppermute | solution.py:244
  3.6 1.0 %load.1 = (f32[3,3,64]{2,1,0:T(4,128)S(1)}, bf16[3,32,768]{2,1,0:T(8,128)(2,1)S(1)}) custom-call(f32[3,3,64]{2,1,0:T(4,128)} %rot_hbm.1, bf16[3,32,768]{2,1,0:T(8,128)(2,1)} %bitcast.4), custom_call_target="tpu_custom_call" | custom-call | tf_op jit(solution)/shard_map/load/pallas_call | solution.py:263
  4.6 3.1 %collective-permute-done.refs_1_ = bf16[3,32,768]{2,1,0:T(8,128)(2,1)S(1)} collective-permute-done((bf16[3,32,768]{2,1,0:T(8,128)(2,1)}, bf16[3,32,768]{2,1,0:T(8,128)(2,1)S(1)}, u32[]{:S(2)}, u32[]{:S(2)}) %collective-permute-start) | collective-permute-done | bytes 147488 | tf_op jit(solution)/shard_map/ppermute | solution.py:244
  7.7 0.9 %rows.1 = (bf16[3,64,768]{2,1,0:T(8,128)(2,1)S(1)}, f32[16,1,2304]{2,1,0:T(1,128)}) custom-call(s32[1]{0:T(128)} %bitcast.1.col, f32[3,3,64]{2,1,0:T(4,128)S(1)} %get-tuple-element.15.rot_ref, bf16[3,32,768]{2,1,0:T(8,128)(2,1)S(1)} %get-tuple-element.16.refs_0_, bf16[3,32,768]{2,1,0:T(8,128)(2,1)S(1)} %collective-permute-done.refs_1_), custom_call_target="tpu_custom_call" | custom-call | tf_op jit(solution)/shard_map/rows/pallas_call | solution.py:272
  8.6 6.2 %all-to-all-start = ((f32[16,1,2304]{2,1,0:T(1,128)}), f32[16,1,2304]{2,1,0:T(1,128)S(1)}, u32[]{:S(2)}, u32[]{:S(2)}) async-start(f32[16,1,2304]{2,1,0:T(1,128)} %get-tuple-element.17), calls=%async_computation | async-start | bytes 294912 | tf_op jit(solution)/shard_map/all_to_all | solution.py:283
  14.8 4.7 %collective-permute-start.2 = (bf16[3,32,768]{2,1,0:T(8,128)(2,1)}, bf16[3,32,768]{2,1,0:T(8,128)(2,1)S(1)}, u32[]{:S(2)}, u32[]{:S(2)}) collective-permute-start(bf16[3,32,768]{2,1,0:T(8,128)(2,1)} %bitcast.5), channel_id=1, source_target_pairs={{17,1},{19,3},{21,5},{23,7},{25,9},{27,11},{29,13},{31,15},{0,16},... | collective-permute-start | bytes 442376 | tf_op jit(solution)/shard_map/ppermute | solution.py:244
  19.5 0.7 collective-permute-start.1
  20.2 3.1 %collective-permute-done.2.refs_1_ = bf16[3,32,768]{2,1,0:T(8,128)(2,1)S(1)} collective-permute-done((bf16[3,32,768]{2,1,0:T(8,128)(2,1)}, bf16[3,32,768]{2,1,0:T(8,128)(2,1)S(1)}, u32[]{:S(2)}, u32[]{:S(2)}) %collective-permute-start.2) | collective-permute-done | bytes 147488 | tf_op jit(solution)/shard_map/ppermute | solution.py:244
  23.3 0.0 collective-permute-done.1.refs_0_
  23.3 5.5 %collective-permute-start.5 = (bf16[3,64,768]{2,1,0:T(8,128)(2,1)S(1)}, bf16[3,64,768]{2,1,0:T(8,128)(2,1)S(1)}, u32[]{:S(2)}, u32[]{:S(2)}) collective-permute-start(bf16[3,64,768]{2,1,0:T(8,128)(2,1)S(1)} %assemble.1.refs_0_), channel_id=1, source_target_pairs={{12,0},{13,1},{14,2},{15,3},{8,4},{9,5},{10,6},{11,7},{4,8},{5,9},... | collective-permute-start | bytes 884744 | tf_op jit(solution)/shard_map/ppermute | solution.py:244
  28.9 0.0 collective-permute-start.4
  28.9 0.6 collective-permute-start.3
  29.5 0.0 all-to-all-done.centres_ref
  29.5 8.1 %weighted_fit.1 = f32[32,8,128]{2,1,0:T(8,128)} custom-call(s32[1]{0:T(128)} %bitcast.row, s32[1]{0:T(128)} %bitcast.1.col, f32[768,6144]{1,0:T(8,128)} %inv_ref.1, f32[16,1,2304]{2,1,0:T(1,128)S(1)} %all-to-all-done.centres_ref, bf16[3,64,768]{2,1,0:T(8,128)(2,1)S(1)} %get-tuple-element.18.rows_ref), custom_call_target="tpu_custom_call" | custom-call | flops 28311552 | bytes 18874368 | tf_op jit(solution)/shard_map/weighted_fit/pallas_call | solution.py:297
  37.7 8.2 %all-to-all-start.1 = ((f32[32,8,128]{2,1,0:T(8,128)}), f32[32,8,128]{2,1,0:T(8,128)S(1)}, u32[]{:S(2)}, u32[]{:S(2)}) async-start(f32[32,8,128]{2,1,0:T(8,128)} %weighted_fit.1), calls=%async_computation.1 | async-start | bytes 262144 | tf_op jit(solution)/shard_map/all_to_all | solution.py:314
  45.9 0.0 collective-permute-done.5.refs_3_
  45.9 0.0 collective-permute-done.4.refs_2_
  45.9 0.0 collective-permute-done.3.refs_1_
  45.9 8.6 %all-to-all-done.1.fits_ref = f32[32,8,128]{2,1,0:T(8,128)S(1)} async-done(((f32[32,8,128]{2,1,0:T(8,128)}), f32[32,8,128]{2,1,0:T(8,128)S(1)}, u32[]{:S(2)}, u32[]{:S(2)}) %all-to-all-start.1) | async-done | bytes 131104 | tf_op jit(solution)/shard_map/all_to_all | solution.py:314
  54.5 0.0 collective-permute-start.6
  54.5 0.5 collective-permute-start.7
  55.0 0.0 collective-permute-start.8
  55.0 0.5 collective-permute-start.9
  55.5 7.2 %steps_and_even_tiles.1 = (f32[768,6144]{1,0:T(8,128)}, f32[3,3,32]{2,1,0:T(4,128)}, f32[9,64,128]{2,1,0:T(8,128)S(1)}, bf16[768,192]{1,0:T(8,128)(2,1)S(1)}) custom-call(s32[1]{0:T(128)} %bitcast.row, s32[1]{0:T(128)} %bitcast.1.col, f32[32,8,128]{2,1,0:T(8,128)S(1)} %all-to-all-done.1.fits_ref, bf16[3,64,768]{2,1,0:T(8,128)(2,1)S(1)} %get-tuple-element.18.rows_ref, ...), custom_call_target="tpu_custom_call" | custom-call | flops 905969664 | bytes 9437184 | tf_op jit(solution)/shard_map/steps_and_even_tiles/pallas_call | solution.py:325
  62.8 0.0 collective-permute-done.6.refs_0_
  62.8 0.0 collective-permute-done.7.refs_1_
  62.8 0.0 collective-permute-done.8.refs_2_
  62.8 0.0 collective-permute-done.9.refs_3_
  62.8 4.8 %odd_tiles.1 = f32[768,6144]{1,0:T(8,128)} custom-call(s32[1]{0:T(128)} %bitcast.row, s32[1]{0:T(128)} %bitcast.1.col, f32[768,6144]{1,0:T(8,128)} %get-tuple-element.24.before_ref, f32[9,64,128]{2,1,0:T(8,128)S(1)} %get-tuple-element.25.wide_ref, bf16[768,192]{1,0:T(8,128)(2,1)S(1)} %get-tuple-element.26.rows_dev_ref, ...), custom_call_target="tpu_custom_call", output_to_operand_aliasing={{}: (2, {})} | custom-call | flops 905969664 | bytes 9437184 | tf_op jit(solution)/shard_map/odd_tiles/pallas_call | solution.py:344
  (1 shorter events, 0.0 us)
Async XLA Ops:
  0.6 7.1 %collective-permute-start = (bf16[3,32,768]{2,1,0:T(8,128)(2,1)}, bf16[3,32,768]{2,1,0:T(8,128)(2,1)S(1)}, u32[]{:S(2)}, u32[]{:S(2)}) collective-permute-start(bf16[3,32,768]{2,1,0:T(8,128)(2,1)} %bitcast.3), channel_id=1, source_target_pairs={{1,0},{0,1},{3,2},{2,3},{5,4},{4,5},{7,6},{6,7},{9,8},{8,9},{11,10... | collective-permute-start | bytes 442376 | tf_op jit(solution)/shard_map/ppermute | solution.py:244
  8.6 20.9 %all-to-all-start = ((f32[16,1,2304]{2,1,0:T(1,128)}), f32[16,1,2304]{2,1,0:T(1,128)S(1)}, u32[]{:S(2)}, u32[]{:S(2)}) async-start(f32[16,1,2304]{2,1,0:T(1,128)} %get-tuple-element.17), calls=%async_computation | async-start | bytes 294912 | tf_op jit(solution)/shard_map/all_to_all | solution.py:283
  14.8 8.5 %collective-permute-start.2 = (bf16[3,32,768]{2,1,0:T(8,128)(2,1)}, bf16[3,32,768]{2,1,0:T(8,128)(2,1)S(1)}, u32[]{:S(2)}, u32[]{:S(2)}) collective-permute-start(bf16[3,32,768]{2,1,0:T(8,128)(2,1)} %bitcast.5), channel_id=1, source_target_pairs={{17,1},{19,3},{21,5},{23,7},{25,9},{27,11},{29,13},{31,15},{0,16},... | collective-permute-start | bytes 442376 | tf_op jit(solution)/shard_map/ppermute | solution.py:244
  19.5 3.8 %collective-permute-start.1 = (bf16[3,32,768]{2,1,0:T(8,128)(2,1)}, bf16[3,32,768]{2,1,0:T(8,128)(2,1)S(1)}, u32[]{:S(2)}, u32[]{:S(2)}) collective-permute-start(bf16[3,32,768]{2,1,0:T(8,128)(2,1)} %bitcast.6), channel_id=1, source_target_pairs={{16,1},{18,3},{20,5},{22,7},{24,9},{26,11},{28,13},{30,15},{1,16},... | collective-permute-start | bytes 442376 | tf_op jit(solution)/shard_map/ppermute | solution.py:244
  23.3 22.6 %collective-permute-start.5 = (bf16[3,64,768]{2,1,0:T(8,128)(2,1)S(1)}, bf16[3,64,768]{2,1,0:T(8,128)(2,1)S(1)}, u32[]{:S(2)}, u32[]{:S(2)}) collective-permute-start(bf16[3,64,768]{2,1,0:T(8,128)(2,1)S(1)} %assemble.1.refs_0_), channel_id=1, source_target_pairs={{12,0},{13,1},{14,2},{15,3},{8,4},{9,5},{10,6},{11,7},{4,8},{5,9},... | collective-permute-start | bytes 884744 | tf_op jit(solution)/shard_map/ppermute | solution.py:244
  28.9 17.0 %collective-permute-start.4 = (bf16[3,64,768]{2,1,0:T(8,128)(2,1)S(1)}, bf16[3,64,768]{2,1,0:T(8,128)(2,1)S(1)}, u32[]{:S(2)}, u32[]{:S(2)}) collective-permute-start(bf16[3,64,768]{2,1,0:T(8,128)(2,1)S(1)} %assemble.1.refs_0_), channel_id=1, source_target_pairs={{8,0},{9,1},{10,2},{11,3},{12,4},{13,5},{14,6},{15,7},{0,8},{1,9},... | collective-permute-start | bytes 884744 | tf_op jit(solution)/shard_map/ppermute | solution.py:244
  28.9 17.0 %collective-permute-start.3 = (bf16[3,64,768]{2,1,0:T(8,128)(2,1)S(1)}, bf16[3,64,768]{2,1,0:T(8,128)(2,1)S(1)}, u32[]{:S(2)}, u32[]{:S(2)}) collective-permute-start(bf16[3,64,768]{2,1,0:T(8,128)(2,1)S(1)} %assemble.1.refs_0_), channel_id=1, source_target_pairs={{4,0},{5,1},{6,2},{7,3},{0,4},{1,5},{2,6},{3,7},{12,8},{13,9},{14,... | collective-permute-start | bytes 884744 | tf_op jit(solution)/shard_map/ppermute | solution.py:244
  37.7 16.9 %all-to-all-start.1 = ((f32[32,8,128]{2,1,0:T(8,128)}), f32[32,8,128]{2,1,0:T(8,128)S(1)}, u32[]{:S(2)}, u32[]{:S(2)}) async-start(f32[32,8,128]{2,1,0:T(8,128)} %weighted_fit.1), calls=%async_computation.1 | async-start | bytes 262144 | tf_op jit(solution)/shard_map/all_to_all | solution.py:314
  54.5 8.3 %collective-permute-start.6 = (bf16[3,64,768]{2,1,0:T(8,128)(2,1)S(1)}, bf16[3,64,768]{2,1,0:T(8,128)(2,1)S(1)}, u32[]{:S(2)}, u32[]{:S(2)}) collective-permute-start(bf16[3,64,768]{2,1,0:T(8,128)(2,1)S(1)} %assemble.1.refs_0_), channel_id=1, source_target_pairs={{2,0},{3,1},{0,2},{1,3},{6,4},{7,5},{4,6},{5,7},{10,8},{11,9},{8,1... | collective-permute-start | bytes 884744 | tf_op jit(solution)/shard_map/ppermute | solution.py:244
  54.5 8.3 %collective-permute-start.7 = (bf16[3,64,768]{2,1,0:T(8,128)(2,1)S(1)}, bf16[3,64,768]{2,1,0:T(8,128)(2,1)S(1)}, u32[]{:S(2)}, u32[]{:S(2)}) collective-permute-start(bf16[3,64,768]{2,1,0:T(8,128)(2,1)S(1)} %collective-permute-done.3.refs_1_), channel_id=1, source_target_pairs={{2,0},{3,1},{0,2},{1,3},{6,4},{7,5},{4,6},{5,7},{10,8},{11,9},{8,1... | collective-permute-start | bytes 884744 | tf_op jit(solution)/shard_map/ppermute | solution.py:244
  55.0 7.8 %collective-permute-start.8 = (bf16[3,64,768]{2,1,0:T(8,128)(2,1)S(1)}, bf16[3,64,768]{2,1,0:T(8,128)(2,1)S(1)}, u32[]{:S(2)}, u32[]{:S(2)}) collective-permute-start(bf16[3,64,768]{2,1,0:T(8,128)(2,1)S(1)} %collective-permute-done.4.refs_2_), channel_id=1, source_target_pairs={{2,0},{3,1},{0,2},{1,3},{6,4},{7,5},{4,6},{5,7},{10,8},{11,9},{8,1... | collective-permute-start | bytes 884744 | tf_op jit(solution)/shard_map/ppermute | solution.py:244
  55.0 7.8 %collective-permute-start.9 = (bf16[3,64,768]{2,1,0:T(8,128)(2,1)S(1)}, bf16[3,64,768]{2,1,0:T(8,128)(2,1)S(1)}, u32[]{:S(2)}, u32[]{:S(2)}) collective-permute-start(bf16[3,64,768]{2,1,0:T(8,128)(2,1)S(1)} %collective-permute-done.5.refs_3_), channel_id=1, source_target_pairs={{2,0},{3,1},{0,2},{1,3},{6,4},{7,5},{4,6},{5,7},{10,8},{11,9},{8,1... | collective-permute-start | bytes 884744 | tf_op jit(solution)/shard_map/ppermute | solution.py:244

commit v15 on v12

--- a/solution.py
+++ b/solution.py
@@ -180,9 +180,9 @@
         out_ref[:, start : start + stride] = product * scale
 
 
-def first_tiles_kernel(count, row, col, fits_ref, rows_ref, centres_ref, *refs):
-    panel_refs = refs[:count]
-    out_ref, rot_out_ref, wide_ref, rows_dev_ref, dev_ref = refs[count:]
+def covariance_kernel(members, row, col, fits_ref, rows_ref, centres_ref, *refs):
+    panel_refs = refs[:members]
+    out_ref, rot_out_ref, wide_ref, rows_dev_ref, dev_ref = refs[members:]
     frame_total = rows_ref.shape[1]
     local = rot_out_ref.shape[2]
 
@@ -203,22 +203,11 @@
             put_deviations(wide_ref, rows_ref, centres_ref, row[0], chunk, dev_ref)
         rows_dev_ref[...] = dev_ref[...].T
 
-    for step in range(count):
+    for step in range(members):
 
         @pl.when(pl.program_id(0) == step)
         def _(step=step):
-            block = col[0] * 2 * count + (lax.rem(row[0], 2 * count) ^ (2 * step))
-            put_tile(wide_ref, panel_refs[step], centres_ref, block, rows_dev_ref, dev_ref, out_ref)
-
-
-def last_tiles_kernel(count, row, col, before_ref, wide_ref, rows_dev_ref, centres_ref, *refs):
-    panel_refs = refs[:count]
-    out_ref, dev_ref = refs[count:]
-    for step in range(count):
-
-        @pl.when(pl.program_id(0) == step)
-        def _(step=step):
-            block = col[0] * 2 * count + (lax.rem(row[0], 2 * count) ^ (2 * step + 1))
+            block = col[0] * members + (lax.rem(row[0], members) ^ step)
             put_tile(wide_ref, panel_refs[step], centres_ref, block, rows_dev_ref, dev_ref, out_ref)
 
 
@@ -320,50 +309,36 @@
         name="weighted_fit",
     )(row, col, in_hbm(inverse_cov), centres, rows_all)
     fits = lax.all_to_all(message, ("row", "col"), split_axis=0, concat_axis=0, tiled=True)
-    fits, evens = lax.optimization_barrier((fits, evens))
-    odds = [from_member(block, 1) for block in evens]
-
-    def tile_spec(odd):
-        return pl.BlockSpec((width, width), lambda i, row, *_: (0, lax.rem(row[0], members) ^ (2 * i + odd)))
-
-    tiles_cost = pl.CostEstimate(
-        flops=3 * frame_total * width * col_width, bytes_accessed=2 * width * col_width, transcendentals=0
-    )
-    dev_scratch = pltpu.VMEM((3 * frame_total, width), BF16)
-    half_done, transforms, wide, rows_dev = pl.pallas_call(
-        functools.partial(first_tiles_kernel, half),
+    panel = [None] * members
+    panel[0::2] = evens
+    panel[1::2] = [from_member(block, 1) for block in evens]
+
+    covariance, transforms = pl.pallas_call(
+        functools.partial(covariance_kernel, members),
         grid_spec=pltpu.PrefetchScalarGridSpec(
             num_scalar_prefetch=2,
-            grid=(half,),
-            in_specs=[vmem()] * (3 + half),
-            out_specs=(tile_spec(0), vmem(), vmem(), vmem()),
-            scratch_shapes=[dev_scratch],
+            grid=(members,),
+            in_specs=[vmem()] * (3 + members),
+            out_specs=(
+                pl.BlockSpec((width, width), lambda i, row, col: (0, lax.rem(row[0], members) ^ i)),
+                vmem(),
+            ),
+            scratch_shapes=[
+                pltpu.VMEM((9, frame_total, LANES), F32),
+                pltpu.VMEM((width, 3 * frame_total), BF16),
+                pltpu.VMEM((3 * frame_total, width), BF16),
+            ],
         ),
         out_shape=(
             jax.ShapeDtypeStruct((width, col_width), F32),
             jax.ShapeDtypeStruct((3, 3, local), F32),
-            jax.ShapeDtypeStruct((9, frame_total, LANES), F32),
-            jax.ShapeDtypeStruct((width, 3 * frame_total), BF16),
         ),
         compiler_params=limit(16),
-        cost_estimate=tiles_cost,
-        name="steps_and_even_tiles",
-    )(row, col, fits, rows_all, centres, *evens)
-    covariance = pl.pallas_call(
-        functools.partial(last_tiles_kernel, half),
-        grid_spec=pltpu.PrefetchScalarGridSpec(
-            num_scalar_prefetch=2,
-            grid=(half,),
-            in_specs=[pl.BlockSpec(memory_space=pl.ANY)] + [vmem()] * (3 + half),
-            out_specs=tile_spec(1),
-            scratch_shapes=[dev_scratch],
-        ),
-        out_shape=jax.ShapeDtypeStruct((width, col_width), F32),
-        input_output_aliases={2: 0},
-        compiler_params=limit(16),
-        cost_estimate=tiles_cost,
-        name="odd_tiles",
-    )(row, col, half_done, wide, rows_dev, centres, *odds)
+        cost_estimate=pl.CostEstimate(
+            flops=6 * frame_total * width * col_width, bytes_accessed=4 * width * col_width, transcendentals=0
+        ),
+        name="covariance",
+    )(row, col, fits, rows_all, centres, *panel)
     return (covariance, transforms)
 
 

time: 61.3 us -> 70.4 us (1.15)
  waiting for transfers between devices: 12.8 us -> 24.2 us
  starting transfers between devices: 25.5 us -> 23.9 us
  Pallas kernels: 22 us -> 21.2 us
    ppermute x10, waiting for transfers between devices: 4.19 us -> 10.5 us  [move(): return lax.ppermute(value, ('row', 'col'), pairs)]
    all_to_all x1, waiting for transfers between devices: 0.01 us -> 5.11 us  [per_device(): lax.all_to_all(repeated, 'row', split_axis=0, concat_axis=0, tiled=True)]
    all_to_all x1, starting transfers between devices: 5.71 us -> 2.81 us  [per_device(): lax.all_to_all(message, ('row', 'col'), split_axis=0, concat_axis=0, tile...]
    all_to_all x1, starting transfers between devices: 6.19 us -> 7.43 us  [per_device(): lax.all_to_all(repeated, 'row', split_axis=0, concat_axis=0, tiled=True)]
    pallas_call x2 -> x1, Pallas kernels: 12 us -> 11.2 us  [per_device(): pl.pallas_call(functools.partial(covariance_kernel, members), grid_spec=p...]
  transfers between devices with their start and end apart: 12 -> 12, of which waited for: 3 -> 5; matrix products, arithmetic and copies ran while one was open for 0% -> 0% of each run, Pallas kernels for 28% -> 14%
where the time goes in v15:
time: 70.4 us; the launch traced here: 70.1 us
  waiting for transfers between devices  24.2 us (34%)
  starting transfers between devices  23.9 us (34%)
  Pallas kernels  21.2 us (30%)
  between operations  0.71 us (1%)
    ppermute x10, starting transfers between devices, move(): return lax.ppermute(value, ('row', 'col'), pairs)  13.7 us
    pallas_call x1, Pallas kernels, per_device(): pl.pallas_call(functools.partial(covariance_kernel, members), grid_spec=p...  11.2 us
    ppermute x10, waiting for transfers between devices, move(): return lax.ppermute(value, ('row', 'col'), pairs)  10.5 us
    all_to_all x1, waiting for transfers between devices, per_device(): lax.all_to_all(message, ('row', 'col'), split_axis=0, concat_axis=0, tile...  8.61 us
    pallas_call x1, Pallas kernels, per_device(): pl.pallas_call(functools.partial(weighted_fit_kernel, members), in_specs=...  8.13 us
    all_to_all x1, starting transfers between devices, per_device(): lax.all_to_all(repeated, 'row', split_axis=0, concat_axis=0, tiled=True)  7.43 us
    all_to_all x1, waiting for transfers between devices, per_device(): lax.all_to_all(repeated, 'row', split_axis=0, concat_axis=0, tiled=True)  5.11 us
    all_to_all x1, starting transfers between devices, per_device(): lax.all_to_all(message, ('row', 'col'), split_axis=0, concat_axis=0, tile...  2.81 us
  transfers between devices with their start and end apart: 12, of which 5 were waited for; matrix products, arithmetic and copies ran while one was open for 0% of the time, Pallas kernels for 14%

profile of v15, /device:TPU:0, one launch (start us, length us, event | category | flops | bytes accessed | tf_op | source)
XLA Modules:
  0.0 70.1 jit_solution(9000442463936742967)
XLA Ops:
  0.6 4.1 %collective-permute-start.1 = (bf16[3,32,768]{2,1,0:T(8,128)(2,1)}, bf16[3,32,768]{2,1,0:T(8,128)(2,1)S(1)}, u32[]{:S(2)}, u32[]{:S(2)}) collective-permute-start(bf16[3,32,768]{2,1,0:T(8,128)(2,1)} %bitcast.3), channel_id=1, source_target_pairs={{16,0},{17,1},{18,2},{19,3},{20,4},{21,5},{22,6},{23,7},{24,8},{25... | collective-permute-start | bytes 442376 | tf_op jit(solution)/shard_map/ppermute | solution.py:238
  4.7 1.5 %collective-permute-start = (bf16[3,32,768]{2,1,0:T(8,128)(2,1)}, bf16[3,32,768]{2,1,0:T(8,128)(2,1)S(1)}, u32[]{:S(2)}, u32[]{:S(2)}) collective-permute-start(bf16[3,32,768]{2,1,0:T(8,128)(2,1)} %bitcast.4), channel_id=1, source_target_pairs={{1,0},{0,1},{3,2},{2,3},{5,4},{4,5},{7,6},{6,7},{9,8},{8,9},{11,10... | collective-permute-start | bytes 442376 | tf_op jit(solution)/shard_map/ppermute | solution.py:238
  6.2 5.7 %collective-permute-done.1.refs_0_ = bf16[3,32,768]{2,1,0:T(8,128)(2,1)S(1)} collective-permute-done((bf16[3,32,768]{2,1,0:T(8,128)(2,1)}, bf16[3,32,768]{2,1,0:T(8,128)(2,1)S(1)}, u32[]{:S(2)}, u32[]{:S(2)}) %collective-permute-start.1) | collective-permute-done | bytes 147488 | tf_op jit(solution)/shard_map/ppermute | solution.py:238
  11.9 3.4 %collective-permute-start.2 = (bf16[3,32,768]{2,1,0:T(8,128)(2,1)S(1)}, bf16[3,32,768]{2,1,0:T(8,128)(2,1)S(1)}, u32[]{:S(2)}, u32[]{:S(2)}) collective-permute-start(bf16[3,32,768]{2,1,0:T(8,128)(2,1)S(1)} %collective-permute-done.1.refs_0_), channel_id=1, source_target_pairs={{0,1},{2,3},{4,5},{6,7},{8,9},{10,11},{12,13},{14,15},{17,16},{19,... | collective-permute-start | bytes 442376 | tf_op jit(solution)/shard_map/ppermute | solution.py:238
  15.4 0.9 %load.1 = (f32[3,3,64]{2,1,0:T(4,128)S(1)}, bf16[3,32,768]{2,1,0:T(8,128)(2,1)S(1)}) custom-call(f32[3,3,64]{2,1,0:T(4,128)} %rot_hbm.1, bf16[3,32,768]{2,1,0:T(8,128)(2,1)} %bitcast.5), custom_call_target="tpu_custom_call" | custom-call | tf_op jit(solution)/shard_map/load/pallas_call | solution.py:254
  16.4 0.0 collective-permute-done.refs_1_
  16.4 0.9 %rows.1 = (bf16[3,64,768]{2,1,0:T(8,128)(2,1)S(1)}, f32[16,1,2304]{2,1,0:T(1,128)}) custom-call(s32[1]{0:T(128)} %bitcast.1.col, f32[3,3,64]{2,1,0:T(4,128)S(1)} %get-tuple-element.6.rot_ref, bf16[3,32,768]{2,1,0:T(8,128)(2,1)S(1)} %get-tuple-element.7.refs_0_, bf16[3,32,768]{2,1,0:T(8,128)(2,1)S(1)} %collective-permute-done.refs_1_), custom_call_target="tpu_custom_call" | custom-call | tf_op jit(solution)/shard_map/rows/pallas_call | solution.py:263
  17.3 0.8 %collective-permute-done.2.refs_1_ = bf16[3,32,768]{2,1,0:T(8,128)(2,1)S(1)} collective-permute-done((bf16[3,32,768]{2,1,0:T(8,128)(2,1)S(1)}, bf16[3,32,768]{2,1,0:T(8,128)(2,1)S(1)}, u32[]{:S(2)}, u32[]{:S(2)}) %collective-permute-start.2) | collective-permute-done | bytes 147488 | tf_op jit(solution)/shard_map/ppermute | solution.py:238
  18.1 2.4 %collective-permute-start.8 = (bf16[3,64,768]{2,1,0:T(8,128)(2,1)S(1)}, bf16[3,64,768]{2,1,0:T(8,128)(2,1)S(1)}, u32[]{:S(2)}, u32[]{:S(2)}) collective-permute-start(bf16[3,64,768]{2,1,0:T(8,128)(2,1)S(1)} %assemble.1.refs_0_), channel_id=1, source_target_pairs={{12,0},{13,1},{14,2},{15,3},{8,4},{9,5},{10,6},{11,7},{4,8},{5,9},... | collective-permute-start | bytes 884744 | tf_op jit(solution)/shard_map/ppermute | solution.py:238
  20.5 0.6 collective-permute-start.6
  21.1 0.5 collective-permute-start.4
  21.6 7.4 %all-to-all-start = ((f32[16,1,2304]{2,1,0:T(1,128)}), f32[16,1,2304]{2,1,0:T(1,128)S(1)}, u32[]{:S(2)}, u32[]{:S(2)}) async-start(f32[16,1,2304]{2,1,0:T(1,128)} %get-tuple-element.8), calls=%async_computation | async-start | bytes 294912 | tf_op jit(solution)/shard_map/all_to_all | solution.py:274
  29.1 0.4 collective-permute-start.3
  29.5 0.0 collective-permute-done.8.refs_6_
  29.5 0.2 collective-permute-start.9
  29.6 4.0 %collective-permute-done.6.refs_4_ = bf16[3,64,768]{2,1,0:T(8,128)(2,1)S(1)} collective-permute-done((bf16[3,64,768]{2,1,0:T(8,128)(2,1)S(1)}, bf16[3,64,768]{2,1,0:T(8,128)(2,1)S(1)}, u32[]{:S(2)}, u32[]{:S(2)}) %collective-permute-start.6) | collective-permute-done | bytes 294944 | tf_op jit(solution)/shard_map/ppermute | solution.py:238
  33.6 0.0 collective-permute-start.7
  33.6 0.0 collective-permute-done.4.refs_2_
  33.6 0.5 collective-permute-start.5
  34.2 5.1 %all-to-all-done.centres_ref = f32[16,1,2304]{2,1,0:T(1,128)S(1)} async-done(((f32[16,1,2304]{2,1,0:T(1,128)}), f32[16,1,2304]{2,1,0:T(1,128)S(1)}, u32[]{:S(2)}, u32[]{:S(2)}) %all-to-all-start) | async-done | bytes 147488 | tf_op jit(solution)/shard_map/all_to_all | solution.py:274
  39.3 8.1 %weighted_fit.1 = f32[32,8,128]{2,1,0:T(8,128)} custom-call(s32[1]{0:T(128)} %bitcast.row, s32[1]{0:T(128)} %bitcast.1.col, f32[768,6144]{1,0:T(8,128)} %inv_ref.1, f32[16,1,2304]{2,1,0:T(1,128)S(1)} %all-to-all-done.centres_ref, bf16[3,64,768]{2,1,0:T(8,128)(2,1)S(1)} %get-tuple-element.9.rows_ref), custom_call_target="tpu_custom_call" | custom-call | flops 28311552 | bytes 18874368 | tf_op jit(solution)/shard_map/weighted_fit/pallas_call | solution.py:294
  47.4 2.8 %all-to-all-start.1 = ((f32[32,8,128]{2,1,0:T(8,128)}), f32[32,8,128]{2,1,0:T(8,128)S(1)}, u32[]{:S(2)}, u32[]{:S(2)}) async-start(f32[32,8,128]{2,1,0:T(8,128)} %weighted_fit.1), calls=%async_computation.1 | async-start | bytes 262144 | tf_op jit(solution)/shard_map/all_to_all | solution.py:311
  50.2 0.0 collective-permute-done.3.refs_1_
  50.2 8.6 %all-to-all-done.1.fits_ref = f32[32,8,128]{2,1,0:T(8,128)S(1)} async-done(((f32[32,8,128]{2,1,0:T(8,128)}), f32[32,8,128]{2,1,0:T(8,128)S(1)}, u32[]{:S(2)}, u32[]{:S(2)}) %all-to-all-start.1) | async-done | bytes 131104 | tf_op jit(solution)/shard_map/all_to_all | solution.py:311
  58.9 0.0 collective-permute-done.9.refs_7_
  58.9 0.0 collective-permute-done.7.refs_5_
  58.9 0.0 collective-permute-done.5.refs_3_
  58.9 11.2 %covariance.1 = (f32[768,6144]{1,0:T(8,128)}, f32[3,3,32]{2,1,0:T(4,128)}) custom-call(s32[1]{0:T(128)} %bitcast.row, s32[1]{0:T(128)} %bitcast.1.col, f32[32,8,128]{2,1,0:T(8,128)S(1)} %all-to-all-done.1.fits_ref, bf16[3,64,768]{2,1,0:T(8,128)(2,1)S(1)} %get-tuple-element.9.rows_ref, f32[16,1,2304]{2,1,0:T(1,128)S(1)} %all-to-all-done.centres_ref, ...), custom_call_target="tpu_custom_call" | custom-call | flops 1811939328 | bytes 18874368 | tf_op jit(solution)/shard_map/covariance/pallas_call | solution.py:316
  (1 shorter events, 0.0 us)
Async XLA Ops:
  0.6 11.3 %collective-permute-start.1 = (bf16[3,32,768]{2,1,0:T(8,128)(2,1)}, bf16[3,32,768]{2,1,0:T(8,128)(2,1)S(1)}, u32[]{:S(2)}, u32[]{:S(2)}) collective-permute-start(bf16[3,32,768]{2,1,0:T(8,128)(2,1)} %bitcast.3), channel_id=1, source_target_pairs={{16,0},{17,1},{18,2},{19,3},{20,4},{21,5},{22,6},{23,7},{24,8},{25... | collective-permute-start | bytes 442376 | tf_op jit(solution)/shard_map/ppermute | solution.py:238
  4.7 11.6 %collective-permute-start = (bf16[3,32,768]{2,1,0:T(8,128)(2,1)}, bf16[3,32,768]{2,1,0:T(8,128)(2,1)S(1)}, u32[]{:S(2)}, u32[]{:S(2)}) collective-permute-start(bf16[3,32,768]{2,1,0:T(8,128)(2,1)} %bitcast.4), channel_id=1, source_target_pairs={{1,0},{0,1},{3,2},{2,3},{5,4},{4,5},{7,6},{6,7},{9,8},{8,9},{11,10... | collective-permute-start | bytes 442376 | tf_op jit(solution)/shard_map/ppermute | solution.py:238
  11.9 6.1 %collective-permute-start.2 = (bf16[3,32,768]{2,1,0:T(8,128)(2,1)S(1)}, bf16[3,32,768]{2,1,0:T(8,128)(2,1)S(1)}, u32[]{:S(2)}, u32[]{:S(2)}) collective-permute-start(bf16[3,32,768]{2,1,0:T(8,128)(2,1)S(1)} %collective-permute-done.1.refs_0_), channel_id=1, source_target_pairs={{0,1},{2,3},{4,5},{6,7},{8,9},{10,11},{12,13},{14,15},{17,16},{19,... | collective-permute-start | bytes 442376 | tf_op jit(solution)/shard_map/ppermute | solution.py:238
  18.1 11.4 %collective-permute-start.8 = (bf16[3,64,768]{2,1,0:T(8,128)(2,1)S(1)}, bf16[3,64,768]{2,1,0:T(8,128)(2,1)S(1)}, u32[]{:S(2)}, u32[]{:S(2)}) collective-permute-start(bf16[3,64,768]{2,1,0:T(8,128)(2,1)S(1)} %assemble.1.refs_0_), channel_id=1, source_target_pairs={{12,0},{13,1},{14,2},{15,3},{8,4},{9,5},{10,6},{11,7},{4,8},{5,9},... | collective-permute-start | bytes 884744 | tf_op jit(solution)/shard_map/ppermute | solution.py:238
  20.5 13.2 %collective-permute-start.6 = (bf16[3,64,768]{2,1,0:T(8,128)(2,1)S(1)}, bf16[3,64,768]{2,1,0:T(8,128)(2,1)S(1)}, u32[]{:S(2)}, u32[]{:S(2)}) collective-permute-start(bf16[3,64,768]{2,1,0:T(8,128)(2,1)S(1)} %assemble.1.refs_0_), channel_id=1, source_target_pairs={{8,0},{9,1},{10,2},{11,3},{12,4},{13,5},{14,6},{15,7},{0,8},{1,9},... | collective-permute-start | bytes 884744 | tf_op jit(solution)/shard_map/ppermute | solution.py:238
  21.1 12.5 %collective-permute-start.4 = (bf16[3,64,768]{2,1,0:T(8,128)(2,1)S(1)}, bf16[3,64,768]{2,1,0:T(8,128)(2,1)S(1)}, u32[]{:S(2)}, u32[]{:S(2)}) collective-permute-start(bf16[3,64,768]{2,1,0:T(8,128)(2,1)S(1)} %assemble.1.refs_0_), channel_id=1, source_target_pairs={{4,0},{5,1},{6,2},{7,3},{0,4},{1,5},{2,6},{3,7},{12,8},{13,9},{14,... | collective-permute-start | bytes 884744 | tf_op jit(solution)/shard_map/ppermute | solution.py:238
  21.6 17.6 %all-to-all-start = ((f32[16,1,2304]{2,1,0:T(1,128)}), f32[16,1,2304]{2,1,0:T(1,128)S(1)}, u32[]{:S(2)}, u32[]{:S(2)}) async-start(f32[16,1,2304]{2,1,0:T(1,128)} %get-tuple-element.8), calls=%async_computation | async-start | bytes 294912 | tf_op jit(solution)/shard_map/all_to_all | solution.py:274
  29.1 21.2 %collective-permute-start.3 = (bf16[3,64,768]{2,1,0:T(8,128)(2,1)S(1)}, bf16[3,64,768]{2,1,0:T(8,128)(2,1)S(1)}, u32[]{:S(2)}, u32[]{:S(2)}) collective-permute-start(bf16[3,64,768]{2,1,0:T(8,128)(2,1)S(1)} %assemble.1.refs_0_), channel_id=1, source_target_pairs={{2,0},{3,1},{0,2},{1,3},{6,4},{7,5},{4,6},{5,7},{10,8},{11,9},{8,1... | collective-permute-start | bytes 884744 | tf_op jit(solution)/shard_map/ppermute | solution.py:238
  29.5 29.4 %collective-permute-start.9 = (bf16[3,64,768]{2,1,0:T(8,128)(2,1)S(1)}, bf16[3,64,768]{2,1,0:T(8,128)(2,1)S(1)}, u32[]{:S(2)}, u32[]{:S(2)}) collective-permute-start(bf16[3,64,768]{2,1,0:T(8,128)(2,1)S(1)} %collective-permute-done.8.refs_6_), channel_id=1, source_target_pairs={{2,0},{3,1},{0,2},{1,3},{6,4},{7,5},{4,6},{5,7},{10,8},{11,9},{8,1... | collective-permute-start | bytes 884744 | tf_op jit(solution)/shard_map/ppermute | solution.py:238
  33.6 25.2 %collective-permute-start.7 = (bf16[3,64,768]{2,1,0:T(8,128)(2,1)S(1)}, bf16[3,64,768]{2,1,0:T(8,128)(2,1)S(1)}, u32[]{:S(2)}, u32[]{:S(2)}) collective-permute-start(bf16[3,64,768]{2,1,0:T(8,128)(2,1)S(1)} %collective-permute-done.6.refs_4_), channel_id=1, source_target_pairs={{2,0},{3,1},{0,2},{1,3},{6,4},{7,5},{4,6},{5,7},{10,8},{11,9},{8,1... | collective-permute-start | bytes 884744 | tf_op jit(solution)/shard_map/ppermute | solution.py:238
  33.6 25.2 %collective-permute-start.5 = (bf16[3,64,768]{2,1,0:T(8,128)(2,1)S(1)}, bf16[3,64,768]{2,1,0:T(8,128)(2,1)S(1)}, u32[]{:S(2)}, u32[]{:S(2)}) collective-permute-start(bf16[3,64,768]{2,1,0:T(8,128)(2,1)S(1)} %collective-permute-done.4.refs_2_), channel_id=1, source_target_pairs={{2,0},{3,1},{0,2},{1,3},{6,4},{7,5},{4,6},{5,7},{10,8},{11,9},{8,1... | collective-permute-start | bytes 884744 | tf_op jit(solution)/shard_map/ppermute | solution.py:238
  47.4 11.4 %all-to-all-start.1 = ((f32[32,8,128]{2,1,0:T(8,128)}), f32[32,8,128]{2,1,0:T(8,128)S(1)}, u32[]{:S(2)}, u32[]{:S(2)}) async-start(f32[32,8,128]{2,1,0:T(8,128)} %weighted_fit.1), calls=%async_computation.1 | async-start | bytes 262144 | tf_op jit(solution)/shard_map/all_to_all | solution.py:311

commit v16 on v15

--- a/solution.py
+++ b/solution.py
@@ -68,7 +68,23 @@
     centre_ref[...] = jnp.broadcast_to(flat[None], centre_ref.shape)
 
 
-def assemble_kernel(members, row, col, rows_ref, *refs):
+def pick_kernel(members, step, row, col, rows_ref, *refs):
+    far_refs, out_ref = refs[:-1], refs[-1]
+    col_count, local = len(far_refs) + 1, out_ref.shape[1]
+    index = lax.rem(col[0] + 2 * col_count - row[0] // members - step, col_count)
+
+    @pl.when(index == 0)
+    def _():
+        out_ref[...] = rows_ref[:, pl.ds(pl.multiple_of(col[0] * local, local), local), :]
+
+    for shift, ref in enumerate(far_refs):
+
+        @pl.when(index == shift + 1)
+        def _(ref=ref):
+            out_ref[...] = ref[...]
+
+
+def assemble_kernel(members, row, col, centres_ref, rows_ref, *refs):
     sources, out_ref = refs[:-1], refs[-1]
     far_refs, across_refs = sources[: len(sources) // 2], sources[len(sources) // 2 :]
     col_count = len(far_refs) + 1
@@ -87,7 +103,7 @@
                 put_block(out_ref, lax.rem(col[0] + 1 + shift, col_count), across_ref[...])
 
 
-def weighted_fit_kernel(members, row, col, inv_ref, centres_ref, rows_ref, out_ref, strips_ref, wide_ref, weighted_ref, sems):
+def weighted_fit_kernel(members, row, col, inv_ref, centres_ref, rows_ref, out_ref, token_ref, strips_ref, wide_ref, weighted_ref, sems):
     strips, height, col_width = strips_ref.shape
     width = rows_ref.shape[2]
 
@@ -134,6 +150,7 @@
     last = jnp.concatenate([entries[8], jnp.zeros((7, frame_total), F32)], axis=0)
     message = jnp.concatenate([first, last], axis=1)
     out_ref[...] = jnp.broadcast_to(message[None], out_ref.shape)
+    token_ref[...] = message
 
 
 def orthogonalized(message, frame_total):
@@ -180,7 +197,7 @@
         out_ref[:, start : start + stride] = product * scale
 
 
-def covariance_kernel(members, row, col, fits_ref, rows_ref, centres_ref, *refs):
+def covariance_kernel(members, row, col, token_ref, fits_ref, rows_ref, centres_ref, *refs):
     panel_refs = refs[:members]
     out_ref, rot_out_ref, wide_ref, rows_dev_ref, dev_ref = refs[members:]
     frame_total = rows_ref.shape[1]
@@ -273,35 +290,42 @@
     )(col, rot_here, coords_here, *others)
     centres = lax.all_to_all(repeated, "row", split_axis=0, concat_axis=0, tiled=True)
 
-    distance = lax.rem(col[0] + col_count - row[0] // members, col_count)
     across = []
     for step in range(1, col_count):
-        held = far[0]
-        if col_count > 2:
-            held = lax.select_n(lax.rem(distance + col_count - step, col_count), coords, *far)
+        held = pl.pallas_call(
+            functools.partial(pick_kernel, members, step),
+            out_shape=jax.ShapeDtypeStruct((3, local, width), BF16),
+            in_specs=[smem(), smem()] + [vmem()] * col_count,
+            out_specs=vmem(),
+            compiler_params=limit(4),
+            name="pick",
+        )(row, col, rows_all, *far)
         across.append(move(held, lambda g, m, c, s=step: (g, m, (c + s) % col_count), lambda g, c: g != c))
     own_block = pl.pallas_call(
         functools.partial(assemble_kernel, members),
         out_shape=jax.ShapeDtypeStruct((3, frame_total, width), BF16),
-        in_specs=[smem(), smem()] + [vmem()] * (2 * col_count - 1),
+        in_specs=[smem(), smem()] + [vmem()] * (2 * col_count),
         out_specs=vmem(),
         compiler_params=limit(8),
         name="assemble",
-    )(row, col, rows_all, *far, *across)
+    )(row, col, centres, rows_all, *far, *across)
     evens = [own_block] + [from_member(own_block, 2 * step) for step in range(1, half)]
 
     height = 64 if width % 64 == 0 else 8
-    message = pl.pallas_call(
+    message, token = pl.pallas_call(
         functools.partial(weighted_fit_kernel, members),
         in_specs=[smem(), smem(), hbm(), vmem(), vmem()],
-        out_specs=vmem(),
+        out_specs=(vmem(), vmem()),
         scratch_shapes=[
             pltpu.VMEM((width // height, height, col_width), F32),
             pltpu.VMEM((3, 8, col_width), F32),
             pltpu.VMEM((width, LANES), F32),
             pltpu.SemaphoreType.DMA((width // height,)),
         ],
-        out_shape=jax.ShapeDtypeStruct((device_total, 8, 2 * frame_total), F32),
+        out_shape=(
+            jax.ShapeDtypeStruct((device_total, 8, 2 * frame_total), F32),
+            jax.ShapeDtypeStruct((8, 2 * frame_total), F32),
+        ),
         compiler_params=limit(28),
         cost_estimate=pl.CostEstimate(
             flops=6 * width * col_width, bytes_accessed=4 * width * col_width, transcendentals=0
@@ -309,6 +333,7 @@
         name="weighted_fit",
     )(row, col, in_hbm(inverse_cov), centres, rows_all)
     fits = lax.all_to_all(message, ("row", "col"), split_axis=0, concat_axis=0, tiled=True)
+    token, evens = lax.optimization_barrier((token, evens))
     panel = [None] * members
     panel[0::2] = evens
     panel[1::2] = [from_member(block, 1) for block in evens]
@@ -318,7 +343,7 @@
         grid_spec=pltpu.PrefetchScalarGridSpec(
             num_scalar_prefetch=2,
             grid=(members,),
-            in_specs=[vmem()] * (3 + members),
+            in_specs=[vmem()] * (4 + members),
             out_specs=(
                 pl.BlockSpec((width, width), lambda i, row, col: (0, lax.rem(row[0], members) ^ i)),
                 vmem(),
@@ -338,7 +363,7 @@
             flops=6 * frame_total * width * col_width, bytes_accessed=4 * width * col_width, transcendentals=0
         ),
         name="covariance",
-    )(row, col, fits, rows_all, centres, *panel)
+    )(row, col, token, fits, rows_all, centres, *panel)
     return (covariance, transforms)
 
 

time: 70.4 us -> 64.2 us (0.912)
  waiting for transfers between devices: 24.2 us -> 9.75 us
  blocking collectives: 0 us -> 13 us
  starting transfers between devices: 23.9 us -> 19.8 us
    all_to_all x0 -> x1, blocking collectives: none -> 13 us  [per_device(): lax.all_to_all(message, ('row', 'col'), split_axis=0, concat_axis=0, tile...]
    all_to_all x1 -> x0, waiting for transfers between devices: 8.61 us -> none  [per_device(): lax.all_to_all(message, ('row', 'col'), split_axis=0, concat_axis=0, tile...]
    all_to_all x1, waiting for transfers between devices: 5.11 us -> 1.05 us  [per_device(): lax.all_to_all(repeated, 'row', split_axis=0, concat_axis=0, tiled=True)]
    all_to_all x1 -> x0, starting transfers between devices: 2.81 us -> none  [per_device(): lax.all_to_all(message, ('row', 'col'), split_axis=0, concat_axis=0, tile...]
    ppermute x10, waiting for transfers between devices: 10.5 us -> 8.7 us  [move(): return lax.ppermute(value, ('row', 'col'), pairs)]
    all_to_all x1, starting transfers between devices: 7.43 us -> 6.19 us  [per_device(): lax.all_to_all(repeated, 'row', split_axis=0, concat_axis=0, tiled=True)]
  transfers between devices with their start and end apart: 12 -> 11, of which waited for: 5 -> 5; matrix products, arithmetic and copies ran while one was open for 0% -> 0% of each run, Pallas kernels for 14% -> 15%
where the time goes in v16:
time: 64.2 us; the launch traced here: 63.9 us
  Pallas kernels  20.6 us (32%)
  starting transfers between devices  19.8 us (31%)
  blocking collectives  13 us (20%)
  waiting for transfers between devices  9.75 us (15%)
  between operations  0.72 us (1%)
    ppermute x10, starting transfers between devices, move(): return lax.ppermute(value, ('row', 'col'), pairs)  13.6 us
    all_to_all x1, blocking collectives, per_device(): lax.all_to_all(message, ('row', 'col'), split_axis=0, concat_axis=0, tile...  13 us
    pallas_call x1, Pallas kernels, per_device(): pl.pallas_call(functools.partial(covariance_kernel, members), grid_spec=p...  11.2 us
    ppermute x10, waiting for transfers between devices, move(): return lax.ppermute(value, ('row', 'col'), pairs)  8.7 us
    pallas_call x1, Pallas kernels, per_device(): pl.pallas_call(functools.partial(weighted_fit_kernel, members), in_specs=...  7.48 us
    all_to_all x1, starting transfers between devices, per_device(): lax.all_to_all(repeated, 'row', split_axis=0, concat_axis=0, tiled=True)  6.19 us
  transfers between devices with their start and end apart: 11, of which 5 were waited for; matrix products, arithmetic and copies ran while one was open for 0% of the time, Pallas kernels for 15%

profile of v16, /device:TPU:0, one launch (start us, length us, event | category | flops | bytes accessed | tf_op | source)
XLA Modules:
  0.0 63.9 jit_solution(11332095773405114804)
XLA Ops:
  0.6 3.0 %collective-permute-start = (bf16[3,32,768]{2,1,0:T(8,128)(2,1)}, bf16[3,32,768]{2,1,0:T(8,128)(2,1)S(1)}, u32[]{:S(2)}, u32[]{:S(2)}) collective-permute-start(bf16[3,32,768]{2,1,0:T(8,128)(2,1)} %bitcast.3), channel_id=1, source_target_pairs={{1,0},{0,1},{3,2},{2,3},{5,4},{4,5},{7,6},{6,7},{9,8},{8,9},{11,10... | collective-permute-start | bytes 442376 | tf_op jit(solution)/shard_map/ppermute | solution.py:255
  3.6 2.6 %collective-permute-start.1 = (bf16[3,32,768]{2,1,0:T(8,128)(2,1)}, bf16[3,32,768]{2,1,0:T(8,128)(2,1)S(1)}, u32[]{:S(2)}, u32[]{:S(2)}) collective-permute-start(bf16[3,32,768]{2,1,0:T(8,128)(2,1)} %bitcast.4), channel_id=1, source_target_pairs={{16,0},{17,1},{18,2},{19,3},{20,4},{21,5},{22,6},{23,7},{24,8},{25... | collective-permute-start | bytes 442376 | tf_op jit(solution)/shard_map/ppermute | solution.py:255
  6.2 1.0 %load.1 = (f32[3,3,64]{2,1,0:T(4,128)S(1)}, bf16[3,32,768]{2,1,0:T(8,128)(2,1)S(1)}) custom-call(f32[3,3,64]{2,1,0:T(4,128)} %rot_hbm.1, bf16[3,32,768]{2,1,0:T(8,128)(2,1)} %bitcast.5), custom_call_target="tpu_custom_call" | custom-call | tf_op jit(solution)/shard_map/load/pallas_call | solution.py:271
  7.2 0.5 collective-permute-done.refs_1_
  7.7 0.9 %rows.1 = (bf16[3,64,768]{2,1,0:T(8,128)(2,1)S(1)}, f32[16,1,2304]{2,1,0:T(1,128)}) custom-call(s32[1]{0:T(128)} %bitcast.1.col, f32[3,3,64]{2,1,0:T(4,128)S(1)} %get-tuple-element.13.rot_ref, bf16[3,32,768]{2,1,0:T(8,128)(2,1)S(1)} %get-tuple-element.14.refs_0_, bf16[3,32,768]{2,1,0:T(8,128)(2,1)S(1)} %collective-permute-done.refs_1_), custom_call_target="tpu_custom_call" | custom-call | tf_op jit(solution)/shard_map/rows/pallas_call | solution.py:280
  8.6 6.2 %all-to-all-start = ((f32[16,1,2304]{2,1,0:T(1,128)}), f32[16,1,2304]{2,1,0:T(1,128)S(1)}, u32[]{:S(2)}, u32[]{:S(2)}) async-start(f32[16,1,2304]{2,1,0:T(1,128)} %get-tuple-element.15), calls=%async_computation | async-start | bytes 294912 | tf_op jit(solution)/shard_map/all_to_all | solution.py:291
  14.8 0.0 collective-permute-done.1.refs_0_
  14.8 3.4 %collective-permute-start.2 = (bf16[3,32,768]{2,1,0:T(8,128)(2,1)S(1)}, bf16[3,32,768]{2,1,0:T(8,128)(2,1)S(1)}, u32[]{:S(2)}, u32[]{:S(2)}) collective-permute-start(bf16[3,32,768]{2,1,0:T(8,128)(2,1)S(1)} %pick.1), channel_id=1, source_target_pairs={{0,1},{2,3},{4,5},{6,7},{8,9},{10,11},{12,13},{14,15},{17,16},{19,... | collective-permute-start | bytes 442376 | tf_op jit(solution)/shard_map/ppermute | solution.py:255
  18.3 3.7 %collective-permute-done.2.refs_1_ = bf16[3,32,768]{2,1,0:T(8,128)(2,1)S(1)} collective-permute-done((bf16[3,32,768]{2,1,0:T(8,128)(2,1)S(1)}, bf16[3,32,768]{2,1,0:T(8,128)(2,1)S(1)}, u32[]{:S(2)}, u32[]{:S(2)}) %collective-permute-start.2) | collective-permute-done | bytes 147488 | tf_op jit(solution)/shard_map/ppermute | solution.py:255
  21.9 1.1 %all-to-all-done.centres_ref = f32[16,1,2304]{2,1,0:T(1,128)S(1)} async-done(((f32[16,1,2304]{2,1,0:T(1,128)}), f32[16,1,2304]{2,1,0:T(1,128)S(1)}, u32[]{:S(2)}, u32[]{:S(2)}) %all-to-all-start) | async-done | bytes 147488 | tf_op jit(solution)/shard_map/all_to_all | solution.py:291
  23.0 1.6 %collective-permute-start.5 = (bf16[3,64,768]{2,1,0:T(8,128)(2,1)S(1)}, bf16[3,64,768]{2,1,0:T(8,128)(2,1)S(1)}, u32[]{:S(2)}, u32[]{:S(2)}) collective-permute-start(bf16[3,64,768]{2,1,0:T(8,128)(2,1)S(1)} %assemble.1.refs_0_), channel_id=1, source_target_pairs={{12,0},{13,1},{14,2},{15,3},{8,4},{9,5},{10,6},{11,7},{4,8},{5,9},... | collective-permute-start | bytes 884744 | tf_op jit(solution)/shard_map/ppermute | solution.py:255
  24.6 0.6 collective-permute-start.4
  25.1 1.4 %collective-permute-start.3 = (bf16[3,64,768]{2,1,0:T(8,128)(2,1)S(1)}, bf16[3,64,768]{2,1,0:T(8,128)(2,1)S(1)}, u32[]{:S(2)}, u32[]{:S(2)}) collective-permute-start(bf16[3,64,768]{2,1,0:T(8,128)(2,1)S(1)} %assemble.1.refs_0_), channel_id=1, source_target_pairs={{4,0},{5,1},{6,2},{7,3},{0,4},{1,5},{2,6},{3,7},{12,8},{13,9},{14,... | collective-permute-start | bytes 884744 | tf_op jit(solution)/shard_map/ppermute | solution.py:255
  26.6 7.5 %weighted_fit.1 = (f32[32,8,128]{2,1,0:T(8,128)S(1)}, f32[8,128]{1,0:T(8,128)S(1)}) custom-call(s32[1]{0:T(128)} %bitcast.row, s32[1]{0:T(128)} %bitcast.1.col, f32[768,6144]{1,0:T(8,128)} %inv_ref.1, f32[16,1,2304]{2,1,0:T(1,128)S(1)} %all-to-all-done.centres_ref, bf16[3,64,768]{2,1,0:T(8,128)(2,1)S(1)} %get-tuple-element.16.rows_ref), custom_call_target="tpu_custom_call" | custom-call | flops 28311552 | bytes 18874368 | tf_op jit(solution)/shard_map/weighted_fit/pallas_call | solution.py:315
  34.1 0.0 collective-permute-done.5.refs_6_
  34.1 3.7 %collective-permute-done.4.refs_4_ = bf16[3,64,768]{2,1,0:T(8,128)(2,1)S(1)} collective-permute-done((bf16[3,64,768]{2,1,0:T(8,128)(2,1)S(1)}, bf16[3,64,768]{2,1,0:T(8,128)(2,1)S(1)}, u32[]{:S(2)}, u32[]{:S(2)}) %collective-permute-start.4) | collective-permute-done | bytes 294944 | tf_op jit(solution)/shard_map/ppermute | solution.py:255
  37.8 0.8 %collective-permute-done.3.refs_2_ = bf16[3,64,768]{2,1,0:T(8,128)(2,1)S(1)} collective-permute-done((bf16[3,64,768]{2,1,0:T(8,128)(2,1)S(1)}, bf16[3,64,768]{2,1,0:T(8,128)(2,1)S(1)}, u32[]{:S(2)}, u32[]{:S(2)}) %collective-permute-start.3) | collective-permute-done | bytes 294944 | tf_op jit(solution)/shard_map/ppermute | solution.py:255
  38.6 0.0 collective-permute-start.6
  38.6 0.5 collective-permute-start.7
  39.1 0.0 collective-permute-start.8
  39.1 0.5 collective-permute-start.9
  39.6 13.0 %all_to_all.10.fits_ref = f32[32,8,128]{2,1,0:T(8,128)S(1)} all-to-all(f32[32,8,128]{2,1,0:T(8,128)S(1)} %get-tuple-element.19), channel_id=1, replica_groups=mesh['row'=16,'col'=2] {'row','col'}, dimensions={0} | all-to-all | bytes 262144 | tf_op jit(solution)/shard_map/all_to_all | solution.py:335
  52.6 0.0 collective-permute-done.6.refs_1_
  52.6 0.0 collective-permute-done.7.refs_3_
  52.6 0.0 collective-permute-done.8.refs_5_
  52.6 0.0 collective-permute-done.9.refs_7_
  52.7 11.2 %covariance.1 = (f32[768,6144]{1,0:T(8,128)}, f32[3,3,32]{2,1,0:T(4,128)}) custom-call(s32[1]{0:T(128)} %bitcast.row, s32[1]{0:T(128)} %bitcast.1.col, f32[8,128]{1,0:T(8,128)S(1)} %get-tuple-element.18.token_ref, f32[32,8,128]{2,1,0:T(8,128)S(1)} %all_to_all.10.fits_ref, bf16[3,64,768]{2,1,0:T(8,128)(2,1)S(1)} %get-tuple-element.16.rows_ref, ...), custom_call_target="tpu_custom_call" | custom-call | flops 1811939328 | bytes 18874368 | tf_op jit(solution)/shard_map/covariance/pallas_call | solution.py:341
  (2 shorter events, 0.1 us)
Async XLA Ops:
  0.6 7.1 %collective-permute-start = (bf16[3,32,768]{2,1,0:T(8,128)(2,1)}, bf16[3,32,768]{2,1,0:T(8,128)(2,1)S(1)}, u32[]{:S(2)}, u32[]{:S(2)}) collective-permute-start(bf16[3,32,768]{2,1,0:T(8,128)(2,1)} %bitcast.3), channel_id=1, source_target_pairs={{1,0},{0,1},{3,2},{2,3},{5,4},{4,5},{7,6},{6,7},{9,8},{8,9},{11,10... | collective-permute-start | bytes 442376 | tf_op jit(solution)/shard_map/ppermute | solution.py:255
  3.6 11.2 %collective-permute-start.1 = (bf16[3,32,768]{2,1,0:T(8,128)(2,1)}, bf16[3,32,768]{2,1,0:T(8,128)(2,1)S(1)}, u32[]{:S(2)}, u32[]{:S(2)}) collective-permute-start(bf16[3,32,768]{2,1,0:T(8,128)(2,1)} %bitcast.4), channel_id=1, source_target_pairs={{16,0},{17,1},{18,2},{19,3},{20,4},{21,5},{22,6},{23,7},{24,8},{25... | collective-permute-start | bytes 442376 | tf_op jit(solution)/shard_map/ppermute | solution.py:255
  8.6 14.4 %all-to-all-start = ((f32[16,1,2304]{2,1,0:T(1,128)}), f32[16,1,2304]{2,1,0:T(1,128)S(1)}, u32[]{:S(2)}, u32[]{:S(2)}) async-start(f32[16,1,2304]{2,1,0:T(1,128)} %get-tuple-element.15), calls=%async_computation | async-start | bytes 294912 | tf_op jit(solution)/shard_map/all_to_all | solution.py:291
  14.8 7.1 %collective-permute-start.2 = (bf16[3,32,768]{2,1,0:T(8,128)(2,1)S(1)}, bf16[3,32,768]{2,1,0:T(8,128)(2,1)S(1)}, u32[]{:S(2)}, u32[]{:S(2)}) collective-permute-start(bf16[3,32,768]{2,1,0:T(8,128)(2,1)S(1)} %pick.1), channel_id=1, source_target_pairs={{0,1},{2,3},{4,5},{6,7},{8,9},{10,11},{12,13},{14,15},{17,16},{19,... | collective-permute-start | bytes 442376 | tf_op jit(solution)/shard_map/ppermute | solution.py:255
  23.0 11.0 %collective-permute-start.5 = (bf16[3,64,768]{2,1,0:T(8,128)(2,1)S(1)}, bf16[3,64,768]{2,1,0:T(8,128)(2,1)S(1)}, u32[]{:S(2)}, u32[]{:S(2)}) collective-permute-start(bf16[3,64,768]{2,1,0:T(8,128)(2,1)S(1)} %assemble.1.refs_0_), channel_id=1, source_target_pairs={{12,0},{13,1},{14,2},{15,3},{8,4},{9,5},{10,6},{11,7},{4,8},{5,9},... | collective-permute-start | bytes 884744 | tf_op jit(solution)/shard_map/ppermute | solution.py:255
  24.6 13.2 %collective-permute-start.4 = (bf16[3,64,768]{2,1,0:T(8,128)(2,1)S(1)}, bf16[3,64,768]{2,1,0:T(8,128)(2,1)S(1)}, u32[]{:S(2)}, u32[]{:S(2)}) collective-permute-start(bf16[3,64,768]{2,1,0:T(8,128)(2,1)S(1)} %assemble.1.refs_0_), channel_id=1, source_target_pairs={{8,0},{9,1},{10,2},{11,3},{12,4},{13,5},{14,6},{15,7},{0,8},{1,9},... | collective-permute-start | bytes 884744 | tf_op jit(solution)/shard_map/ppermute | solution.py:255
  25.1 13.4 %collective-permute-start.3 = (bf16[3,64,768]{2,1,0:T(8,128)(2,1)S(1)}, bf16[3,64,768]{2,1,0:T(8,128)(2,1)S(1)}, u32[]{:S(2)}, u32[]{:S(2)}) collective-permute-start(bf16[3,64,768]{2,1,0:T(8,128)(2,1)S(1)} %assemble.1.refs_0_), channel_id=1, source_target_pairs={{4,0},{5,1},{6,2},{7,3},{0,4},{1,5},{2,6},{3,7},{12,8},{13,9},{14,... | collective-permute-start | bytes 884744 | tf_op jit(solution)/shard_map/ppermute | solution.py:255
  38.6 14.0 %collective-permute-start.6 = (bf16[3,64,768]{2,1,0:T(8,128)(2,1)S(1)}, bf16[3,64,768]{2,1,0:T(8,128)(2,1)S(1)}, u32[]{:S(2)}, u32[]{:S(2)}) collective-permute-start(bf16[3,64,768]{2,1,0:T(8,128)(2,1)S(1)} %assemble.1.refs_0_), channel_id=1, source_target_pairs={{2,0},{3,1},{0,2},{1,3},{6,4},{7,5},{4,6},{5,7},{10,8},{11,9},{8,1... | collective-permute-start | bytes 884744 | tf_op jit(solution)/shard_map/ppermute | solution.py:255
  38.6 14.0 %collective-permute-start.7 = (bf16[3,64,768]{2,1,0:T(8,128)(2,1)S(1)}, bf16[3,64,768]{2,1,0:T(8,128)(2,1)S(1)}, u32[]{:S(2)}, u32[]{:S(2)}) collective-permute-start(bf16[3,64,768]{2,1,0:T(8,128)(2,1)S(1)} %collective-permute-done.3.refs_2_), channel_id=1, source_target_pairs={{2,0},{3,1},{0,2},{1,3},{6,4},{7,5},{4,6},{5,7},{10,8},{11,9},{8,1... | collective-permute-start | bytes 884744 | tf_op jit(solution)/shard_map/ppermute | solution.py:255
  39.1 13.5 %collective-permute-start.8 = (bf16[3,64,768]{2,1,0:T(8,128)(2,1)S(1)}, bf16[3,64,768]{2,1,0:T(8,128)(2,1)S(1)}, u32[]{:S(2)}, u32[]{:S(2)}) collective-permute-start(bf16[3,64,768]{2,1,0:T(8,128)(2,1)S(1)} %collective-permute-done.4.refs_4_), channel_id=1, source_target_pairs={{2,0},{3,1},{0,2},{1,3},{6,4},{7,5},{4,6},{5,7},{10,8},{11,9},{8,1... | collective-permute-start | bytes 884744 | tf_op jit(solution)/shard_map/ppermute | solution.py:255
  39.1 13.5 %collective-permute-start.9 = (bf16[3,64,768]{2,1,0:T(8,128)(2,1)S(1)}, bf16[3,64,768]{2,1,0:T(8,128)(2,1)S(1)}, u32[]{:S(2)}, u32[]{:S(2)}) collective-permute-start(bf16[3,64,768]{2,1,0:T(8,128)(2,1)S(1)} %collective-permute-done.5.refs_6_), channel_id=1, source_target_pairs={{2,0},{3,1},{0,2},{1,3},{6,4},{7,5},{4,6},{5,7},{10,8},{11,9},{8,1... | collective-permute-start | bytes 884744 | tf_op jit(solution)/shard_map/ppermute | solution.py:255

commit v17 on v10

--- a/solution.py
+++ b/solution.py
@@ -48,20 +48,21 @@
     out_ref[:, pl.ds(pl.multiple_of(block * local, local), local), :] = value
 
 
-def rows_kernel(col, rot_hbm, coords_hbm, *refs):
-    others, (rows_ref, centre_ref, rot_ref, sems) = refs[:-4], refs[-4:]
-    local = coords_hbm.shape[1]
-    own_rows = rows_ref.at[:, pl.ds(pl.multiple_of(col[0] * local, local), local), :]
+def load_kernel(rot_hbm, coords_hbm, rot_ref, coords_ref, sems):
     copies = [
         pltpu.make_async_copy(rot_hbm, rot_ref, sems.at[0]),
-        pltpu.make_async_copy(coords_hbm, own_rows, sems.at[1]),
+        pltpu.make_async_copy(coords_hbm, coords_ref, sems.at[1]),
     ]
     for copy in copies:
         copy.start()
-    for shift, ref in enumerate(others):
-        put_block(rows_ref, lax.rem(col[0] + 1 + shift, len(others) + 1), ref[...])
     for copy in copies:
         copy.wait()
+
+
+def rows_kernel(col, rot_ref, *refs):
+    blocks, (rows_ref, centre_ref) = refs[:-2], refs[-2:]
+    for shift, ref in enumerate(blocks):
+        put_block(rows_ref, lax.rem(col[0] + shift, len(blocks)), ref[...])
     centre = rotated_sum(rot_ref[...], rows_ref[...]) * (1.0 / rows_ref.shape[1])
     flat = jnp.concatenate([centre[comp : comp + 1, :] for comp in range(3)], axis=1)
     centre_ref[...] = jnp.broadcast_to(flat[None], centre_ref.shape)
@@ -149,6 +150,11 @@
     last = jnp.concatenate([entries[8], jnp.zeros((7, frame_total), F32)], axis=0)
     message = jnp.concatenate([first, last], axis=1)
     out_ref[...] = jnp.broadcast_to(message[None], out_ref.shape)
+
+
+def stack_kernel(*refs):
+    for index, ref in enumerate(refs[:-1]):
+        refs[-1][index] = ref[...]
 
 
 def orthogonalized(message, frame_total):
@@ -226,15 +232,13 @@
             put_tile(wide_ref, panel_refs[step], centres_ref, block, rows_dev_ref, dev_ref, out_ref)
 
 
-def last_tiles_kernel(count, row, col, before_ref, wide_ref, rows_dev_ref, centres_ref, *refs):
-    panel_refs = refs[:count]
-    out_ref, dev_ref = refs[count:]
+def last_tiles_kernel(count, row, col, before_ref, wide_ref, rows_dev_ref, centres_ref, panel_ref, out_ref, dev_ref):
     for step in range(count):
 
         @pl.when(pl.program_id(0) == step)
         def _(step=step):
             block = col[0] * 2 * count + (lax.rem(row[0], 2 * count) ^ (2 * step + 1))
-            put_tile(wide_ref, panel_refs[step], centres_ref, block, rows_dev_ref, dev_ref, out_ref)
+            put_tile(wide_ref, panel_ref.at[step], centres_ref, block, rows_dev_ref, dev_ref, out_ref)
 
 
 def per_device(frames, rotations, inverse_cov):
@@ -277,18 +281,26 @@
 
     far = [move(coords, lambda g, m, c, s=step: ((g + s) % col_count, m, c)) for step in range(1, col_count)]
     others = [move(coords, lambda g, m, c, s=step: (g, m, (c + s) % col_count)) for step in range(1, col_count)]
+    rot_here, coords_here = pl.pallas_call(
+        load_kernel,
+        out_shape=(jax.ShapeDtypeStruct(rotations.shape, F32), jax.ShapeDtypeStruct(coords.shape, BF16)),
+        in_specs=[hbm(), hbm()],
+        out_specs=(vmem(), vmem()),
+        scratch_shapes=[pltpu.SemaphoreType.DMA((2,))],
+        compiler_params=limit(4),
+        name="load",
+    )(in_hbm(rotations), in_hbm(coords))
     rows_all, repeated = pl.pallas_call(
         rows_kernel,
         out_shape=(
             jax.ShapeDtypeStruct((3, frame_total, width), BF16),
             jax.ShapeDtypeStruct((row_count, 1, 3 * width), F32),
         ),
-        in_specs=[smem(), hbm(), hbm()] + [vmem()] * (col_count - 1),
+        in_specs=[smem()] + [vmem()] * (1 + col_count),
         out_specs=(vmem(), vmem()),
-        scratch_shapes=[pltpu.VMEM(rotations.shape, F32), pltpu.SemaphoreType.DMA((2,))],
         compiler_params=limit(8),
         name="rows",
-    )(col, in_hbm(rotations), in_hbm(coords), *others)
+    )(col, rot_here, coords_here, *others)
     centres = lax.all_to_all(repeated, "row", split_axis=0, concat_axis=0, tiled=True)
 
     across = []
@@ -332,7 +344,15 @@
     )(row, col, in_hbm(inverse_cov), centres, rows_all)
     fits = lax.all_to_all(message, ("row", "col"), split_axis=0, concat_axis=0, tiled=True)
     fits, evens = lax.optimization_barrier((fits, evens))
-    odds = [from_member(block, 1) for block in evens]
+    stacked = pl.pallas_call(
+        stack_kernel,
+        out_shape=jax.ShapeDtypeStruct((half, 3, frame_total, width), BF16),
+        in_specs=[vmem()] * half,
+        out_specs=vmem(),
+        compiler_params=limit(8),
+        name="stack_panel",
+    )(*evens)
+    odds = from_member(stacked, 1)
 
     def tile_spec(odd):
         return pl.BlockSpec((width, width), lambda i, row, *_: (0, lax.rem(row[0], members) ^ (2 * i + odd)))
@@ -365,7 +385,7 @@
         grid_spec=pltpu.PrefetchScalarGridSpec(
             num_scalar_prefetch=2,
             grid=(half,),
-            in_specs=[pl.BlockSpec(memory_space=pl.ANY)] + [vmem()] * (3 + half),
+            in_specs=[pl.BlockSpec(memory_space=pl.ANY)] + [vmem()] * 4,
             out_specs=tile_spec(1),
             scratch_shapes=[dev_scratch],
         ),
@@ -374,7 +394,7 @@
         compiler_params=limit(16),
         cost_estimate=tiles_cost,
         name="odd_tiles",
-    )(row, col, half_done, wide, rows_dev, centres, *odds)
+    )(row, col, half_done, wide, rows_dev, centres, odds)
     return (covariance, transforms)
 
 

time: 61.5 us -> 59.6 us (0.969)
  starting transfers between devices: 19.8 us -> 18.8 us
  waiting for transfers between devices: 6.22 us -> 5.24 us
    pallas_call x0 -> x2, Pallas kernels: none -> 1.04 us  [the longest x1 0.96 us: per_device(): pl.pallas_call(load_kernel, out_shape=(jax.ShapeDtypeStruct(rotations.sha...]
    ppermute x10 -> x7, starting transfers between devices: 13.6 us -> 12.6 us  [move(): return lax.ppermute(value, ('row', 'col'), pairs)]
    ppermute x10 -> x7, waiting for transfers between devices: 5.16 us -> 4.19 us  [move(): return lax.ppermute(value, ('row', 'col'), pairs)]
    pallas_call x1, Pallas kernels: 1.85 us -> 0.91 us  [per_device(): pl.pallas_call(rows_kernel, out_shape=(jax.ShapeDtypeStruct((3, frame_tot...]
  transfers between devices with their start and end apart: 11 -> 8, of which waited for: 3 -> 3; matrix products, arithmetic and copies ran while one was open for 0% -> 0% of each run, Pallas kernels for 27% -> 28%
where the time goes in v17:
time: 59.6 us; the launch traced here: 59.3 us
  Pallas kernels  21.5 us (36%)
  starting transfers between devices  18.8 us (32%)
  blocking collectives  13.1 us (22%)
  waiting for transfers between devices  5.24 us (9%)
  between operations  0.72 us (1%)
    all_to_all x1, blocking collectives, per_device(): lax.all_to_all(message, ('row', 'col'), split_axis=0, concat_axis=0, tile...  13.1 us
    ppermute x7, starting transfers between devices, move(): return lax.ppermute(value, ('row', 'col'), pairs)  12.6 us
    pallas_call x1, Pallas kernels, per_device(): pl.pallas_call(functools.partial(weighted_fit_kernel, members), in_specs=...  7.48 us
    pallas_call x1, Pallas kernels, per_device(): pl.pallas_call(functools.partial(first_tiles_kernel, half), grid_spec=plt...  7.28 us
    all_to_all x1, starting transfers between devices, per_device(): lax.all_to_all(repeated, 'row', split_axis=0, concat_axis=0, tiled=True)  6.19 us
    pallas_call x1, Pallas kernels, per_device(): pl.pallas_call(functools.partial(last_tiles_kernel, half), grid_spec=pltp...  4.73 us
    ppermute x7, waiting for transfers between devices, move(): return lax.ppermute(value, ('row', 'col'), pairs)  4.19 us
  transfers between devices with their start and end apart: 8, of which 3 were waited for; matrix products, arithmetic and copies ran while one was open for 0% of the time, Pallas kernels for 28%

profile of v17, /device:TPU:0, one launch (start us, length us, event | category | flops | bytes accessed | tf_op | source)
XLA Modules:
  0.0 59.3 jit_solution(17709785954305984259)
XLA Ops:
  0.6 3.0 %collective-permute-start = (bf16[3,32,768]{2,1,0:T(8,128)(2,1)}, bf16[3,32,768]{2,1,0:T(8,128)(2,1)S(1)}, u32[]{:S(2)}, u32[]{:S(2)}) collective-permute-start(bf16[3,32,768]{2,1,0:T(8,128)(2,1)} %bitcast.3), channel_id=1, source_target_pairs={{1,0},{0,1},{3,2},{2,3},{5,4},{4,5},{7,6},{6,7},{9,8},{8,9},{11,10... | collective-permute-start | bytes 442376 | tf_op jit(solution)/shard_map/ppermute | solution.py:268
  3.6 2.6 %collective-permute-start.1 = (bf16[3,32,768]{2,1,0:T(8,128)(2,1)}, bf16[3,32,768]{2,1,0:T(8,128)(2,1)S(1)}, u32[]{:S(2)}, u32[]{:S(2)}) collective-permute-start(bf16[3,32,768]{2,1,0:T(8,128)(2,1)} %bitcast.4), channel_id=1, source_target_pairs={{16,0},{17,1},{18,2},{19,3},{20,4},{21,5},{22,6},{23,7},{24,8},{25... | collective-permute-start | bytes 442376 | tf_op jit(solution)/shard_map/ppermute | solution.py:268
  6.2 1.0 %load.1 = (f32[3,3,64]{2,1,0:T(4,128)S(1)}, bf16[3,32,768]{2,1,0:T(8,128)(2,1)S(1)}) custom-call(f32[3,3,64]{2,1,0:T(4,128)} %rot_hbm.1, bf16[3,32,768]{2,1,0:T(8,128)(2,1)} %bitcast.5), custom_call_target="tpu_custom_call" | custom-call | tf_op jit(solution)/shard_map/load/pallas_call | solution.py:284
  7.2 0.5 collective-permute-done.refs_1_
  7.7 0.9 %rows.1 = (bf16[3,64,768]{2,1,0:T(8,128)(2,1)S(1)}, f32[16,1,2304]{2,1,0:T(1,128)}) custom-call(s32[1]{0:T(128)} %bitcast.1.col, f32[3,3,64]{2,1,0:T(4,128)S(1)} %get-tuple-element.15.rot_ref, bf16[3,32,768]{2,1,0:T(8,128)(2,1)S(1)} %get-tuple-element.16.refs_0_, bf16[3,32,768]{2,1,0:T(8,128)(2,1)S(1)} %collective-permute-done.refs_1_), custom_call_target="tpu_custom_call" | custom-call | tf_op jit(solution)/shard_map/rows/pallas_call | solution.py:293
  8.6 6.2 %all-to-all-start = ((f32[16,1,2304]{2,1,0:T(1,128)}), f32[16,1,2304]{2,1,0:T(1,128)S(1)}, u32[]{:S(2)}, u32[]{:S(2)}) async-start(f32[16,1,2304]{2,1,0:T(1,128)} %get-tuple-element.17), calls=%async_computation | async-start | bytes 294912 | tf_op jit(solution)/shard_map/all_to_all | solution.py:304
  14.8 0.0 collective-permute-done.1.refs_0_
  14.8 3.4 %collective-permute-start.2 = (bf16[3,32,768]{2,1,0:T(8,128)(2,1)S(1)}, bf16[3,32,768]{2,1,0:T(8,128)(2,1)S(1)}, u32[]{:S(2)}, u32[]{:S(2)}) collective-permute-start(bf16[3,32,768]{2,1,0:T(8,128)(2,1)S(1)} %pick.1), channel_id=1, source_target_pairs={{0,1},{2,3},{4,5},{6,7},{8,9},{10,11},{12,13},{14,15},{17,16},{19,... | collective-permute-start | bytes 442376 | tf_op jit(solution)/shard_map/ppermute | solution.py:268
  18.3 3.7 %collective-permute-done.2.refs_1_ = bf16[3,32,768]{2,1,0:T(8,128)(2,1)S(1)} collective-permute-done((bf16[3,32,768]{2,1,0:T(8,128)(2,1)S(1)}, bf16[3,32,768]{2,1,0:T(8,128)(2,1)S(1)}, u32[]{:S(2)}, u32[]{:S(2)}) %collective-permute-start.2) | collective-permute-done | bytes 147488 | tf_op jit(solution)/shard_map/ppermute | solution.py:268
  21.9 1.1 %all-to-all-done.centres_ref = f32[16,1,2304]{2,1,0:T(1,128)S(1)} async-done(((f32[16,1,2304]{2,1,0:T(1,128)}), f32[16,1,2304]{2,1,0:T(1,128)S(1)}, u32[]{:S(2)}, u32[]{:S(2)}) %all-to-all-start) | async-done | bytes 147488 | tf_op jit(solution)/shard_map/all_to_all | solution.py:304
  23.0 1.6 %collective-permute-start.5 = (bf16[3,64,768]{2,1,0:T(8,128)(2,1)S(1)}, bf16[3,64,768]{2,1,0:T(8,128)(2,1)S(1)}, u32[]{:S(2)}, u32[]{:S(2)}) collective-permute-start(bf16[3,64,768]{2,1,0:T(8,128)(2,1)S(1)} %assemble.1.refs_0_), channel_id=1, source_target_pairs={{12,0},{13,1},{14,2},{15,3},{8,4},{9,5},{10,6},{11,7},{4,8},{5,9},... | collective-permute-start | bytes 884744 | tf_op jit(solution)/shard_map/ppermute | solution.py:268
  24.6 0.6 collective-permute-start.4
  25.1 1.4 %collective-permute-start.3 = (bf16[3,64,768]{2,1,0:T(8,128)(2,1)S(1)}, bf16[3,64,768]{2,1,0:T(8,128)(2,1)S(1)}, u32[]{:S(2)}, u32[]{:S(2)}) collective-permute-start(bf16[3,64,768]{2,1,0:T(8,128)(2,1)S(1)} %assemble.1.refs_0_), channel_id=1, source_target_pairs={{4,0},{5,1},{6,2},{7,3},{0,4},{1,5},{2,6},{3,7},{12,8},{13,9},{14,... | collective-permute-start | bytes 884744 | tf_op jit(solution)/shard_map/ppermute | solution.py:268
  26.6 7.5 %weighted_fit.1 = f32[32,8,128]{2,1,0:T(8,128)S(1)} custom-call(s32[1]{0:T(128)} %bitcast.row, s32[1]{0:T(128)} %bitcast.1.col, f32[768,6144]{1,0:T(8,128)} %inv_ref.1, f32[16,1,2304]{2,1,0:T(1,128)S(1)} %all-to-all-done.centres_ref, bf16[3,64,768]{2,1,0:T(8,128)(2,1)S(1)} %get-tuple-element.18.rows_ref), custom_call_target="tpu_custom_call" | custom-call | flops 28311552 | bytes 18874368 | tf_op jit(solution)/shard_map/weighted_fit/pallas_call | solution.py:328
  34.1 13.1 %all_to_all.10.fits_ref = f32[32,8,128]{2,1,0:T(8,128)S(1)} all-to-all(f32[32,8,128]{2,1,0:T(8,128)S(1)} %weighted_fit.1), channel_id=1, replica_groups=mesh['row'=16,'col'=2] {'row','col'}, dimensions={0} | all-to-all | bytes 262144 | tf_op jit(solution)/shard_map/all_to_all | solution.py:345
  47.1 0.0 collective-permute-done.5.refs_3_
  47.1 0.0 collective-permute-done.4.refs_2_
  47.1 0.0 collective-permute-done.3.refs_1_
  47.2 0.1 stack_panel.1
  47.2 0.1 collective-permute-start.6
  47.3 7.3 %steps_and_even_tiles.1 = (f32[768,6144]{1,0:T(8,128)}, f32[3,3,32]{2,1,0:T(4,128)}, f32[9,64,128]{2,1,0:T(8,128)S(1)}, bf16[768,192]{1,0:T(8,128)(2,1)S(1)}) custom-call(s32[1]{0:T(128)} %bitcast.row, s32[1]{0:T(128)} %bitcast.1.col, f32[32,8,128]{2,1,0:T(8,128)S(1)} %all_to_all.10.fits_ref, bf16[3,64,768]{2,1,0:T(8,128)(2,1)S(1)} %get-tuple-element.18.rows_ref, ...), custom_call_target="tpu_custom_call" | custom-call | flops 905969664 | bytes 9437184 | tf_op jit(solution)/shard_map/steps_and_even_tiles/pallas_call | solution.py:364
  54.6 0.0 collective-permute-done.6.panel_ref
  54.6 4.7 %odd_tiles.1 = f32[768,6144]{1,0:T(8,128)} custom-call(s32[1]{0:T(128)} %bitcast.row, s32[1]{0:T(128)} %bitcast.1.col, f32[768,6144]{1,0:T(8,128)} %get-tuple-element.24.before_ref, f32[9,64,128]{2,1,0:T(8,128)S(1)} %get-tuple-element.25.wide_ref, bf16[768,192]{1,0:T(8,128)(2,1)S(1)} %get-tuple-element.26.rows_dev_ref, ...), custom_call_target="tpu_custom_call", output_to_operand_aliasing={{}: (2, {})} | custom-call | flops 905969664 | bytes 9437184 | tf_op jit(solution)/shard_map/odd_tiles/pallas_call | solution.py:383
  (2 shorter events, 0.1 us)
Async XLA Ops:
  0.6 7.1 %collective-permute-start = (bf16[3,32,768]{2,1,0:T(8,128)(2,1)}, bf16[3,32,768]{2,1,0:T(8,128)(2,1)S(1)}, u32[]{:S(2)}, u32[]{:S(2)}) collective-permute-start(bf16[3,32,768]{2,1,0:T(8,128)(2,1)} %bitcast.3), channel_id=1, source_target_pairs={{1,0},{0,1},{3,2},{2,3},{5,4},{4,5},{7,6},{6,7},{9,8},{8,9},{11,10... | collective-permute-start | bytes 442376 | tf_op jit(solution)/shard_map/ppermute | solution.py:268
  3.6 11.2 %collective-permute-start.1 = (bf16[3,32,768]{2,1,0:T(8,128)(2,1)}, bf16[3,32,768]{2,1,0:T(8,128)(2,1)S(1)}, u32[]{:S(2)}, u32[]{:S(2)}) collective-permute-start(bf16[3,32,768]{2,1,0:T(8,128)(2,1)} %bitcast.4), channel_id=1, source_target_pairs={{16,0},{17,1},{18,2},{19,3},{20,4},{21,5},{22,6},{23,7},{24,8},{25... | collective-permute-start | bytes 442376 | tf_op jit(solution)/shard_map/ppermute | solution.py:268
  8.6 14.4 %all-to-all-start = ((f32[16,1,2304]{2,1,0:T(1,128)}), f32[16,1,2304]{2,1,0:T(1,128)S(1)}, u32[]{:S(2)}, u32[]{:S(2)}) async-start(f32[16,1,2304]{2,1,0:T(1,128)} %get-tuple-element.17), calls=%async_computation | async-start | bytes 294912 | tf_op jit(solution)/shard_map/all_to_all | solution.py:304
  14.8 7.1 %collective-permute-start.2 = (bf16[3,32,768]{2,1,0:T(8,128)(2,1)S(1)}, bf16[3,32,768]{2,1,0:T(8,128)(2,1)S(1)}, u32[]{:S(2)}, u32[]{:S(2)}) collective-permute-start(bf16[3,32,768]{2,1,0:T(8,128)(2,1)S(1)} %pick.1), channel_id=1, source_target_pairs={{0,1},{2,3},{4,5},{6,7},{8,9},{10,11},{12,13},{14,15},{17,16},{19,... | collective-permute-start | bytes 442376 | tf_op jit(solution)/shard_map/ppermute | solution.py:268
  23.0 24.1 %collective-permute-start.5 = (bf16[3,64,768]{2,1,0:T(8,128)(2,1)S(1)}, bf16[3,64,768]{2,1,0:T(8,128)(2,1)S(1)}, u32[]{:S(2)}, u32[]{:S(2)}) collective-permute-start(bf16[3,64,768]{2,1,0:T(8,128)(2,1)S(1)} %assemble.1.refs_0_), channel_id=1, source_target_pairs={{12,0},{13,1},{14,2},{15,3},{8,4},{9,5},{10,6},{11,7},{4,8},{5,9},... | collective-permute-start | bytes 884744 | tf_op jit(solution)/shard_map/ppermute | solution.py:268
  24.6 22.6 %collective-permute-start.4 = (bf16[3,64,768]{2,1,0:T(8,128)(2,1)S(1)}, bf16[3,64,768]{2,1,0:T(8,128)(2,1)S(1)}, u32[]{:S(2)}, u32[]{:S(2)}) collective-permute-start(bf16[3,64,768]{2,1,0:T(8,128)(2,1)S(1)} %assemble.1.refs_0_), channel_id=1, source_target_pairs={{8,0},{9,1},{10,2},{11,3},{12,4},{13,5},{14,6},{15,7},{0,8},{1,9},... | collective-permute-start | bytes 884744 | tf_op jit(solution)/shard_map/ppermute | solution.py:268
  25.1 22.0 %collective-permute-start.3 = (bf16[3,64,768]{2,1,0:T(8,128)(2,1)S(1)}, bf16[3,64,768]{2,1,0:T(8,128)(2,1)S(1)}, u32[]{:S(2)}, u32[]{:S(2)}) collective-permute-start(bf16[3,64,768]{2,1,0:T(8,128)(2,1)S(1)} %assemble.1.refs_0_), channel_id=1, source_target_pairs={{4,0},{5,1},{6,2},{7,3},{0,4},{1,5},{2,6},{3,7},{12,8},{13,9},{14,... | collective-permute-start | bytes 884744 | tf_op jit(solution)/shard_map/ppermute | solution.py:268
  47.2 7.4 %collective-permute-start.6 = (bf16[4,3,64,768]{3,2,1,0:T(8,128)(2,1)S(1)}, bf16[4,3,64,768]{3,2,1,0:T(8,128)(2,1)S(1)}, u32[]{:S(2)}, u32[]{:S(2)}) collective-permute-start(bf16[4,3,64,768]{3,2,1,0:T(8,128)(2,1)S(1)} %stack_panel.1), channel_id=1, source_target_pairs={{2,0},{3,1},{0,2},{1,3},{6,4},{7,5},{4,6},{5,7},{10,8},{11,9},{8,1... | collective-permute-start | bytes 3538952 | tf_op jit(solution)/shard_map/ppermute | solution.py:268

commit v18 on v17

--- a/solution.py
+++ b/solution.py
@@ -201,44 +201,61 @@
         out_ref[:, start : start + stride] = product * scale
 
 
+def put_tiles(odd, row, col, wide_ref, centres_ref, panel, rows_dev_ref, dev_ref, tile_ref, sems, out_ref):
+    width = tile_ref.shape[1]
+    members = out_ref.shape[1] // width
+    parts = sems.shape[1]
+    strip = width // parts
+    writes = []
+    for step, coords_ref in enumerate(panel):
+        slot = step % 2
+        if step >= 2:
+            for write in writes[step - 2]:
+                write.wait()
+        block = lax.rem(row[0], members) ^ (2 * step + odd)
+        tile = tile_ref.at[slot]
+        put_tile(wide_ref, coords_ref, centres_ref, col[0] * members + block, rows_dev_ref, dev_ref, tile)
+        columns = pl.ds(pl.multiple_of(block * width, LANES), width)
+        copies = []
+        for part in range(parts):
+            span = pl.ds(part * strip, strip)
+            copies.append(pltpu.make_async_copy(tile.at[span, :], out_ref.at[span, columns], sems.at[slot, part]))
+            copies[-1].start()
+        writes.append(copies)
+    for copies in writes[-2:]:
+        for write in copies:
+            write.wait()
+
+
 def first_tiles_kernel(count, row, col, fits_ref, rows_ref, centres_ref, *refs):
     panel_refs = refs[:count]
-    out_ref, rot_out_ref, wide_ref, rows_dev_ref, dev_ref = refs[count:]
+    out_ref, rot_out_ref, wide_ref, rows_dev_ref, rows_t_ref, dev_ref, tile_ref, sems = refs[count:]
     frame_total = rows_ref.shape[1]
     local = rot_out_ref.shape[2]
 
-    @pl.when(pl.program_id(0) == 0)
-    def _():
-        current = orthogonalized(jnp.sum(fits_ref[...], axis=0), frame_total)
-        for a in range(3):
-            flat = jnp.concatenate(current[a], axis=0)
-            kept = flat[:, :local]
-            for block in range(1, frame_total // local):
-                kept = jnp.where(col[0] == block, flat[:, block * local : (block + 1) * local], kept)
-            rot_out_ref[a] = kept
-        entries = [current[a][b] for a in range(3) for b in range(3)]
-        columns = jnp.concatenate(entries + [jnp.zeros((7, frame_total), F32)], axis=0).T
-        for entry in range(9):
-            wide_ref[entry] = jnp.broadcast_to(columns[:, entry : entry + 1], (frame_total, LANES))
-        for chunk in range(rows_ref.shape[2] // LANES):
-            put_deviations(wide_ref, rows_ref, centres_ref, row[0], chunk, dev_ref)
-        rows_dev_ref[...] = dev_ref[...].T
-
-    for step in range(count):
-
-        @pl.when(pl.program_id(0) == step)
-        def _(step=step):
-            block = col[0] * 2 * count + (lax.rem(row[0], 2 * count) ^ (2 * step))
-            put_tile(wide_ref, panel_refs[step], centres_ref, block, rows_dev_ref, dev_ref, out_ref)
-
-
-def last_tiles_kernel(count, row, col, before_ref, wide_ref, rows_dev_ref, centres_ref, panel_ref, out_ref, dev_ref):
-    for step in range(count):
-
-        @pl.when(pl.program_id(0) == step)
-        def _(step=step):
-            block = col[0] * 2 * count + (lax.rem(row[0], 2 * count) ^ (2 * step + 1))
-            put_tile(wide_ref, panel_ref.at[step], centres_ref, block, rows_dev_ref, dev_ref, out_ref)
+    current = orthogonalized(jnp.sum(fits_ref[...], axis=0), frame_total)
+    for a in range(3):
+        flat = jnp.concatenate(current[a], axis=0)
+        kept = flat[:, :local]
+        for block in range(1, frame_total // local):
+            kept = jnp.where(col[0] == block, flat[:, block * local : (block + 1) * local], kept)
+        rot_out_ref[a] = kept
+    entries = [current[a][b] for a in range(3) for b in range(3)]
+    columns = jnp.concatenate(entries + [jnp.zeros((7, frame_total), F32)], axis=0).T
+    for entry in range(9):
+        wide_ref[entry] = jnp.broadcast_to(columns[:, entry : entry + 1], (frame_total, LANES))
+    for chunk in range(rows_ref.shape[2] // LANES):
+        put_deviations(wide_ref, rows_ref, centres_ref, row[0], chunk, rows_t_ref)
+    rows_dev_ref[...] = rows_t_ref[...].T
+
+    put_tiles(0, row, col, wide_ref, centres_ref, panel_refs, rows_dev_ref, dev_ref, tile_ref, sems, out_ref)
+
+
+def last_tiles_kernel(
+    count, row, col, before_ref, wide_ref, rows_dev_ref, centres_ref, panel_ref, out_ref, dev_ref, tile_ref, sems
+):
+    panel = [panel_ref.at[step] for step in range(count)]
+    put_tiles(1, row, col, wide_ref, centres_ref, panel, rows_dev_ref, dev_ref, tile_ref, sems, out_ref)
 
 
 def per_device(frames, rotations, inverse_cov):
@@ -354,27 +371,26 @@
     )(*evens)
     odds = from_member(stacked, 1)
 
-    def tile_spec(odd):
-        return pl.BlockSpec((width, width), lambda i, row, *_: (0, lax.rem(row[0], members) ^ (2 * i + odd)))
-
+    depth = 3 * frame_total
+    parts = 4 if width % 64 == 0 else 1
+    tile_scratch = [
+        pltpu.VMEM((depth, width), BF16),
+        pltpu.VMEM((2, width, width), F32),
+        pltpu.SemaphoreType.DMA((2, parts)),
+    ]
     tiles_cost = pl.CostEstimate(
         flops=3 * frame_total * width * col_width, bytes_accessed=2 * width * col_width, transcendentals=0
     )
-    dev_scratch = pltpu.VMEM((3 * frame_total, width), BF16)
     half_done, transforms, wide, rows_dev = pl.pallas_call(
         functools.partial(first_tiles_kernel, half),
-        grid_spec=pltpu.PrefetchScalarGridSpec(
-            num_scalar_prefetch=2,
-            grid=(half,),
-            in_specs=[vmem()] * (3 + half),
-            out_specs=(tile_spec(0), vmem(), vmem(), vmem()),
-            scratch_shapes=[dev_scratch],
-        ),
+        in_specs=[smem(), smem()] + [vmem()] * (3 + half),
+        out_specs=(hbm(), vmem(), vmem(), vmem()),
+        scratch_shapes=[pltpu.VMEM((depth, width), BF16)] + tile_scratch,
         out_shape=(
             jax.ShapeDtypeStruct((width, col_width), F32),
             jax.ShapeDtypeStruct((3, 3, local), F32),
             jax.ShapeDtypeStruct((9, frame_total, LANES), F32),
-            jax.ShapeDtypeStruct((width, 3 * frame_total), BF16),
+            jax.ShapeDtypeStruct((width, depth), BF16),
         ),
         compiler_params=limit(16),
         cost_estimate=tiles_cost,
@@ -382,13 +398,9 @@
     )(row, col, fits, rows_all, centres, *evens)
     covariance = pl.pallas_call(
         functools.partial(last_tiles_kernel, half),
-        grid_spec=pltpu.PrefetchScalarGridSpec(
-            num_scalar_prefetch=2,
-            grid=(half,),
-            in_specs=[pl.BlockSpec(memory_space=pl.ANY)] + [vmem()] * 4,
-            out_specs=tile_spec(1),
-            scratch_shapes=[dev_scratch],
-        ),
+        in_specs=[smem(), smem(), hbm()] + [vmem()] * 4,
+        out_specs=hbm(),
+        scratch_shapes=tile_scratch,
         out_shape=jax.ShapeDtypeStruct((width, col_width), F32),
         input_output_aliases={2: 0},
         compiler_params=limit(16),

time: 59.6 us -> 60.8 us (1.020)
  Pallas kernels: 21.5 us -> 22.7 us
    pallas_call x2, Pallas kernels: 12 us -> 13.2 us  [the longest x1 8.09 us: per_device(): pl.pallas_call(functools.partial(first_tiles_kernel, half), in_specs=[sme...]
  transfers between devices with their start and end apart: 8 -> 8, of which waited for: 3 -> 3; matrix products, arithmetic and copies ran while one was open for 0% -> 0% of each run, Pallas kernels for 28% -> 29%
where the time goes in v18:
time: 60.8 us; the launch traced here: 60.5 us
  Pallas kernels  22.7 us (37%)
  starting transfers between devices  18.8 us (31%)
  blocking collectives  13.1 us (22%)
  waiting for transfers between devices  5.24 us (9%)
  between operations  0.73 us (1%)
    all_to_all x1, blocking collectives, per_device(): lax.all_to_all(message, ('row', 'col'), split_axis=0, concat_axis=0, tile...  13.1 us
    ppermute x7, starting transfers between devices, move(): return lax.ppermute(value, ('row', 'col'), pairs)  12.6 us
    pallas_call x1, Pallas kernels, per_device(): pl.pallas_call(functools.partial(first_tiles_kernel, half), in_specs=[sme...  8.09 us
    pallas_call x1, Pallas kernels, per_device(): pl.pallas_call(functools.partial(weighted_fit_kernel, members), in_specs=...  7.48 us
    all_to_all x1, starting transfers between devices, per_device(): lax.all_to_all(repeated, 'row', split_axis=0, concat_axis=0, tiled=True)  6.19 us
    pallas_call x1, Pallas kernels, per_device(): pl.pallas_call(functools.partial(last_tiles_kernel, half), in_specs=[smem...  5.09 us
    ppermute x7, waiting for transfers between devices, move(): return lax.ppermute(value, ('row', 'col'), pairs)  4.19 us
  transfers between devices with their start and end apart: 8, of which 3 were waited for; matrix products, arithmetic and copies ran while one was open for 0% of the time, Pallas kernels for 29%

profile of v18, /device:TPU:0, one launch (start us, length us, event | category | flops | bytes accessed | tf_op | source)
XLA Modules:
  0.0 60.5 jit_solution(16751604366934773802)
XLA Ops:
  0.6 3.0 %collective-permute-start = (bf16[3,32,768]{2,1,0:T(8,128)(2,1)}, bf16[3,32,768]{2,1,0:T(8,128)(2,1)S(1)}, u32[]{:S(2)}, u32[]{:S(2)}) collective-permute-start(bf16[3,32,768]{2,1,0:T(8,128)(2,1)} %bitcast.3), channel_id=1, source_target_pairs={{1,0},{0,1},{3,2},{2,3},{5,4},{4,5},{7,6},{6,7},{9,8},{8,9},{11,10... | collective-permute-start | bytes 442376 | tf_op jit(solution)/shard_map/ppermute | solution.py:285
  3.6 2.6 %collective-permute-start.1 = (bf16[3,32,768]{2,1,0:T(8,128)(2,1)}, bf16[3,32,768]{2,1,0:T(8,128)(2,1)S(1)}, u32[]{:S(2)}, u32[]{:S(2)}) collective-permute-start(bf16[3,32,768]{2,1,0:T(8,128)(2,1)} %bitcast.4), channel_id=1, source_target_pairs={{16,0},{17,1},{18,2},{19,3},{20,4},{21,5},{22,6},{23,7},{24,8},{25... | collective-permute-start | bytes 442376 | tf_op jit(solution)/shard_map/ppermute | solution.py:285
  6.2 1.0 %load.1 = (f32[3,3,64]{2,1,0:T(4,128)S(1)}, bf16[3,32,768]{2,1,0:T(8,128)(2,1)S(1)}) custom-call(f32[3,3,64]{2,1,0:T(4,128)} %rot_hbm.1, bf16[3,32,768]{2,1,0:T(8,128)(2,1)} %bitcast.5), custom_call_target="tpu_custom_call" | custom-call | tf_op jit(solution)/shard_map/load/pallas_call | solution.py:301
  7.2 0.5 collective-permute-done.refs_1_
  7.7 0.9 %rows.1 = (bf16[3,64,768]{2,1,0:T(8,128)(2,1)S(1)}, f32[16,1,2304]{2,1,0:T(1,128)}) custom-call(s32[1]{0:T(128)} %bitcast.1.col, f32[3,3,64]{2,1,0:T(4,128)S(1)} %get-tuple-element.15.rot_ref, bf16[3,32,768]{2,1,0:T(8,128)(2,1)S(1)} %get-tuple-element.16.refs_0_, bf16[3,32,768]{2,1,0:T(8,128)(2,1)S(1)} %collective-permute-done.refs_1_), custom_call_target="tpu_custom_call" | custom-call | tf_op jit(solution)/shard_map/rows/pallas_call | solution.py:310
  8.6 6.2 %all-to-all-start = ((f32[16,1,2304]{2,1,0:T(1,128)}), f32[16,1,2304]{2,1,0:T(1,128)S(1)}, u32[]{:S(2)}, u32[]{:S(2)}) async-start(f32[16,1,2304]{2,1,0:T(1,128)} %get-tuple-element.17), calls=%async_computation | async-start | bytes 294912 | tf_op jit(solution)/shard_map/all_to_all | solution.py:321
  14.8 0.0 collective-permute-done.1.refs_0_
  14.8 3.4 %collective-permute-start.2 = (bf16[3,32,768]{2,1,0:T(8,128)(2,1)S(1)}, bf16[3,32,768]{2,1,0:T(8,128)(2,1)S(1)}, u32[]{:S(2)}, u32[]{:S(2)}) collective-permute-start(bf16[3,32,768]{2,1,0:T(8,128)(2,1)S(1)} %pick.1), channel_id=1, source_target_pairs={{0,1},{2,3},{4,5},{6,7},{8,9},{10,11},{12,13},{14,15},{17,16},{19,... | collective-permute-start | bytes 442376 | tf_op jit(solution)/shard_map/ppermute | solution.py:285
  18.3 3.7 %collective-permute-done.2.refs_1_ = bf16[3,32,768]{2,1,0:T(8,128)(2,1)S(1)} collective-permute-done((bf16[3,32,768]{2,1,0:T(8,128)(2,1)S(1)}, bf16[3,32,768]{2,1,0:T(8,128)(2,1)S(1)}, u32[]{:S(2)}, u32[]{:S(2)}) %collective-permute-start.2) | collective-permute-done | bytes 147488 | tf_op jit(solution)/shard_map/ppermute | solution.py:285
  21.9 1.1 %all-to-all-done.centres_ref = f32[16,1,2304]{2,1,0:T(1,128)S(1)} async-done(((f32[16,1,2304]{2,1,0:T(1,128)}), f32[16,1,2304]{2,1,0:T(1,128)S(1)}, u32[]{:S(2)}, u32[]{:S(2)}) %all-to-all-start) | async-done | bytes 147488 | tf_op jit(solution)/shard_map/all_to_all | solution.py:321
  23.0 1.6 %collective-permute-start.5 = (bf16[3,64,768]{2,1,0:T(8,128)(2,1)S(1)}, bf16[3,64,768]{2,1,0:T(8,128)(2,1)S(1)}, u32[]{:S(2)}, u32[]{:S(2)}) collective-permute-start(bf16[3,64,768]{2,1,0:T(8,128)(2,1)S(1)} %assemble.1.refs_0_), channel_id=1, source_target_pairs={{12,0},{13,1},{14,2},{15,3},{8,4},{9,5},{10,6},{11,7},{4,8},{5,9},... | collective-permute-start | bytes 884744 | tf_op jit(solution)/shard_map/ppermute | solution.py:285
  24.6 0.6 collective-permute-start.4
  25.1 1.4 %collective-permute-start.3 = (bf16[3,64,768]{2,1,0:T(8,128)(2,1)S(1)}, bf16[3,64,768]{2,1,0:T(8,128)(2,1)S(1)}, u32[]{:S(2)}, u32[]{:S(2)}) collective-permute-start(bf16[3,64,768]{2,1,0:T(8,128)(2,1)S(1)} %assemble.1.refs_0_), channel_id=1, source_target_pairs={{4,0},{5,1},{6,2},{7,3},{0,4},{1,5},{2,6},{3,7},{12,8},{13,9},{14,... | collective-permute-start | bytes 884744 | tf_op jit(solution)/shard_map/ppermute | solution.py:285
  26.6 7.5 %weighted_fit.1 = f32[32,8,128]{2,1,0:T(8,128)S(1)} custom-call(s32[1]{0:T(128)} %bitcast.row, s32[1]{0:T(128)} %bitcast.1.col, f32[768,6144]{1,0:T(8,128)} %inv_ref.1, f32[16,1,2304]{2,1,0:T(1,128)S(1)} %all-to-all-done.centres_ref, bf16[3,64,768]{2,1,0:T(8,128)(2,1)S(1)} %get-tuple-element.18.rows_ref), custom_call_target="tpu_custom_call" | custom-call | flops 28311552 | bytes 18874368 | tf_op jit(solution)/shard_map/weighted_fit/pallas_call | solution.py:345
  34.1 13.1 %all_to_all.10.fits_ref = f32[32,8,128]{2,1,0:T(8,128)S(1)} all-to-all(f32[32,8,128]{2,1,0:T(8,128)S(1)} %weighted_fit.1), channel_id=1, replica_groups=mesh['row'=16,'col'=2] {'row','col'}, dimensions={0} | all-to-all | bytes 262144 | tf_op jit(solution)/shard_map/all_to_all | solution.py:362
  47.1 0.0 collective-permute-done.5.refs_3_
  47.1 0.0 collective-permute-done.4.refs_2_
  47.1 0.0 collective-permute-done.3.refs_1_
  47.2 0.1 stack_panel.1
  47.2 0.1 collective-permute-start.6
  47.3 8.1 %steps_and_even_tiles.1 = (f32[768,6144]{1,0:T(8,128)}, f32[3,3,32]{2,1,0:T(4,128)}, f32[9,64,128]{2,1,0:T(8,128)S(1)}, bf16[768,192]{1,0:T(8,128)(2,1)S(1)}) custom-call(s32[1]{0:T(128)} %bitcast.row, s32[1]{0:T(128)} %bitcast.1.col, f32[32,8,128]{2,1,0:T(8,128)S(1)} %all_to_all.10.fits_ref, bf16[3,64,768]{2,1,0:T(8,128)(2,1)S(1)} %get-tuple-element.18.rows_ref, ...), custom_call_target="tpu_custom_call" | custom-call | flops 905969664 | bytes 9437184 | tf_op jit(solution)/shard_map/steps_and_even_tiles/pallas_call | solution.py:384
  55.4 0.0 collective-permute-done.6.panel_ref
  55.4 5.1 %odd_tiles.1 = f32[768,6144]{1,0:T(8,128)} custom-call(s32[1]{0:T(128)} %bitcast.row, s32[1]{0:T(128)} %bitcast.1.col, f32[768,6144]{1,0:T(8,128)} %get-tuple-element.24.before_ref, f32[9,64,128]{2,1,0:T(8,128)S(1)} %get-tuple-element.25.wide_ref, bf16[768,192]{1,0:T(8,128)(2,1)S(1)} %get-tuple-element.26.rows_dev_ref, ...), custom_call_target="tpu_custom_call", output_to_operand_aliasing={{}: (2, {})} | custom-call | flops 905969664 | bytes 9437184 | tf_op jit(solution)/shard_map/odd_tiles/pallas_call | solution.py:399
  (2 shorter events, 0.1 us)
Async XLA Ops:
  0.6 7.1 %collective-permute-start = (bf16[3,32,768]{2,1,0:T(8,128)(2,1)}, bf16[3,32,768]{2,1,0:T(8,128)(2,1)S(1)}, u32[]{:S(2)}, u32[]{:S(2)}) collective-permute-start(bf16[3,32,768]{2,1,0:T(8,128)(2,1)} %bitcast.3), channel_id=1, source_target_pairs={{1,0},{0,1},{3,2},{2,3},{5,4},{4,5},{7,6},{6,7},{9,8},{8,9},{11,10... | collective-permute-start | bytes 442376 | tf_op jit(solution)/shard_map/ppermute | solution.py:285
  3.6 11.2 %collective-permute-start.1 = (bf16[3,32,768]{2,1,0:T(8,128)(2,1)}, bf16[3,32,768]{2,1,0:T(8,128)(2,1)S(1)}, u32[]{:S(2)}, u32[]{:S(2)}) collective-permute-start(bf16[3,32,768]{2,1,0:T(8,128)(2,1)} %bitcast.4), channel_id=1, source_target_pairs={{16,0},{17,1},{18,2},{19,3},{20,4},{21,5},{22,6},{23,7},{24,8},{25... | collective-permute-start | bytes 442376 | tf_op jit(solution)/shard_map/ppermute | solution.py:285
  8.6 14.4 %all-to-all-start = ((f32[16,1,2304]{2,1,0:T(1,128)}), f32[16,1,2304]{2,1,0:T(1,128)S(1)}, u32[]{:S(2)}, u32[]{:S(2)}) async-start(f32[16,1,2304]{2,1,0:T(1,128)} %get-tuple-element.17), calls=%async_computation | async-start | bytes 294912 | tf_op jit(solution)/shard_map/all_to_all | solution.py:321
  14.8 7.1 %collective-permute-start.2 = (bf16[3,32,768]{2,1,0:T(8,128)(2,1)S(1)}, bf16[3,32,768]{2,1,0:T(8,128)(2,1)S(1)}, u32[]{:S(2)}, u32[]{:S(2)}) collective-permute-start(bf16[3,32,768]{2,1,0:T(8,128)(2,1)S(1)} %pick.1), channel_id=1, source_target_pairs={{0,1},{2,3},{4,5},{6,7},{8,9},{10,11},{12,13},{14,15},{17,16},{19,... | collective-permute-start | bytes 442376 | tf_op jit(solution)/shard_map/ppermute | solution.py:285
  23.0 24.1 %collective-permute-start.5 = (bf16[3,64,768]{2,1,0:T(8,128)(2,1)S(1)}, bf16[3,64,768]{2,1,0:T(8,128)(2,1)S(1)}, u32[]{:S(2)}, u32[]{:S(2)}) collective-permute-start(bf16[3,64,768]{2,1,0:T(8,128)(2,1)S(1)} %assemble.1.refs_0_), channel_id=1, source_target_pairs={{12,0},{13,1},{14,2},{15,3},{8,4},{9,5},{10,6},{11,7},{4,8},{5,9},... | collective-permute-start | bytes 884744 | tf_op jit(solution)/shard_map/ppermute | solution.py:285
  24.6 22.6 %collective-permute-start.4 = (bf16[3,64,768]{2,1,0:T(8,128)(2,1)S(1)}, bf16[3,64,768]{2,1,0:T(8,128)(2,1)S(1)}, u32[]{:S(2)}, u32[]{:S(2)}) collective-permute-start(bf16[3,64,768]{2,1,0:T(8,128)(2,1)S(1)} %assemble.1.refs_0_), channel_id=1, source_target_pairs={{8,0},{9,1},{10,2},{11,3},{12,4},{13,5},{14,6},{15,7},{0,8},{1,9},... | collective-permute-start | bytes 884744 | tf_op jit(solution)/shard_map/ppermute | solution.py:285
  25.1 22.0 %collective-permute-start.3 = (bf16[3,64,768]{2,1,0:T(8,128)(2,1)S(1)}, bf16[3,64,768]{2,1,0:T(8,128)(2,1)S(1)}, u32[]{:S(2)}, u32[]{:S(2)}) collective-permute-start(bf16[3,64,768]{2,1,0:T(8,128)(2,1)S(1)} %assemble.1.refs_0_), channel_id=1, source_target_pairs={{4,0},{5,1},{6,2},{7,3},{0,4},{1,5},{2,6},{3,7},{12,8},{13,9},{14,... | collective-permute-start | bytes 884744 | tf_op jit(solution)/shard_map/ppermute | solution.py:285
  47.2 8.2 %collective-permute-start.6 = (bf16[4,3,64,768]{3,2,1,0:T(8,128)(2,1)S(1)}, bf16[4,3,64,768]{3,2,1,0:T(8,128)(2,1)S(1)}, u32[]{:S(2)}, u32[]{:S(2)}) collective-permute-start(bf16[4,3,64,768]{3,2,1,0:T(8,128)(2,1)S(1)} %stack_panel.1), channel_id=1, source_target_pairs={{2,0},{3,1},{0,2},{1,3},{6,4},{7,5},{4,6},{5,7},{10,8},{11,9},{8,1... | collective-permute-start | bytes 3538952 | tf_op jit(solution)/shard_map/ppermute | solution.py:285

commit v19 on v17

--- a/solution.py
+++ b/solution.py
@@ -203,12 +203,11 @@
 
 def first_tiles_kernel(count, row, col, fits_ref, rows_ref, centres_ref, *refs):
     panel_refs = refs[:count]
-    out_ref, rot_out_ref, wide_ref, rows_dev_ref, dev_ref = refs[count:]
+    out_ref, rot_out_ref, wide_ref, rows_dev_ref, dev_ref, rows_t_ref = refs[count:]
     frame_total = rows_ref.shape[1]
     local = rot_out_ref.shape[2]
 
-    @pl.when(pl.program_id(0) == 0)
-    def _():
+    def head():
         current = orthogonalized(jnp.sum(fits_ref[...], axis=0), frame_total)
         for a in range(3):
             flat = jnp.concatenate(current[a], axis=0)
@@ -221,13 +220,15 @@
         for entry in range(9):
             wide_ref[entry] = jnp.broadcast_to(columns[:, entry : entry + 1], (frame_total, LANES))
         for chunk in range(rows_ref.shape[2] // LANES):
-            put_deviations(wide_ref, rows_ref, centres_ref, row[0], chunk, dev_ref)
-        rows_dev_ref[...] = dev_ref[...].T
+            put_deviations(wide_ref, rows_ref, centres_ref, row[0], chunk, rows_t_ref)
+        rows_dev_ref[...] = rows_t_ref[...].T
 
     for step in range(count):
 
         @pl.when(pl.program_id(0) == step)
         def _(step=step):
+            if step == 0:
+                head()
             block = col[0] * 2 * count + (lax.rem(row[0], 2 * count) ^ (2 * step))
             put_tile(wide_ref, panel_refs[step], centres_ref, block, rows_dev_ref, dev_ref, out_ref)
 
@@ -368,7 +369,7 @@
             grid=(half,),
             in_specs=[vmem()] * (3 + half),
             out_specs=(tile_spec(0), vmem(), vmem(), vmem()),
-            scratch_shapes=[dev_scratch],
+            scratch_shapes=[dev_scratch, dev_scratch],
         ),
         out_shape=(
             jax.ShapeDtypeStruct((width, col_width), F32),

time: 59.6 us -> 59.6 us (level)
  no operation moved by 1% of the time
where the time goes in v19:
time: 59.6 us; the launch traced here: 59.3 us
  Pallas kernels  21.4 us (36%)
  starting transfers between devices  18.8 us (32%)
  blocking collectives  13.1 us (22%)
  waiting for transfers between devices  5.24 us (9%)
  between operations  0.72 us (1%)
    all_to_all x1, blocking collectives, per_device(): lax.all_to_all(message, ('row', 'col'), split_axis=0, concat_axis=0, tile...  13.1 us
    ppermute x7, starting transfers between devices, move(): return lax.ppermute(value, ('row', 'col'), pairs)  12.6 us
    pallas_call x1, Pallas kernels, per_device(): pl.pallas_call(functools.partial(weighted_fit_kernel, members), in_specs=...  7.48 us
    pallas_call x1, Pallas kernels, per_device(): pl.pallas_call(functools.partial(first_tiles_kernel, half), grid_spec=plt...  7.22 us
    all_to_all x1, starting transfers between devices, per_device(): lax.all_to_all(repeated, 'row', split_axis=0, concat_axis=0, tiled=True)  6.19 us
    pallas_call x1, Pallas kernels, per_device(): pl.pallas_call(functools.partial(last_tiles_kernel, half), grid_spec=pltp...  4.73 us
    ppermute x7, waiting for transfers between devices, move(): return lax.ppermute(value, ('row', 'col'), pairs)  4.19 us
  transfers between devices with their start and end apart: 8, of which 3 were waited for; matrix products, arithmetic and copies ran while one was open for 0% of the time, Pallas kernels for 28%

profile of v19, /device:TPU:0, one launch (start us, length us, event | category | flops | bytes accessed | tf_op | source)
XLA Modules:
  0.0 59.3 jit_solution(3825650827156414721)
XLA Ops:
  0.6 3.0 %collective-permute-start = (bf16[3,32,768]{2,1,0:T(8,128)(2,1)}, bf16[3,32,768]{2,1,0:T(8,128)(2,1)S(1)}, u32[]{:S(2)}, u32[]{:S(2)}) collective-permute-start(bf16[3,32,768]{2,1,0:T(8,128)(2,1)} %bitcast.3), channel_id=1, source_target_pairs={{1,0},{0,1},{3,2},{2,3},{5,4},{4,5},{7,6},{6,7},{9,8},{8,9},{11,10... | collective-permute-start | bytes 442376 | tf_op jit(solution)/shard_map/ppermute | solution.py:269
  3.6 2.6 %collective-permute-start.1 = (bf16[3,32,768]{2,1,0:T(8,128)(2,1)}, bf16[3,32,768]{2,1,0:T(8,128)(2,1)S(1)}, u32[]{:S(2)}, u32[]{:S(2)}) collective-permute-start(bf16[3,32,768]{2,1,0:T(8,128)(2,1)} %bitcast.4), channel_id=1, source_target_pairs={{16,0},{17,1},{18,2},{19,3},{20,4},{21,5},{22,6},{23,7},{24,8},{25... | collective-permute-start | bytes 442376 | tf_op jit(solution)/shard_map/ppermute | solution.py:269
  6.2 1.0 %load.1 = (f32[3,3,64]{2,1,0:T(4,128)S(1)}, bf16[3,32,768]{2,1,0:T(8,128)(2,1)S(1)}) custom-call(f32[3,3,64]{2,1,0:T(4,128)} %rot_hbm.1, bf16[3,32,768]{2,1,0:T(8,128)(2,1)} %bitcast.5), custom_call_target="tpu_custom_call" | custom-call | tf_op jit(solution)/shard_map/load/pallas_call | solution.py:285
  7.2 0.5 collective-permute-done.refs_1_
  7.7 0.9 %rows.1 = (bf16[3,64,768]{2,1,0:T(8,128)(2,1)S(1)}, f32[16,1,2304]{2,1,0:T(1,128)}) custom-call(s32[1]{0:T(128)} %bitcast.1.col, f32[3,3,64]{2,1,0:T(4,128)S(1)} %get-tuple-element.15.rot_ref, bf16[3,32,768]{2,1,0:T(8,128)(2,1)S(1)} %get-tuple-element.16.refs_0_, bf16[3,32,768]{2,1,0:T(8,128)(2,1)S(1)} %collective-permute-done.refs_1_), custom_call_target="tpu_custom_call" | custom-call | tf_op jit(solution)/shard_map/rows/pallas_call | solution.py:294
  8.6 6.2 %all-to-all-start = ((f32[16,1,2304]{2,1,0:T(1,128)}), f32[16,1,2304]{2,1,0:T(1,128)S(1)}, u32[]{:S(2)}, u32[]{:S(2)}) async-start(f32[16,1,2304]{2,1,0:T(1,128)} %get-tuple-element.17), calls=%async_computation | async-start | bytes 294912 | tf_op jit(solution)/shard_map/all_to_all | solution.py:305
  14.8 0.0 collective-permute-done.1.refs_0_
  14.8 3.4 %collective-permute-start.2 = (bf16[3,32,768]{2,1,0:T(8,128)(2,1)S(1)}, bf16[3,32,768]{2,1,0:T(8,128)(2,1)S(1)}, u32[]{:S(2)}, u32[]{:S(2)}) collective-permute-start(bf16[3,32,768]{2,1,0:T(8,128)(2,1)S(1)} %pick.1), channel_id=1, source_target_pairs={{0,1},{2,3},{4,5},{6,7},{8,9},{10,11},{12,13},{14,15},{17,16},{19,... | collective-permute-start | bytes 442376 | tf_op jit(solution)/shard_map/ppermute | solution.py:269
  18.3 3.7 %collective-permute-done.2.refs_1_ = bf16[3,32,768]{2,1,0:T(8,128)(2,1)S(1)} collective-permute-done((bf16[3,32,768]{2,1,0:T(8,128)(2,1)S(1)}, bf16[3,32,768]{2,1,0:T(8,128)(2,1)S(1)}, u32[]{:S(2)}, u32[]{:S(2)}) %collective-permute-start.2) | collective-permute-done | bytes 147488 | tf_op jit(solution)/shard_map/ppermute | solution.py:269
  21.9 1.1 %all-to-all-done.centres_ref = f32[16,1,2304]{2,1,0:T(1,128)S(1)} async-done(((f32[16,1,2304]{2,1,0:T(1,128)}), f32[16,1,2304]{2,1,0:T(1,128)S(1)}, u32[]{:S(2)}, u32[]{:S(2)}) %all-to-all-start) | async-done | bytes 147488 | tf_op jit(solution)/shard_map/all_to_all | solution.py:305
  23.0 1.6 %collective-permute-start.5 = (bf16[3,64,768]{2,1,0:T(8,128)(2,1)S(1)}, bf16[3,64,768]{2,1,0:T(8,128)(2,1)S(1)}, u32[]{:S(2)}, u32[]{:S(2)}) collective-permute-start(bf16[3,64,768]{2,1,0:T(8,128)(2,1)S(1)} %assemble.1.refs_0_), channel_id=1, source_target_pairs={{12,0},{13,1},{14,2},{15,3},{8,4},{9,5},{10,6},{11,7},{4,8},{5,9},... | collective-permute-start | bytes 884744 | tf_op jit(solution)/shard_map/ppermute | solution.py:269
  24.6 0.6 collective-permute-start.4
  25.1 1.4 %collective-permute-start.3 = (bf16[3,64,768]{2,1,0:T(8,128)(2,1)S(1)}, bf16[3,64,768]{2,1,0:T(8,128)(2,1)S(1)}, u32[]{:S(2)}, u32[]{:S(2)}) collective-permute-start(bf16[3,64,768]{2,1,0:T(8,128)(2,1)S(1)} %assemble.1.refs_0_), channel_id=1, source_target_pairs={{4,0},{5,1},{6,2},{7,3},{0,4},{1,5},{2,6},{3,7},{12,8},{13,9},{14,... | collective-permute-start | bytes 884744 | tf_op jit(solution)/shard_map/ppermute | solution.py:269
  26.6 7.5 %weighted_fit.1 = f32[32,8,128]{2,1,0:T(8,128)S(1)} custom-call(s32[1]{0:T(128)} %bitcast.row, s32[1]{0:T(128)} %bitcast.1.col, f32[768,6144]{1,0:T(8,128)} %inv_ref.1, f32[16,1,2304]{2,1,0:T(1,128)S(1)} %all-to-all-done.centres_ref, bf16[3,64,768]{2,1,0:T(8,128)(2,1)S(1)} %get-tuple-element.18.rows_ref), custom_call_target="tpu_custom_call" | custom-call | flops 28311552 | bytes 18874368 | tf_op jit(solution)/shard_map/weighted_fit/pallas_call | solution.py:329
  34.1 13.1 %all_to_all.10.fits_ref = f32[32,8,128]{2,1,0:T(8,128)S(1)} all-to-all(f32[32,8,128]{2,1,0:T(8,128)S(1)} %weighted_fit.1), channel_id=1, replica_groups=mesh['row'=16,'col'=2] {'row','col'}, dimensions={0} | all-to-all | bytes 262144 | tf_op jit(solution)/shard_map/all_to_all | solution.py:346
  47.1 0.0 collective-permute-done.5.refs_3_
  47.1 0.0 collective-permute-done.4.refs_2_
  47.1 0.0 collective-permute-done.3.refs_1_
  47.2 0.1 stack_panel.1
  47.2 0.1 collective-permute-start.6
  47.3 7.2 %steps_and_even_tiles.1 = (f32[768,6144]{1,0:T(8,128)}, f32[3,3,32]{2,1,0:T(4,128)}, f32[9,64,128]{2,1,0:T(8,128)S(1)}, bf16[768,192]{1,0:T(8,128)(2,1)S(1)}) custom-call(s32[1]{0:T(128)} %bitcast.row, s32[1]{0:T(128)} %bitcast.1.col, f32[32,8,128]{2,1,0:T(8,128)S(1)} %all_to_all.10.fits_ref, bf16[3,64,768]{2,1,0:T(8,128)(2,1)S(1)} %get-tuple-element.18.rows_ref, ...), custom_call_target="tpu_custom_call" | custom-call | flops 905969664 | bytes 9437184 | tf_op jit(solution)/shard_map/steps_and_even_tiles/pallas_call | solution.py:365
  54.5 0.0 collective-permute-done.6.panel_ref
  54.5 4.7 %odd_tiles.1 = f32[768,6144]{1,0:T(8,128)} custom-call(s32[1]{0:T(128)} %bitcast.row, s32[1]{0:T(128)} %bitcast.1.col, f32[768,6144]{1,0:T(8,128)} %get-tuple-element.24.before_ref, f32[9,64,128]{2,1,0:T(8,128)S(1)} %get-tuple-element.25.wide_ref, bf16[768,192]{1,0:T(8,128)(2,1)S(1)} %get-tuple-element.26.rows_dev_ref, ...), custom_call_target="tpu_custom_call", output_to_operand_aliasing={{}: (2, {})} | custom-call | flops 905969664 | bytes 9437184 | tf_op jit(solution)/shard_map/odd_tiles/pallas_call | solution.py:384
  (2 shorter events, 0.1 us)
Async XLA Ops:
  0.6 7.1 %collective-permute-start = (bf16[3,32,768]{2,1,0:T(8,128)(2,1)}, bf16[3,32,768]{2,1,0:T(8,128)(2,1)S(1)}, u32[]{:S(2)}, u32[]{:S(2)}) collective-permute-start(bf16[3,32,768]{2,1,0:T(8,128)(2,1)} %bitcast.3), channel_id=1, source_target_pairs={{1,0},{0,1},{3,2},{2,3},{5,4},{4,5},{7,6},{6,7},{9,8},{8,9},{11,10... | collective-permute-start | bytes 442376 | tf_op jit(solution)/shard_map/ppermute | solution.py:269
  3.6 11.2 %collective-permute-start.1 = (bf16[3,32,768]{2,1,0:T(8,128)(2,1)}, bf16[3,32,768]{2,1,0:T(8,128)(2,1)S(1)}, u32[]{:S(2)}, u32[]{:S(2)}) collective-permute-start(bf16[3,32,768]{2,1,0:T(8,128)(2,1)} %bitcast.4), channel_id=1, source_target_pairs={{16,0},{17,1},{18,2},{19,3},{20,4},{21,5},{22,6},{23,7},{24,8},{25... | collective-permute-start | bytes 442376 | tf_op jit(solution)/shard_map/ppermute | solution.py:269
  8.6 14.4 %all-to-all-start = ((f32[16,1,2304]{2,1,0:T(1,128)}), f32[16,1,2304]{2,1,0:T(1,128)S(1)}, u32[]{:S(2)}, u32[]{:S(2)}) async-start(f32[16,1,2304]{2,1,0:T(1,128)} %get-tuple-element.17), calls=%async_computation | async-start | bytes 294912 | tf_op jit(solution)/shard_map/all_to_all | solution.py:305
  14.8 7.1 %collective-permute-start.2 = (bf16[3,32,768]{2,1,0:T(8,128)(2,1)S(1)}, bf16[3,32,768]{2,1,0:T(8,128)(2,1)S(1)}, u32[]{:S(2)}, u32[]{:S(2)}) collective-permute-start(bf16[3,32,768]{2,1,0:T(8,128)(2,1)S(1)} %pick.1), channel_id=1, source_target_pairs={{0,1},{2,3},{4,5},{6,7},{8,9},{10,11},{12,13},{14,15},{17,16},{19,... | collective-permute-start | bytes 442376 | tf_op jit(solution)/shard_map/ppermute | solution.py:269
  23.0 24.1 %collective-permute-start.5 = (bf16[3,64,768]{2,1,0:T(8,128)(2,1)S(1)}, bf16[3,64,768]{2,1,0:T(8,128)(2,1)S(1)}, u32[]{:S(2)}, u32[]{:S(2)}) collective-permute-start(bf16[3,64,768]{2,1,0:T(8,128)(2,1)S(1)} %assemble.1.refs_0_), channel_id=1, source_target_pairs={{12,0},{13,1},{14,2},{15,3},{8,4},{9,5},{10,6},{11,7},{4,8},{5,9},... | collective-permute-start | bytes 884744 | tf_op jit(solution)/shard_map/ppermute | solution.py:269
  24.6 22.6 %collective-permute-start.4 = (bf16[3,64,768]{2,1,0:T(8,128)(2,1)S(1)}, bf16[3,64,768]{2,1,0:T(8,128)(2,1)S(1)}, u32[]{:S(2)}, u32[]{:S(2)}) collective-permute-start(bf16[3,64,768]{2,1,0:T(8,128)(2,1)S(1)} %assemble.1.refs_0_), channel_id=1, source_target_pairs={{8,0},{9,1},{10,2},{11,3},{12,4},{13,5},{14,6},{15,7},{0,8},{1,9},... | collective-permute-start | bytes 884744 | tf_op jit(solution)/shard_map/ppermute | solution.py:269
  25.1 22.0 %collective-permute-start.3 = (bf16[3,64,768]{2,1,0:T(8,128)(2,1)S(1)}, bf16[3,64,768]{2,1,0:T(8,128)(2,1)S(1)}, u32[]{:S(2)}, u32[]{:S(2)}) collective-permute-start(bf16[3,64,768]{2,1,0:T(8,128)(2,1)S(1)} %assemble.1.refs_0_), channel_id=1, source_target_pairs={{4,0},{5,1},{6,2},{7,3},{0,4},{1,5},{2,6},{3,7},{12,8},{13,9},{14,... | collective-permute-start | bytes 884744 | tf_op jit(solution)/shard_map/ppermute | solution.py:269
  47.2 7.3 %collective-permute-start.6 = (bf16[4,3,64,768]{3,2,1,0:T(8,128)(2,1)S(1)}, bf16[4,3,64,768]{3,2,1,0:T(8,128)(2,1)S(1)}, u32[]{:S(2)}, u32[]{:S(2)}) collective-permute-start(bf16[4,3,64,768]{3,2,1,0:T(8,128)(2,1)S(1)} %stack_panel.1), channel_id=1, source_target_pairs={{2,0},{3,1},{0,2},{1,3},{6,4},{7,5},{4,6},{5,7},{10,8},{11,9},{8,1... | collective-permute-start | bytes 3538952 | tf_op jit(solution)/shard_map/ppermute | solution.py:269

commit v20 on v19

--- a/solution.py
+++ b/solution.py
@@ -325,7 +325,7 @@
     )(row, col, centres, rows_all, *far, *across)
     evens = [own_block] + [from_member(own_block, 2 * step) for step in range(1, half)]
 
-    height = 64 if width % 64 == 0 else 8
+    height = 32 if width % 32 == 0 else 8
     message = pl.pallas_call(
         functools.partial(weighted_fit_kernel, members),
         in_specs=[smem(), smem(), hbm(), vmem(), vmem()],

time: 59.6 us -> 60.8 us (1.020)
  Pallas kernels: 21.4 us -> 22.6 us
    pallas_call x1, Pallas kernels: 7.48 us -> 8.67 us  [per_device(): pl.pallas_call(functools.partial(weighted_fit_kernel, members), in_specs=...]
  transfers between devices with their start and end apart: 8 -> 8, of which waited for: 3 -> 3; matrix products, arithmetic and copies ran while one was open for 0% -> 0% of each run, Pallas kernels for 28% -> 29%
where the time goes in v20:
time: 60.8 us; the launch traced here: 60.5 us
  Pallas kernels  22.6 us (37%)
  starting transfers between devices  18.8 us (31%)
  blocking collectives  13.1 us (22%)
  waiting for transfers between devices  5.24 us (9%)
  between operations  0.72 us (1%)
    all_to_all x1, blocking collectives, per_device(): lax.all_to_all(message, ('row', 'col'), split_axis=0, concat_axis=0, tile...  13.1 us
    ppermute x7, starting transfers between devices, move(): return lax.ppermute(value, ('row', 'col'), pairs)  12.6 us
    pallas_call x1, Pallas kernels, per_device(): pl.pallas_call(functools.partial(weighted_fit_kernel, members), in_specs=...  8.67 us
    pallas_call x1, Pallas kernels, per_device(): pl.pallas_call(functools.partial(first_tiles_kernel, half), grid_spec=plt...  7.22 us
    all_to_all x1, starting transfers between devices, per_device(): lax.all_to_all(repeated, 'row', split_axis=0, concat_axis=0, tiled=True)  6.19 us
    pallas_call x1, Pallas kernels, per_device(): pl.pallas_call(functools.partial(last_tiles_kernel, half), grid_spec=pltp...  4.73 us
    ppermute x7, waiting for transfers between devices, move(): return lax.ppermute(value, ('row', 'col'), pairs)  4.19 us
  transfers between devices with their start and end apart: 8, of which 3 were waited for; matrix products, arithmetic and copies ran while one was open for 0% of the time, Pallas kernels for 29%

profile of v20, /device:TPU:0, one launch (start us, length us, event | category | flops | bytes accessed | tf_op | source)
XLA Modules:
  0.0 60.5 jit_solution(11748846685525245813)
XLA Ops:
  0.6 3.0 %collective-permute-start = (bf16[3,32,768]{2,1,0:T(8,128)(2,1)}, bf16[3,32,768]{2,1,0:T(8,128)(2,1)S(1)}, u32[]{:S(2)}, u32[]{:S(2)}) collective-permute-start(bf16[3,32,768]{2,1,0:T(8,128)(2,1)} %bitcast.3), channel_id=1, source_target_pairs={{1,0},{0,1},{3,2},{2,3},{5,4},{4,5},{7,6},{6,7},{9,8},{8,9},{11,10... | collective-permute-start | bytes 442376 | tf_op jit(solution)/shard_map/ppermute | solution.py:269
  3.6 2.6 %collective-permute-start.1 = (bf16[3,32,768]{2,1,0:T(8,128)(2,1)}, bf16[3,32,768]{2,1,0:T(8,128)(2,1)S(1)}, u32[]{:S(2)}, u32[]{:S(2)}) collective-permute-start(bf16[3,32,768]{2,1,0:T(8,128)(2,1)} %bitcast.4), channel_id=1, source_target_pairs={{16,0},{17,1},{18,2},{19,3},{20,4},{21,5},{22,6},{23,7},{24,8},{25... | collective-permute-start | bytes 442376 | tf_op jit(solution)/shard_map/ppermute | solution.py:269
  6.2 1.0 %load.1 = (f32[3,3,64]{2,1,0:T(4,128)S(1)}, bf16[3,32,768]{2,1,0:T(8,128)(2,1)S(1)}) custom-call(f32[3,3,64]{2,1,0:T(4,128)} %rot_hbm.1, bf16[3,32,768]{2,1,0:T(8,128)(2,1)} %bitcast.5), custom_call_target="tpu_custom_call" | custom-call | tf_op jit(solution)/shard_map/load/pallas_call | solution.py:285
  7.2 0.5 collective-permute-done.refs_1_
  7.7 0.9 %rows.1 = (bf16[3,64,768]{2,1,0:T(8,128)(2,1)S(1)}, f32[16,1,2304]{2,1,0:T(1,128)}) custom-call(s32[1]{0:T(128)} %bitcast.1.col, f32[3,3,64]{2,1,0:T(4,128)S(1)} %get-tuple-element.15.rot_ref, bf16[3,32,768]{2,1,0:T(8,128)(2,1)S(1)} %get-tuple-element.16.refs_0_, bf16[3,32,768]{2,1,0:T(8,128)(2,1)S(1)} %collective-permute-done.refs_1_), custom_call_target="tpu_custom_call" | custom-call | tf_op jit(solution)/shard_map/rows/pallas_call | solution.py:294
  8.6 6.2 %all-to-all-start = ((f32[16,1,2304]{2,1,0:T(1,128)}), f32[16,1,2304]{2,1,0:T(1,128)S(1)}, u32[]{:S(2)}, u32[]{:S(2)}) async-start(f32[16,1,2304]{2,1,0:T(1,128)} %get-tuple-element.17), calls=%async_computation | async-start | bytes 294912 | tf_op jit(solution)/shard_map/all_to_all | solution.py:305
  14.8 0.0 collective-permute-done.1.refs_0_
  14.8 3.4 %collective-permute-start.2 = (bf16[3,32,768]{2,1,0:T(8,128)(2,1)S(1)}, bf16[3,32,768]{2,1,0:T(8,128)(2,1)S(1)}, u32[]{:S(2)}, u32[]{:S(2)}) collective-permute-start(bf16[3,32,768]{2,1,0:T(8,128)(2,1)S(1)} %pick.1), channel_id=1, source_target_pairs={{0,1},{2,3},{4,5},{6,7},{8,9},{10,11},{12,13},{14,15},{17,16},{19,... | collective-permute-start | bytes 442376 | tf_op jit(solution)/shard_map/ppermute | solution.py:269
  18.3 3.7 %collective-permute-done.2.refs_1_ = bf16[3,32,768]{2,1,0:T(8,128)(2,1)S(1)} collective-permute-done((bf16[3,32,768]{2,1,0:T(8,128)(2,1)S(1)}, bf16[3,32,768]{2,1,0:T(8,128)(2,1)S(1)}, u32[]{:S(2)}, u32[]{:S(2)}) %collective-permute-start.2) | collective-permute-done | bytes 147488 | tf_op jit(solution)/shard_map/ppermute | solution.py:269
  21.9 1.1 %all-to-all-done.centres_ref = f32[16,1,2304]{2,1,0:T(1,128)S(1)} async-done(((f32[16,1,2304]{2,1,0:T(1,128)}), f32[16,1,2304]{2,1,0:T(1,128)S(1)}, u32[]{:S(2)}, u32[]{:S(2)}) %all-to-all-start) | async-done | bytes 147488 | tf_op jit(solution)/shard_map/all_to_all | solution.py:305
  23.0 1.6 %collective-permute-start.5 = (bf16[3,64,768]{2,1,0:T(8,128)(2,1)S(1)}, bf16[3,64,768]{2,1,0:T(8,128)(2,1)S(1)}, u32[]{:S(2)}, u32[]{:S(2)}) collective-permute-start(bf16[3,64,768]{2,1,0:T(8,128)(2,1)S(1)} %assemble.1.refs_0_), channel_id=1, source_target_pairs={{12,0},{13,1},{14,2},{15,3},{8,4},{9,5},{10,6},{11,7},{4,8},{5,9},... | collective-permute-start | bytes 884744 | tf_op jit(solution)/shard_map/ppermute | solution.py:269
  24.6 0.6 collective-permute-start.4
  25.1 1.4 %collective-permute-start.3 = (bf16[3,64,768]{2,1,0:T(8,128)(2,1)S(1)}, bf16[3,64,768]{2,1,0:T(8,128)(2,1)S(1)}, u32[]{:S(2)}, u32[]{:S(2)}) collective-permute-start(bf16[3,64,768]{2,1,0:T(8,128)(2,1)S(1)} %assemble.1.refs_0_), channel_id=1, source_target_pairs={{4,0},{5,1},{6,2},{7,3},{0,4},{1,5},{2,6},{3,7},{12,8},{13,9},{14,... | collective-permute-start | bytes 884744 | tf_op jit(solution)/shard_map/ppermute | solution.py:269
  26.6 8.7 %weighted_fit.1 = f32[32,8,128]{2,1,0:T(8,128)S(1)} custom-call(s32[1]{0:T(128)} %bitcast.row, s32[1]{0:T(128)} %bitcast.1.col, f32[768,6144]{1,0:T(8,128)} %inv_ref.1, f32[16,1,2304]{2,1,0:T(1,128)S(1)} %all-to-all-done.centres_ref, bf16[3,64,768]{2,1,0:T(8,128)(2,1)S(1)} %get-tuple-element.18.rows_ref), custom_call_target="tpu_custom_call" | custom-call | flops 28311552 | bytes 18874368 | tf_op jit(solution)/shard_map/weighted_fit/pallas_call | solution.py:329
  35.3 13.1 %all_to_all.10.fits_ref = f32[32,8,128]{2,1,0:T(8,128)S(1)} all-to-all(f32[32,8,128]{2,1,0:T(8,128)S(1)} %weighted_fit.1), channel_id=1, replica_groups=mesh['row'=16,'col'=2] {'row','col'}, dimensions={0} | all-to-all | bytes 262144 | tf_op jit(solution)/shard_map/all_to_all | solution.py:346
  48.3 0.0 collective-permute-done.5.refs_3_
  48.3 0.0 collective-permute-done.4.refs_2_
  48.3 0.0 collective-permute-done.3.refs_1_
  48.3 0.1 stack_panel.1
  48.4 0.1 collective-permute-start.6
  48.5 7.2 %steps_and_even_tiles.1 = (f32[768,6144]{1,0:T(8,128)}, f32[3,3,32]{2,1,0:T(4,128)}, f32[9,64,128]{2,1,0:T(8,128)S(1)}, bf16[768,192]{1,0:T(8,128)(2,1)S(1)}) custom-call(s32[1]{0:T(128)} %bitcast.row, s32[1]{0:T(128)} %bitcast.1.col, f32[32,8,128]{2,1,0:T(8,128)S(1)} %all_to_all.10.fits_ref, bf16[3,64,768]{2,1,0:T(8,128)(2,1)S(1)} %get-tuple-element.18.rows_ref, ...), custom_call_target="tpu_custom_call" | custom-call | flops 905969664 | bytes 9437184 | tf_op jit(solution)/shard_map/steps_and_even_tiles/pallas_call | solution.py:365
  55.7 0.0 collective-permute-done.6.panel_ref
  55.7 4.7 %odd_tiles.1 = f32[768,6144]{1,0:T(8,128)} custom-call(s32[1]{0:T(128)} %bitcast.row, s32[1]{0:T(128)} %bitcast.1.col, f32[768,6144]{1,0:T(8,128)} %get-tuple-element.24.before_ref, f32[9,64,128]{2,1,0:T(8,128)S(1)} %get-tuple-element.25.wide_ref, bf16[768,192]{1,0:T(8,128)(2,1)S(1)} %get-tuple-element.26.rows_dev_ref, ...), custom_call_target="tpu_custom_call", output_to_operand_aliasing={{}: (2, {})} | custom-call | flops 905969664 | bytes 9437184 | tf_op jit(solution)/shard_map/odd_tiles/pallas_call | solution.py:384
  (2 shorter events, 0.1 us)
Async XLA Ops:
  0.6 7.1 %collective-permute-start = (bf16[3,32,768]{2,1,0:T(8,128)(2,1)}, bf16[3,32,768]{2,1,0:T(8,128)(2,1)S(1)}, u32[]{:S(2)}, u32[]{:S(2)}) collective-permute-start(bf16[3,32,768]{2,1,0:T(8,128)(2,1)} %bitcast.3), channel_id=1, source_target_pairs={{1,0},{0,1},{3,2},{2,3},{5,4},{4,5},{7,6},{6,7},{9,8},{8,9},{11,10... | collective-permute-start | bytes 442376 | tf_op jit(solution)/shard_map/ppermute | solution.py:269
  3.6 11.2 %collective-permute-start.1 = (bf16[3,32,768]{2,1,0:T(8,128)(2,1)}, bf16[3,32,768]{2,1,0:T(8,128)(2,1)S(1)}, u32[]{:S(2)}, u32[]{:S(2)}) collective-permute-start(bf16[3,32,768]{2,1,0:T(8,128)(2,1)} %bitcast.4), channel_id=1, source_target_pairs={{16,0},{17,1},{18,2},{19,3},{20,4},{21,5},{22,6},{23,7},{24,8},{25... | collective-permute-start | bytes 442376 | tf_op jit(solution)/shard_map/ppermute | solution.py:269
  8.6 14.4 %all-to-all-start = ((f32[16,1,2304]{2,1,0:T(1,128)}), f32[16,1,2304]{2,1,0:T(1,128)S(1)}, u32[]{:S(2)}, u32[]{:S(2)}) async-start(f32[16,1,2304]{2,1,0:T(1,128)} %get-tuple-element.17), calls=%async_computation | async-start | bytes 294912 | tf_op jit(solution)/shard_map/all_to_all | solution.py:305
  14.8 7.1 %collective-permute-start.2 = (bf16[3,32,768]{2,1,0:T(8,128)(2,1)S(1)}, bf16[3,32,768]{2,1,0:T(8,128)(2,1)S(1)}, u32[]{:S(2)}, u32[]{:S(2)}) collective-permute-start(bf16[3,32,768]{2,1,0:T(8,128)(2,1)S(1)} %pick.1), channel_id=1, source_target_pairs={{0,1},{2,3},{4,5},{6,7},{8,9},{10,11},{12,13},{14,15},{17,16},{19,... | collective-permute-start | bytes 442376 | tf_op jit(solution)/shard_map/ppermute | solution.py:269
  23.0 25.3 %collective-permute-start.5 = (bf16[3,64,768]{2,1,0:T(8,128)(2,1)S(1)}, bf16[3,64,768]{2,1,0:T(8,128)(2,1)S(1)}, u32[]{:S(2)}, u32[]{:S(2)}) collective-permute-start(bf16[3,64,768]{2,1,0:T(8,128)(2,1)S(1)} %assemble.1.refs_0_), channel_id=1, source_target_pairs={{12,0},{13,1},{14,2},{15,3},{8,4},{9,5},{10,6},{11,7},{4,8},{5,9},... | collective-permute-start | bytes 884744 | tf_op jit(solution)/shard_map/ppermute | solution.py:269
  24.6 23.8 %collective-permute-start.4 = (bf16[3,64,768]{2,1,0:T(8,128)(2,1)S(1)}, bf16[3,64,768]{2,1,0:T(8,128)(2,1)S(1)}, u32[]{:S(2)}, u32[]{:S(2)}) collective-permute-start(bf16[3,64,768]{2,1,0:T(8,128)(2,1)S(1)} %assemble.1.refs_0_), channel_id=1, source_target_pairs={{8,0},{9,1},{10,2},{11,3},{12,4},{13,5},{14,6},{15,7},{0,8},{1,9},... | collective-permute-start | bytes 884744 | tf_op jit(solution)/shard_map/ppermute | solution.py:269
  25.1 23.2 %collective-permute-start.3 = (bf16[3,64,768]{2,1,0:T(8,128)(2,1)S(1)}, bf16[3,64,768]{2,1,0:T(8,128)(2,1)S(1)}, u32[]{:S(2)}, u32[]{:S(2)}) collective-permute-start(bf16[3,64,768]{2,1,0:T(8,128)(2,1)S(1)} %assemble.1.refs_0_), channel_id=1, source_target_pairs={{4,0},{5,1},{6,2},{7,3},{0,4},{1,5},{2,6},{3,7},{12,8},{13,9},{14,... | collective-permute-start | bytes 884744 | tf_op jit(solution)/shard_map/ppermute | solution.py:269
  48.4 7.3 %collective-permute-start.6 = (bf16[4,3,64,768]{3,2,1,0:T(8,128)(2,1)S(1)}, bf16[4,3,64,768]{3,2,1,0:T(8,128)(2,1)S(1)}, u32[]{:S(2)}, u32[]{:S(2)}) collective-permute-start(bf16[4,3,64,768]{3,2,1,0:T(8,128)(2,1)S(1)} %stack_panel.1), channel_id=1, source_target_pairs={{2,0},{3,1},{0,2},{1,3},{6,4},{7,5},{4,6},{5,7},{10,8},{11,9},{8,1... | collective-permute-start | bytes 3538952 | tf_op jit(solution)/shard_map/ppermute | solution.py:269
